TPU v7x, 32 devices: a whole 2x2x4 slice. The times are simulated.
32 devices in a mesh: seq: 16 (over z, y, x), head: 2 (over core).
Axes of the slice: x: 2, y: 2, z: 4, core: 2. Of those that a mesh axis runs over, the one named last changes fastest.
Arguments:
- trunk_query: bfloat16 [8192, 16, 128], P('seq', 'head'), may hold values from -5 to 5
- trunk_key: bfloat16 [8192, 16, 128], P('seq', 'head'), may hold values from -5 to 5
- trunk_value: bfloat16 [8192, 16, 128], P('seq', 'head'), may hold values from -5 to 5
- trunk_wquery: bfloat16 [8192, 16, 128], P('seq', 'head'), may hold values from -5 to 5
- trunk_wkey: bfloat16 [8192, 4, 128], P('seq', 'head'), may hold values from -5 to 5
- trunk_wvalue: bfloat16 [8192, 4, 128], P('seq', 'head'), may hold values from -5 to 5
- branch_query: bfloat16 [16384, 16, 128], P('seq', 'head'), may hold values from -5 to 5
- branch_wquery: bfloat16 [16384, 16, 128], P('seq', 'head'), may hold values from -5 to 5
- branch_wkey: bfloat16 [16384, 4, 128], P('seq', 'head'), may hold values from -5 to 5
- branch_wvalue: bfloat16 [16384, 4, 128], P('seq', 'head'), may hold values from -5 to 5
- level_gain: float32 [16, 11], P('head'), may hold values from 0.1 to 1.9
- fork_block: int32 [16], P('seq'), may hold values from 0 to 3
Outputs:
- trunk_out: bfloat16 [8192, 16, 128], P('seq', 'head')
- branch_out: bfloat16 [16384, 16, 128], P('seq', 'head')
All inputs are finite; a program needn't handle non-finite values.
Results may differ from a plain program's by a relative error of at most 0.0045.
The roundings to bfloat16 on the way count: a program that leaves them out, or rounds other values in their place, can miss the bound.
Values may be sent and summed in bfloat16 or wider, within the bound.
No kernel may reach another device: no remote copies, remote signals or barrier semaphores. Data moves between devices by JAX's collectives and lax.ppermute only.
A program may use at most 128 MiB of HBM per device.

v0:
```python
import functools
import math

import jax
import jax.numpy as jnp
from jax import lax
from jax.experimental import pallas as pl
from jax.experimental.pallas import tpu as pltpu
from jax.sharding import PartitionSpec as P

BLK = 128
WIN = 512
COLS = 4
MASKED = -1e30
F32 = jnp.float32
BF16 = jnp.bfloat16
VMEM_BYTES = 48 * 1024 * 1024


def params():
    return pltpu.CompilerParams(vmem_limit_bytes=VMEM_BYTES)


def smem():
    return pl.BlockSpec(memory_space=pltpu.SMEM)


def gain_factor(level, width):
    return 1.0 / math.sqrt(width * BLK * 2 ** max(level - 1, 0))


def every(rows_ref, wide, count, each):
    return wide[pl.ds(each, rows_ref.shape[0] // count, stride=count), :].astype(BF16)


def state_kernel(depth, heads, gain_ref, k_ref, v_ref, *rest):
    piece_refs, sum_ref, kf, vf, levels = rest[:COLS], rest[COLS], *rest[COLS + 1 :]
    block = pl.program_id(0)
    width = k_ref.shape[1]

    @pl.when(block == 0)
    def _():
        levels[...] = jnp.zeros_like(levels)

    kf[...] = k_ref[...].astype(F32)
    vf[...] = v_ref[...].astype(F32)
    per_piece = heads // COLS
    for h in range(heads):
        k = every(k_ref, kf, heads, h)
        v = every(v_ref, vf, heads, h)
        state = lax.dot_general(k, v, (((0,), (0,)), ((), ())), preferred_element_type=F32)
        before = jnp.zeros_like(state)
        merged = state
        for bit in range(depth):
            held = levels[bit, h]
            present = (block >> bit) & 1
            before = before + held * (present.astype(F32) * gain_ref[h, bit + 1] * gain_factor(bit + 1, width))
            low = (2 << bit) - 1
            merged = merged + held * ((block & low) == low).astype(F32)
        for bit in range(depth):
            low = (2 << bit) - 1
            newest = ((block + 1) & low) == (1 << bit)
            levels[bit, h] = jnp.where(newest, merged, levels[bit, h])
        piece_refs[h // per_piece][0, h % per_piece] = before.astype(BF16)
        sum_ref[h] = merged.astype(BF16)


def block_sums(gain, keys, values, heads, depth):
    blocks = 1 << depth
    rows, width = keys.shape[0] // blocks, keys.shape[1]
    piece = jax.ShapeDtypeStruct((blocks - 1, heads // COLS, width, width), BF16)
    at_block = pl.BlockSpec((rows, width), lambda b: (b, 0))
    return pl.pallas_call(
        functools.partial(state_kernel, depth, heads),
        grid=(blocks,),
        in_specs=[smem(), at_block, at_block],
        out_specs=[
            pl.BlockSpec((1, heads // COLS, width, width), lambda b: (jnp.maximum(b - 1, 0), 0, 0, 0))
        ]
        * COLS
        + [pl.BlockSpec((heads, width, width), lambda b: (0, 0, 0))],
        out_shape=[piece] * COLS + [jax.ShapeDtypeStruct((heads, width, width), BF16)],
        scratch_shapes=[
            pltpu.VMEM((rows, width), F32),
            pltpu.VMEM((rows, width), F32),
            pltpu.VMEM((depth, heads, width, width), F32),
        ],
        compiler_params=params(),
        cost_estimate=pl.CostEstimate(
            flops=2 * keys.size * width, bytes_accessed=4 * keys.size + 2 * heads * width * width * blocks, transcendentals=0
        ),
        name="block_sums",
    )(gain, keys, values)


def cross_kernel(count, depth, width, where_ref, gain_ref, sums_ref, out_ref):
    bits = count.bit_length() - 1
    heads = gain_ref.shape[0]
    head = where_ref[0] * heads // count
    group = [sums_ref[s].astype(F32) for s in range(count)]
    total = [jnp.zeros_like(group[0]) for _ in range(count)]
    for bit in range(bits):
        level = depth + bit + 1
        weight = gain_ref[head, level] * gain_factor(level, width)
        scaled = [g * weight for g in group]
        for d in range(count):
            if d >> bit & 1:
                total[d] = total[d] + scaled[(d >> bit) ^ 1]
        group = [group[2 * i] + group[2 * i + 1] for i in range(len(group) // 2)]
    last = total[count - 1].astype(BF16)
    for d in range(count):
        out_ref[d, 0] = total[d].astype(BF16)
        out_ref[d, 1] = last


def cross_sums(where, gain, sums, depth, width):
    count, rows, lanes = sums.shape
    return pl.pallas_call(
        functools.partial(cross_kernel, count, depth, width),
        in_specs=[smem(), smem(), pl.BlockSpec(memory_space=pltpu.VMEM)],
        out_specs=pl.BlockSpec(memory_space=pltpu.VMEM),
        out_shape=jax.ShapeDtypeStruct((count, 2, rows, lanes), BF16),
        compiler_params=params(),
        cost_estimate=pl.CostEstimate(flops=20 * sums.size, bytes_accessed=6 * sums.size, transcendentals=0),
        name="cross_sums",
    )(where, gain, sums)


def place(src_ref, wide, dst, start, groups):
    tokens = src_ref.shape[0] // groups
    wide[...] = src_ref[...].astype(F32)
    for g in range(groups):
        part = wide[pl.ds(g, tokens, stride=groups), :].astype(BF16)
        dst[g, pl.ds(start, tokens), : src_ref.shape[1]] = part


def window_rows(queries, keys, values, bias=None):
    rows, width = queries.shape
    logits = lax.dot_general(queries, keys, (((1,), (1,)), ((), ())), preferred_element_type=F32)
    row = lax.broadcasted_iota(jnp.int32, (rows, rows), 0)
    col = lax.broadcasted_iota(jnp.int32, (rows, rows), 1)
    first = jnp.where(col > row, logits[:, :rows], MASKED)
    last = jnp.where(col <= row, logits[:, -rows:], MASKED)
    logits = jnp.concatenate([first, logits[:, rows:-rows], last], axis=1)
    if bias is not None:
        logits = logits + bias
    top = jnp.max(logits, axis=1, keepdims=True)
    weights = jnp.exp2((logits - top) * (math.log2(math.e) / math.sqrt(width))).astype(BF16)
    both = jnp.dot(weights, values, preferred_element_type=F32)
    return both[:, :width] / both[:, width:]


def square_sums(total):
    ones = jnp.ones((8, total.shape[1]), F32)
    return lax.dot_general(
        ones, total, (((1,), (1,)), ((), ())), precision=lax.Precision.HIGHEST, preferred_element_type=F32
    )


def far_kernel(heads, groups, q_ref, pk_ref, pv_ref, ck_ref, cv_ref, out_ref, qf, kf, kh, vh, of):
    step = pl.program_id(0)
    width = q_ref.shape[1]

    @pl.when(step == 0)
    def _():
        vh[:, :, width:] = jnp.ones((groups, vh.shape[1], width), BF16)
        place(pk_ref, kf, kh, 0, groups)
        place(ck_ref, kf, kh, WIN, groups)
        place(pv_ref, kf, vh, 0, groups)
        place(cv_ref, kf, vh, WIN, groups)

    qf[...] = q_ref[...].astype(F32)
    base = pl.multiple_of(step * BLK, BLK)
    for h in range(heads):
        g = h * groups // heads
        out = window_rows(
            every(q_ref, qf, heads, h), kh[g, pl.ds(base, WIN + BLK), :], vh[g, pl.ds(base, WIN + BLK), :]
        )
        of[pl.ds(h, BLK, stride=heads), :] = out
    out_ref[...] = of[...]


def attention_cost(tokens, heads, width, extra=0):
    span = WIN + BLK
    return pl.CostEstimate(
        flops=6 * tokens * heads * span * width + extra,
        bytes_accessed=12 * tokens * heads * width,
        transcendentals=tokens * heads * span,
    )


def far_attention(queries, keys, values, heads, groups):
    width = queries.shape[1]
    steps = queries.shape[0] // (BLK * heads) - WIN // BLK
    skip = WIN // BLK
    at_first = pl.BlockSpec((WIN * groups, width), lambda i: (0, 0))
    at_next = pl.BlockSpec((WIN * groups, width), lambda i: (1, 0))
    return pl.pallas_call(
        functools.partial(far_kernel, heads, groups),
        grid=(steps,),
        in_specs=[
            pl.BlockSpec((BLK * heads, width), lambda i: (i + skip, 0)),
            at_first,
            at_first,
            at_next,
            at_next,
        ],
        out_specs=pl.BlockSpec((BLK * heads, width), lambda i: (i, 0)),
        out_shape=jax.ShapeDtypeStruct((steps * BLK * heads, width), F32),
        scratch_shapes=[
            pltpu.VMEM((BLK * heads, width), F32),
            pltpu.VMEM((WIN * groups, width), F32),
            pltpu.VMEM((groups, 2 * WIN, width), BF16),
            pltpu.VMEM((groups, 2 * WIN, 2 * width), BF16),
            pltpu.VMEM((BLK * heads, width), F32),
        ],
        compiler_params=params(),
        cost_estimate=attention_cost(steps * BLK, heads, width),
        name="far_attention",
    )(queries, keys, values, keys, values)


def trunk_kernel(heads, groups, where_ref, gain_ref, q_ref, k_ref, v_ref, wq_ref, pk_ref, pv_ref, ck_ref, cv_ref, cross_ref, *rest):
    piece_refs, out_ref, square_ref = rest[:COLS], rest[COLS], rest[COLS + 1]
    qf, nf, tf, sf, kf, kh, vh, of, cs = rest[COLS + 2 :]
    step = pl.program_id(0)
    width = q_ref.shape[1]

    @pl.when(step == 0)
    def _():
        vh[:, :, width:] = jnp.ones((groups, vh.shape[1], width), BF16)
        place(pk_ref, kf, kh, 0, groups)
        place(ck_ref, kf, kh, WIN, groups)
        place(pv_ref, kf, vh, 0, groups)
        place(cv_ref, kf, vh, WIN, groups)
        cs[...] = cross_ref[:, 0].reshape(heads, width, width)

    qf[...] = wq_ref[...].astype(F32)
    nf[...] = q_ref[...].astype(F32)
    tf[...] = k_ref[...].astype(F32)
    sf[...] = v_ref[...].astype(F32)
    base = pl.multiple_of(step * BLK, BLK)
    span = WIN + BLK
    reach = jnp.where(where_ref[0] == 0, WIN - step * BLK, 0)
    bias = jnp.where(lax.broadcasted_iota(jnp.int32, (1, span), 1) < reach, MASKED, 0.0).astype(F32)
    row = lax.broadcasted_iota(jnp.int32, (BLK, BLK), 0)
    col = lax.broadcasted_iota(jnp.int32, (BLK, BLK), 1)
    inner = (step > 0).astype(F32).astype(BF16)
    total = jnp.zeros((BLK, width), F32)
    per_piece = heads // COLS
    for h in range(heads):
        g = h * groups // heads
        out = window_rows(
            every(wq_ref, qf, heads, h), kh[g, pl.ds(base, span), :], vh[g, pl.ds(base, span), :], bias
        )
        q = every(q_ref, nf, heads, h)
        k = every(k_ref, tf, heads, h)
        v = every(v_ref, sf, heads, h)
        inside = lax.dot_general(q, k, (((1,), (1,)), ((), ())), preferred_element_type=F32)
        inside = jnp.where(col <= row, inside, 0.0) * (gain_ref[h, 0] * gain_factor(0, width))
        left = jnp.concatenate([inside.astype(BF16), q, q], axis=1)
        right = jnp.concatenate([v, cs[h], piece_refs[h // per_piece][0, h % per_piece] * inner], axis=0)
        out = out + jnp.dot(left, right, preferred_element_type=F32)
        total = total + out * out
        of[pl.ds(h, BLK, stride=heads), :] = out
    out_ref[...] = of[...]
    square_ref[0] = square_sums(total)


def trunk_attention(where, gain, q, k, v, wq, pk, pv, ck, cv, cross, pieces, heads, groups):
    width = q.shape[1]
    blocks = q.shape[0] // (BLK * heads)
    at_block = pl.BlockSpec((BLK * heads, width), lambda i: (i, 0))
    whole = pl.BlockSpec((WIN * groups, width), lambda i: (0, 0))
    own = pl.BlockSpec((cross.shape[0], 1, *cross.shape[2:]), lambda i: (0, 0, 0, 0))
    piece = pl.BlockSpec((1, heads // COLS, width, width), lambda i: (jnp.maximum(i - 1, 0), 0, 0, 0))
    wide = pltpu.VMEM((BLK * heads, width), F32)
    return pl.pallas_call(
        functools.partial(trunk_kernel, heads, groups),
        grid=(blocks,),
        in_specs=[smem(), smem()] + [at_block] * 4 + [whole] * 4 + [own] + [piece] * COLS,
        out_specs=[at_block, pl.BlockSpec((1, 8, BLK), lambda i: (i, 0, 0))],
        out_shape=[
            jax.ShapeDtypeStruct(q.shape, F32),
            jax.ShapeDtypeStruct((blocks, 8, BLK), F32),
        ],
        scratch_shapes=[
            wide,
            wide,
            wide,
            wide,
            pltpu.VMEM((WIN * groups, width), F32),
            pltpu.VMEM((groups, 2 * WIN, width), BF16),
            pltpu.VMEM((groups, 2 * WIN, 2 * width), BF16),
            wide,
            pltpu.VMEM((heads, width, width), BF16),
        ],
        compiler_params=params(),
        cost_estimate=attention_cost(blocks * BLK, heads, width, 2 * blocks * BLK * BLK * heads * 4 * width),
        name="trunk_attention",
    )(where, gain, q, k, v, wq, pk, pv, ck, cv, cross, *pieces)


def branch_kernel(heads, groups, where_ref, fork_ref, q_ref, wq_ref, far_ref, ck_ref, cv_ref, cross_ref, *rest):
    kv_refs, piece_refs = rest[:COLS], rest[COLS : 2 * COLS]
    out_ref, square_ref = rest[2 * COLS : 2 * COLS + 2]
    qf, nf, kf, kh, vh, kt, of, es = rest[2 * COLS + 2 :]
    step = pl.program_id(0)
    near = WIN // BLK
    width = q_ref.shape[1]
    fork = fork_ref[0]
    column = where_ref[0] & (COLS - 1)
    span = WIN + BLK
    start = pl.multiple_of(fork * BLK, BLK)

    @pl.when(step == 0)
    def _():
        for i in range(COLS):
            kt[column ^ i] = kv_refs[i][...]
        vh[:, :, width:] = jnp.ones((groups, vh.shape[1], width), BF16)
        place(kt.at[0], kf, vh, 0, groups)
        place(kt.at[1], kf, vh, WIN, groups)
        place(kt.at[2], kf, kh, 0, groups)
        place(kt.at[3], kf, kh, WIN, groups)
        place(ck_ref, kf, kh, pl.multiple_of(start + WIN, BLK), groups)
        place(cv_ref, kf, vh, pl.multiple_of(start + WIN, BLK), groups)
        es[:, :width, :] = cross_ref[:, 0].reshape(heads, width, width)
        inner = (fork > 0).astype(F32).astype(BF16)
        chosen = jnp.maximum(fork - 1, 0)
        per_piece = heads // COLS
        for i in range(COLS):
            mine = (column ^ i) * per_piece
            for j in range(per_piece):
                es[mine + j, width:, :] = piece_refs[i][chosen, j] * inner

    nf[...] = q_ref[...].astype(F32)

    @pl.when(step < near)
    def _():
        qf[...] = wq_ref[...].astype(F32)
        base = pl.multiple_of(start + step * BLK, BLK)
        for h in range(heads):
            g = h * groups // heads
            of[pl.ds(h, BLK, stride=heads), :] = window_rows(
                every(wq_ref, qf, heads, h), kh[g, pl.ds(base, span), :], vh[g, pl.ds(base, span), :]
            )

    @pl.when(step >= near)
    def _():
        of[...] = far_ref[...]

    total = jnp.zeros((BLK, width), F32)
    for h in range(heads):
        q = every(q_ref, nf, heads, h)
        at = pl.ds(h, BLK, stride=heads)
        out = of[at, :] + jnp.dot(jnp.concatenate([q, q], axis=1), es[h], preferred_element_type=F32)
        total = total + out * out
        of[at, :] = out
    out_ref[...] = of[...]
    square_ref[0] = square_sums(total)


def branch_attention(where, fork, q, wq, far, ck, cv, cross, kvs, pieces, heads, groups):
    width = q.shape[1]
    blocks = q.shape[0] // (BLK * heads)
    near = WIN // BLK
    at_block = pl.BlockSpec((BLK * heads, width), lambda i: (i, 0))
    at_near = pl.BlockSpec((BLK * heads, width), lambda i: (jnp.minimum(i, near - 1), 0))
    at_far = pl.BlockSpec((BLK * heads, width), lambda i: (jnp.maximum(i - near, 0), 0))
    whole = pl.BlockSpec((WIN * groups, width), lambda i: (0, 0))
    end = pl.BlockSpec((cross.shape[0], 1, *cross.shape[2:]), lambda i: (0, 1, 0, 0))
    piece = pl.BlockSpec(pieces[0].shape, lambda i: (0, 0, 0, 0))
    wide = pltpu.VMEM((BLK * heads, width), F32)
    return pl.pallas_call(
        functools.partial(branch_kernel, heads, groups),
        grid=(blocks,),
        in_specs=[smem(), smem(), at_block, at_near, at_far, whole, whole, end] + [whole] * COLS + [piece] * COLS,
        out_specs=[at_block, pl.BlockSpec((1, 8, BLK), lambda i: (i, 0, 0))],
        out_shape=[
            jax.ShapeDtypeStruct(q.shape, F32),
            jax.ShapeDtypeStruct((blocks, 8, BLK), F32),
        ],
        scratch_shapes=[
            wide,
            wide,
            pltpu.VMEM((WIN * groups, width), F32),
            pltpu.VMEM((groups, 3 * WIN, width), BF16),
            pltpu.VMEM((groups, 3 * WIN, 2 * width), BF16),
            pltpu.VMEM((COLS, WIN * groups, width), BF16),
            wide,
            pltpu.VMEM((heads, 2 * width, width), BF16),
        ],
        compiler_params=params(),
        cost_estimate=attention_cost(near * BLK, heads, width, 4 * blocks * BLK * heads * width * width),
        name="branch_attention",
    )(where, fork, q, wq, far, ck, cv, cross, *kvs, *pieces)


def norm_kernel(heads, features, full_ref, square_ref, out_ref):
    width = full_ref.shape[1]
    scale = lax.rsqrt(square_ref[0, 0:1, :] / features + 1e-06)
    scale = jnp.broadcast_to(scale, (width, BLK)).T
    full = full_ref[...].reshape(BLK, heads, width)
    out_ref[...] = (full * scale[:, None, :]).astype(BF16).reshape(BLK * heads, width)


def normalize(full, squares, heads, features, name):
    width = full.shape[1]
    blocks = full.shape[0] // (BLK * heads)
    at_block = pl.BlockSpec((BLK * heads, width), lambda i: (i, 0))
    return pl.pallas_call(
        functools.partial(norm_kernel, heads, features),
        grid=(blocks,),
        in_specs=[at_block, pl.BlockSpec((1, 8, BLK), lambda i: (i, 0, 0))],
        out_specs=at_block,
        out_shape=jax.ShapeDtypeStruct(full.shape, BF16),
        compiler_params=params(),
        cost_estimate=pl.CostEstimate(flops=2 * full.size, bytes_accessed=6 * full.size, transcendentals=0),
        name=name,
    )(full, squares)


def shards(
    trunk_query,
    trunk_key,
    trunk_value,
    trunk_wquery,
    trunk_wkey,
    trunk_wvalue,
    branch_query,
    branch_wquery,
    branch_wkey,
    branch_wvalue,
    level_gain,
    fork_block,
):
    tokens, heads, width = trunk_query.shape
    groups = trunk_wkey.shape[1]
    depth = (tokens // BLK).bit_length() - 1
    count = lax.axis_size("seq")
    planes = count // COLS
    features = heads * lax.axis_size("head") * width
    me = lax.axis_index("seq")
    column, plane = me % COLS, me // COLS
    where = me.astype(jnp.int32).reshape(1)
    root = count - 1
    top = planes - 1

    def flat(x):
        return x.reshape(x.shape[0] * x.shape[1], x.shape[2])

    tq, tk, tv, twq = flat(trunk_query), flat(trunk_key), flat(trunk_value), flat(trunk_wquery)
    twk, twv = flat(trunk_wkey), flat(trunk_wvalue)
    bq, bwq, bwk, bwv = flat(branch_query), flat(branch_wquery), flat(branch_wkey), flat(branch_wvalue)

    def send(x, pairs):
        return lax.ppermute(x, "seq", pairs)

    def down(x):
        step = planes // 2
        while step:
            starts = [p for p in range(planes) if (top - p) % (2 * step) == 0 and p >= step]
            pairs = [(p * COLS + c, (p - step) * COLS + c) for p in starts for c in range(COLS)]
            got = send(x, pairs)
            hit = functools.reduce(jnp.logical_or, [plane == p - step for p in starts])
            x = jnp.where(hit, got, x)
            step //= 2
        return x

    def around(x):
        return [x] + [send(x, [(i, i ^ d) for i in range(count)]) for d in range(1, COLS)]

    half = COLS // 2
    got = send(twv, [(root - i, root - i - half) for i in range(half)])
    kvs = around(down(jnp.where(column >= half, twk, got)))
    shift = [(i, i + 1) for i in range(count - 1)]
    pk, pv = send(twk, shift), send(twv, shift)

    *pieces, shard_sum = block_sums(level_gain, tk, tv, heads, depth)
    chosen = pieces[COLS - 1]
    for c in range(COLS - 1):
        got = send(pieces[c], [(root, root - (COLS - 1) + c)])
        chosen = jnp.where(column == c, got, chosen)
    ends = around(down(chosen))

    slices = shard_sum.reshape(count, heads * width // count, width)
    slices = lax.all_to_all(slices, "seq", 0, 0, tiled=True)
    cross = cross_sums(where, level_gain, slices, depth, width)
    cross = lax.all_to_all(cross, "seq", 0, 0, tiled=True)

    far = far_attention(bwq, bwk, bwv, heads, groups)
    trunk_full, trunk_square = trunk_attention(
        where, level_gain, tq, tk, tv, twq, pk, pv, twk, twv, cross, pieces, heads, groups
    )
    trunk_square = lax.psum(trunk_square, "head")
    trunk_out = normalize(trunk_full, trunk_square, heads, features, "trunk_norm")
    branch_full, branch_square = branch_attention(
        where, fork_block, bq, bwq, far, bwk, bwv, cross, kvs, ends, heads, groups
    )
    branch_square = lax.psum(branch_square, "head")
    branch_out = normalize(branch_full, branch_square, heads, features, "branch_norm")
    return trunk_out.reshape(trunk_query.shape), branch_out.reshape(branch_query.shape)


def solution(mesh):
    rows = P("seq", "head", None)
    return jax.shard_map(
        shards,
        mesh=mesh,
        in_specs=(rows,) * 10 + (P("head", None), P("seq")),
        out_specs=(rows, rows),
        check_vma=False,
    )
```

profile of v0, /device:TPU:0, one launch (start us, length us, event | category | flops | bytes accessed | tf_op | source)
XLA Modules:
  0.0 129.7 jit_solution(9504840230035613402)
XLA Ops:
  0.6 0.0 copy-start.5
  0.6 1.2 copy-done.5
  1.9 1.2 copy-done.7
  3.1 0.7 copy-done.15
  3.8 3.2 %block_sums.1 = (bf16[3,2,128,128]{3,2,1,0:T(8,128)(2,1)S(1)}, bf16[3,2,128,128]{3,2,1,0:T(8,128)(2,1)S(1)}, bf16[3,2,128,128]{3,2,1,0:T(8,128)(2,1)S(1)}, bf16[...) custom-call(f32[8,11]{1,0:T(8,128)S(1)} %copy-done.15, bf16[4096,128]{1,0:T(8,128)(2,1)S(1)} %bitcast.17, ...), custom_call_target="tpu_custom_call" | custom-call | flops 134217728 | bytes 3145728 | tf_op jit(solution)/shard_map/block_sums/pallas_call | solution.py:73
  7.0 0.7 collective-permute-start.10
  7.6 0.7 collective-permute-start.8
  8.3 0.7 collective-permute-start.9
  9.0 0.7 collective-permute-start.2
  9.7 11.9 %all-to-all-start = ((bf16[16,64,128]{2,1,0:T(8,128)(2,1)}), bf16[16,64,128]{2,1,0:T(8,128)(2,1)S(1)}, u32[]{:S(2)}, u32[]{:S(2)}) async-start(bf16[16,64,128]{2,1,0:T(8,128)(2,1)} %bitcast.7), calls=%async_computation | async-start | bytes 524288 | tf_op jit(solution)/shard_map/all_to_all | solution.py:487
  21.6 0.0 collective-permute-done.10
  21.7 0.0 collective-permute-done.8
  21.7 0.0 collective-permute-done.9
  21.7 1.3 %collective-permute-start.11 = (bf16[3,2,128,128]{3,2,1,0:T(8,128)(2,1)S(1)}, bf16[3,2,128,128]{3,2,1,0:T(8,128)(2,1)}, u32[]{:S(2)}, u32[]{:S(2)}) collective-permute-start(bf16[3,2,128,128]{3,2,1,0:T(8,128)(2,1)S(1)} %select_select_fusion), channel_id=1, source_target_pairs={{24,8},{26,10},{28,12},{30,14},{25,9},{27,11},{29,13},{31,15}} | collective-permute-start | bytes 589832 | tf_op jit(solution)/shard_map/ppermute | solution.py:457
  23.1 0.0 collective-permute-done.2
  23.1 1.4 %collective-permute-start.3 = (bf16[1024,128]{1,0:T(8,128)(2,1)S(1)}, bf16[1024,128]{1,0:T(8,128)(2,1)}, u32[]{:S(2)}, u32[]{:S(2)}) collective-permute-start(bf16[1024,128]{1,0:T(8,128)(2,1)S(1)} %broadcast_select_fusion), channel_id=1, source_target_pairs={{24,8},{26,10},{28,12},{30,14},{25,9},{27,11},{29,13},{31,15}} | collective-permute-start | bytes 786440 | tf_op jit(solution)/shard_map/ppermute | solution.py:457
  24.5 8.3 %all-to-all-done.sums_ref = bf16[16,64,128]{2,1,0:T(8,128)(2,1)S(1)} async-done(((bf16[16,64,128]{2,1,0:T(8,128)(2,1)}), bf16[16,64,128]{2,1,0:T(8,128)(2,1)S(1)}, u32[]{:S(2)}, u32[]{:S(2)}) %all-to-all-start) | async-done | bytes 262176 | tf_op jit(solution)/shard_map/all_to_all | solution.py:487
  32.8 0.0 copy-done.20
  32.8 1.5 %cross_sums.1 = bf16[16,2,64,128]{3,2,1,0:T(8,128)(2,1)} custom-call(s32[1]{0:T(128)} %bitcast.where_ref, f32[8,11]{1,0:T(8,128)S(1)} %copy-done.16, bf16[16,64,128]{2,1,0:T(8,128)(2,1)S(1)} %all-to-all-done.sums_ref), custom_call_target="tpu_custom_call" | custom-call | flops 2621440 | bytes 786432 | tf_op jit(solution)/shard_map/cross_sums/pallas_call | solution.py:118
  34.3 12.9 %all-to-all-start.1 = ((bf16[16,2,64,128]{3,2,1,0:T(8,128)(2,1)}), bf16[16,2,64,128]{3,2,1,0:T(8,128)(2,1)S(1)}, u32[]{:S(2)}, u32[]{:S(2)}) async-start(bf16[16,2,64,128]{3,2,1,0:T(8,128)(2,1)} %cross_sums.1), calls=%async_computation.1 | async-start | bytes 1048576 | tf_op jit(solution)/shard_map/all_to_all | solution.py:489
  47.2 0.0 collective-permute-done.11
  47.2 0.7 broadcast_select_fusion.3
  47.9 1.3 collective-permute-start.12
  49.2 0.0 collective-permute-done.3
  49.3 1.3 collective-permute-start.4
  50.6 4.5 %collective-permute-start = (bf16[1024,128]{1,0:T(8,128)(2,1)}, bf16[1024,128]{1,0:T(8,128)(2,1)}, u32[]{:S(2)}, u32[]{:S(2)}) collective-permute-start(bf16[1024,128]{1,0:T(8,128)(2,1)} %bitcast.5.ck_ref), channel_id=1, source_target_pairs={{0,2},{2,4},{4,6},{6,8},{8,10},{10,12},{12,14},{14,16},{16,18},{18... | collective-permute-start | bytes 786440 | tf_op jit(solution)/shard_map/ppermute | solution.py:457
  55.1 3.4 %collective-permute-start.1 = (bf16[1024,128]{1,0:T(8,128)(2,1)}, bf16[1024,128]{1,0:T(8,128)(2,1)}, u32[]{:S(2)}, u32[]{:S(2)}) collective-permute-start(bf16[1024,128]{1,0:T(8,128)(2,1)} %bitcast.6.cv_ref), channel_id=1, source_target_pairs={{0,2},{2,4},{4,6},{6,8},{8,10},{10,12},{12,14},{14,16},{16,18},{18... | collective-permute-start | bytes 786440 | tf_op jit(solution)/shard_map/ppermute | solution.py:457
  58.5 0.0 collective-permute-done.12
  58.5 1.0 broadcast_select_fusion.4.rest_4_
  59.4 0.8 collective-permute-start.13
  60.3 0.0 collective-permute-done.4
  60.3 1.0 broadcast_select_fusion.2.rest_0_
  61.3 1.7 %collective-permute-start.5 = (bf16[1024,128]{1,0:T(8,128)(2,1)S(1)}, bf16[1024,128]{1,0:T(8,128)(2,1)S(1)}, u32[]{:S(2)}, u32[]{:S(2)}) collective-permute-start(bf16[1024,128]{1,0:T(8,128)(2,1)S(1)} %broadcast_select_fusion.2.rest_0_), channel_id=1, source_target_pairs={{0,2},{2,0},{4,6},{6,4},{8,10},{10,8},{12,14},{14,12},{16,18},{18,... | collective-permute-start | bytes 786440 | tf_op jit(solution)/shard_map/ppermute | solution.py:457
  63.0 3.7 %collective-permute-start.6 = (bf16[1024,128]{1,0:T(8,128)(2,1)S(1)}, bf16[1024,128]{1,0:T(8,128)(2,1)}, u32[]{:S(2)}, u32[]{:S(2)}) collective-permute-start(bf16[1024,128]{1,0:T(8,128)(2,1)S(1)} %broadcast_select_fusion.2.rest_0_), channel_id=1, source_target_pairs={{0,4},{2,6},{4,0},{6,2},{8,12},{10,14},{12,8},{14,10},{16,20},{18,... | collective-permute-start | bytes 786440 | tf_op jit(solution)/shard_map/ppermute | solution.py:457
  66.6 0.0 collective-permute-done.pk_ref
  66.6 1.2 collective-permute-start.7
  67.8 1.0 copy-done.9
  68.8 1.0 copy-done.11
  69.9 6.4 %far_attention.1.far_ref = f32[4096,128]{1,0:T(8,128)S(1)} custom-call(bf16[8192,128]{1,0:T(8,128)(2,1)S(1)} %bitcast.16, bf16[2048,128]{1,0:T(8,128)(2,1)S(1)} %bitcast.21, bf16[2048,128]{1,0:T(8,128)(2,1)S(1)} %bitcast.24, bf16[2048,128]{1,0:T(8,128)(2,1)S(1)} %bitcast.22, bf16[2048,128]{1,0:T(8,128)(2,1)S(1)} %bitcast.25), custom_call_target="tpu_custom_call" | custom-call | flops 2013265920 | bytes 6291456 | tf_op jit(solution)/shard_map/far_attention/pallas_call | solution.py:198
  76.2 0.0 copy-start.3
  76.3 1.3 %copy-done.3 = f32[4096,128]{1,0:T(8,128)} copy-done((f32[4096,128]{1,0:T(8,128)}, f32[4096,128]{1,0:T(8,128)S(1)}, u32[]{:S(2)}) %copy-start.3) | copy-done | bytes 2097176
  78.2 0.0 collective-permute-done.1.pv_ref
  78.2 2.1 %collective-permute-start.14 = (bf16[3,2,128,128]{3,2,1,0:T(8,128)(2,1)S(1)}, bf16[3,2,128,128]{3,2,1,0:T(8,128)(2,1)S(1)}, u32[]{:S(2)}, u32[]{:S(2)}) collective-permute-start(bf16[3,2,128,128]{3,2,1,0:T(8,128)(2,1)S(1)} %broadcast_select_fusion.4.rest_4_), channel_id=1, source_target_pairs={{0,4},{2,6},{4,0},{6,2},{8,12},{10,14},{12,8},{14,10},{16,20},{18,... | collective-permute-start | bytes 589832 | tf_op jit(solution)/shard_map/ppermute | solution.py:457
  80.3 0.0 collective-permute-done.13.rest_5_
  80.3 0.7 copy-done.13
  81.0 0.0 collective-permute-start.15
  81.0 0.0 all-to-all-done.1.cross_ref
  81.0 1.2 copy-done.6
  82.2 1.2 copy-done.8
  83.5 1.2 copy-done.17
  84.7 0.9 copy-done.19
  85.6 0.9 copy-done.21
  86.5 0.9 copy-done.23
  87.5 16.4 %trunk_attention.1 = (f32[4096,128]{1,0:T(8,128)}, f32[4,8,128]{2,1,0:T(8,128)S(1)}) custom-call(s32[1]{0:T(128)} %bitcast.where_ref, f32[8,11]{1,0:T(8,128)S(1)} %copy-done.16, bf16[4096,128]{1,0:T(8,128)(2,1)S(1)} %bitcast.27, bf16[4096,128]{1,0:T(8,128)(2,1)S(1)} %bitcast.18, bf16[4096,128]{1,0:T(8,128)(2,1)S(1)} %bitcast.20, bf16[4096,128]{1,0:T(8,128)(2,1)} %bitcast.30, ...), custom_call_target="tpu_custom_call" | custom-call | flops 2550136832 | bytes 6291456 | tf_op jit(solution)/shard_map/trunk_attention/pallas_call | solution.py:278
  103.9 0.0 collective-permute-done.14.rest_6_
  103.9 0.0 collective-permute-done.15.rest_7_
  103.9 0.0 collective-permute-done.5.rest_1_
  103.9 0.0 collective-permute-done.6.rest_2_
  103.9 0.0 collective-permute-done.7.rest_3_
  104.0 14.6 %branch_attention.1 = (f32[8192,128]{1,0:T(8,128)}, f32[8,8,128]{2,1,0:T(8,128)S(1)}) custom-call(s32[1]{0:T(128)} %bitcast.where_ref, s32[1]{0:T(128)S(6)} %copy.14.fork_ref, bf16[8192,128]{1,0:T(8,128)(2,1)S(1)} %bitcast.14, bf16[8192,128]{1,0:T(8,128)(2,1)} %bitcast.15, f32[4096,128]{1,0:T(8,128)} %copy-done.3, bf16[2048,128]{1,0:T(8,128)(2,1)S(1)} %bitcast.23, ...), custom_call_target="tpu_custom_call" | custom-call | flops 2550136832 | bytes 6291456 | tf_op jit(solution)/shard_map/branch_attention/pallas_call | solution.py:374
  118.5 3.5 %all-reduce = (f32[4,8,128]{2,1,0:T(8,128)S(1)}, f32[8,8,128]{2,1,0:T(8,128)S(1)}) all-reduce(f32[4,8,128]{2,1,0:T(8,128)S(1)} %get-tuple-element.17, f32[8,8,128]{2,1,0:T(8,128)S(1)} %get-tuple-element.19), channel_id=1, replica_groups=mesh['seq'=16,'head'=2] {'head'}, use_global_device_ids=true, to_apply=%region_0.1 | all-reduce | flops 12288 | bytes 98304 | tf_op jit(solution)/shard_map/psum | solution.py:495
  122.1 2.2 %copy-done = f32[8192,128]{1,0:T(8,128)S(1)} copy-done((f32[8192,128]{1,0:T(8,128)S(1)}, f32[8192,128]{1,0:T(8,128)}, u32[]{:S(2)}) %copy-start) | copy-done | bytes 4194328
  124.2 3.6 %branch_norm.1 = bf16[8192,128]{1,0:T(8,128)(2,1)} custom-call(f32[8192,128]{1,0:T(8,128)S(1)} %copy-done, f32[8,8,128]{2,1,0:T(8,128)S(1)} %get-tuple-element.21.square_ref), custom_call_target="tpu_custom_call" | custom-call | flops 2097152 | bytes 6291456 | tf_op jit(solution)/shard_map/branch_norm/pallas_call | solution.py:411
  127.8 1.9 %trunk_norm.1 = bf16[4096,128]{1,0:T(8,128)(2,1)} custom-call(f32[4096,128]{1,0:T(8,128)S(1)} %copy-done.4, f32[4,8,128]{2,1,0:T(8,128)S(1)} %get-tuple-element.20.square_ref), custom_call_target="tpu_custom_call" | custom-call | flops 1048576 | bytes 3145728 | tf_op jit(solution)/shard_map/trunk_norm/pallas_call | solution.py:411
  (34 shorter events, 0.2 us)
Async XLA Ops:
  0.6 1.2 copy-start.5
  1.9 1.2 copy-start.7
  3.1 0.7 copy-start.15
  3.8 29.0 %copy-start.16 = (f32[8,11]{1,0:T(8,128)S(1)}, f32[8,11]{1,0:T(8,128)}, u32[]{:S(2)}) copy-start(f32[8,11]{1,0:T(8,128)} %gain_ref.5) | copy-start | bytes 1060
  7.0 25.8 %copy-start.18 = (bf16[3,2,128,128]{3,2,1,0:T(8,128)(2,1)}, bf16[3,2,128,128]{3,2,1,0:T(8,128)(2,1)S(1)}, u32[]{:S(2)}) copy-start(bf16[3,2,128,128]{3,2,1,0:T(8,128)(2,1)S(1)} %get-tuple-element.12.rest_0_) | copy-start | bytes 589828
  7.0 25.8 %copy-start.20 = (bf16[3,2,128,128]{3,2,1,0:T(8,128)(2,1)}, bf16[3,2,128,128]{3,2,1,0:T(8,128)(2,1)S(1)}, u32[]{:S(2)}) copy-start(bf16[3,2,128,128]{3,2,1,0:T(8,128)(2,1)S(1)} %get-tuple-element.13.rest_1_) | copy-start | bytes 589828
  7.0 25.8 %copy-start.22 = (bf16[3,2,128,128]{3,2,1,0:T(8,128)(2,1)}, bf16[3,2,128,128]{3,2,1,0:T(8,128)(2,1)S(1)}, u32[]{:S(2)}) copy-start(bf16[3,2,128,128]{3,2,1,0:T(8,128)(2,1)S(1)} %get-tuple-element.14.rest_2_) | copy-start | bytes 589828
  7.0 14.7 %collective-permute-start.10 = (bf16[3,2,128,128]{3,2,1,0:T(8,128)(2,1)S(1)}, bf16[3,2,128,128]{3,2,1,0:T(8,128)(2,1)S(1)}, u32[]{:S(2)}, u32[]{:S(2)}) collective-permute-start(bf16[3,2,128,128]{3,2,1,0:T(8,128)(2,1)S(1)} %get-tuple-element.12.rest_0_), channel_id=1, source_target_pairs={{30,24},{31,25}} | collective-permute-start | bytes 589832 | tf_op jit(solution)/shard_map/ppermute | solution.py:457
  7.6 14.0 %collective-permute-start.8 = (bf16[3,2,128,128]{3,2,1,0:T(8,128)(2,1)S(1)}, bf16[3,2,128,128]{3,2,1,0:T(8,128)(2,1)S(1)}, u32[]{:S(2)}, u32[]{:S(2)}) collective-permute-start(bf16[3,2,128,128]{3,2,1,0:T(8,128)(2,1)S(1)} %get-tuple-element.14.rest_2_), channel_id=1, source_target_pairs={{30,28},{31,29}} | collective-permute-start | bytes 589832 | tf_op jit(solution)/shard_map/ppermute | solution.py:457
  8.3 13.4 %collective-permute-start.9 = (bf16[3,2,128,128]{3,2,1,0:T(8,128)(2,1)S(1)}, bf16[3,2,128,128]{3,2,1,0:T(8,128)(2,1)S(1)}, u32[]{:S(2)}, u32[]{:S(2)}) collective-permute-start(bf16[3,2,128,128]{3,2,1,0:T(8,128)(2,1)S(1)} %get-tuple-element.13.rest_1_), channel_id=1, source_target_pairs={{30,26},{31,27}} | collective-permute-start | bytes 589832 | tf_op jit(solution)/shard_map/ppermute | solution.py:457
  9.0 14.1 %collective-permute-start.2 = (bf16[1024,128]{1,0:T(8,128)(2,1)}, bf16[1024,128]{1,0:T(8,128)(2,1)S(1)}, u32[]{:S(2)}, u32[]{:S(2)}) collective-permute-start(bf16[1024,128]{1,0:T(8,128)(2,1)} %bitcast.6.cv_ref), channel_id=1, source_target_pairs={{30,26},{28,24},{31,27},{29,25}} | collective-permute-start | bytes 786440 | tf_op jit(solution)/shard_map/ppermute | solution.py:457
  9.7 23.1 %all-to-all-start = ((bf16[16,64,128]{2,1,0:T(8,128)(2,1)}), bf16[16,64,128]{2,1,0:T(8,128)(2,1)S(1)}, u32[]{:S(2)}, u32[]{:S(2)}) async-start(bf16[16,64,128]{2,1,0:T(8,128)(2,1)} %bitcast.7), calls=%async_computation | async-start | bytes 524288 | tf_op jit(solution)/shard_map/all_to_all | solution.py:487
  21.7 25.5 %collective-permute-start.11 = (bf16[3,2,128,128]{3,2,1,0:T(8,128)(2,1)S(1)}, bf16[3,2,128,128]{3,2,1,0:T(8,128)(2,1)}, u32[]{:S(2)}, u32[]{:S(2)}) collective-permute-start(bf16[3,2,128,128]{3,2,1,0:T(8,128)(2,1)S(1)} %select_select_fusion), channel_id=1, source_target_pairs={{24,8},{26,10},{28,12},{30,14},{25,9},{27,11},{29,13},{31,15}} | collective-permute-start | bytes 589832 | tf_op jit(solution)/shard_map/ppermute | solution.py:457
  23.1 26.1 %collective-permute-start.3 = (bf16[1024,128]{1,0:T(8,128)(2,1)S(1)}, bf16[1024,128]{1,0:T(8,128)(2,1)}, u32[]{:S(2)}, u32[]{:S(2)}) collective-permute-start(bf16[1024,128]{1,0:T(8,128)(2,1)S(1)} %broadcast_select_fusion), channel_id=1, source_target_pairs={{24,8},{26,10},{28,12},{30,14},{25,9},{27,11},{29,13},{31,15}} | collective-permute-start | bytes 786440 | tf_op jit(solution)/shard_map/ppermute | solution.py:457
  34.3 33.5 %copy-start.2 = (bf16[1024,8,128]{2,1,0:T(8,128)(2,1)S(1)}, bf16[1024,8,128]{2,1,0:T(8,128)(2,1)}, u32[]{:S(2)}) copy-start(bf16[1024,8,128]{2,1,0:T(8,128)(2,1)} %param.19) | copy-start | bytes 6291460
  34.3 46.7 %all-to-all-start.1 = ((bf16[16,2,64,128]{3,2,1,0:T(8,128)(2,1)}), bf16[16,2,64,128]{3,2,1,0:T(8,128)(2,1)S(1)}, u32[]{:S(2)}, u32[]{:S(2)}) async-start(bf16[16,2,64,128]{3,2,1,0:T(8,128)(2,1)} %cross_sums.1), calls=%async_computation.1 | async-start | bytes 1048576 | tf_op jit(solution)/shard_map/all_to_all | solution.py:489
  47.9 10.6 %collective-permute-start.12 = (bf16[3,2,128,128]{3,2,1,0:T(8,128)(2,1)}, bf16[3,2,128,128]{3,2,1,0:T(8,128)(2,1)}, u32[]{:S(2)}, u32[]{:S(2)}) collective-permute-start(bf16[3,2,128,128]{3,2,1,0:T(8,128)(2,1)} %broadcast_select_fusion.3), channel_id=1, source_target_pairs={{8,0},{10,2},{12,4},{14,6},{24,16},{26,18},{28,20},{30,22},{9,1},{... | collective-permute-start | bytes 589832 | tf_op jit(solution)/shard_map/ppermute | solution.py:457
  49.3 11.0 %collective-permute-start.4 = (bf16[1024,128]{1,0:T(8,128)(2,1)S(1)}, bf16[1024,128]{1,0:T(8,128)(2,1)}, u32[]{:S(2)}, u32[]{:S(2)}) collective-permute-start(bf16[1024,128]{1,0:T(8,128)(2,1)S(1)} %broadcast_select_fusion.1), channel_id=1, source_target_pairs={{8,0},{10,2},{12,4},{14,6},{24,16},{26,18},{28,20},{30,22},{9,1},{... | collective-permute-start | bytes 786440 | tf_op jit(solution)/shard_map/ppermute | solution.py:457
  50.6 16.1 %collective-permute-start = (bf16[1024,128]{1,0:T(8,128)(2,1)}, bf16[1024,128]{1,0:T(8,128)(2,1)}, u32[]{:S(2)}, u32[]{:S(2)}) collective-permute-start(bf16[1024,128]{1,0:T(8,128)(2,1)} %bitcast.5.ck_ref), channel_id=1, source_target_pairs={{0,2},{2,4},{4,6},{6,8},{8,10},{10,12},{12,14},{14,16},{16,18},{18... | collective-permute-start | bytes 786440 | tf_op jit(solution)/shard_map/ppermute | solution.py:457
  55.1 23.1 %collective-permute-start.1 = (bf16[1024,128]{1,0:T(8,128)(2,1)}, bf16[1024,128]{1,0:T(8,128)(2,1)}, u32[]{:S(2)}, u32[]{:S(2)}) collective-permute-start(bf16[1024,128]{1,0:T(8,128)(2,1)} %bitcast.6.cv_ref), channel_id=1, source_target_pairs={{0,2},{2,4},{4,6},{6,8},{8,10},{10,12},{12,14},{14,16},{16,18},{18... | collective-permute-start | bytes 786440 | tf_op jit(solution)/shard_map/ppermute | solution.py:457
  59.4 20.9 %collective-permute-start.13 = (bf16[3,2,128,128]{3,2,1,0:T(8,128)(2,1)S(1)}, bf16[3,2,128,128]{3,2,1,0:T(8,128)(2,1)S(1)}, u32[]{:S(2)}, u32[]{:S(2)}) collective-permute-start(bf16[3,2,128,128]{3,2,1,0:T(8,128)(2,1)S(1)} %broadcast_select_fusion.4.rest_4_), channel_id=1, source_target_pairs={{0,2},{2,0},{4,6},{6,4},{8,10},{10,8},{12,14},{14,12},{16,18},{18,... | collective-permute-start | bytes 589832 | tf_op jit(solution)/shard_map/ppermute | solution.py:457
  61.3 42.6 %collective-permute-start.5 = (bf16[1024,128]{1,0:T(8,128)(2,1)S(1)}, bf16[1024,128]{1,0:T(8,128)(2,1)S(1)}, u32[]{:S(2)}, u32[]{:S(2)}) collective-permute-start(bf16[1024,128]{1,0:T(8,128)(2,1)S(1)} %broadcast_select_fusion.2.rest_0_), channel_id=1, source_target_pairs={{0,2},{2,0},{4,6},{6,4},{8,10},{10,8},{12,14},{14,12},{16,18},{18,... | collective-permute-start | bytes 786440 | tf_op jit(solution)/shard_map/ppermute | solution.py:457
  63.0 40.9 %collective-permute-start.6 = (bf16[1024,128]{1,0:T(8,128)(2,1)S(1)}, bf16[1024,128]{1,0:T(8,128)(2,1)}, u32[]{:S(2)}, u32[]{:S(2)}) collective-permute-start(bf16[1024,128]{1,0:T(8,128)(2,1)S(1)} %broadcast_select_fusion.2.rest_0_), channel_id=1, source_target_pairs={{0,4},{2,6},{4,0},{6,2},{8,12},{10,14},{12,8},{14,10},{16,20},{18,... | collective-permute-start | bytes 786440 | tf_op jit(solution)/shard_map/ppermute | solution.py:457
  66.6 37.3 %collective-permute-start.7 = (bf16[1024,128]{1,0:T(8,128)(2,1)S(1)}, bf16[1024,128]{1,0:T(8,128)(2,1)}, u32[]{:S(2)}, u32[]{:S(2)}) collective-permute-start(bf16[1024,128]{1,0:T(8,128)(2,1)S(1)} %broadcast_select_fusion.2.rest_0_), channel_id=1, source_target_pairs={{0,6},{2,4},{4,2},{6,0},{8,14},{10,12},{12,10},{14,8},{16,22},{18,... | collective-permute-start | bytes 786440 | tf_op jit(solution)/shard_map/ppermute | solution.py:457
  67.8 1.0 copy-start.9
  68.8 1.0 copy-start.11
  76.2 1.3 %copy-start.3 = (f32[4096,128]{1,0:T(8,128)}, f32[4096,128]{1,0:T(8,128)S(1)}, u32[]{:S(2)}) copy-start(f32[4096,128]{1,0:T(8,128)S(1)} %far_attention.1.far_ref) | copy-start | bytes 6291460
  78.2 25.7 %collective-permute-start.14 = (bf16[3,2,128,128]{3,2,1,0:T(8,128)(2,1)S(1)}, bf16[3,2,128,128]{3,2,1,0:T(8,128)(2,1)S(1)}, u32[]{:S(2)}, u32[]{:S(2)}) collective-permute-start(bf16[3,2,128,128]{3,2,1,0:T(8,128)(2,1)S(1)} %broadcast_select_fusion.4.rest_4_), channel_id=1, source_target_pairs={{0,4},{2,6},{4,0},{6,2},{8,12},{10,14},{12,8},{14,10},{16,20},{18,... | collective-permute-start | bytes 589832 | tf_op jit(solution)/shard_map/ppermute | solution.py:457
  80.3 0.7 copy-start.13
  81.0 22.9 %collective-permute-start.15 = (bf16[3,2,128,128]{3,2,1,0:T(8,128)(2,1)S(1)}, bf16[3,2,128,128]{3,2,1,0:T(8,128)(2,1)S(1)}, u32[]{:S(2)}, u32[]{:S(2)}) collective-permute-start(bf16[3,2,128,128]{3,2,1,0:T(8,128)(2,1)S(1)} %broadcast_select_fusion.4.rest_4_), channel_id=1, source_target_pairs={{0,6},{2,4},{4,2},{6,0},{8,14},{10,12},{12,10},{14,8},{16,22},{18,... | collective-permute-start | bytes 589832 | tf_op jit(solution)/shard_map/ppermute | solution.py:457
  81.0 1.2 copy-start.6
  82.2 1.2 copy-start.8
  83.5 1.2 copy-start.17
  84.7 0.9 copy-start.19
  85.6 0.9 copy-start.21
  86.5 0.9 copy-start.23
  87.5 16.5 %copy-start.1 = (bf16[1024,8,128]{2,1,0:T(8,128)(2,1)S(1)}, bf16[1024,8,128]{2,1,0:T(8,128)(2,1)}, u32[]{:S(2)}) copy-start(bf16[1024,8,128]{2,1,0:T(8,128)(2,1)} %param.18) | copy-start | bytes 6291460
  87.5 16.5 %copy-start.10 = (bf16[1024,2,128]{2,1,0:T(2,128)(2,1)S(1)}, bf16[1024,2,128]{2,1,0:T(2,128)(2,1)}, u32[]{:S(2)}) copy-start(bf16[1024,2,128]{2,1,0:T(2,128)(2,1)} %param.20) | copy-start | bytes 1572868
  87.5 16.5 %copy-start.12 = (bf16[1024,2,128]{2,1,0:T(2,128)(2,1)S(1)}, bf16[1024,2,128]{2,1,0:T(2,128)(2,1)}, u32[]{:S(2)}) copy-start(bf16[1024,2,128]{2,1,0:T(2,128)(2,1)} %param.21) | copy-start | bytes 1572868
  87.5 16.5 %copy-start.14 = (bf16[3,2,128,128]{3,2,1,0:T(8,128)(2,1)S(1)}, bf16[3,2,128,128]{3,2,1,0:T(8,128)(2,1)}, u32[]{:S(2)}) copy-start(bf16[3,2,128,128]{3,2,1,0:T(8,128)(2,1)} %copy-done.13) | copy-start | bytes 589828
  122.1 2.2 %copy-start = (f32[8192,128]{1,0:T(8,128)S(1)}, f32[8192,128]{1,0:T(8,128)}, u32[]{:S(2)}) copy-start(f32[8192,128]{1,0:T(8,128)} %get-tuple-element.18.full_ref) | copy-start | bytes 12582916
  124.2 3.6 %copy-start.4 = (f32[4096,128]{1,0:T(8,128)S(1)}, f32[4096,128]{1,0:T(8,128)}, u32[]{:S(2)}) copy-start(f32[4096,128]{1,0:T(8,128)} %get-tuple-element.16.full_ref) | copy-start | bytes 6291460
where the time goes:
time: 131 us; the launch traced here: 130 us
  starting transfers between devices  50.2 us (38%)
  Pallas kernels  47.5 us (36%)
  local copies, waits for them, and re-layouts  15.9 us (12%)
  waiting for transfers between devices  8.33 us (6%)
  blocking collectives  3.53 us (3%)
  other arithmetic  2.76 us (2%)
  between operations  1.58 us (1%)
    ppermute x16, starting transfers between devices, send(): return lax.ppermute(x, 'seq', pairs)  25.3 us
    pallas_call x1, Pallas kernels, trunk_attention(): pl.pallas_call(functools.partial(trunk_kernel, heads, groups), grid=(bloc...  16.4 us
    unnamed x48, local copies, waits for them, and re-layouts  15.9 us
    pallas_call x1, Pallas kernels, branch_attention(): pl.pallas_call(functools.partial(branch_kernel, heads, groups), grid=(blo...  14.6 us
    all_to_all x1, starting transfers between devices, shards(): cross = lax.all_to_all(cross, 'seq', 0, 0, tiled=True)  12.9 us
    all_to_all x1, starting transfers between devices, shards(): slices = lax.all_to_all(slices, 'seq', 0, 0, tiled=True)  11.9 us
    all_to_all x1, waiting for transfers between devices, shards(): slices = lax.all_to_all(slices, 'seq', 0, 0, tiled=True)  8.29 us
    pallas_call x1, Pallas kernels, far_attention(): pl.pallas_call(functools.partial(far_kernel, heads, groups), grid=(steps,...  6.37 us
  transfers between devices with their start and end apart: 18, of which 1 were waited for; matrix products, arithmetic and copies ran while one was open for 2% of the time, Pallas kernels for 19%

commit v1 on v0

--- a/solution.py
+++ b/solution.py
@@ -14,7 +14,7 @@
 MASKED = -1e30
 F32 = jnp.float32
 BF16 = jnp.bfloat16
-VMEM_BYTES = 48 * 1024 * 1024
+VMEM_BYTES = 60 * 1024 * 1024
 
 
 def params():
@@ -134,30 +134,78 @@
         dst[g, pl.ds(start, tokens), : src_ref.shape[1]] = part
 
 
-def window_rows(queries, keys, values, bias=None):
-    rows, width = queries.shape
+def split_groups(wide):
+    rows, width = wide.shape
+    pairs = wide.reshape(rows // 16, 16, width)
+    low, high = pairs[:, :8], pairs[:, 8:]
+    upper = lax.broadcasted_iota(jnp.int32, low.shape, 1) < 4
+    first = jnp.where(upper, low, pltpu.roll(high, 4, 1))
+    second = jnp.where(upper, pltpu.roll(low, 4, 1), high)
+    return [part.reshape(rows // 2, width) for part in (first, second)]
+
+
+def join_groups(first, second):
+    rows, width = first.shape
+    first, second = (part.reshape(rows // 8, 8, width) for part in (first, second))
+    upper = lax.broadcasted_iota(jnp.int32, first.shape, 1) < 4
+    low = jnp.where(upper, first, pltpu.roll(second, 4, 1))
+    high = jnp.where(upper, pltpu.roll(first, 4, 1), second)
+    return jnp.concatenate([low, high], axis=1).reshape(2 * rows, width)
+
+
+def window_logits(queries, keys, token, share, bias):
+    rows = queries.shape[0]
     logits = lax.dot_general(queries, keys, (((1,), (1,)), ((), ())), preferred_element_type=F32)
-    row = lax.broadcasted_iota(jnp.int32, (rows, rows), 0)
-    col = lax.broadcasted_iota(jnp.int32, (rows, rows), 1)
-    first = jnp.where(col > row, logits[:, :rows], MASKED)
-    last = jnp.where(col <= row, logits[:, -rows:], MASKED)
-    logits = jnp.concatenate([first, logits[:, rows:-rows], last], axis=1)
-    if bias is not None:
-        logits = logits + bias
+    row = token + lax.broadcasted_iota(jnp.int32, (rows, BLK), 0) // share
+    col = lax.broadcasted_iota(jnp.int32, (rows, BLK), 1)
+    late = col > row
+    first = jnp.where(late, logits[:, :BLK], MASKED)
+    last = jnp.where(late, MASKED, logits[:, -BLK:])
+    logits = jnp.concatenate([first, logits[:, BLK:-BLK], last], axis=1)
+    return logits if bias is None else logits + bias
+
+
+def window_outputs(logits, values, width):
     top = jnp.max(logits, axis=1, keepdims=True)
     weights = jnp.exp2((logits - top) * (math.log2(math.e) / math.sqrt(width))).astype(BF16)
     both = jnp.dot(weights, values, preferred_element_type=F32)
     return both[:, :width] / both[:, width:]
 
 
-def square_sums(total):
-    ones = jnp.ones((8, total.shape[1]), F32)
+def window_block(q_ref, kh, vh, base, groups, bias=None):
+    width = q_ref.shape[1]
+    span = WIN + BLK
+    share = q_ref.shape[0] // BLK // groups
+    parts = [part.astype(BF16) for part in split_groups(q_ref[...].astype(F32))]
+    chunks = [(g, c) for g in range(groups) for c in range(0, BLK * share, BLK)]
+
+    def logits_of(chunk):
+        g, c = chunk
+        return window_logits(parts[g][c : c + BLK], kh[g, pl.ds(base, span), :], c // share, share, bias)
+
+    outs = []
+    ahead = logits_of(chunks[0])
+    for i, (g, c) in enumerate(chunks):
+        now = ahead
+        if i + 1 < len(chunks):
+            ahead = logits_of(chunks[i + 1])
+        outs.append(window_outputs(now, vh[g, pl.ds(base, span), :], width))
+    half = len(outs) // 2
+    return join_groups(jnp.concatenate(outs[:half], axis=0), jnp.concatenate(outs[half:], axis=0))
+
+
+def square_sums(full, heads):
+    tokens = full.shape[0] // heads
+    row = lax.broadcasted_iota(jnp.int32, (tokens, full.shape[0]), 1) // heads
+    mine = row == lax.broadcasted_iota(jnp.int32, (tokens, full.shape[0]), 0)
+    sums = jnp.dot(mine.astype(BF16), (full * full).astype(BF16), preferred_element_type=F32)
+    ones = jnp.ones((8, full.shape[1]), F32)
     return lax.dot_general(
-        ones, total, (((1,), (1,)), ((), ())), precision=lax.Precision.HIGHEST, preferred_element_type=F32
+        ones, sums, (((1,), (1,)), ((), ())), precision=lax.Precision.HIGHEST, preferred_element_type=F32
     )
 
 
-def far_kernel(heads, groups, q_ref, pk_ref, pv_ref, ck_ref, cv_ref, out_ref, qf, kf, kh, vh, of):
+def far_kernel(heads, groups, q_ref, pk_ref, pv_ref, ck_ref, cv_ref, out_ref, kf, kh, vh):
     step = pl.program_id(0)
     width = q_ref.shape[1]
 
@@ -169,15 +217,7 @@
         place(pv_ref, kf, vh, 0, groups)
         place(cv_ref, kf, vh, WIN, groups)
 
-    qf[...] = q_ref[...].astype(F32)
-    base = pl.multiple_of(step * BLK, BLK)
-    for h in range(heads):
-        g = h * groups // heads
-        out = window_rows(
-            every(q_ref, qf, heads, h), kh[g, pl.ds(base, WIN + BLK), :], vh[g, pl.ds(base, WIN + BLK), :]
-        )
-        of[pl.ds(h, BLK, stride=heads), :] = out
-    out_ref[...] = of[...]
+    out_ref[...] = window_block(q_ref, kh, vh, pl.multiple_of(step * BLK, BLK), groups)
 
 
 def attention_cost(tokens, heads, width, extra=0):
@@ -208,11 +248,9 @@
         out_specs=pl.BlockSpec((BLK * heads, width), lambda i: (i, 0)),
         out_shape=jax.ShapeDtypeStruct((steps * BLK * heads, width), F32),
         scratch_shapes=[
-            pltpu.VMEM((BLK * heads, width), F32),
             pltpu.VMEM((WIN * groups, width), F32),
             pltpu.VMEM((groups, 2 * WIN, width), BF16),
             pltpu.VMEM((groups, 2 * WIN, 2 * width), BF16),
-            pltpu.VMEM((BLK * heads, width), F32),
         ],
         compiler_params=params(),
         cost_estimate=attention_cost(steps * BLK, heads, width),
@@ -222,7 +260,7 @@
 
 def trunk_kernel(heads, groups, where_ref, gain_ref, q_ref, k_ref, v_ref, wq_ref, pk_ref, pv_ref, ck_ref, cv_ref, cross_ref, *rest):
     piece_refs, out_ref, square_ref = rest[:COLS], rest[COLS], rest[COLS + 1]
-    qf, nf, tf, sf, kf, kh, vh, of, cs = rest[COLS + 2 :]
+    nf, tf, sf, kf, kh, vh, of, cs = rest[COLS + 2 :]
     step = pl.program_id(0)
     width = q_ref.shape[1]
 
@@ -235,7 +273,6 @@
         place(cv_ref, kf, vh, WIN, groups)
         cs[...] = cross_ref[:, 0].reshape(heads, width, width)
 
-    qf[...] = wq_ref[...].astype(F32)
     nf[...] = q_ref[...].astype(F32)
     tf[...] = k_ref[...].astype(F32)
     sf[...] = v_ref[...].astype(F32)
@@ -246,25 +283,22 @@
     row = lax.broadcasted_iota(jnp.int32, (BLK, BLK), 0)
     col = lax.broadcasted_iota(jnp.int32, (BLK, BLK), 1)
     inner = (step > 0).astype(F32).astype(BF16)
-    total = jnp.zeros((BLK, width), F32)
     per_piece = heads // COLS
+    q = [every(q_ref, nf, heads, h) for h in range(heads)]
+    inside = [
+        lax.dot_general(q[h], every(k_ref, tf, heads, h), (((1,), (1,)), ((), ())), preferred_element_type=F32)
+        for h in range(heads)
+    ]
     for h in range(heads):
-        g = h * groups // heads
-        out = window_rows(
-            every(wq_ref, qf, heads, h), kh[g, pl.ds(base, span), :], vh[g, pl.ds(base, span), :], bias
+        weight = jnp.where(col <= row, inside[h], 0.0) * (gain_ref[h, 0] * gain_factor(0, width))
+        left = jnp.concatenate([weight.astype(BF16), q[h], q[h]], axis=1)
+        right = jnp.concatenate(
+            [every(v_ref, sf, heads, h), cs[h], piece_refs[h // per_piece][0, h % per_piece] * inner], axis=0
         )
-        q = every(q_ref, nf, heads, h)
-        k = every(k_ref, tf, heads, h)
-        v = every(v_ref, sf, heads, h)
-        inside = lax.dot_general(q, k, (((1,), (1,)), ((), ())), preferred_element_type=F32)
-        inside = jnp.where(col <= row, inside, 0.0) * (gain_ref[h, 0] * gain_factor(0, width))
-        left = jnp.concatenate([inside.astype(BF16), q, q], axis=1)
-        right = jnp.concatenate([v, cs[h], piece_refs[h // per_piece][0, h % per_piece] * inner], axis=0)
-        out = out + jnp.dot(left, right, preferred_element_type=F32)
-        total = total + out * out
-        of[pl.ds(h, BLK, stride=heads), :] = out
-    out_ref[...] = of[...]
-    square_ref[0] = square_sums(total)
+        of[pl.ds(h, BLK, stride=heads), :] = jnp.dot(left, right, preferred_element_type=F32)
+    full = window_block(wq_ref, kh, vh, base, groups, bias) + of[...]
+    out_ref[...] = full
+    square_ref[0] = square_sums(full, heads)
 
 
 def trunk_attention(where, gain, q, k, v, wq, pk, pv, ck, cv, cross, pieces, heads, groups):
@@ -288,7 +322,6 @@
             wide,
             wide,
             wide,
-            wide,
             pltpu.VMEM((WIN * groups, width), F32),
             pltpu.VMEM((groups, 2 * WIN, width), BF16),
             pltpu.VMEM((groups, 2 * WIN, 2 * width), BF16),
@@ -304,13 +337,12 @@
 def branch_kernel(heads, groups, where_ref, fork_ref, q_ref, wq_ref, far_ref, ck_ref, cv_ref, cross_ref, *rest):
     kv_refs, piece_refs = rest[:COLS], rest[COLS : 2 * COLS]
     out_ref, square_ref = rest[2 * COLS : 2 * COLS + 2]
-    qf, nf, kf, kh, vh, kt, of, es = rest[2 * COLS + 2 :]
+    nf, kf, kh, vh, kt, of, es = rest[2 * COLS + 2 :]
     step = pl.program_id(0)
     near = WIN // BLK
     width = q_ref.shape[1]
     fork = fork_ref[0]
     column = where_ref[0] & (COLS - 1)
-    span = WIN + BLK
     start = pl.multiple_of(fork * BLK, BLK)
 
     @pl.when(step == 0)
@@ -334,30 +366,23 @@
                 es[mine + j, width:, :] = piece_refs[i][chosen, j] * inner
 
     nf[...] = q_ref[...].astype(F32)
+    for h in range(heads):
+        q = every(q_ref, nf, heads, h)
+        both = jnp.concatenate([q, q], axis=1)
+        of[pl.ds(h, BLK, stride=heads), :] = jnp.dot(both, es[h], preferred_element_type=F32)
 
     @pl.when(step < near)
     def _():
-        qf[...] = wq_ref[...].astype(F32)
         base = pl.multiple_of(start + step * BLK, BLK)
-        for h in range(heads):
-            g = h * groups // heads
-            of[pl.ds(h, BLK, stride=heads), :] = window_rows(
-                every(wq_ref, qf, heads, h), kh[g, pl.ds(base, span), :], vh[g, pl.ds(base, span), :]
-            )
+        full = window_block(wq_ref, kh, vh, base, groups) + of[...]
+        out_ref[...] = full
+        square_ref[0] = square_sums(full, heads)
 
     @pl.when(step >= near)
     def _():
-        of[...] = far_ref[...]
-
-    total = jnp.zeros((BLK, width), F32)
-    for h in range(heads):
-        q = every(q_ref, nf, heads, h)
-        at = pl.ds(h, BLK, stride=heads)
-        out = of[at, :] + jnp.dot(jnp.concatenate([q, q], axis=1), es[h], preferred_element_type=F32)
-        total = total + out * out
-        of[at, :] = out
-    out_ref[...] = of[...]
-    square_ref[0] = square_sums(total)
+        full = far_ref[...] + of[...]
+        out_ref[...] = full
+        square_ref[0] = square_sums(full, heads)
 
 
 def branch_attention(where, fork, q, wq, far, ck, cv, cross, kvs, pieces, heads, groups):
@@ -381,7 +406,6 @@
             jax.ShapeDtypeStruct((blocks, 8, BLK), F32),
         ],
         scratch_shapes=[
-            wide,
             wide,
             pltpu.VMEM((WIN * groups, width), F32),
             pltpu.VMEM((groups, 3 * WIN, width), BF16),

time: 131 us -> 120 us (0.916)
  local copies, waits for them, and re-layouts: 15.9 us -> 2.43 us
  Pallas kernels: 47.5 us -> 53 us
  starting transfers between devices: 50.2 us -> 46.2 us
  other arithmetic: 2.76 us -> 0.18 us
  waiting for transfers between devices: 8.33 us -> 10.4 us
    unnamed x48 -> x30, local copies, waits for them, and re-layouts: 15.9 us -> 2.43 us
    pallas_call x2, Pallas kernels: 5.47 us -> 10.4 us  [normalize(): pl.pallas_call(functools.partial(norm_kernel, heads, features), grid=(blo...]
    pallas_call x1, Pallas kernels: 16.4 us -> 12 us  [trunk_attention(): pl.pallas_call(functools.partial(trunk_kernel, heads, groups), grid=(bloc...]
    ppermute x16, starting transfers between devices: 25.3 us -> 22.6 us  [send(): return lax.ppermute(x, 'seq', pairs)]
    select_n x4, other arithmetic: 2.69 us -> 0.11 us  [down(): x = jnp.where(hit, got, x)]
    pallas_call x1, Pallas kernels: 14.6 us -> 16.4 us  [branch_attention(): pl.pallas_call(functools.partial(branch_kernel, heads, groups), grid=(blo...]
    pallas_call x1, Pallas kernels: 6.37 us -> 7.94 us  [far_attention(): pl.pallas_call(functools.partial(far_kernel, heads, groups), grid=(steps,...]
  transfers between devices with their start and end apart: 18 -> 18, of which waited for: 1 -> 3; matrix products, arithmetic and copies ran while one was open for 2% -> 0% of each run, Pallas kernels for 19% -> 18%
where the time goes in v1:
time: 120 us; the launch traced here: 119 us
  Pallas kernels  53 us (44%)
  starting transfers between devices  46.2 us (38%)
  waiting for transfers between devices  10.4 us (9%)
  blocking collectives  4.68 us (4%)
  local copies, waits for them, and re-layouts  2.43 us (2%)
  between operations  1.69 us (1%)
    ppermute x16, starting transfers between devices, send(): return lax.ppermute(x, 'seq', pairs)  22.6 us
    pallas_call x1, Pallas kernels, branch_attention(): pl.pallas_call(functools.partial(branch_kernel, heads, groups), grid=(blo...  16.4 us
    pallas_call x1, Pallas kernels, trunk_attention(): pl.pallas_call(functools.partial(trunk_kernel, heads, groups), grid=(bloc...  12 us
    all_to_all x1, starting transfers between devices, shards(): slices = lax.all_to_all(slices, 'seq', 0, 0, tiled=True)  11.9 us
    all_to_all x1, starting transfers between devices, shards(): cross = lax.all_to_all(cross, 'seq', 0, 0, tiled=True)  11.7 us
    pallas_call x2, Pallas kernels, normalize(): pl.pallas_call(functools.partial(norm_kernel, heads, features), grid=(blo...  10.4 us
    all_to_all x1, waiting for transfers between devices, shards(): slices = lax.all_to_all(slices, 'seq', 0, 0, tiled=True)  9.04 us
    pallas_call x1, Pallas kernels, far_attention(): pl.pallas_call(functools.partial(far_kernel, heads, groups), grid=(steps,...  7.94 us
  transfers between devices with their start and end apart: 18, of which 3 were waited for; matrix products, arithmetic and copies ran while one was open for 0% of the time, Pallas kernels for 18%

profile of v1, /device:TPU:0, one launch (start us, length us, event | category | flops | bytes accessed | tf_op | source)
XLA Modules:
  0.0 118.5 jit_solution(16591365464639834631)
XLA Ops:
  0.6 0.0 copy-start.12
  0.6 0.0 copy-start.7
  0.7 4.4 %block_sums.1 = (bf16[3,2,128,128]{3,2,1,0:T(8,128)(2,1)}, bf16[3,2,128,128]{3,2,1,0:T(8,128)(2,1)}, bf16[3,2,128,128]{3,2,1,0:T(8,128)(2,1)}, bf16[3,2,128,128]{3,2,1,0:T(8,128)(2,1)}, bf16[8,128,128]{2,1,0:T(8,128)(2,1)}) custom-call(f32[8,11]{1,0:T(8,128)} %gain_ref.5, bf16[4096,128]{1,0:T(8,128)(2,1)} %bitcast.19, bf16[4096,128]{1,0:T(8,128)(2,1)} %bitcast.21), custom_call_target="tpu_custom_call" | custom-call | flops 134217728 | bytes 3145728 | tf_op jit(solution)/shard_map/block_sums/pallas_call | solution.py:73
  5.1 0.7 collective-permute-start.10
  5.8 0.7 collective-permute-start.8
  6.5 0.7 collective-permute-start.9
  7.1 0.0 copy-done.12
  7.2 0.7 collective-permute-start.2
  7.8 11.9 %all-to-all-start = ((bf16[16,64,128]{2,1,0:T(8,128)(2,1)}), bf16[16,64,128]{2,1,0:T(8,128)(2,1)S(1)}, u32[]{:S(2)}, u32[]{:S(2)}) async-start(bf16[16,64,128]{2,1,0:T(8,128)(2,1)} %bitcast.29), calls=%async_computation | async-start | bytes 524288 | tf_op jit(solution)/shard_map/all_to_all | solution.py:511
  19.8 0.0 collective-permute-done.10
  19.8 0.0 collective-permute-done.8
  19.8 0.0 collective-permute-done.9
  19.9 0.7 collective-permute-start.11
  20.6 0.0 collective-permute-done.2
  20.6 0.0 copy-done.7
  20.6 0.7 collective-permute-start.3
  21.3 9.0 %all-to-all-done.sums_ref = bf16[16,64,128]{2,1,0:T(8,128)(2,1)S(1)} async-done(((bf16[16,64,128]{2,1,0:T(8,128)(2,1)}), bf16[16,64,128]{2,1,0:T(8,128)(2,1)S(1)}, u32[]{:S(2)}, u32[]{:S(2)}) %all-to-all-start) | async-done | bytes 262176 | tf_op jit(solution)/shard_map/all_to_all | solution.py:511
  30.4 0.7 copy-done.2
  31.1 1.9 %cross_sums.1 = bf16[16,2,64,128]{3,2,1,0:T(8,128)(2,1)} custom-call(s32[1]{0:T(128)} %bitcast.where_ref, f32[8,11]{1,0:T(8,128)} %gain_ref.5, bf16[16,64,128]{2,1,0:T(8,128)(2,1)} %copy-done.2), custom_call_target="tpu_custom_call" | custom-call | flops 2621440 | bytes 786432 | tf_op jit(solution)/shard_map/cross_sums/pallas_call | solution.py:118
  32.9 11.7 %all-to-all-start.1 = ((bf16[16,2,64,128]{3,2,1,0:T(8,128)(2,1)}), bf16[16,2,64,128]{3,2,1,0:T(8,128)(2,1)S(1)}, u32[]{:S(2)}, u32[]{:S(2)}) async-start(bf16[16,2,64,128]{3,2,1,0:T(8,128)(2,1)} %cross_sums.1), calls=%async_computation.1 | async-start | bytes 1048576 | tf_op jit(solution)/shard_map/all_to_all | solution.py:513
  44.6 0.0 collective-permute-done.11
  44.7 1.3 %collective-permute-start.12 = (bf16[3,2,128,128]{3,2,1,0:T(8,128)(2,1)S(1)}, bf16[3,2,128,128]{3,2,1,0:T(8,128)(2,1)S(1)}, u32[]{:S(2)}, u32[]{:S(2)}) collective-permute-start(bf16[3,2,128,128]{3,2,1,0:T(8,128)(2,1)S(1)} %broadcast_select_fusion.3), channel_id=1, source_target_pairs={{8,0},{10,2},{12,4},{14,6},{24,16},{26,18},{28,20},{30,22},{9,1},{... | collective-permute-start | bytes 589832 | tf_op jit(solution)/shard_map/ppermute | solution.py:481
  46.0 0.0 collective-permute-done.3
  46.0 1.3 %collective-permute-start.4 = (bf16[1024,128]{1,0:T(8,128)(2,1)S(1)}, bf16[1024,128]{1,0:T(8,128)(2,1)S(1)}, u32[]{:S(2)}, u32[]{:S(2)}) collective-permute-start(bf16[1024,128]{1,0:T(8,128)(2,1)S(1)} %broadcast_select_fusion.1), channel_id=1, source_target_pairs={{8,0},{10,2},{12,4},{14,6},{24,16},{26,18},{28,20},{30,22},{9,1},{... | collective-permute-start | bytes 786440 | tf_op jit(solution)/shard_map/ppermute | solution.py:481
  47.3 3.8 %collective-permute-start = (bf16[1024,128]{1,0:T(8,128)(2,1)S(1)}, bf16[1024,128]{1,0:T(8,128)(2,1)S(1)}, u32[]{:S(2)}, u32[]{:S(2)}) collective-permute-start(bf16[1024,128]{1,0:T(8,128)(2,1)S(1)} %bitcast.32), channel_id=1, source_target_pairs={{0,2},{2,4},{4,6},{6,8},{8,10},{10,12},{12,14},{14,16},{16,18},{18... | collective-permute-start | bytes 786440 | tf_op jit(solution)/shard_map/ppermute | solution.py:481
  51.2 3.4 %collective-permute-start.1 = (bf16[1024,128]{1,0:T(8,128)(2,1)S(1)}, bf16[1024,128]{1,0:T(8,128)(2,1)S(1)}, u32[]{:S(2)}, u32[]{:S(2)}) collective-permute-start(bf16[1024,128]{1,0:T(8,128)(2,1)S(1)} %bitcast.37), channel_id=1, source_target_pairs={{0,2},{2,4},{4,6},{6,8},{8,10},{10,12},{12,14},{14,16},{16,18},{18... | collective-permute-start | bytes 786440 | tf_op jit(solution)/shard_map/ppermute | solution.py:481
  54.5 0.1 collective-permute-done.12
  54.6 0.0 copy-start.3
  54.6 1.5 %collective-permute-start.13 = (bf16[3,2,128,128]{3,2,1,0:T(8,128)(2,1)S(1)}, bf16[3,2,128,128]{3,2,1,0:T(8,128)(2,1)S(1)}, u32[]{:S(2)}, u32[]{:S(2)}) collective-permute-start(bf16[3,2,128,128]{3,2,1,0:T(8,128)(2,1)S(1)} %broadcast_select_fusion.4.rest_4_), channel_id=1, source_target_pairs={{0,2},{2,0},{4,6},{6,4},{8,10},{10,8},{12,14},{14,12},{16,18},{18,... | collective-permute-start | bytes 589832 | tf_op jit(solution)/shard_map/ppermute | solution.py:481
  56.2 1.2 %collective-permute-done.4 = bf16[1024,128]{1,0:T(8,128)(2,1)S(1)} collective-permute-done((bf16[1024,128]{1,0:T(8,128)(2,1)S(1)}, bf16[1024,128]{1,0:T(8,128)(2,1)S(1)}, u32[]{:S(2)}, u32[]{:S(2)}) %collective-permute-start.4) | collective-permute-done | bytes 262176 | tf_op jit(solution)/shard_map/ppermute | solution.py:481
  57.4 0.0 copy-start.1
  57.5 1.5 %collective-permute-start.5 = (bf16[1024,128]{1,0:T(8,128)(2,1)S(1)}, bf16[1024,128]{1,0:T(8,128)(2,1)S(1)}, u32[]{:S(2)}, u32[]{:S(2)}) collective-permute-start(bf16[1024,128]{1,0:T(8,128)(2,1)S(1)} %broadcast_select_fusion.2.rest_0_), channel_id=1, source_target_pairs={{0,2},{2,0},{4,6},{6,4},{8,10},{10,8},{12,14},{14,12},{16,18},{18,... | collective-permute-start | bytes 786440 | tf_op jit(solution)/shard_map/ppermute | solution.py:481
  59.0 1.5 %collective-permute-start.6 = (bf16[1024,128]{1,0:T(8,128)(2,1)S(1)}, bf16[1024,128]{1,0:T(8,128)(2,1)S(1)}, u32[]{:S(2)}, u32[]{:S(2)}) collective-permute-start(bf16[1024,128]{1,0:T(8,128)(2,1)S(1)} %broadcast_select_fusion.2.rest_0_), channel_id=1, source_target_pairs={{0,4},{2,6},{4,0},{6,2},{8,12},{10,14},{12,8},{14,10},{16,20},{18,... | collective-permute-start | bytes 786440 | tf_op jit(solution)/shard_map/ppermute | solution.py:481
  60.4 0.0 collective-permute-done.pk_ref
  60.5 1.2 collective-permute-start.7
  61.6 7.9 %far_attention.1.far_ref = f32[4096,128]{1,0:T(8,128)} custom-call(bf16[8192,128]{1,0:T(8,128)(2,1)} %bitcast.15, bf16[2048,128]{1,0:T(8,128)(2,1)} %bitcast.23, bf16[2048,128]{1,0:T(8,128)(2,1)} %bitcast.26, bf16[2048,128]{1,0:T(8,128)(2,1)} %bitcast.24, bf16[2048,128]{1,0:T(8,128)(2,1)} %bitcast.27), custom_call_target="tpu_custom_call" | custom-call | flops 2013265920 | bytes 6291456 | tf_op jit(solution)/shard_map/far_attention/pallas_call | solution.py:238
  69.6 0.0 copy-done.1
  69.6 0.0 copy-done.13
  70.2 0.0 collective-permute-done.1.pv_ref
  70.2 0.0 copy-start.14
  70.2 0.9 collective-permute-start.14
  71.1 0.0 collective-permute-done.13.rest_5_
  71.1 0.0 copy-done.3
  71.2 2.1 %collective-permute-start.15 = (bf16[3,2,128,128]{3,2,1,0:T(8,128)(2,1)S(1)}, bf16[3,2,128,128]{3,2,1,0:T(8,128)(2,1)S(1)}, u32[]{:S(2)}, u32[]{:S(2)}) collective-permute-start(bf16[3,2,128,128]{3,2,1,0:T(8,128)(2,1)S(1)} %broadcast_select_fusion.4.rest_4_), channel_id=1, source_target_pairs={{0,6},{2,4},{4,2},{6,0},{8,14},{10,12},{12,10},{14,8},{16,22},{18,... | collective-permute-start | bytes 589832 | tf_op jit(solution)/shard_map/ppermute | solution.py:481
  73.3 0.0 all-to-all-done.1.cross_ref
  73.3 0.0 copy-done.14
  73.3 0.8 copy-done
  74.1 12.0 %trunk_attention.1 = (f32[4096,128]{1,0:T(8,128)}, f32[4,8,128]{2,1,0:T(8,128)}) custom-call(s32[1]{0:T(128)} %bitcast.where_ref, f32[8,11]{1,0:T(8,128)} %gain_ref.5, bf16[4096,128]{1,0:T(8,128)(2,1)} %bitcast.33, bf16[4096,128]{1,0:T(8,128)(2,1)} %bitcast.20, bf16[4096,128]{1,0:T(8,128)(2,1)} %bitcast.22, bf16[4096,128]{1,0:T(8,128)(2,1)} %bitcast.34, ...), custom_call_target="tpu_custom_call" | custom-call | flops 2550136832 | bytes 6291456 | tf_op jit(solution)/shard_map/trunk_attention/pallas_call | solution.py:312
  86.1 0.0 collective-permute-done.14.rest_6_
  86.1 0.0 copy-start.9
  86.1 0.0 collective-permute-done.15.rest_7_
  86.1 0.0 collective-permute-done.5.rest_1_
  86.1 0.0 collective-permute-done.6.rest_2_
  86.1 0.0 copy-start.5
  86.1 0.0 collective-permute-done.7.rest_3_
  86.2 0.6 copy-done.9
  86.8 0.1 copy-done.10
  86.8 0.1 copy-done.4
  86.9 0.1 copy-done.5
  87.0 0.1 copy-done.6
  87.1 16.4 %branch_attention.1 = (f32[8192,128]{1,0:T(8,128)}, f32[8,8,128]{2,1,0:T(8,128)}) custom-call(s32[1]{0:T(128)} %bitcast.where_ref, s32[1]{0:T(128)S(6)} %copy.14.fork_ref, bf16[8192,128]{1,0:T(8,128)(2,1)} %bitcast.14, bf16[8192,128]{1,0:T(8,128)(2,1)} %bitcast.16, f32[4096,128]{1,0:T(8,128)} %far_attention.1.far_ref, bf16[2048,128]{1,0:T(8,128)(2,1)} %bitcast.25, ...), custom_call_target="tpu_custom_call" | custom-call | flops 2550136832 | bytes 6291456 | tf_op jit(solution)/shard_map/branch_attention/pallas_call | solution.py:399
  103.4 4.7 %all-reduce = (f32[4,8,128]{2,1,0:T(8,128)}, f32[8,8,128]{2,1,0:T(8,128)}) all-reduce(f32[4,8,128]{2,1,0:T(8,128)S(1)} %copy-done.11, f32[8,8,128]{2,1,0:T(8,128)} %get-tuple-element.19), channel_id=1, replica_groups=mesh['seq'=16,'head'=2] {'head'}, use_global_device_ids=true, to_apply=%region_0.1 | all-reduce | flops 12288 | bytes 98304 | tf_op jit(solution)/shard_map/psum | solution.py:519
  108.1 6.6 %branch_norm.1 = bf16[8192,128]{1,0:T(8,128)(2,1)} custom-call(f32[8192,128]{1,0:T(8,128)} %get-tuple-element.18.full_ref, f32[8,8,128]{2,1,0:T(8,128)} %get-tuple-element.21.square_ref), custom_call_target="tpu_custom_call" | custom-call | flops 2097152 | bytes 6291456 | tf_op jit(solution)/shard_map/branch_norm/pallas_call | solution.py:435
  114.7 3.8 %trunk_norm.1 = bf16[4096,128]{1,0:T(8,128)(2,1)} custom-call(f32[4096,128]{1,0:T(8,128)} %get-tuple-element.16.full_ref, f32[4,8,128]{2,1,0:T(8,128)} %get-tuple-element.20.square_ref), custom_call_target="tpu_custom_call" | custom-call | flops 1048576 | bytes 3145728 | tf_op jit(solution)/shard_map/trunk_norm/pallas_call | solution.py:435
  (16 shorter events, 0.2 us)
Async XLA Ops:
  0.6 6.5 %copy-start.12 = (bf16[512,2,128]{2,1,0:T(2,128)(2,1)S(1)}, bf16[512,2,128]{2,1,0:T(2,128)(2,1)}, u32[]{:S(2)}) copy-start(bf16[512,2,128]{2,1,0:T(2,128)(2,1)} %param.17) | copy-start | bytes 786436
  0.6 19.9 %copy-start.7 = (bf16[512,2,128]{2,1,0:T(2,128)(2,1)S(1)}, bf16[512,2,128]{2,1,0:T(2,128)(2,1)}, u32[]{:S(2)}) copy-start(bf16[512,2,128]{2,1,0:T(2,128)(2,1)} %param.16) | copy-start | bytes 786436
  5.1 14.7 %collective-permute-start.10 = (bf16[3,2,128,128]{3,2,1,0:T(8,128)(2,1)}, bf16[3,2,128,128]{3,2,1,0:T(8,128)(2,1)S(1)}, u32[]{:S(2)}, u32[]{:S(2)}) collective-permute-start(bf16[3,2,128,128]{3,2,1,0:T(8,128)(2,1)} %get-tuple-element.12.rest_0_), channel_id=1, source_target_pairs={{30,24},{31,25}} | collective-permute-start | bytes 589832 | tf_op jit(solution)/shard_map/ppermute | solution.py:481
  5.8 14.0 %collective-permute-start.8 = (bf16[3,2,128,128]{3,2,1,0:T(8,128)(2,1)}, bf16[3,2,128,128]{3,2,1,0:T(8,128)(2,1)S(1)}, u32[]{:S(2)}, u32[]{:S(2)}) collective-permute-start(bf16[3,2,128,128]{3,2,1,0:T(8,128)(2,1)} %get-tuple-element.14.rest_2_), channel_id=1, source_target_pairs={{30,28},{31,29}} | collective-permute-start | bytes 589832 | tf_op jit(solution)/shard_map/ppermute | solution.py:481
  6.5 13.4 %collective-permute-start.9 = (bf16[3,2,128,128]{3,2,1,0:T(8,128)(2,1)}, bf16[3,2,128,128]{3,2,1,0:T(8,128)(2,1)S(1)}, u32[]{:S(2)}, u32[]{:S(2)}) collective-permute-start(bf16[3,2,128,128]{3,2,1,0:T(8,128)(2,1)} %get-tuple-element.13.rest_1_), channel_id=1, source_target_pairs={{30,26},{31,27}} | collective-permute-start | bytes 589832 | tf_op jit(solution)/shard_map/ppermute | solution.py:481
  7.2 13.4 %collective-permute-start.2 = (bf16[1024,128]{1,0:T(8,128)(2,1)S(1)}, bf16[1024,128]{1,0:T(8,128)(2,1)S(1)}, u32[]{:S(2)}, u32[]{:S(2)}) collective-permute-start(bf16[1024,128]{1,0:T(8,128)(2,1)S(1)} %bitcast.36), channel_id=1, source_target_pairs={{30,26},{28,24},{31,27},{29,25}} | collective-permute-start | bytes 786440 | tf_op jit(solution)/shard_map/ppermute | solution.py:481
  7.8 22.5 %all-to-all-start = ((bf16[16,64,128]{2,1,0:T(8,128)(2,1)}), bf16[16,64,128]{2,1,0:T(8,128)(2,1)S(1)}, u32[]{:S(2)}, u32[]{:S(2)}) async-start(bf16[16,64,128]{2,1,0:T(8,128)(2,1)} %bitcast.29), calls=%async_computation | async-start | bytes 524288 | tf_op jit(solution)/shard_map/all_to_all | solution.py:511
  19.9 24.7 %collective-permute-start.11 = (bf16[3,2,128,128]{3,2,1,0:T(8,128)(2,1)S(1)}, bf16[3,2,128,128]{3,2,1,0:T(8,128)(2,1)S(1)}, u32[]{:S(2)}, u32[]{:S(2)}) collective-permute-start(bf16[3,2,128,128]{3,2,1,0:T(8,128)(2,1)S(1)} %select_select_fusion), channel_id=1, source_target_pairs={{24,8},{26,10},{28,12},{30,14},{25,9},{27,11},{29,13},{31,15}} | collective-permute-start | bytes 589832 | tf_op jit(solution)/shard_map/ppermute | solution.py:481
  20.6 25.3 %collective-permute-start.3 = (bf16[1024,128]{1,0:T(8,128)(2,1)S(1)}, bf16[1024,128]{1,0:T(8,128)(2,1)S(1)}, u32[]{:S(2)}, u32[]{:S(2)}) collective-permute-start(bf16[1024,128]{1,0:T(8,128)(2,1)S(1)} %broadcast_select_fusion), channel_id=1, source_target_pairs={{24,8},{26,10},{28,12},{30,14},{25,9},{27,11},{29,13},{31,15}} | collective-permute-start | bytes 786440 | tf_op jit(solution)/shard_map/ppermute | solution.py:481
  30.4 0.7 copy-start.2
  32.9 40.4 %all-to-all-start.1 = ((bf16[16,2,64,128]{3,2,1,0:T(8,128)(2,1)}), bf16[16,2,64,128]{3,2,1,0:T(8,128)(2,1)S(1)}, u32[]{:S(2)}, u32[]{:S(2)}) async-start(bf16[16,2,64,128]{3,2,1,0:T(8,128)(2,1)} %cross_sums.1), calls=%async_computation.1 | async-start | bytes 1048576 | tf_op jit(solution)/shard_map/all_to_all | solution.py:513
  44.7 9.9 %collective-permute-start.12 = (bf16[3,2,128,128]{3,2,1,0:T(8,128)(2,1)S(1)}, bf16[3,2,128,128]{3,2,1,0:T(8,128)(2,1)S(1)}, u32[]{:S(2)}, u32[]{:S(2)}) collective-permute-start(bf16[3,2,128,128]{3,2,1,0:T(8,128)(2,1)S(1)} %broadcast_select_fusion.3), channel_id=1, source_target_pairs={{8,0},{10,2},{12,4},{14,6},{24,16},{26,18},{28,20},{30,22},{9,1},{... | collective-permute-start | bytes 589832 | tf_op jit(solution)/shard_map/ppermute | solution.py:481
  46.0 11.4 %collective-permute-start.4 = (bf16[1024,128]{1,0:T(8,128)(2,1)S(1)}, bf16[1024,128]{1,0:T(8,128)(2,1)S(1)}, u32[]{:S(2)}, u32[]{:S(2)}) collective-permute-start(bf16[1024,128]{1,0:T(8,128)(2,1)S(1)} %broadcast_select_fusion.1), channel_id=1, source_target_pairs={{8,0},{10,2},{12,4},{14,6},{24,16},{26,18},{28,20},{30,22},{9,1},{... | collective-permute-start | bytes 786440 | tf_op jit(solution)/shard_map/ppermute | solution.py:481
  47.3 13.1 %collective-permute-start = (bf16[1024,128]{1,0:T(8,128)(2,1)S(1)}, bf16[1024,128]{1,0:T(8,128)(2,1)S(1)}, u32[]{:S(2)}, u32[]{:S(2)}) collective-permute-start(bf16[1024,128]{1,0:T(8,128)(2,1)S(1)} %bitcast.32), channel_id=1, source_target_pairs={{0,2},{2,4},{4,6},{6,8},{8,10},{10,12},{12,14},{14,16},{16,18},{18... | collective-permute-start | bytes 786440 | tf_op jit(solution)/shard_map/ppermute | solution.py:481
  51.2 19.1 %collective-permute-start.1 = (bf16[1024,128]{1,0:T(8,128)(2,1)S(1)}, bf16[1024,128]{1,0:T(8,128)(2,1)S(1)}, u32[]{:S(2)}, u32[]{:S(2)}) collective-permute-start(bf16[1024,128]{1,0:T(8,128)(2,1)S(1)} %bitcast.37), channel_id=1, source_target_pairs={{0,2},{2,4},{4,6},{6,8},{8,10},{10,12},{12,14},{14,16},{16,18},{18... | collective-permute-start | bytes 786440 | tf_op jit(solution)/shard_map/ppermute | solution.py:481
  54.6 16.5 %copy-start.3 = (bf16[3,2,128,128]{3,2,1,0:T(8,128)(2,1)}, bf16[3,2,128,128]{3,2,1,0:T(8,128)(2,1)S(1)}, u32[]{:S(2)}) copy-start(bf16[3,2,128,128]{3,2,1,0:T(8,128)(2,1)S(1)} %broadcast_select_fusion.4.rest_4_) | copy-start | bytes 589828
  54.6 16.5 %collective-permute-start.13 = (bf16[3,2,128,128]{3,2,1,0:T(8,128)(2,1)S(1)}, bf16[3,2,128,128]{3,2,1,0:T(8,128)(2,1)S(1)}, u32[]{:S(2)}, u32[]{:S(2)}) collective-permute-start(bf16[3,2,128,128]{3,2,1,0:T(8,128)(2,1)S(1)} %broadcast_select_fusion.4.rest_4_), channel_id=1, source_target_pairs={{0,2},{2,0},{4,6},{6,4},{8,10},{10,8},{12,14},{14,12},{16,18},{18,... | collective-permute-start | bytes 589832 | tf_op jit(solution)/shard_map/ppermute | solution.py:481
  57.4 12.1 %copy-start.1 = (bf16[1024,128]{1,0:T(8,128)(2,1)}, bf16[1024,128]{1,0:T(8,128)(2,1)S(1)}, u32[]{:S(2)}) copy-start(bf16[1024,128]{1,0:T(8,128)(2,1)S(1)} %broadcast_select_fusion.2.rest_0_) | copy-start | bytes 786436
  57.5 28.6 %collective-permute-start.5 = (bf16[1024,128]{1,0:T(8,128)(2,1)S(1)}, bf16[1024,128]{1,0:T(8,128)(2,1)S(1)}, u32[]{:S(2)}, u32[]{:S(2)}) collective-permute-start(bf16[1024,128]{1,0:T(8,128)(2,1)S(1)} %broadcast_select_fusion.2.rest_0_), channel_id=1, source_target_pairs={{0,2},{2,0},{4,6},{6,4},{8,10},{10,8},{12,14},{14,12},{16,18},{18,... | collective-permute-start | bytes 786440 | tf_op jit(solution)/shard_map/ppermute | solution.py:481
  59.0 27.1 %collective-permute-start.6 = (bf16[1024,128]{1,0:T(8,128)(2,1)S(1)}, bf16[1024,128]{1,0:T(8,128)(2,1)S(1)}, u32[]{:S(2)}, u32[]{:S(2)}) collective-permute-start(bf16[1024,128]{1,0:T(8,128)(2,1)S(1)} %broadcast_select_fusion.2.rest_0_), channel_id=1, source_target_pairs={{0,4},{2,6},{4,0},{6,2},{8,12},{10,14},{12,8},{14,10},{16,20},{18,... | collective-permute-start | bytes 786440 | tf_op jit(solution)/shard_map/ppermute | solution.py:481
  60.5 9.1 %copy-start.13 = (bf16[1024,128]{1,0:T(8,128)(2,1)}, bf16[1024,128]{1,0:T(8,128)(2,1)S(1)}, u32[]{:S(2)}) copy-start(bf16[1024,128]{1,0:T(8,128)(2,1)S(1)} %collective-permute-done.pk_ref) | copy-start | bytes 786436
  60.5 25.7 %collective-permute-start.7 = (bf16[1024,128]{1,0:T(8,128)(2,1)S(1)}, bf16[1024,128]{1,0:T(8,128)(2,1)S(1)}, u32[]{:S(2)}, u32[]{:S(2)}) collective-permute-start(bf16[1024,128]{1,0:T(8,128)(2,1)S(1)} %broadcast_select_fusion.2.rest_0_), channel_id=1, source_target_pairs={{0,6},{2,4},{4,2},{6,0},{8,14},{10,12},{12,10},{14,8},{16,22},{18,... | collective-permute-start | bytes 786440 | tf_op jit(solution)/shard_map/ppermute | solution.py:481
  70.2 3.1 %copy-start.14 = (bf16[1024,128]{1,0:T(8,128)(2,1)}, bf16[1024,128]{1,0:T(8,128)(2,1)S(1)}, u32[]{:S(2)}) copy-start(bf16[1024,128]{1,0:T(8,128)(2,1)S(1)} %collective-permute-done.1.pv_ref) | copy-start | bytes 786436
  70.2 15.8 %collective-permute-start.14 = (bf16[3,2,128,128]{3,2,1,0:T(8,128)(2,1)S(1)}, bf16[3,2,128,128]{3,2,1,0:T(8,128)(2,1)S(1)}, u32[]{:S(2)}, u32[]{:S(2)}) collective-permute-start(bf16[3,2,128,128]{3,2,1,0:T(8,128)(2,1)S(1)} %broadcast_select_fusion.4.rest_4_), channel_id=1, source_target_pairs={{0,4},{2,6},{4,0},{6,2},{8,12},{10,14},{12,8},{14,10},{16,20},{18,... | collective-permute-start | bytes 589832 | tf_op jit(solution)/shard_map/ppermute | solution.py:481
  71.2 15.0 %copy-start.8 = (bf16[3,2,128,128]{3,2,1,0:T(8,128)(2,1)}, bf16[3,2,128,128]{3,2,1,0:T(8,128)(2,1)S(1)}, u32[]{:S(2)}) copy-start(bf16[3,2,128,128]{3,2,1,0:T(8,128)(2,1)S(1)} %collective-permute-done.13.rest_5_) | copy-start | bytes 589828
  71.2 14.9 %collective-permute-start.15 = (bf16[3,2,128,128]{3,2,1,0:T(8,128)(2,1)S(1)}, bf16[3,2,128,128]{3,2,1,0:T(8,128)(2,1)S(1)}, u32[]{:S(2)}, u32[]{:S(2)}) collective-permute-start(bf16[3,2,128,128]{3,2,1,0:T(8,128)(2,1)S(1)} %broadcast_select_fusion.4.rest_4_), channel_id=1, source_target_pairs={{0,6},{2,4},{4,2},{6,0},{8,14},{10,12},{12,10},{14,8},{16,22},{18,... | collective-permute-start | bytes 589832 | tf_op jit(solution)/shard_map/ppermute | solution.py:481
  73.3 0.8 copy-start
  86.1 0.7 copy-start.9
  86.1 0.8 copy-start.10
  86.1 0.8 copy-start.4
  86.1 0.9 copy-start.5
  86.2 0.9 copy-start.6
  87.1 16.4 %copy-start.11 = (f32[4,8,128]{2,1,0:T(8,128)S(1)}, f32[4,8,128]{2,1,0:T(8,128)}, u32[]{:S(2)}) copy-start(f32[4,8,128]{2,1,0:T(8,128)} %get-tuple-element.17) | copy-start | bytes 49156

commit v2 on v1

v2 whole, which is shorter than its diff:
```python
import functools
import math

import jax
import jax.numpy as jnp
from jax import lax
from jax.experimental import pallas as pl
from jax.experimental.pallas import tpu as pltpu
from jax.sharding import PartitionSpec as P

BLK = 128
WIN = 512
COLS = 4
MASKED = -1e30
F32 = jnp.float32
BF16 = jnp.bfloat16
VMEM_BYTES = 60 * 1024 * 1024
SMALL_BYTES = 28 * 1024 * 1024


def params(limit=VMEM_BYTES):
    return pltpu.CompilerParams(vmem_limit_bytes=limit)


def hbm():
    return pl.BlockSpec(memory_space=pltpu.HBM)


def vmem():
    return pl.BlockSpec(memory_space=pltpu.VMEM)


def block_copy(src, dst, sems, block, rows, src_block=None):
    src_block = block if src_block is None else src_block
    return pltpu.make_async_copy(
        src.at[pl.ds(src_block * rows, rows)], dst.at[pl.ds(block * rows, rows)], sems.at[block]
    )


def smem():
    return pl.BlockSpec(memory_space=pltpu.SMEM)


def gain_factor(level, width):
    return 1.0 / math.sqrt(width * BLK * 2 ** max(level - 1, 0))


def every(rows_ref, wide, count, each):
    return wide[pl.ds(each, rows_ref.shape[0] // count, stride=count), :].astype(BF16)


def state_kernel(depth, heads, gain_ref, k_hbm, v_hbm, *rest):
    piece_refs, sum_ref = rest[:COLS], rest[COLS]
    keys, values, kf, vf, levels, key_sems, value_sems = rest[COLS + 1 :]
    rows, width = kf.shape
    per_piece = heads // COLS
    copies = [
        (block_copy(k_hbm, keys, key_sems, b, rows), block_copy(v_hbm, values, value_sems, b, rows))
        for b in range(1 << depth)
    ]
    for pair in copies:
        for copy in pair:
            copy.start()
    for b, pair in enumerate(copies):
        for copy in pair:
            copy.wait()
        kf[...] = keys[b * rows : (b + 1) * rows].astype(F32)
        vf[...] = values[b * rows : (b + 1) * rows].astype(F32)
        for h in range(heads):
            k = kf[pl.ds(h, BLK, stride=heads), :].astype(BF16)
            v = vf[pl.ds(h, BLK, stride=heads), :].astype(BF16)
            merged = lax.dot_general(k, v, (((0,), (0,)), ((), ())), preferred_element_type=F32)
            before = None
            for bit in range(depth):
                if b >> bit & 1:
                    part = levels[bit, h] * (gain_ref[h, bit + 1] * gain_factor(bit + 1, width))
                    before = part if before is None else before + part
            carry = 0
            while b >> carry & 1:
                merged = merged + levels[carry, h]
                carry += 1
            if before is not None:
                piece_refs[h // per_piece][b - 1, h % per_piece] = before.astype(BF16)
            if carry < depth:
                levels[carry, h] = merged
            else:
                sum_ref[h // per_piece, h % per_piece] = merged.astype(BF16)


def block_sums(gain, keys, values, heads, depth):
    blocks = 1 << depth
    rows, width = keys.shape[0] // blocks, keys.shape[1]
    piece = jax.ShapeDtypeStruct((blocks - 1, heads // COLS, width, width), BF16)
    return pl.pallas_call(
        functools.partial(state_kernel, depth, heads),
        in_specs=[smem(), hbm(), hbm()],
        out_specs=[vmem()] * (COLS + 1),
        out_shape=[piece] * COLS + [jax.ShapeDtypeStruct((COLS, heads // COLS, width, width), BF16)],
        scratch_shapes=[
            pltpu.VMEM(keys.shape, BF16),
            pltpu.VMEM(values.shape, BF16),
            pltpu.VMEM((rows, width), F32),
            pltpu.VMEM((rows, width), F32),
            pltpu.VMEM((depth, heads, width, width), F32),
            pltpu.SemaphoreType.DMA((blocks,)),
            pltpu.SemaphoreType.DMA((blocks,)),
        ],
        compiler_params=params(),
        cost_estimate=pl.CostEstimate(
            flops=2 * keys.size * width, bytes_accessed=4 * keys.size + 2 * heads * width * width * blocks, transcendentals=0
        ),
        name="block_sums",
    )(gain, keys, values)


def in_plane(sums, column, weight):
    total = None
    for bit in range(COLS.bit_length() - 1):
        if column >> bit & 1:
            first = ((column >> bit) ^ 1) << bit
            part = functools.reduce(jnp.add, sums[first : first + (1 << bit)]) * weight(bit)
            total = part if total is None else total + part
    return total


def level_weight(gain_ref, head, depth, width, bit):
    return gain_ref[head, depth + bit + 1] * gain_factor(depth + bit + 1, width)


def plane_kernel(depth, where_ref, gain_ref, sums_ref, local_ref, plane_ref, ends_ref):
    each, width = sums_ref.shape[1], sums_ref.shape[2]
    first = (where_ref[0] & (COLS - 1)) * each
    for j in range(each):
        sums = [sums_ref[c, j].astype(F32) for c in range(COLS)]
        whole = functools.reduce(jnp.add, sums).astype(BF16)
        for p in range(plane_ref.shape[0]):
            plane_ref[p, j] = whole
        before = in_plane(sums, COLS - 1, lambda bit: level_weight(gain_ref, first + j, depth, width, bit))
        ends_ref[0, j] = before.astype(BF16)
        for f in range(local_ref.shape[0]):
            ends_ref[f + 1, j] = (before + local_ref[f, j].astype(F32)).astype(BF16)


def plane_sums(where, gain, sums, local, planes, depth):
    quarter = sums.shape[1:]
    return pl.pallas_call(
        functools.partial(plane_kernel, depth),
        in_specs=[smem(), smem(), vmem(), vmem()],
        out_specs=[vmem(), vmem()],
        out_shape=[
            jax.ShapeDtypeStruct((planes, *quarter), BF16),
            jax.ShapeDtypeStruct((local.shape[0] + 1, *quarter), BF16),
        ],
        compiler_params=params(),
        cost_estimate=pl.CostEstimate(flops=4 * sums.size, bytes_accessed=8 * sums.size, transcendentals=0),
        name="plane_sums",
    )(where, gain, sums, local)


def cross_kernel(depth, where_ref, gain_ref, sums_ref, planes_ref, out_ref, top_ref):
    each, width = sums_ref.shape[1], sums_ref.shape[2]
    planes = planes_ref.shape[0]
    col_bits = COLS.bit_length() - 1
    plane = where_ref[0] >> col_bits
    first = (where_ref[0] & (COLS - 1)) * each
    for j in range(each):
        sums = [sums_ref[c, j].astype(F32) for c in range(COLS)]
        above = jnp.zeros((width, width), F32)
        top = jnp.zeros((width, width), F32)
        for s in range(planes - 1):
            state = planes_ref[s, j].astype(F32)
            share = jnp.float32(0.0)
            for bit in range(planes.bit_length() - 1):
                weight = level_weight(gain_ref, first + j, depth, width, col_bits + bit)
                held = jnp.logical_and((plane >> bit) & 1 == 1, (plane >> bit) ^ 1 == s >> bit)
                share = share + jnp.where(held, weight, 0.0)
                if ((planes - 1) >> bit) ^ 1 == s >> bit:
                    top = top + state * weight
            above = above + state * share
        top_ref[j] = top
        for c in range(COLS):
            before = in_plane(sums, c, lambda bit: level_weight(gain_ref, first + j, depth, width, bit))
            out_ref[c, j] = (above if before is None else above + before).astype(BF16)


def cross_sums(where, gain, sums, planes, depth):
    return pl.pallas_call(
        functools.partial(cross_kernel, depth),
        in_specs=[smem(), smem(), vmem(), vmem()],
        out_specs=[vmem(), vmem()],
        out_shape=[jax.ShapeDtypeStruct(sums.shape, BF16), jax.ShapeDtypeStruct(sums.shape[1:], F32)],
        compiler_params=params(),
        cost_estimate=pl.CostEstimate(flops=20 * sums.size, bytes_accessed=8 * sums.size, transcendentals=0),
        name="cross_sums",
    )(where, gain, sums, planes)


def place(src_ref, wide, dst, start, groups):
    tokens = src_ref.shape[0] // groups
    wide[...] = src_ref[...].astype(F32)
    for g in range(groups):
        part = wide[pl.ds(g, tokens, stride=groups), :].astype(BF16)
        dst[g, pl.ds(start, tokens), : src_ref.shape[1]] = part


def split_groups(wide):
    rows, width = wide.shape
    pairs = wide.reshape(rows // 16, 16, width)
    low, high = pairs[:, :8], pairs[:, 8:]
    upper = lax.broadcasted_iota(jnp.int32, low.shape, 1) < 4
    first = jnp.where(upper, low, pltpu.roll(high, 4, 1))
    second = jnp.where(upper, pltpu.roll(low, 4, 1), high)
    return [part.reshape(rows // 2, width) for part in (first, second)]


def join_groups(first, second):
    rows, width = first.shape
    first, second = (part.reshape(rows // 8, 8, width) for part in (first, second))
    upper = lax.broadcasted_iota(jnp.int32, first.shape, 1) < 4
    low = jnp.where(upper, first, pltpu.roll(second, 4, 1))
    high = jnp.where(upper, pltpu.roll(first, 4, 1), second)
    return jnp.concatenate([low, high], axis=1).reshape(2 * rows, width)


def window_logits(queries, keys, token, share, bias):
    rows = queries.shape[0]
    logits = lax.dot_general(queries, keys, (((1,), (1,)), ((), ())), preferred_element_type=F32)
    row = token + lax.broadcasted_iota(jnp.int32, (rows, BLK), 0) // share
    col = lax.broadcasted_iota(jnp.int32, (rows, BLK), 1)
    late = col > row
    first = jnp.where(late, logits[:, :BLK], MASKED)
    last = jnp.where(late, MASKED, logits[:, -BLK:])
    logits = jnp.concatenate([first, logits[:, BLK:-BLK], last], axis=1)
    return logits if bias is None else logits + bias


def window_outputs(logits, values, width):
    top = jnp.max(logits, axis=1, keepdims=True)
    weights = jnp.exp2((logits - top) * (math.log2(math.e) / math.sqrt(width))).astype(BF16)
    both = jnp.dot(weights, values, preferred_element_type=F32)
    return both[:, :width] / both[:, width:]


def window_block(q_ref, kh, vh, base, groups, bias=None):
    width = q_ref.shape[1]
    span = WIN + BLK
    share = q_ref.shape[0] // BLK // groups
    parts = [part.astype(BF16) for part in split_groups(q_ref[...].astype(F32))]
    chunks = [(g, c) for g in range(groups) for c in range(0, BLK * share, BLK)]

    def logits_of(chunk):
        g, c = chunk
        return window_logits(parts[g][c : c + BLK], kh[g, pl.ds(base, span), :], c // share, share, bias)

    outs = []
    ahead = logits_of(chunks[0])
    for i, (g, c) in enumerate(chunks):
        now = ahead
        if i + 1 < len(chunks):
            ahead = logits_of(chunks[i + 1])
        outs.append(window_outputs(now, vh[g, pl.ds(base, span), :], width))
    half = len(outs) // 2
    return join_groups(jnp.concatenate(outs[:half], axis=0), jnp.concatenate(outs[half:], axis=0))


def square_sums(full, heads):
    tokens = full.shape[0] // heads
    row = lax.broadcasted_iota(jnp.int32, (tokens, full.shape[0]), 1) // heads
    mine = row == lax.broadcasted_iota(jnp.int32, (tokens, full.shape[0]), 0)
    sums = jnp.dot(mine.astype(BF16), (full * full).astype(BF16), preferred_element_type=F32)
    ones = jnp.ones((8, full.shape[1]), F32)
    return lax.dot_general(
        ones, sums, (((1,), (1,)), ((), ())), precision=lax.Precision.HIGHEST, preferred_element_type=F32
    )


def far_kernel(heads, groups, q_ref, pk_ref, pv_ref, ck_ref, cv_ref, out_ref, kf, kh, vh):
    step = pl.program_id(0)
    width = q_ref.shape[1]

    @pl.when(step == 0)
    def _():
        vh[:, :, width:] = jnp.ones((groups, vh.shape[1], width), BF16)
        place(pk_ref, kf, kh, 0, groups)
        place(ck_ref, kf, kh, WIN, groups)
        place(pv_ref, kf, vh, 0, groups)
        place(cv_ref, kf, vh, WIN, groups)

    out_ref[...] = window_block(q_ref, kh, vh, pl.multiple_of(step * BLK, BLK), groups).astype(BF16)


def attention_cost(tokens, heads, width, extra=0):
    span = WIN + BLK
    return pl.CostEstimate(
        flops=6 * tokens * heads * span * width + extra,
        bytes_accessed=12 * tokens * heads * width,
        transcendentals=tokens * heads * span,
    )


def far_attention(queries, keys, values, heads, groups):
    width = queries.shape[1]
    steps = queries.shape[0] // (BLK * heads) - WIN // BLK
    skip = WIN // BLK
    at_first = pl.BlockSpec((WIN * groups, width), lambda i: (0, 0))
    at_next = pl.BlockSpec((WIN * groups, width), lambda i: (1, 0))
    return pl.pallas_call(
        functools.partial(far_kernel, heads, groups),
        grid=(steps,),
        in_specs=[
            pl.BlockSpec((BLK * heads, width), lambda i: (i + skip, 0)),
            at_first,
            at_first,
            at_next,
            at_next,
        ],
        out_specs=pl.BlockSpec((BLK * heads, width), lambda i: (i, 0)),
        out_shape=jax.ShapeDtypeStruct((steps * BLK * heads, width), BF16),
        scratch_shapes=[
            pltpu.VMEM((WIN * groups, width), F32),
            pltpu.VMEM((groups, 2 * WIN, width), BF16),
            pltpu.VMEM((groups, 2 * WIN, 2 * width), BF16),
        ],
        compiler_params=params(),
        cost_estimate=attention_cost(steps * BLK, heads, width),
        name="far_attention",
    )(queries, keys, values, keys, values)


def trunk_kernel(heads, groups, where_ref, gain_ref, q_ref, k_ref, v_ref, wq_ref, pk_ref, pv_ref, ck_ref, cv_ref, cross_ref, *rest):
    piece_refs, out_ref, square_ref = rest[:COLS], rest[COLS], rest[COLS + 1]
    nf, tf, sf, kf, kh, vh, of = rest[COLS + 2 :]
    step = pl.program_id(0)
    width = q_ref.shape[1]

    @pl.when(step == 0)
    def _():
        vh[:, :, width:] = jnp.ones((groups, vh.shape[1], width), BF16)
        place(pk_ref, kf, kh, 0, groups)
        place(ck_ref, kf, kh, WIN, groups)
        place(pv_ref, kf, vh, 0, groups)
        place(cv_ref, kf, vh, WIN, groups)

    nf[...] = q_ref[...].astype(F32)
    tf[...] = k_ref[...].astype(F32)
    sf[...] = v_ref[...].astype(F32)
    base = pl.multiple_of(step * BLK, BLK)
    span = WIN + BLK
    reach = jnp.where(where_ref[0] == 0, WIN - step * BLK, 0)
    bias = jnp.where(lax.broadcasted_iota(jnp.int32, (1, span), 1) < reach, MASKED, 0.0).astype(F32)
    row = lax.broadcasted_iota(jnp.int32, (BLK, BLK), 0)
    col = lax.broadcasted_iota(jnp.int32, (BLK, BLK), 1)
    inner = (step > 0).astype(F32).astype(BF16)
    per_piece = heads // COLS
    q = [every(q_ref, nf, heads, h) for h in range(heads)]
    inside = [
        lax.dot_general(q[h], every(k_ref, tf, heads, h), (((1,), (1,)), ((), ())), preferred_element_type=F32)
        for h in range(heads)
    ]
    for h in range(heads):
        weight = jnp.where(col <= row, inside[h], 0.0) * (gain_ref[h, 0] * gain_factor(0, width))
        left = jnp.concatenate([weight.astype(BF16), q[h], q[h]], axis=1)
        right = jnp.concatenate(
            [every(v_ref, sf, heads, h), cross_ref[h // per_piece, h % per_piece], piece_refs[h // per_piece][0, h % per_piece] * inner], axis=0
        )
        of[pl.ds(h, BLK, stride=heads), :] = jnp.dot(left, right, preferred_element_type=F32)
    full = window_block(wq_ref, kh, vh, base, groups, bias) + of[...]
    out_ref[...] = full
    square_ref[0] = square_sums(full, heads)


def trunk_attention(where, gain, q, k, v, wq, pk, pv, ck, cv, cross, pieces, heads, groups):
    width = q.shape[1]
    blocks = q.shape[0] // (BLK * heads)
    at_block = pl.BlockSpec((BLK * heads, width), lambda i: (i, 0))
    whole = pl.BlockSpec((WIN * groups, width), lambda i: (0, 0))
    own = pl.BlockSpec(cross.shape, lambda i: (0, 0, 0, 0))
    piece = pl.BlockSpec((1, heads // COLS, width, width), lambda i: (jnp.maximum(i - 1, 0), 0, 0, 0))
    wide = pltpu.VMEM((BLK * heads, width), F32)
    return pl.pallas_call(
        functools.partial(trunk_kernel, heads, groups),
        grid=(blocks,),
        in_specs=[smem(), smem()] + [at_block] * 4 + [whole] * 4 + [own] + [piece] * COLS,
        out_specs=[at_block, pl.BlockSpec((1, 8, BLK), lambda i: (i, 0, 0))],
        out_shape=[
            jax.ShapeDtypeStruct(q.shape, F32),
            jax.ShapeDtypeStruct((blocks, 8, BLK), F32),
        ],
        scratch_shapes=[
            wide,
            wide,
            wide,
            pltpu.VMEM((WIN * groups, width), F32),
            pltpu.VMEM((groups, 2 * WIN, width), BF16),
            pltpu.VMEM((groups, 2 * WIN, 2 * width), BF16),
            wide,
        ],
        compiler_params=params(),
        cost_estimate=attention_cost(blocks * BLK, heads, width, 2 * blocks * BLK * BLK * heads * 4 * width),
        name="trunk_attention",
    )(where, gain, q, k, v, wq, pk, pv, ck, cv, cross, *pieces)


def near_kernel(groups, where_ref, fork_ref, q_ref, ck_ref, cv_ref, *rest):
    kv_refs, out_ref = rest[:COLS], rest[COLS]
    kf, kh, vh, kt = rest[COLS + 1 :]
    step = pl.program_id(0)
    width = q_ref.shape[1]
    column = where_ref[0] & (COLS - 1)
    start = pl.multiple_of(fork_ref[0] * BLK, BLK)

    @pl.when(step == 0)
    def _():
        for i in range(COLS):
            kt[column ^ i] = kv_refs[i][...]
        vh[:, :, width:] = jnp.ones((groups, vh.shape[1], width), BF16)
        place(kt.at[0], kf, vh, 0, groups)
        place(kt.at[1], kf, vh, WIN, groups)
        place(kt.at[2], kf, kh, 0, groups)
        place(kt.at[3], kf, kh, WIN, groups)
        place(ck_ref, kf, kh, pl.multiple_of(start + WIN, BLK), groups)
        place(cv_ref, kf, vh, pl.multiple_of(start + WIN, BLK), groups)

    base = pl.multiple_of(start + step * BLK, BLK)
    out_ref[...] = window_block(q_ref, kh, vh, base, groups).astype(BF16)


def near_attention(where, fork, wq, ck, cv, kvs, heads, groups):
    width = wq.shape[1]
    steps = WIN // BLK
    at_block = pl.BlockSpec((BLK * heads, width), lambda i: (i, 0))
    whole = pl.BlockSpec((WIN * groups, width), lambda i: (0, 0))
    return pl.pallas_call(
        functools.partial(near_kernel, groups),
        grid=(steps,),
        in_specs=[smem(), smem(), at_block, whole, whole] + [whole] * COLS,
        out_specs=at_block,
        out_shape=jax.ShapeDtypeStruct((steps * BLK * heads, width), BF16),
        scratch_shapes=[
            pltpu.VMEM((WIN * groups, width), F32),
            pltpu.VMEM((groups, 3 * WIN, width), BF16),
            pltpu.VMEM((groups, 3 * WIN, 2 * width), BF16),
            pltpu.VMEM((COLS, WIN * groups, width), BF16),
        ],
        compiler_params=params(),
        cost_estimate=attention_cost(steps * BLK, heads, width),
        name="near_attention",
    )(where, fork, wq, ck, cv, *kvs)


def branch_kernel(heads, where_ref, fork_ref, q_hbm, near_hbm, far_hbm, *rest):
    piece_refs = rest[:COLS]
    full_ref, square_ref, qs, ws, nf, of, es, q_sems, w_sems = rest[COLS:]
    rows = nf.shape[0]
    blocks = qs.shape[0] // rows
    skip = WIN // BLK
    per_piece = heads // COLS
    column = where_ref[0] & (COLS - 1)
    for b in range(blocks):
        block_copy(q_hbm, qs, q_sems, b, rows).start()
        if b < skip:
            block_copy(near_hbm, ws, w_sems, b, rows).start()
        else:
            block_copy(far_hbm, ws, w_sems, b, rows, b - skip).start()
    for i in range(COLS):
        for j in range(per_piece):
            es[(column ^ i) * per_piece + j] = piece_refs[i][fork_ref[0], j]

    def one_block(b, carry):
        block_copy(q_hbm, qs, q_sems, b, rows).wait()
        block_copy(near_hbm, ws, w_sems, b, rows, 0).wait()
        at = pl.ds(pl.multiple_of(b * rows, rows), rows)
        nf[...] = qs[at, :].astype(F32)
        for h in range(heads):
            q = nf[pl.ds(h, BLK, stride=heads), :].astype(BF16)
            of[pl.ds(h, BLK, stride=heads), :] = jnp.dot(q, es[h], preferred_element_type=F32)
        full = ws[at, :].astype(F32) + of[...]
        full_ref[at, :] = full
        square_ref[b] = square_sums(full, heads)
        return carry

    lax.fori_loop(0, blocks, one_block, 0)


def branch_linear(where, fork, q, near, far, pieces, heads):
    width = q.shape[1]
    rows = BLK * heads
    blocks = q.shape[0] // rows
    wide = pltpu.VMEM((rows, width), F32)
    return pl.pallas_call(
        functools.partial(branch_kernel, heads),
        in_specs=[smem(), smem(), hbm(), hbm(), hbm()] + [vmem()] * COLS,
        out_specs=[vmem(), vmem()],
        out_shape=[
            jax.ShapeDtypeStruct(q.shape, F32),
            jax.ShapeDtypeStruct((blocks, 8, BLK), F32),
        ],
        scratch_shapes=[
            pltpu.VMEM(q.shape, BF16),
            pltpu.VMEM(q.shape, BF16),
            wide,
            wide,
            pltpu.VMEM((heads, width, width), BF16),
            pltpu.SemaphoreType.DMA((blocks,)),
            pltpu.SemaphoreType.DMA((blocks,)),
        ],
        compiler_params=params(SMALL_BYTES),
        cost_estimate=pl.CostEstimate(
            flops=4 * blocks * BLK * heads * width * width, bytes_accessed=8 * q.size, transcendentals=0
        ),
        name="branch_linear",
    )(where, fork, q, near, far, *pieces)


def norm_kernel(heads, features, trunk_hbm, trunk_square, branch_ref, branch_square, trunk_out, branch_out, held, done, in_sems, out_sems):
    rows, width = BLK * heads, branch_ref.shape[1]
    trunk_blocks = trunk_hbm.shape[0] // rows
    branch_blocks = branch_ref.shape[0] // rows
    for b in range(trunk_blocks):
        block_copy(trunk_hbm, held, in_sems, b, rows).start()

    def scaled(full, square):
        scale = lax.rsqrt(square[0:1, :] / features + 1e-06)
        scale = jnp.broadcast_to(scale, (width, BLK)).T
        return (full.reshape(BLK, heads, width) * scale[:, None, :]).astype(BF16).reshape(rows, width)

    def leave(out_hbm, block, slot):
        return pltpu.make_async_copy(
            done.at[pl.ds(slot * rows, rows)], out_hbm.at[pl.ds(block * rows, rows)], out_sems.at[slot]
        )

    def branch_block(b, carry):
        at = pl.ds(pl.multiple_of(b * rows, rows), rows)
        done[at, :] = scaled(branch_ref[at, :], branch_square[b])
        leave(branch_out, b, b).start()
        return carry

    def trunk_block(b, carry):
        block_copy(trunk_hbm, held, in_sems, b, rows).wait()
        slot = branch_blocks + b
        full = held[pl.ds(pl.multiple_of(b * rows, rows), rows), :]
        done[pl.ds(pl.multiple_of(slot * rows, rows), rows), :] = scaled(full, trunk_square[b])
        leave(trunk_out, b, slot).start()
        return carry

    lax.fori_loop(0, branch_blocks, branch_block, 0)
    lax.fori_loop(0, trunk_blocks, trunk_block, 0)
    for b in range(branch_blocks):
        leave(branch_out, b, b).wait()
    for b in range(trunk_blocks):
        leave(trunk_out, b, branch_blocks + b).wait()


def normalize(trunk, trunk_square, branch, branch_square, heads, features):
    width = trunk.shape[1]
    rows = BLK * heads
    trunk_blocks, branch_blocks = trunk.shape[0] // rows, branch.shape[0] // rows
    total = trunk_blocks + branch_blocks
    return pl.pallas_call(
        functools.partial(norm_kernel, heads, features),
        in_specs=[hbm(), vmem(), vmem(), vmem()],
        out_specs=[hbm(), hbm()],
        out_shape=[jax.ShapeDtypeStruct(trunk.shape, BF16), jax.ShapeDtypeStruct(branch.shape, BF16)],
        scratch_shapes=[
            pltpu.VMEM(trunk.shape, F32),
            pltpu.VMEM((total * rows, width), BF16),
            pltpu.SemaphoreType.DMA((trunk_blocks,)),
            pltpu.SemaphoreType.DMA((total,)),
        ],
        compiler_params=params(SMALL_BYTES),
        cost_estimate=pl.CostEstimate(
            flops=2 * (trunk.size + branch.size), bytes_accessed=6 * (trunk.size + branch.size), transcendentals=0
        ),
        name="normalize",
    )(trunk, trunk_square, branch, branch_square)


def shards(
    trunk_query,
    trunk_key,
    trunk_value,
    trunk_wquery,
    trunk_wkey,
    trunk_wvalue,
    branch_query,
    branch_wquery,
    branch_wkey,
    branch_wvalue,
    level_gain,
    fork_block,
):
    tokens, heads, width = trunk_query.shape
    groups = trunk_wkey.shape[1]
    depth = (tokens // BLK).bit_length() - 1
    count = lax.axis_size("seq")
    planes = count // COLS
    features = heads * lax.axis_size("head") * width
    me = lax.axis_index("seq")
    column, plane = me % COLS, me // COLS
    where = me.astype(jnp.int32).reshape(1)
    root = count - 1
    top = planes - 1

    def flat(x):
        return x.reshape(x.shape[0] * x.shape[1], x.shape[2])

    tq, tk, tv, twq = flat(trunk_query), flat(trunk_key), flat(trunk_value), flat(trunk_wquery)
    twk, twv = flat(trunk_wkey), flat(trunk_wvalue)
    bq, bwq, bwk, bwv = flat(branch_query), flat(branch_wquery), flat(branch_wkey), flat(branch_wvalue)

    def send(x, pairs):
        return lax.ppermute(x, "seq", pairs)

    def down(x):
        step = planes // 2
        while step:
            starts = [p for p in range(planes) if (top - p) % (2 * step) == 0 and p >= step]
            pairs = [(p * COLS + c, (p - step) * COLS + c) for p in starts for c in range(COLS)]
            got = send(x, pairs)
            hit = functools.reduce(jnp.logical_or, [plane == p - step for p in starts])
            x = jnp.where(hit, got, x)
            step //= 2
        return x

    def around(x):
        return [x] + [send(x, [(i, i ^ d) for i in range(count)]) for d in range(1, COLS)]

    def in_groups(x, groups_of):
        return lax.all_to_all(x, "seq", 0, 0, tiled=True, axis_index_groups=groups_of)

    in_one_plane = [[p * COLS + c for c in range(COLS)] for p in range(planes)]
    in_one_column = [[p * COLS + c for p in range(planes)] for c in range(COLS)]

    half = COLS // 2
    got = send(twv, [(root - i, root - i - half) for i in range(half)])
    kv = down(jnp.where(column >= half, twk, got))
    shift = [(i, i + 1) for i in range(count - 1)]
    pk, pv = send(twk, shift), send(twv, shift)

    *pieces, shard_sum = block_sums(level_gain, tk, tv, heads, depth)
    local = pieces[COLS - 1]
    for c in range(COLS - 1):
        got = send(pieces[c], [(root, root - (COLS - 1) + c)])
        local = jnp.where(column == c, got, local)
    sums = in_groups(shard_sum, in_one_plane)
    plane_sum, ends = plane_sums(where, level_gain, sums, local, planes, depth)
    plane_sum = in_groups(plane_sum, in_one_column)
    ends = down(ends)
    cross, above = cross_sums(where, level_gain, sums, plane_sum, depth)
    cross = in_groups(cross, in_one_plane)

    far = far_attention(bwq, bwk, bwv, heads, groups)
    kv, far = lax.optimization_barrier((kv, far))
    kvs = around(kv)
    ends = around((ends.astype(F32) + above).astype(BF16))

    trunk_full, trunk_square = trunk_attention(
        where, level_gain, tq, tk, tv, twq, pk, pv, twk, twv, cross, pieces, heads, groups
    )
    near = near_attention(where, fork_block, bwq, bwk, bwv, kvs, heads, groups)
    branch_full, branch_square = branch_linear(where, fork_block, bq, near, far, ends, heads)
    trunk_square, branch_square = lax.psum((trunk_square, branch_square), "head")
    trunk_out, branch_out = normalize(trunk_full, trunk_square, branch_full, branch_square, heads, features)
    return trunk_out.reshape(trunk_query.shape), branch_out.reshape(branch_query.shape)


def solution(mesh):
    rows = P("seq", "head", None)
    return jax.shard_map(
        shards,
        mesh=mesh,
        in_specs=(rows,) * 10 + (P("head", None), P("seq")),
        out_specs=(rows, rows),
        check_vma=False,
    )
```

time: 120 us -> 116 us (0.967)
  local copies, waits for them, and re-layouts: 2.43 us -> 14.1 us
  Pallas kernels: 53 us -> 45.5 us
  waiting for transfers between devices: 10.4 us -> 4.97 us
  starting transfers between devices: 46.2 us -> 42.6 us
  other arithmetic: 0.18 us -> 2.81 us
    unnamed x30 -> x44, local copies, waits for them, and re-layouts: 2.43 us -> 14.1 us
    pallas_call x5 -> x6, Pallas kernels: 33.1 us -> 25.6 us  [the longest x1 8.33 us: near_attention(): pl.pallas_call(functools.partial(near_kernel, groups), grid=(steps,), in_...]
    all_to_all x2 -> x3, waiting for transfers between devices: 9.04 us -> 3.88 us  [in_groups(): lax.all_to_all(x, 'seq', 0, 0, tiled=True, axis_index_groups=groups_of)]
    all_to_all x2 -> x3, starting transfers between devices: 23.6 us -> 20.5 us  [in_groups(): lax.all_to_all(x, 'seq', 0, 0, tiled=True, axis_index_groups=groups_of)]
  transfers between devices with their start and end apart: 18 -> 19, of which waited for: 3 -> 2; matrix products, arithmetic and copies ran while one was open for 0% -> 2% of each run, Pallas kernels for 18% -> 32%
where the time goes in v2:
time: 116 us; the launch traced here: 115 us
  Pallas kernels  45.5 us (39%)
  starting transfers between devices  42.6 us (37%)
  local copies, waits for them, and re-layouts  14.1 us (12%)
  waiting for transfers between devices  4.97 us (4%)
  blocking collectives  3.53 us (3%)
  other arithmetic  2.81 us (2%)
  between operations  1.63 us (1%)
    ppermute x16, starting transfers between devices, send(): return lax.ppermute(x, 'seq', pairs)  22.1 us
    all_to_all x3, starting transfers between devices, in_groups(): lax.all_to_all(x, 'seq', 0, 0, tiled=True, axis_index_groups=groups_of)  20.5 us
    unnamed x44, local copies, waits for them, and re-layouts  14.1 us
    pallas_call x1, Pallas kernels, trunk_attention(): pl.pallas_call(functools.partial(trunk_kernel, heads, groups), grid=(bloc...  12.1 us
    pallas_call x1, Pallas kernels, near_attention(): pl.pallas_call(functools.partial(near_kernel, groups), grid=(steps,), in_...  8.33 us
    pallas_call x1, Pallas kernels, far_attention(): pl.pallas_call(functools.partial(far_kernel, heads, groups), grid=(steps,...  7.87 us
    pallas_call x1, Pallas kernels, branch_linear(): pl.pallas_call(functools.partial(branch_kernel, heads), in_specs=[smem(),...  6.32 us
    pallas_call x1, Pallas kernels, block_sums(): pl.pallas_call(functools.partial(state_kernel, depth, heads), in_specs=[s...  4.35 us
  transfers between devices with their start and end apart: 19, of which 2 were waited for; matrix products, arithmetic and copies ran while one was open for 2% of the time, Pallas kernels for 32%

profile of v2, /device:TPU:0, one launch (start us, length us, event | category | flops | bytes accessed | tf_op | source)
XLA Modules:
  0.0 115.2 jit_solution(12063534752039480590)
XLA Ops:
  0.6 0.0 copy-start.15
  0.6 0.8 collective-permute-start.5
  1.5 0.0 copy-start.18
  1.5 4.3 %block_sums.1 = (bf16[3,2,128,128]{3,2,1,0:T(8,128)(2,1)}, bf16[3,2,128,128]{3,2,1,0:T(8,128)(2,1)}, bf16[3,2,128,128]{3,2,1,0:T(8,128)(2,1)}, bf16[3,2,128,128]{3,2,1,0:T(8,128)(2,1)}, bf16[4,2,128,128]{3,2,1,0:T(8,128)(2,1)}) custom-call(f32[8,11]{1,0:T(8,128)} %gain_ref.7, bf16[4096,128]{1,0:T(8,128)(2,1)} %bitcast.14, bf16[4096,128]{1,0:T(8,128)(2,1)} %bitcast.16), custom_call_target="tpu_custom_call" | custom-call | flops 134217728 | bytes 3145728 | tf_op jit(solution)/shard_map/block_sums/pallas_call | solution.py:94
  5.8 0.7 collective-permute-start.2
  6.5 0.7 collective-permute-start.3
  7.2 0.7 collective-permute-start.4
  7.9 5.2 %all-to-all-start = ((bf16[4,2,128,128]{3,2,1,0:T(8,128)(2,1)}), bf16[4,2,128,128]{3,2,1,0:T(8,128)(2,1)S(1)}, u32[]{:S(2)}, u32[]{:S(2)}) async-start(bf16[4,2,128,128]{3,2,1,0:T(8,128)(2,1)} %get-tuple-element.19), calls=%async_computation | async-start | bytes 524288 | tf_op jit(solution)/shard_map/all_to_all | solution.py:629
  13.0 0.0 collective-permute-done.5
  13.1 0.7 collective-permute-start.6
  13.8 0.0 collective-permute-done.2
  13.8 0.0 collective-permute-done.3
  13.8 0.0 collective-permute-done.4
  13.8 0.7 select_select_fusion.local_ref
  14.5 3.9 %all-to-all-done.sums_ref = bf16[4,2,128,128]{3,2,1,0:T(8,128)(2,1)S(1)} async-done(((bf16[4,2,128,128]{3,2,1,0:T(8,128)(2,1)}), bf16[4,2,128,128]{3,2,1,0:T(8,128)(2,1)S(1)}, u32[]{:S(2)}, u32[]{:S(2)}) %all-to-all-start) | async-done | bytes 262176 | tf_op jit(solution)/shard_map/all_to_all | solution.py:629
  18.4 0.7 copy-done.12
  19.1 1.9 %plane_sums.1 = (bf16[4,2,128,128]{3,2,1,0:T(8,128)(2,1)}, bf16[4,2,128,128]{3,2,1,0:T(8,128)(2,1)}) custom-call(s32[1]{0:T(128)} %bitcast.where_ref, f32[8,11]{1,0:T(8,128)} %gain_ref.7, bf16[4,2,128,128]{3,2,1,0:T(8,128)(2,1)} %copy-done.12, bf16[3,2,128,128]{3,2,1,0:T(8,128)(2,1)} %select_select_fusion.local_ref), custom_call_target="tpu_custom_call" | custom-call | flops 524288 | bytes 1048576 | tf_op jit(solution)/shard_map/plane_sums/pallas_call | solution.py:146
  21.0 0.7 collective-permute-start.11
  21.7 3.2 %collective-permute-start = (bf16[1024,128]{1,0:T(8,128)(2,1)S(1)}, bf16[1024,128]{1,0:T(8,128)(2,1)S(1)}, u32[]{:S(2)}, u32[]{:S(2)}) collective-permute-start(bf16[1024,128]{1,0:T(8,128)(2,1)S(1)} %bitcast.20), channel_id=1, source_target_pairs={{0,2},{2,4},{4,6},{6,8},{8,10},{10,12},{12,14},{14,16},{16,18},{18... | collective-permute-start | bytes 786440 | tf_op jit(solution)/shard_map/ppermute | solution.py:612
  24.9 3.4 %collective-permute-start.1 = (bf16[1024,128]{1,0:T(8,128)(2,1)S(1)}, bf16[1024,128]{1,0:T(8,128)(2,1)S(1)}, u32[]{:S(2)}, u32[]{:S(2)}) collective-permute-start(bf16[1024,128]{1,0:T(8,128)(2,1)S(1)} %bitcast.35), channel_id=1, source_target_pairs={{0,2},{2,4},{4,6},{6,8},{8,10},{10,12},{12,14},{14,16},{16,18},{18... | collective-permute-start | bytes 786440 | tf_op jit(solution)/shard_map/ppermute | solution.py:612
  28.3 11.9 %all-to-all-start.1 = ((bf16[4,2,128,128]{3,2,1,0:T(8,128)(2,1)}), bf16[4,2,128,128]{3,2,1,0:T(8,128)(2,1)S(1)}, u32[]{:S(2)}, u32[]{:S(2)}) async-start(bf16[4,2,128,128]{3,2,1,0:T(8,128)(2,1)} %get-tuple-element.24), calls=%async_computation.1 | async-start | bytes 524288 | tf_op jit(solution)/shard_map/all_to_all | solution.py:629
  40.2 0.0 collective-permute-done.6
  40.2 1.3 %collective-permute-start.7 = (bf16[1024,128]{1,0:T(8,128)(2,1)S(1)}, bf16[1024,128]{1,0:T(8,128)(2,1)S(1)}, u32[]{:S(2)}, u32[]{:S(2)}) collective-permute-start(bf16[1024,128]{1,0:T(8,128)(2,1)S(1)} %broadcast_select_fusion.2), channel_id=1, source_target_pairs={{8,0},{10,2},{12,4},{14,6},{24,16},{26,18},{28,20},{30,22},{9,1},{... | collective-permute-start | bytes 786440 | tf_op jit(solution)/shard_map/ppermute | solution.py:612
  41.5 0.0 collective-permute-done.11
  41.5 1.0 broadcast_select_fusion
  42.5 1.3 %collective-permute-start.12 = (bf16[4,2,128,128]{3,2,1,0:T(8,128)(2,1)S(1)}, bf16[4,2,128,128]{3,2,1,0:T(8,128)(2,1)S(1)}, u32[]{:S(2)}, u32[]{:S(2)}) collective-permute-start(bf16[4,2,128,128]{3,2,1,0:T(8,128)(2,1)S(1)} %broadcast_select_fusion), channel_id=1, source_target_pairs={{8,0},{10,2},{12,4},{14,6},{24,16},{26,18},{28,20},{30,22},{9,1},{... | collective-permute-start | bytes 786440 | tf_op jit(solution)/shard_map/ppermute | solution.py:612
  43.8 7.9 %far_attention.1.far_hbm = bf16[4096,128]{1,0:T(8,128)(2,1)} custom-call(bf16[8192,128]{1,0:T(8,128)(2,1)} %bitcast.21, bf16[2048,128]{1,0:T(8,128)(2,1)} %bitcast.27, bf16[2048,128]{1,0:T(8,128)(2,1)} %bitcast.30, bf16[2048,128]{1,0:T(8,128)(2,1)} %bitcast.28, bf16[2048,128]{1,0:T(8,128)(2,1)} %bitcast.31), custom_call_target="tpu_custom_call" | custom-call | flops 2013265920 | bytes 6291456 | tf_op jit(solution)/shard_map/far_attention/pallas_call | solution.py:307
  51.7 1.0 collective-permute-done.7
  52.8 1.8 %collective-permute-start.10 = (bf16[1024,128]{1,0:T(8,128)(2,1)S(1)}, bf16[1024,128]{1,0:T(8,128)(2,1)S(1)}, u32[]{:S(2)}, u32[]{:S(2)}) collective-permute-start(bf16[1024,128]{1,0:T(8,128)(2,1)S(1)} %broadcast_select_fusion.3.rest_0_), channel_id=1, source_target_pairs={{0,6},{2,4},{4,2},{6,0},{8,14},{10,12},{12,10},{14,8},{16,22},{18,... | collective-permute-start | bytes 786440 | tf_op jit(solution)/shard_map/ppermute | solution.py:612
  55.2 0.0 all-to-all-done.1.planes_ref
  55.2 0.0 copy-start.13
  55.2 0.7 copy-done.13
  55.9 1.9 %cross_sums.1 = (bf16[4,2,128,128]{3,2,1,0:T(8,128)(2,1)}, f32[2,128,128]{2,1,0:T(8,128)}) custom-call(s32[1]{0:T(128)} %bitcast.where_ref, f32[8,11]{1,0:T(8,128)} %gain_ref.7, bf16[4,2,128,128]{3,2,1,0:T(8,128)(2,1)} %copy-done.12, bf16[4,2,128,128]{3,2,1,0:T(8,128)(2,1)} %copy-done.13), custom_call_target="tpu_custom_call" | custom-call | flops 2621440 | bytes 1048576 | tf_op jit(solution)/shard_map/cross_sums/pallas_call | solution.py:187
  57.8 3.4 %all-to-all-start.2 = ((bf16[4,2,128,128]{3,2,1,0:T(8,128)(2,1)}), bf16[4,2,128,128]{3,2,1,0:T(8,128)(2,1)S(1)}, u32[]{:S(2)}, u32[]{:S(2)}) async-start(bf16[4,2,128,128]{3,2,1,0:T(8,128)(2,1)} %get-tuple-element.25), calls=%async_computation.2 | async-start | bytes 524288 | tf_op jit(solution)/shard_map/all_to_all | solution.py:629
  61.2 2.0 %collective-permute-start.8 = (bf16[1024,128]{1,0:T(8,128)(2,1)S(1)}, bf16[1024,128]{1,0:T(8,128)(2,1)}, u32[]{:S(2)}, u32[]{:S(2)}) collective-permute-start(bf16[1024,128]{1,0:T(8,128)(2,1)S(1)} %broadcast_select_fusion.3.rest_0_), channel_id=1, source_target_pairs={{0,2},{2,0},{4,6},{6,4},{8,10},{10,8},{12,14},{14,12},{16,18},{18,... | collective-permute-start | bytes 786440 | tf_op jit(solution)/shard_map/ppermute | solution.py:612
  63.2 0.0 collective-permute-done.12
  63.2 1.5 %collective-permute-start.9 = (bf16[1024,128]{1,0:T(8,128)(2,1)S(1)}, bf16[1024,128]{1,0:T(8,128)(2,1)}, u32[]{:S(2)}, u32[]{:S(2)}) collective-permute-start(bf16[1024,128]{1,0:T(8,128)(2,1)S(1)} %broadcast_select_fusion.3.rest_0_), channel_id=1, source_target_pairs={{0,4},{2,6},{4,0},{6,2},{8,12},{10,14},{12,8},{14,10},{16,20},{18,... | collective-permute-start | bytes 786440 | tf_op jit(solution)/shard_map/ppermute | solution.py:612
  64.6 1.0 add_convert_fusion.rest_0_
  65.6 0.0 collective-permute-done.pk_ref
  65.7 0.0 copy-start.19
  65.7 0.6 collective-permute-start.13
  66.3 0.1 collective-permute-start.14
  66.4 0.0 collective-permute-done.10.rest_3_
  66.4 2.8 %collective-permute-start.15 = (bf16[4,2,128,128]{3,2,1,0:T(8,128)(2,1)S(1)}, bf16[4,2,128,128]{3,2,1,0:T(8,128)(2,1)S(1)}, u32[]{:S(2)}, u32[]{:S(2)}) collective-permute-start(bf16[4,2,128,128]{3,2,1,0:T(8,128)(2,1)S(1)} %add_convert_fusion.rest_0_), channel_id=1, source_target_pairs={{0,6},{2,4},{4,2},{6,0},{8,14},{10,12},{12,10},{14,8},{16,22},{18,... | collective-permute-start | bytes 786440 | tf_op jit(solution)/shard_map/ppermute | solution.py:612
  69.2 0.7 copy-done.14
  70.0 12.1 %trunk_attention.1 = (f32[4096,128]{1,0:T(8,128)}, f32[4,8,128]{2,1,0:T(8,128)}) custom-call(s32[1]{0:T(128)} %bitcast.where_ref, f32[8,11]{1,0:T(8,128)} %gain_ref.7, bf16[4096,128]{1,0:T(8,128)(2,1)} %bitcast.24, bf16[4096,128]{1,0:T(8,128)(2,1)} %bitcast.15, bf16[4096,128]{1,0:T(8,128)(2,1)} %bitcast.17, bf16[4096,128]{1,0:T(8,128)(2,1)} %bitcast.25, ...), custom_call_target="tpu_custom_call" | custom-call | flops 2550136832 | bytes 6291456 | tf_op jit(solution)/shard_map/trunk_attention/pallas_call | solution.py:380
  82.1 0.0 collective-permute-done.8.rest_1_
  82.1 0.0 collective-permute-done.9.rest_2_
  82.1 8.3 %near_attention.1.near_hbm = bf16[4096,128]{1,0:T(8,128)(2,1)} custom-call(s32[1]{0:T(128)} %bitcast.where_ref, s32[1]{0:T(128)S(6)} %copy.14.fork_ref, bf16[8192,128]{1,0:T(8,128)(2,1)} %bitcast.22, bf16[2048,128]{1,0:T(8,128)(2,1)} %bitcast.29, bf16[2048,128]{1,0:T(8,128)(2,1)} %bitcast.32, bf16[1024,128]{1,0:T(8,128)(2,1)} %copy-done.16, ...), custom_call_target="tpu_custom_call" | custom-call | flops 2013265920 | bytes 6291456 | tf_op jit(solution)/shard_map/near_attention/pallas_call | solution.py:433
  90.4 0.0 collective-permute-done.13.rest_1_
  90.4 0.7 copy-done.6
  91.2 0.7 copy-done.8
  91.9 0.0 collective-permute-done.15.rest_3_
  91.9 0.7 copy-done.10
  92.6 1.6 %copy-done.3 = bf16[1024,8,128]{2,1,0:T(8,128)(2,1)S(1)} copy-done((bf16[1024,8,128]{2,1,0:T(8,128)(2,1)S(1)}, bf16[1024,8,128]{2,1,0:T(8,128)(2,1)}, u32[]{:S(2)}) %copy-start.3) | copy-done | bytes 2097176
  94.2 1.2 %copy-done.5 = bf16[4096,128]{1,0:T(8,128)(2,1)S(1)} copy-done((bf16[4096,128]{1,0:T(8,128)(2,1)S(1)}, bf16[4096,128]{1,0:T(8,128)(2,1)}, u32[]{:S(2)}) %copy-start.5) | copy-done | bytes 1048600
  95.4 0.9 copy-done.7
  96.4 0.9 copy-done.9
  97.3 0.9 copy-done.11
  98.3 6.3 %branch_linear.1 = (f32[8192,128]{1,0:T(8,128)S(1)}, f32[8,8,128]{2,1,0:T(8,128)S(1)}) custom-call(s32[1]{0:T(128)} %bitcast.where_ref, s32[1]{0:T(128)S(6)} %copy.14.fork_ref, bf16[8192,128]{1,0:T(8,128)(2,1)S(1)} %bitcast.13, bf16[4096,128]{1,0:T(8,128)(2,1)S(1)} %copy-done.5, bf16[4096,128]{1,0:T(8,128)(2,1)S(1)} %copy-done.4, ...), custom_call_target="tpu_custom_call" | custom-call | flops 536870912 | bytes 8388608 | tf_op jit(solution)/shard_map/branch_linear/pallas_call | solution.py:490
  104.6 2.0 %copy-done = f32[8192,128]{1,0:T(8,128)} copy-done((f32[8192,128]{1,0:T(8,128)}, f32[8192,128]{1,0:T(8,128)S(1)}, u32[]{:S(2)}) %copy-start) | copy-done | bytes 4194328
  106.6 3.5 %all-reduce = (f32[4,8,128]{2,1,0:T(8,128)S(1)}, f32[8,8,128]{2,1,0:T(8,128)S(1)}) all-reduce(f32[4,8,128]{2,1,0:T(8,128)S(1)} %copy-done.17, f32[8,8,128]{2,1,0:T(8,128)S(1)} %get-tuple-element.33), channel_id=1, replica_groups=mesh['seq'=16,'head'=2] {'head'}, use_global_device_ids=true, to_apply=%region_0.1 | all-reduce | flops 12288 | bytes 98304 | tf_op jit(solution)/shard_map/psum | solution.py:662
  110.1 2.2 %copy-done.1 = f32[8192,128]{1,0:T(8,128)S(1)} copy-done((f32[8192,128]{1,0:T(8,128)S(1)}, f32[8192,128]{1,0:T(8,128)}, u32[]{:S(2)}) %copy-start.1) | copy-done | bytes 4194328
  112.3 2.8 %normalize.1 = (bf16[4096,128]{1,0:T(8,128)(2,1)}, bf16[8192,128]{1,0:T(8,128)(2,1)}) custom-call(f32[4096,128]{1,0:T(8,128)S(1)} %copy-done.2, f32[4,8,128]{2,1,0:T(8,128)S(1)} %get-tuple-element.36.trunk_square, f32[8192,128]{1,0:T(8,128)S(1)} %copy-done.1, f32[8,8,128]{2,1,0:T(8,128)S(1)} %get-tuple-element.37.branch_square), custom_call_target="tpu_custom_call" | custom-call | flops 3145728 | bytes 9437184 | tf_op jit(solution)/shard_map/normalize/pallas_call | solution.py:559
  (33 shorter events, 0.1 us)
Async XLA Ops:
  0.6 12.4 %copy-start.15 = (bf16[512,2,128]{2,1,0:T(2,128)(2,1)S(1)}, bf16[512,2,128]{2,1,0:T(2,128)(2,1)}, u32[]{:S(2)}) copy-start(bf16[512,2,128]{2,1,0:T(2,128)(2,1)} %param.16) | copy-start | bytes 786436
  0.6 12.4 %collective-permute-start.5 = (bf16[1024,128]{1,0:T(8,128)(2,1)}, bf16[1024,128]{1,0:T(8,128)(2,1)S(1)}, u32[]{:S(2)}, u32[]{:S(2)}) collective-permute-start(bf16[1024,128]{1,0:T(8,128)(2,1)} %bitcast.33), channel_id=1, source_target_pairs={{30,26},{28,24},{31,27},{29,25}} | collective-permute-start | bytes 786440 | tf_op jit(solution)/shard_map/ppermute | solution.py:612
  1.5 23.4 %copy-start.18 = (bf16[512,2,128]{2,1,0:T(2,128)(2,1)S(1)}, bf16[512,2,128]{2,1,0:T(2,128)(2,1)}, u32[]{:S(2)}) copy-start(bf16[512,2,128]{2,1,0:T(2,128)(2,1)} %param.17) | copy-start | bytes 786436
  5.8 8.0 %collective-permute-start.2 = (bf16[3,2,128,128]{3,2,1,0:T(8,128)(2,1)}, bf16[3,2,128,128]{3,2,1,0:T(8,128)(2,1)S(1)}, u32[]{:S(2)}, u32[]{:S(2)}) collective-permute-start(bf16[3,2,128,128]{3,2,1,0:T(8,128)(2,1)} %get-tuple-element.20.rest_2_), channel_id=1, source_target_pairs={{30,28},{31,29}} | collective-permute-start | bytes 589832 | tf_op jit(solution)/shard_map/ppermute | solution.py:612
  6.5 7.3 %collective-permute-start.3 = (bf16[3,2,128,128]{3,2,1,0:T(8,128)(2,1)}, bf16[3,2,128,128]{3,2,1,0:T(8,128)(2,1)S(1)}, u32[]{:S(2)}, u32[]{:S(2)}) collective-permute-start(bf16[3,2,128,128]{3,2,1,0:T(8,128)(2,1)} %get-tuple-element.21.rest_1_), channel_id=1, source_target_pairs={{30,26},{31,27}} | collective-permute-start | bytes 589832 | tf_op jit(solution)/shard_map/ppermute | solution.py:612
  7.2 6.6 %collective-permute-start.4 = (bf16[3,2,128,128]{3,2,1,0:T(8,128)(2,1)}, bf16[3,2,128,128]{3,2,1,0:T(8,128)(2,1)S(1)}, u32[]{:S(2)}, u32[]{:S(2)}) collective-permute-start(bf16[3,2,128,128]{3,2,1,0:T(8,128)(2,1)} %get-tuple-element.22.rest_0_), channel_id=1, source_target_pairs={{30,24},{31,25}} | collective-permute-start | bytes 589832 | tf_op jit(solution)/shard_map/ppermute | solution.py:612
  7.9 10.5 %all-to-all-start = ((bf16[4,2,128,128]{3,2,1,0:T(8,128)(2,1)}), bf16[4,2,128,128]{3,2,1,0:T(8,128)(2,1)S(1)}, u32[]{:S(2)}, u32[]{:S(2)}) async-start(bf16[4,2,128,128]{3,2,1,0:T(8,128)(2,1)} %get-tuple-element.19), calls=%async_computation | async-start | bytes 524288 | tf_op jit(solution)/shard_map/all_to_all | solution.py:629
  13.1 27.1 %collective-permute-start.6 = (bf16[1024,128]{1,0:T(8,128)(2,1)S(1)}, bf16[1024,128]{1,0:T(8,128)(2,1)S(1)}, u32[]{:S(2)}, u32[]{:S(2)}) collective-permute-start(bf16[1024,128]{1,0:T(8,128)(2,1)S(1)} %broadcast_select_fusion.1), channel_id=1, source_target_pairs={{24,8},{26,10},{28,12},{30,14},{25,9},{27,11},{29,13},{31,15}} | collective-permute-start | bytes 786440 | tf_op jit(solution)/shard_map/ppermute | solution.py:612
  18.4 0.7 copy-start.12
  21.0 20.5 %collective-permute-start.11 = (bf16[4,2,128,128]{3,2,1,0:T(8,128)(2,1)}, bf16[4,2,128,128]{3,2,1,0:T(8,128)(2,1)S(1)}, u32[]{:S(2)}, u32[]{:S(2)}) collective-permute-start(bf16[4,2,128,128]{3,2,1,0:T(8,128)(2,1)} %get-tuple-element.30), channel_id=1, source_target_pairs={{24,8},{26,10},{28,12},{30,14},{25,9},{27,11},{29,13},{31,15}} | collective-permute-start | bytes 786440 | tf_op jit(solution)/shard_map/ppermute | solution.py:612
  21.7 44.0 %collective-permute-start = (bf16[1024,128]{1,0:T(8,128)(2,1)S(1)}, bf16[1024,128]{1,0:T(8,128)(2,1)S(1)}, u32[]{:S(2)}, u32[]{:S(2)}) collective-permute-start(bf16[1024,128]{1,0:T(8,128)(2,1)S(1)} %bitcast.20), channel_id=1, source_target_pairs={{0,2},{2,4},{4,6},{6,8},{8,10},{10,12},{12,14},{14,16},{16,18},{18... | collective-permute-start | bytes 786440 | tf_op jit(solution)/shard_map/ppermute | solution.py:612
  24.9 41.4 %collective-permute-start.1 = (bf16[1024,128]{1,0:T(8,128)(2,1)S(1)}, bf16[1024,128]{1,0:T(8,128)(2,1)S(1)}, u32[]{:S(2)}, u32[]{:S(2)}) collective-permute-start(bf16[1024,128]{1,0:T(8,128)(2,1)S(1)} %bitcast.35), channel_id=1, source_target_pairs={{0,2},{2,4},{4,6},{6,8},{8,10},{10,12},{12,14},{14,16},{16,18},{18... | collective-permute-start | bytes 786440 | tf_op jit(solution)/shard_map/ppermute | solution.py:612
  28.3 26.9 %all-to-all-start.1 = ((bf16[4,2,128,128]{3,2,1,0:T(8,128)(2,1)}), bf16[4,2,128,128]{3,2,1,0:T(8,128)(2,1)S(1)}, u32[]{:S(2)}, u32[]{:S(2)}) async-start(bf16[4,2,128,128]{3,2,1,0:T(8,128)(2,1)} %get-tuple-element.24), calls=%async_computation.1 | async-start | bytes 524288 | tf_op jit(solution)/shard_map/all_to_all | solution.py:629
  40.2 12.5 %collective-permute-start.7 = (bf16[1024,128]{1,0:T(8,128)(2,1)S(1)}, bf16[1024,128]{1,0:T(8,128)(2,1)S(1)}, u32[]{:S(2)}, u32[]{:S(2)}) collective-permute-start(bf16[1024,128]{1,0:T(8,128)(2,1)S(1)} %broadcast_select_fusion.2), channel_id=1, source_target_pairs={{8,0},{10,2},{12,4},{14,6},{24,16},{26,18},{28,20},{30,22},{9,1},{... | collective-permute-start | bytes 786440 | tf_op jit(solution)/shard_map/ppermute | solution.py:612
  42.5 20.7 %collective-permute-start.12 = (bf16[4,2,128,128]{3,2,1,0:T(8,128)(2,1)S(1)}, bf16[4,2,128,128]{3,2,1,0:T(8,128)(2,1)S(1)}, u32[]{:S(2)}, u32[]{:S(2)}) collective-permute-start(bf16[4,2,128,128]{3,2,1,0:T(8,128)(2,1)S(1)} %broadcast_select_fusion), channel_id=1, source_target_pairs={{8,0},{10,2},{12,4},{14,6},{24,16},{26,18},{28,20},{30,22},{9,1},{... | collective-permute-start | bytes 786440 | tf_op jit(solution)/shard_map/ppermute | solution.py:612
  52.7 29.4 %copy-start.16 = (bf16[1024,128]{1,0:T(8,128)(2,1)}, bf16[1024,128]{1,0:T(8,128)(2,1)S(1)}, u32[]{:S(2)}) copy-start(bf16[1024,128]{1,0:T(8,128)(2,1)S(1)} %broadcast_select_fusion.3.rest_0_) | copy-start | bytes 786436
  52.8 13.6 %collective-permute-start.10 = (bf16[1024,128]{1,0:T(8,128)(2,1)S(1)}, bf16[1024,128]{1,0:T(8,128)(2,1)S(1)}, u32[]{:S(2)}, u32[]{:S(2)}) collective-permute-start(bf16[1024,128]{1,0:T(8,128)(2,1)S(1)} %broadcast_select_fusion.3.rest_0_), channel_id=1, source_target_pairs={{0,6},{2,4},{4,2},{6,0},{8,14},{10,12},{12,10},{14,8},{16,22},{18,... | collective-permute-start | bytes 786440 | tf_op jit(solution)/shard_map/ppermute | solution.py:612
  55.2 0.7 copy-start.13
  57.8 11.5 %all-to-all-start.2 = ((bf16[4,2,128,128]{3,2,1,0:T(8,128)(2,1)}), bf16[4,2,128,128]{3,2,1,0:T(8,128)(2,1)S(1)}, u32[]{:S(2)}, u32[]{:S(2)}) async-start(bf16[4,2,128,128]{3,2,1,0:T(8,128)(2,1)} %get-tuple-element.25), calls=%async_computation.2 | async-start | bytes 524288 | tf_op jit(solution)/shard_map/all_to_all | solution.py:629
  61.2 20.9 %collective-permute-start.8 = (bf16[1024,128]{1,0:T(8,128)(2,1)S(1)}, bf16[1024,128]{1,0:T(8,128)(2,1)}, u32[]{:S(2)}, u32[]{:S(2)}) collective-permute-start(bf16[1024,128]{1,0:T(8,128)(2,1)S(1)} %broadcast_select_fusion.3.rest_0_), channel_id=1, source_target_pairs={{0,2},{2,0},{4,6},{6,4},{8,10},{10,8},{12,14},{14,12},{16,18},{18,... | collective-permute-start | bytes 786440 | tf_op jit(solution)/shard_map/ppermute | solution.py:612
  63.2 18.9 %collective-permute-start.9 = (bf16[1024,128]{1,0:T(8,128)(2,1)S(1)}, bf16[1024,128]{1,0:T(8,128)(2,1)}, u32[]{:S(2)}, u32[]{:S(2)}) collective-permute-start(bf16[1024,128]{1,0:T(8,128)(2,1)S(1)} %broadcast_select_fusion.3.rest_0_), channel_id=1, source_target_pairs={{0,4},{2,6},{4,0},{6,2},{8,12},{10,14},{12,8},{14,10},{16,20},{18,... | collective-permute-start | bytes 786440 | tf_op jit(solution)/shard_map/ppermute | solution.py:612
  65.7 3.6 %copy-start.19 = (bf16[1024,128]{1,0:T(8,128)(2,1)}, bf16[1024,128]{1,0:T(8,128)(2,1)S(1)}, u32[]{:S(2)}) copy-start(bf16[1024,128]{1,0:T(8,128)(2,1)S(1)} %collective-permute-done.pk_ref) | copy-start | bytes 786436
  65.7 24.8 %collective-permute-start.13 = (bf16[4,2,128,128]{3,2,1,0:T(8,128)(2,1)S(1)}, bf16[4,2,128,128]{3,2,1,0:T(8,128)(2,1)S(1)}, u32[]{:S(2)}, u32[]{:S(2)}) collective-permute-start(bf16[4,2,128,128]{3,2,1,0:T(8,128)(2,1)S(1)} %add_convert_fusion.rest_0_), channel_id=1, source_target_pairs={{0,2},{2,0},{4,6},{6,4},{8,10},{10,8},{12,14},{14,12},{16,18},{18,... | collective-permute-start | bytes 786440 | tf_op jit(solution)/shard_map/ppermute | solution.py:612
  66.3 2.9 %copy-start.20 = (bf16[1024,128]{1,0:T(8,128)(2,1)}, bf16[1024,128]{1,0:T(8,128)(2,1)S(1)}, u32[]{:S(2)}) copy-start(bf16[1024,128]{1,0:T(8,128)(2,1)S(1)} %collective-permute-done.1.pv_ref) | copy-start | bytes 786436
  66.3 24.9 %collective-permute-start.14 = (bf16[4,2,128,128]{3,2,1,0:T(8,128)(2,1)S(1)}, bf16[4,2,128,128]{3,2,1,0:T(8,128)(2,1)S(1)}, u32[]{:S(2)}, u32[]{:S(2)}) collective-permute-start(bf16[4,2,128,128]{3,2,1,0:T(8,128)(2,1)S(1)} %add_convert_fusion.rest_0_), channel_id=1, source_target_pairs={{0,4},{2,6},{4,0},{6,2},{8,12},{10,14},{12,8},{14,10},{16,20},{18,... | collective-permute-start | bytes 786440 | tf_op jit(solution)/shard_map/ppermute | solution.py:612
  66.4 15.7 %copy-start.21 = (bf16[1024,128]{1,0:T(8,128)(2,1)}, bf16[1024,128]{1,0:T(8,128)(2,1)S(1)}, u32[]{:S(2)}) copy-start(bf16[1024,128]{1,0:T(8,128)(2,1)S(1)} %collective-permute-done.10.rest_3_) | copy-start | bytes 786436
  66.4 25.5 %collective-permute-start.15 = (bf16[4,2,128,128]{3,2,1,0:T(8,128)(2,1)S(1)}, bf16[4,2,128,128]{3,2,1,0:T(8,128)(2,1)S(1)}, u32[]{:S(2)}, u32[]{:S(2)}) collective-permute-start(bf16[4,2,128,128]{3,2,1,0:T(8,128)(2,1)S(1)} %add_convert_fusion.rest_0_), channel_id=1, source_target_pairs={{0,6},{2,4},{4,2},{6,0},{8,14},{10,12},{12,10},{14,8},{16,22},{18,... | collective-permute-start | bytes 786440 | tf_op jit(solution)/shard_map/ppermute | solution.py:612
  69.2 0.7 copy-start.14
  82.1 10.6 %copy-start.4 = (bf16[4096,128]{1,0:T(8,128)(2,1)S(1)}, bf16[4096,128]{1,0:T(8,128)(2,1)}, u32[]{:S(2)}) copy-start(bf16[4096,128]{1,0:T(8,128)(2,1)} %far_attention.1.far_hbm) | copy-start | bytes 3145732
  90.4 0.7 copy-start.6
  91.2 0.7 copy-start.8
  91.9 0.7 copy-start.10
  92.6 1.6 %copy-start.3 = (bf16[1024,8,128]{2,1,0:T(8,128)(2,1)S(1)}, bf16[1024,8,128]{2,1,0:T(8,128)(2,1)}, u32[]{:S(2)}) copy-start(bf16[1024,8,128]{2,1,0:T(8,128)(2,1)} %param.18) | copy-start | bytes 6291460
  94.2 1.2 %copy-start.5 = (bf16[4096,128]{1,0:T(8,128)(2,1)S(1)}, bf16[4096,128]{1,0:T(8,128)(2,1)}, u32[]{:S(2)}) copy-start(bf16[4096,128]{1,0:T(8,128)(2,1)} %near_attention.1.near_hbm) | copy-start | bytes 3145732
  95.4 0.9 copy-start.7
  96.4 0.9 copy-start.9
  97.3 0.9 copy-start.11
  98.3 8.3 %copy-start.17 = (f32[4,8,128]{2,1,0:T(8,128)S(1)}, f32[4,8,128]{2,1,0:T(8,128)}, u32[]{:S(2)}) copy-start(f32[4,8,128]{2,1,0:T(8,128)} %get-tuple-element.27) | copy-start | bytes 49156
  98.3 11.8 %copy-start.2 = (f32[4096,128]{1,0:T(8,128)S(1)}, f32[4096,128]{1,0:T(8,128)}, u32[]{:S(2)}) copy-start(f32[4096,128]{1,0:T(8,128)} %get-tuple-element.26.trunk_hbm) | copy-start | bytes 6291460
  104.6 2.0 %copy-start = (f32[8192,128]{1,0:T(8,128)}, f32[8192,128]{1,0:T(8,128)S(1)}, u32[]{:S(2)}) copy-start(f32[8192,128]{1,0:T(8,128)S(1)} %get-tuple-element.32.branch_ref) | copy-start | bytes 12582916
  110.1 2.2 %copy-start.1 = (f32[8192,128]{1,0:T(8,128)S(1)}, f32[8192,128]{1,0:T(8,128)}, u32[]{:S(2)}) copy-start(f32[8192,128]{1,0:T(8,128)} %copy-done) | copy-start | bytes 12582916

commit v3 on v2

v3 whole, which is shorter than its diff:
```python
import functools
import math

import jax
import jax.numpy as jnp
from jax import lax
from jax.experimental import pallas as pl
from jax.experimental.pallas import tpu as pltpu
from jax.sharding import PartitionSpec as P

BLK = 128
WIN = 512
COLS = 4
MASKED = -1e30
F32 = jnp.float32
BF16 = jnp.bfloat16
VMEM_BYTES = 60 * 1024 * 1024
SMALL_BYTES = 28 * 1024 * 1024


def params(limit=VMEM_BYTES):
    return pltpu.CompilerParams(vmem_limit_bytes=limit)


def hbm():
    return pl.BlockSpec(memory_space=pltpu.HBM)


def vmem():
    return pl.BlockSpec(memory_space=pltpu.VMEM)


def block_copy(src, dst, sems, block, rows, src_block=None):
    src_block = block if src_block is None else src_block
    return pltpu.make_async_copy(
        src.at[pl.ds(src_block * rows, rows)], dst.at[pl.ds(block * rows, rows)], sems.at[block]
    )


def smem():
    return pl.BlockSpec(memory_space=pltpu.SMEM)


def gain_factor(level, width):
    return 1.0 / math.sqrt(width * BLK * 2 ** max(level - 1, 0))


def exchange(parts):
    parts = list(parts)
    rows = lax.broadcasted_iota(jnp.int32, parts[0].shape, 1)
    for step in (4, 2, 1):
        upper = (rows & step) == 0
        for i in range(8):
            if i & step == 0:
                low, high = parts[i], parts[i + step]
                parts[i] = jnp.where(upper, low, pltpu.roll(high, step, 1))
                parts[i + step] = jnp.where(upper, pltpu.roll(low, 8 - step, 1), high)
    return parts


def split_heads(wide):
    rows, width = wide.shape
    octets = wide.reshape(rows // 64, 8, 8, width)
    return [part.reshape(rows // 8, width) for part in exchange([octets[:, t] for t in range(8)])]


def join_heads(heads):
    rows, width = heads[0].shape
    tokens = exchange([head.reshape(rows // 8, 8, width) for head in heads])
    return jnp.stack(tokens, axis=1).reshape(rows * 8, width)


def state_kernel(depth, heads, where_ref, gain_ref, k_hbm, v_hbm, *rest):
    piece_refs, sum_refs = rest[:COLS], rest[COLS : 2 * COLS]
    keys, values, levels, sums, key_sems, value_sems = rest[2 * COLS :]
    width = keys.shape[1]
    rows = keys.shape[0] >> depth
    per_piece = heads // COLS
    column = where_ref[0] & (COLS - 1)
    copies = [
        (block_copy(k_hbm, keys, key_sems, b, rows), block_copy(v_hbm, values, value_sems, b, rows))
        for b in range(1 << depth)
    ]
    for pair in copies:
        for copy in pair:
            copy.start()
    for b, pair in enumerate(copies):
        for copy in pair:
            copy.wait()
        key_heads = split_heads(keys[b * rows : (b + 1) * rows].astype(F32))
        value_heads = split_heads(values[b * rows : (b + 1) * rows].astype(F32))
        for h in range(heads):
            k, v = key_heads[h].astype(BF16), value_heads[h].astype(BF16)
            merged = lax.dot_general(k, v, (((0,), (0,)), ((), ())), preferred_element_type=F32)
            before = None
            for bit in range(depth):
                if b >> bit & 1:
                    part = levels[bit, h] * (gain_ref[h, bit + 1] * gain_factor(bit + 1, width))
                    before = part if before is None else before + part
            carry = 0
            while b >> carry & 1:
                merged = merged + levels[carry, h]
                carry += 1
            if before is not None:
                piece_refs[h // per_piece][b - 1, h % per_piece] = before.astype(BF16)
            if carry < depth:
                levels[carry, h] = merged
            else:
                sums[column ^ (h // per_piece), h % per_piece] = merged.astype(BF16)
    for d in range(COLS):
        sum_refs[d][...] = sums[d]


def block_sums(where, gain, keys, values, heads, depth):
    blocks = 1 << depth
    width = keys.shape[1]
    each = heads // COLS
    piece = jax.ShapeDtypeStruct((blocks - 1, each, width, width), BF16)
    return pl.pallas_call(
        functools.partial(state_kernel, depth, heads),
        in_specs=[smem(), smem(), hbm(), hbm()],
        out_specs=[vmem()] * (2 * COLS),
        out_shape=[piece] * COLS + [jax.ShapeDtypeStruct((each, width, width), BF16)] * COLS,
        scratch_shapes=[
            pltpu.VMEM(keys.shape, BF16),
            pltpu.VMEM(values.shape, BF16),
            pltpu.VMEM((depth, heads, width, width), F32),
            pltpu.VMEM((COLS, each, width, width), BF16),
            pltpu.SemaphoreType.DMA((blocks,)),
            pltpu.SemaphoreType.DMA((blocks,)),
        ],
        compiler_params=params(),
        cost_estimate=pl.CostEstimate(
            flops=2 * keys.size * width, bytes_accessed=4 * keys.size + 2 * heads * width * width * blocks, transcendentals=0
        ),
        name="block_sums",
    )(where, gain, keys, values)


def in_plane(sums, column, weight):
    total = None
    for bit in range(COLS.bit_length() - 1):
        if column >> bit & 1:
            first = ((column >> bit) ^ 1) << bit
            part = functools.reduce(jnp.add, sums[first : first + (1 << bit)]) * weight(bit)
            total = part if total is None else total + part
    return total


def level_weight(gain_ref, head, depth, width, bit):
    return gain_ref[head, depth + bit + 1] * gain_factor(depth + bit + 1, width)


def in_order(where_ref, refs, held):
    for d, ref in enumerate(refs):
        held[(where_ref[0] & (COLS - 1)) ^ d] = ref[...]


def plane_kernel(depth, where_ref, gain_ref, *rest):
    sum_refs, (plane_ref, before_ref, held) = rest[:COLS], rest[COLS:]
    each, width = plane_ref.shape[:2]
    first = (where_ref[0] & (COLS - 1)) * each
    in_order(where_ref, sum_refs, held)
    for j in range(each):
        sums = [held[c, j].astype(F32) for c in range(COLS)]
        plane_ref[j] = functools.reduce(jnp.add, sums).astype(BF16)
        before_ref[j] = in_plane(sums, COLS - 1, lambda bit: level_weight(gain_ref, first + j, depth, width, bit))


def plane_sums(where, gain, sums, depth):
    quarter = sums[0].shape
    return pl.pallas_call(
        functools.partial(plane_kernel, depth),
        in_specs=[smem(), smem()] + [vmem()] * COLS,
        out_specs=[vmem(), vmem()],
        out_shape=[jax.ShapeDtypeStruct(quarter, BF16), jax.ShapeDtypeStruct(quarter, F32)],
        scratch_shapes=[pltpu.VMEM((COLS, *quarter), BF16)],
        compiler_params=params(SMALL_BYTES),
        cost_estimate=pl.CostEstimate(flops=16 * sums[0].size, bytes_accessed=16 * sums[0].size, transcendentals=0),
        name="plane_sums",
    )(where, gain, *sums)


def cross_kernel(depth, planes, where_ref, gain_ref, *rest):
    sum_refs, plane_refs = rest[:COLS], rest[COLS : COLS + planes]
    out_refs, (top_ref, held, states, outs) = rest[COLS + planes : 2 * COLS + planes], rest[2 * COLS + planes :]
    each, width = top_ref.shape[:2]
    col_bits = COLS.bit_length() - 1
    plane = where_ref[0] >> col_bits
    column = where_ref[0] & (COLS - 1)
    in_order(where_ref, sum_refs, held)
    for d, ref in enumerate(plane_refs):
        states[plane ^ d] = ref[...]
    for j in range(each):
        head = column * each + j
        sums = [held[c, j].astype(F32) for c in range(COLS)]
        above = jnp.zeros((width, width), F32)
        top = jnp.zeros((width, width), F32)
        for s in range(planes - 1):
            state = states[s, j].astype(F32)
            share = jnp.float32(0.0)
            for bit in range(planes.bit_length() - 1):
                weight = level_weight(gain_ref, head, depth, width, col_bits + bit)
                inside = jnp.logical_and((plane >> bit) & 1 == 1, (plane >> bit) ^ 1 == s >> bit)
                share = share + jnp.where(inside, weight, 0.0)
                if ((planes - 1) >> bit) ^ 1 == s >> bit:
                    top = top + state * weight
            above = above + state * share
        top_ref[j] = top
        for c in range(COLS):
            before = in_plane(sums, c, lambda bit: level_weight(gain_ref, head, depth, width, bit))
            outs[column ^ c, j] = (above if before is None else above + before).astype(BF16)
    for d in range(COLS):
        out_refs[d][...] = outs[d]


def cross_sums(where, gain, sums, planes, depth):
    quarter = sums[0].shape
    return pl.pallas_call(
        functools.partial(cross_kernel, depth, len(planes)),
        in_specs=[smem(), smem()] + [vmem()] * (COLS + len(planes)),
        out_specs=[vmem()] * (COLS + 1),
        out_shape=[jax.ShapeDtypeStruct(quarter, BF16)] * COLS + [jax.ShapeDtypeStruct(quarter, F32)],
        scratch_shapes=[
            pltpu.VMEM((COLS, *quarter), BF16),
            pltpu.VMEM((len(planes), *quarter), BF16),
            pltpu.VMEM((COLS, *quarter), BF16),
        ],
        compiler_params=params(SMALL_BYTES),
        cost_estimate=pl.CostEstimate(flops=60 * sums[0].size, bytes_accessed=30 * sums[0].size, transcendentals=0),
        name="cross_sums",
    )(where, gain, *sums, *planes)


def place(src_ref, dst, start):
    rows, width = src_ref.shape
    pairs = src_ref[...].astype(F32).reshape(rows // 16, 16, width)
    low, high = pairs[:, :8], pairs[:, 8:]
    even = (lax.broadcasted_iota(jnp.int32, low.shape, 1) & 1) == 0
    first = jnp.where(even, low, pltpu.roll(high, 1, 1))
    second = jnp.where(even, pltpu.roll(low, 7, 1), high)
    for g, part in enumerate((first, second)):
        dst[g, pl.ds(start, rows // 2), :width] = part.reshape(rows // 2, width).astype(BF16)


def token_at(place_of):
    return (place_of & -8) | ((place_of & 1) << 2) | ((place_of & 7) >> 1)


def split_groups(wide):
    rows, width = wide.shape
    pairs = wide.reshape(rows // 16, 16, width)
    low, high = pairs[:, :8], pairs[:, 8:]
    upper = lax.broadcasted_iota(jnp.int32, low.shape, 1) < 4
    first = jnp.where(upper, low, pltpu.roll(high, 4, 1))
    second = jnp.where(upper, pltpu.roll(low, 4, 1), high)
    return [part.reshape(rows // 2, width) for part in (first, second)]


def join_groups(first, second):
    rows, width = first.shape
    first, second = (part.reshape(rows // 8, 8, width) for part in (first, second))
    upper = lax.broadcasted_iota(jnp.int32, first.shape, 1) < 4
    low = jnp.where(upper, first, pltpu.roll(second, 4, 1))
    high = jnp.where(upper, pltpu.roll(first, 4, 1), second)
    return jnp.concatenate([low, high], axis=1).reshape(2 * rows, width)


def window_logits(queries, keys, token, share, bias):
    rows = queries.shape[0]
    logits = lax.dot_general(queries, keys, (((1,), (1,)), ((), ())), preferred_element_type=F32)
    row = token + lax.broadcasted_iota(jnp.int32, (rows, BLK), 0) // share
    col = token_at(lax.broadcasted_iota(jnp.int32, (rows, BLK), 1))
    late = col > row
    first = jnp.where(late, logits[:, :BLK], MASKED)
    last = jnp.where(late, MASKED, logits[:, -BLK:])
    logits = jnp.concatenate([first, logits[:, BLK:-BLK], last], axis=1)
    return logits if bias is None else logits + bias


def window_outputs(logits, values, width):
    top = jnp.max(logits, axis=1, keepdims=True)
    weights = jnp.exp2((logits - top) * (math.log2(math.e) / math.sqrt(width))).astype(BF16)
    both = jnp.dot(weights, values, preferred_element_type=F32)
    return both[:, :width] / both[:, width:]


def window_block(q_ref, kh, vh, base, groups, bias=None):
    width = q_ref.shape[1]
    span = WIN + BLK
    share = q_ref.shape[0] // BLK // groups
    parts = [part.astype(BF16) for part in split_groups(q_ref[...].astype(F32))]
    chunks = [(g, c) for g in range(groups) for c in range(0, BLK * share, BLK)]

    def logits_of(chunk):
        g, c = chunk
        return window_logits(parts[g][c : c + BLK], kh[g, pl.ds(base, span), :], c // share, share, bias)

    outs = []
    ahead = logits_of(chunks[0])
    for i, (g, c) in enumerate(chunks):
        now = ahead
        if i + 1 < len(chunks):
            ahead = logits_of(chunks[i + 1])
        outs.append(window_outputs(now, vh[g, pl.ds(base, span), :], width))
    half = len(outs) // 2
    return join_groups(jnp.concatenate(outs[:half], axis=0), jnp.concatenate(outs[half:], axis=0))


def square_sums(full, heads):
    tokens = full.shape[0] // heads
    row = lax.broadcasted_iota(jnp.int32, (tokens, full.shape[0]), 1) // heads
    mine = row == lax.broadcasted_iota(jnp.int32, (tokens, full.shape[0]), 0)
    sums = jnp.dot(mine.astype(BF16), (full * full).astype(BF16), preferred_element_type=F32)
    ones = jnp.ones((8, full.shape[1]), F32)
    return lax.dot_general(
        ones, sums, (((1,), (1,)), ((), ())), precision=lax.Precision.HIGHEST, preferred_element_type=F32
    )


def far_kernel(heads, groups, q_ref, pk_ref, pv_ref, ck_ref, cv_ref, out_ref, kh, vh):
    step = pl.program_id(0)
    width = q_ref.shape[1]

    @pl.when(step == 0)
    def _():
        vh[:, :, width:] = jnp.ones((groups, vh.shape[1], width), BF16)
        place(pk_ref, kh, 0)
        place(ck_ref, kh, WIN)
        place(pv_ref, vh, 0)
        place(cv_ref, vh, WIN)

    out_ref[...] = window_block(q_ref, kh, vh, pl.multiple_of(step * BLK, BLK), groups).astype(BF16)


def attention_cost(tokens, heads, width, extra=0):
    span = WIN + BLK
    return pl.CostEstimate(
        flops=6 * tokens * heads * span * width + extra,
        bytes_accessed=12 * tokens * heads * width,
        transcendentals=tokens * heads * span,
    )


def far_attention(queries, keys, values, heads, groups):
    width = queries.shape[1]
    steps = queries.shape[0] // (BLK * heads) - WIN // BLK
    skip = WIN // BLK
    at_first = pl.BlockSpec((WIN * groups, width), lambda i: (0, 0))
    at_next = pl.BlockSpec((WIN * groups, width), lambda i: (1, 0))
    return pl.pallas_call(
        functools.partial(far_kernel, heads, groups),
        grid=(steps,),
        in_specs=[
            pl.BlockSpec((BLK * heads, width), lambda i: (i + skip, 0)),
            at_first,
            at_first,
            at_next,
            at_next,
        ],
        out_specs=pl.BlockSpec((BLK * heads, width), lambda i: (i, 0)),
        out_shape=jax.ShapeDtypeStruct((steps * BLK * heads, width), BF16),
        scratch_shapes=[
            pltpu.VMEM((groups, 2 * WIN, width), BF16),
            pltpu.VMEM((groups, 2 * WIN, 2 * width), BF16),
        ],
        compiler_params=params(),
        cost_estimate=attention_cost(steps * BLK, heads, width),
        name="far_attention",
    )(queries, keys, values, keys, values)


def trunk_kernel(heads, groups, where_ref, gain_ref, q_ref, k_ref, v_ref, wq_ref, pk_ref, pv_ref, ck_ref, cv_ref, *rest):
    cross_refs, piece_refs = rest[:COLS], rest[COLS : 2 * COLS]
    out_ref, square_ref, kh, vh, cs = rest[2 * COLS :]
    step = pl.program_id(0)
    width = q_ref.shape[1]

    @pl.when(step == 0)
    def _():
        vh[:, :, width:] = jnp.ones((groups, vh.shape[1], width), BF16)
        place(pk_ref, kh, 0)
        place(ck_ref, kh, WIN)
        place(pv_ref, vh, 0)
        place(cv_ref, vh, WIN)
        in_order(where_ref, cross_refs, cs)

    base = pl.multiple_of(step * BLK, BLK)
    span = WIN + BLK
    reach = jnp.where(where_ref[0] == 0, WIN - step * BLK, 0)
    bias = jnp.where(lax.broadcasted_iota(jnp.int32, (1, span), 1) < reach, MASKED, 0.0).astype(F32)
    row = lax.broadcasted_iota(jnp.int32, (BLK, BLK), 0)
    col = lax.broadcasted_iota(jnp.int32, (BLK, BLK), 1)
    inner = (step > 0).astype(F32).astype(BF16)
    per_piece = heads // COLS
    q, k, v = (
        [part.astype(BF16) for part in split_heads(ref[...].astype(F32))] for ref in (q_ref, k_ref, v_ref)
    )
    inside = [
        lax.dot_general(q[h], k[h], (((1,), (1,)), ((), ())), preferred_element_type=F32) for h in range(heads)
    ]
    outs = []
    for h in range(heads):
        weight = jnp.where(col <= row, inside[h], 0.0) * (gain_ref[h, 0] * gain_factor(0, width))
        left = jnp.concatenate([weight.astype(BF16), q[h], q[h]], axis=1)
        j, i = h // per_piece, h % per_piece
        right = jnp.concatenate([v[h], cs[j, i], piece_refs[j][0, i] * inner], axis=0)
        outs.append(jnp.dot(left, right, preferred_element_type=F32))
    full = window_block(wq_ref, kh, vh, base, groups, bias) + join_heads(outs)
    out_ref[...] = full
    square_ref[0] = square_sums(full, heads)


def trunk_attention(where, gain, q, k, v, wq, pk, pv, ck, cv, cross, pieces, heads, groups):
    width = q.shape[1]
    blocks = q.shape[0] // (BLK * heads)
    at_block = pl.BlockSpec((BLK * heads, width), lambda i: (i, 0))
    whole = pl.BlockSpec((WIN * groups, width), lambda i: (0, 0))
    own = pl.BlockSpec(cross[0].shape, lambda i: (0, 0, 0))
    piece = pl.BlockSpec((1, heads // COLS, width, width), lambda i: (jnp.maximum(i - 1, 0), 0, 0, 0))
    return pl.pallas_call(
        functools.partial(trunk_kernel, heads, groups),
        grid=(blocks,),
        in_specs=[smem(), smem()] + [at_block] * 4 + [whole] * 4 + [own] * COLS + [piece] * COLS,
        out_specs=[at_block, pl.BlockSpec((1, 8, BLK), lambda i: (i, 0, 0))],
        out_shape=[
            jax.ShapeDtypeStruct(q.shape, F32),
            jax.ShapeDtypeStruct((blocks, 8, BLK), F32),
        ],
        scratch_shapes=[
            pltpu.VMEM((groups, 2 * WIN, width), BF16),
            pltpu.VMEM((groups, 2 * WIN, 2 * width), BF16),
            pltpu.VMEM((COLS, *cross[0].shape), BF16),
        ],
        compiler_params=params(),
        cost_estimate=attention_cost(blocks * BLK, heads, width, 2 * blocks * BLK * BLK * heads * 4 * width),
        name="trunk_attention",
    )(where, gain, q, k, v, wq, pk, pv, ck, cv, *cross, *pieces)


def near_kernel(groups, where_ref, fork_ref, q_ref, ck_ref, cv_ref, *rest):
    kv_refs, out_ref = rest[:COLS], rest[COLS]
    kh, vh, kt = rest[COLS + 1 :]
    step = pl.program_id(0)
    width = q_ref.shape[1]
    column = where_ref[0] & (COLS - 1)
    start = pl.multiple_of(fork_ref[0] * BLK, BLK)

    @pl.when(step == 0)
    def _():
        for i in range(COLS):
            kt[column ^ i] = kv_refs[i][...]
        vh[:, :, width:] = jnp.ones((groups, vh.shape[1], width), BF16)
        place(kt.at[0], vh, 0)
        place(kt.at[1], vh, WIN)
        place(kt.at[2], kh, 0)
        place(kt.at[3], kh, WIN)
        place(ck_ref, kh, pl.multiple_of(start + WIN, BLK))
        place(cv_ref, vh, pl.multiple_of(start + WIN, BLK))

    base = pl.multiple_of(start + step * BLK, BLK)
    out_ref[...] = window_block(q_ref, kh, vh, base, groups).astype(BF16)


def near_attention(where, fork, wq, ck, cv, kvs, heads, groups):
    width = wq.shape[1]
    steps = WIN // BLK
    at_block = pl.BlockSpec((BLK * heads, width), lambda i: (i, 0))
    whole = pl.BlockSpec((WIN * groups, width), lambda i: (0, 0))
    return pl.pallas_call(
        functools.partial(near_kernel, groups),
        grid=(steps,),
        in_specs=[smem(), smem(), at_block, whole, whole] + [whole] * COLS,
        out_specs=at_block,
        out_shape=jax.ShapeDtypeStruct((steps * BLK * heads, width), BF16),
        scratch_shapes=[
            pltpu.VMEM((groups, 3 * WIN, width), BF16),
            pltpu.VMEM((groups, 3 * WIN, 2 * width), BF16),
            pltpu.VMEM((COLS, WIN * groups, width), BF16),
        ],
        compiler_params=params(),
        cost_estimate=attention_cost(steps * BLK, heads, width),
        name="near_attention",
    )(where, fork, wq, ck, cv, *kvs)


def branch_kernel(heads, where_ref, fork_ref, q_hbm, near_hbm, far_hbm, *rest):
    piece_hbms = rest[:COLS]
    full_hbm, square_ref, qs, ws, fs, es, q_sems, w_sems, f_sems, e_sems = rest[COLS:]
    rows = BLK * heads
    blocks = qs.shape[0] // rows
    skip = WIN // BLK
    per_piece = heads // COLS
    column = where_ref[0] & (COLS - 1)
    ends = [
        pltpu.make_async_copy(piece_hbms[i].at[fork_ref[0]], es.at[column ^ i], e_sems.at[i]) for i in range(COLS)
    ]
    for copy in ends:
        copy.start()
    for b in range(blocks):
        block_copy(q_hbm, qs, q_sems, b, rows).start()
        if b < skip:
            block_copy(near_hbm, ws, w_sems, b, rows).start()
        else:
            block_copy(far_hbm, ws, w_sems, b, rows, b - skip).start()
    for copy in ends:
        copy.wait()

    def one_block(b, carry):
        block_copy(q_hbm, qs, q_sems, b, rows).wait()
        block_copy(near_hbm, ws, w_sems, b, rows, 0).wait()
        at = pl.ds(pl.multiple_of(b * rows, rows), rows)
        q = split_heads(qs[at, :].astype(F32))
        outs = [
            jnp.dot(q[h].astype(BF16), es[h // per_piece, h % per_piece], preferred_element_type=F32)
            for h in range(heads)
        ]
        full = ws[at, :].astype(F32) + join_heads(outs)
        fs[at, :] = full
        block_copy(fs, full_hbm, f_sems, b, rows).start()
        square_ref[b] = square_sums(full, heads)
        return carry

    lax.fori_loop(0, blocks, one_block, 0)
    for b in range(blocks):
        block_copy(fs, full_hbm, f_sems, b, rows).wait()


def branch_linear(where, fork, q, near, far, pieces, heads):
    width = q.shape[1]
    blocks = q.shape[0] // (BLK * heads)
    return pl.pallas_call(
        functools.partial(branch_kernel, heads),
        in_specs=[smem(), smem()] + [hbm()] * (3 + COLS),
        out_specs=[hbm(), vmem()],
        out_shape=[
            jax.ShapeDtypeStruct(q.shape, F32),
            jax.ShapeDtypeStruct((blocks, 8, BLK), F32),
        ],
        scratch_shapes=[
            pltpu.VMEM(q.shape, BF16),
            pltpu.VMEM(q.shape, BF16),
            pltpu.VMEM(q.shape, F32),
            pltpu.VMEM((COLS, *pieces[0].shape[1:]), BF16),
            pltpu.SemaphoreType.DMA((blocks,)),
            pltpu.SemaphoreType.DMA((blocks,)),
            pltpu.SemaphoreType.DMA((blocks,)),
            pltpu.SemaphoreType.DMA((COLS,)),
        ],
        compiler_params=params(),
        cost_estimate=pl.CostEstimate(
            flops=4 * blocks * BLK * heads * width * width, bytes_accessed=8 * q.size, transcendentals=0
        ),
        name="branch_linear",
    )(where, fork, q, near, far, *pieces)


def norm_kernel(heads, features, trunk_hbm, trunk_square, branch_hbm, branch_square, trunk_out, branch_out, held, done, in_sems, out_sems):
    rows = BLK * heads
    width = held.shape[1]
    trunk_blocks = trunk_hbm.shape[0] // rows
    branch_blocks = branch_hbm.shape[0] // rows

    def arrive(src, block, slot):
        return pltpu.make_async_copy(
            src.at[pl.ds(block * rows, rows)], held.at[pl.ds(slot * rows, rows)], in_sems.at[slot]
        )

    def leave(dst, block, slot):
        return pltpu.make_async_copy(
            done.at[pl.ds(slot * rows, rows)], dst.at[pl.ds(block * rows, rows)], out_sems.at[slot]
        )

    parts = ((branch_hbm, branch_square, branch_out, 0, branch_blocks), (trunk_hbm, trunk_square, trunk_out, branch_blocks, trunk_blocks))
    for src, _, _, first, blocks in parts:
        for b in range(blocks):
            arrive(src, b, first + b).start()
    for src, squares, dst, first, blocks in parts:

        def one_block(b, carry):
            slot = first + b
            arrive(src, b, slot).wait()
            at = pl.ds(pl.multiple_of(slot * rows, rows), rows)
            scale = lax.rsqrt(squares[b, 0:1, :] / features + 1e-06)
            scale = jnp.broadcast_to(scale, (width, BLK)).T
            full = held[at, :].reshape(BLK, heads, width)
            done[at, :] = (full * scale[:, None, :]).astype(BF16).reshape(rows, width)
            leave(dst, b, slot).start()
            return carry

        lax.fori_loop(0, blocks, one_block, 0)
    for _, _, dst, first, blocks in parts:
        for b in range(blocks):
            leave(dst, b, first + b).wait()


def normalize(trunk, trunk_square, branch, branch_square, heads, features):
    total = trunk.shape[0] + branch.shape[0]
    slots = total // (BLK * heads)
    return pl.pallas_call(
        functools.partial(norm_kernel, heads, features),
        in_specs=[hbm(), vmem(), hbm(), vmem()],
        out_specs=[hbm(), hbm()],
        out_shape=[jax.ShapeDtypeStruct(trunk.shape, BF16), jax.ShapeDtypeStruct(branch.shape, BF16)],
        scratch_shapes=[
            pltpu.VMEM((total, trunk.shape[1]), F32),
            pltpu.VMEM((total, trunk.shape[1]), BF16),
            pltpu.SemaphoreType.DMA((slots,)),
            pltpu.SemaphoreType.DMA((slots,)),
        ],
        compiler_params=params(),
        cost_estimate=pl.CostEstimate(
            flops=2 * (trunk.size + branch.size), bytes_accessed=6 * (trunk.size + branch.size), transcendentals=0
        ),
        name="normalize",
    )(trunk, trunk_square, branch, branch_square)


def shards(
    trunk_query,
    trunk_key,
    trunk_value,
    trunk_wquery,
    trunk_wkey,
    trunk_wvalue,
    branch_query,
    branch_wquery,
    branch_wkey,
    branch_wvalue,
    level_gain,
    fork_block,
):
    tokens, heads, width = trunk_query.shape
    groups = trunk_wkey.shape[1]
    depth = (tokens // BLK).bit_length() - 1
    count = lax.axis_size("seq")
    planes = count // COLS
    features = heads * lax.axis_size("head") * width
    me = lax.axis_index("seq")
    column, plane = me % COLS, me // COLS
    where = me.astype(jnp.int32).reshape(1)
    root = count - 1
    top = planes - 1

    def flat(x):
        return x.reshape(x.shape[0] * x.shape[1], x.shape[2])

    tq, tk, tv, twq = flat(trunk_query), flat(trunk_key), flat(trunk_value), flat(trunk_wquery)
    twk, twv = flat(trunk_wkey), flat(trunk_wvalue)
    bq, bwq, bwk, bwv = flat(branch_query), flat(branch_wquery), flat(branch_wkey), flat(branch_wvalue)

    def send(x, pairs):
        return lax.ppermute(x, "seq", pairs)

    def down(x):
        step = planes // 2
        while step:
            starts = [p for p in range(planes) if (top - p) % (2 * step) == 0 and p >= step]
            pairs = [(p * COLS + c, (p - step) * COLS + c) for p in starts for c in range(COLS)]
            got = send(x, pairs)
            hit = functools.reduce(jnp.logical_or, [plane == p - step for p in starts])
            x = jnp.where(hit, got, x)
            step //= 2
        return x

    def around(x):
        return [x] + [send(x, [(i, i ^ d) for i in range(count)]) for d in range(1, COLS)]

    def along(x):
        return [x] + [send(x, [(i, i ^ (d * COLS)) for i in range(count)]) for d in range(1, planes)]

    def swap(parts):
        return [parts[0]] + [send(parts[d], [(i, i ^ d) for i in range(count)]) for d in range(1, COLS)]

    half = COLS // 2
    got = send(twv, [(root - i, root - i - half) for i in range(half)])
    kv = down(jnp.where(column >= half, twk, got))
    shift = [(i, i + 1) for i in range(count - 1)]

    outs = block_sums(where, level_gain, tk, tv, heads, depth)
    pieces, shard_sum = outs[:COLS], outs[COLS:]
    sums = swap(shard_sum)
    local = pieces[COLS - 1]
    for c in range(COLS - 1):
        got = send(pieces[c], [(root, root - (COLS - 1) + c)])
        local = jnp.where(column == c, got, local)
    plane_sum, before = plane_sums(where, level_gain, sums, depth)
    plane_list = along(plane_sum)
    ends = jnp.concatenate([jnp.zeros_like(local[:1]), local], axis=0)
    pk, pv = send(twk, shift), send(twv, shift)

    far = far_attention(bwq, bwk, bwv, heads, groups)
    plane_list, far, kv, ends = lax.optimization_barrier((plane_list, far, kv, ends))
    ends = down((before[None] + ends.astype(F32)).astype(BF16))
    *cross, above = cross_sums(where, level_gain, sums, plane_list, depth)
    cross = swap(cross)
    kvs = around(kv)
    ends = around((ends.astype(F32) + above).astype(BF16))

    trunk_full, trunk_square = trunk_attention(
        where, level_gain, tq, tk, tv, twq, pk, pv, twk, twv, cross, pieces, heads, groups
    )
    trunk_full, kvs = lax.optimization_barrier((trunk_full, kvs))
    near = near_attention(where, fork_block, bwq, bwk, bwv, kvs, heads, groups)
    branch_full, branch_square = branch_linear(where, fork_block, bq, near, far, ends, heads)
    trunk_square, branch_square = lax.psum((trunk_square, branch_square), "head")
    trunk_out, branch_out = normalize(trunk_full, trunk_square, branch_full, branch_square, heads, features)
    return trunk_out.reshape(trunk_query.shape), branch_out.reshape(branch_query.shape)


def solution(mesh):
    rows = P("seq", "head", None)
    return jax.shard_map(
        shards,
        mesh=mesh,
        in_specs=(rows,) * 10 + (P("head", None), P("seq")),
        out_specs=(rows, rows),
        check_vma=False,
    )
```

time: 116 us -> 122 us (1.052)
  local copies, waits for them, and re-layouts: 14.1 us -> 1.71 us
  starting transfers between devices: 42.6 us -> 50.1 us
  waiting for transfers between devices: 4.97 us -> 11.6 us
  Pallas kernels: 45.5 us -> 50.6 us
  other arithmetic: 2.81 us -> 0.39 us
    ppermute x16 -> x25, starting transfers between devices: 22.1 us -> 50.1 us  [send(): return lax.ppermute(x, 'seq', pairs)]
    all_to_all x3 -> x0, starting transfers between devices: 20.5 us -> none  [in_groups(): lax.all_to_all(x, 'seq', 0, 0, tiled=True, axis_index_groups=groups_of)]
    unnamed x44 -> x40, local copies, waits for them, and re-layouts: 14.1 us -> 1.69 us
    ppermute x16 -> x25, waiting for transfers between devices: 1.09 us -> 11.6 us  [send(): return lax.ppermute(x, 'seq', pairs)]
    all_to_all x3 -> x0, waiting for transfers between devices: 3.88 us -> none  [in_groups(): lax.all_to_all(x, 'seq', 0, 0, tiled=True, axis_index_groups=groups_of)]
    pallas_call x1, Pallas kernels: 6.32 us -> 9.88 us  [branch_linear(): pl.pallas_call(functools.partial(branch_kernel, heads), in_specs=[smem(),...]
    pallas_call x1, Pallas kernels: 2.83 us -> 5.36 us  [normalize(): pl.pallas_call(functools.partial(norm_kernel, heads, features), in_specs=...]
  transfers between devices with their start and end apart: 19 -> 25, of which waited for: 2 -> 5; matrix products, arithmetic and copies ran while one was open for 2% -> 0% of each run, Pallas kernels for 32% -> 29%
where the time goes in v3:
time: 122 us; the launch traced here: 121 us
  Pallas kernels  50.6 us (41%)
  starting transfers between devices  50.1 us (41%)
  waiting for transfers between devices  11.6 us (10%)
  blocking collectives  4.68 us (4%)
  between operations  1.76 us (1%)
  local copies, waits for them, and re-layouts  1.71 us (1%)
    ppermute x25, starting transfers between devices, send(): return lax.ppermute(x, 'seq', pairs)  50.1 us
    pallas_call x1, Pallas kernels, trunk_attention(): pl.pallas_call(functools.partial(trunk_kernel, heads, groups), grid=(bloc...  12.9 us
    ppermute x25, waiting for transfers between devices, send(): return lax.ppermute(x, 'seq', pairs)  11.6 us
    pallas_call x1, Pallas kernels, branch_linear(): pl.pallas_call(functools.partial(branch_kernel, heads), in_specs=[smem(),...  9.88 us
    pallas_call x1, Pallas kernels, near_attention(): pl.pallas_call(functools.partial(near_kernel, groups), grid=(steps,), in_...  8.55 us
    pallas_call x1, Pallas kernels, far_attention(): pl.pallas_call(functools.partial(far_kernel, heads, groups), grid=(steps,...  7.98 us
    pallas_call x1, Pallas kernels, normalize(): pl.pallas_call(functools.partial(norm_kernel, heads, features), in_specs=...  5.36 us
    psum x1, blocking collectives, shards(): lax.psum((trunk_square, branch_square), 'head')  4.68 us
  transfers between devices with their start and end apart: 25, of which 5 were waited for; matrix products, arithmetic and copies ran while one was open for 0% of the time, Pallas kernels for 29%

profile of v3, /device:TPU:0, one launch (start us, length us, event | category | flops | bytes accessed | tf_op | source)
XLA Modules:
  0.0 120.9 jit_solution(1516752552482959388)
XLA Ops:
  0.6 0.7 collective-permute-start.8
  1.3 0.0 collective-permute-done.8
  1.4 0.7 collective-permute-start.9
  2.1 4.5 %block_sums.1 = (bf16[3,2,128,128]{3,2,1,0:T(8,128)(2,1)}, bf16[3,2,128,128]{3,2,1,0:T(8,128)(2,1)}, bf16[3,2,128,128]{3,2,1,0:T(8,128)(2,1)}, bf16[3,2,128,128]...) custom-call(s32[1]{0:T(128)} %bitcast.where_ref, ...), custom_call_target="tpu_custom_call" | custom-call | flops 134217728 | bytes 3145728 | tf_op jit(solution)/shard_map/block_sums/pallas_call | solution.py:119
  6.6 3.0 %collective-permute-start.2 = (bf16[2,128,128]{2,1,0:T(8,128)(2,1)}, bf16[2,128,128]{2,1,0:T(8,128)(2,1)S(1)}, u32[]{:S(2)}, u32[]{:S(2)}) collective-permute-start(bf16[2,128,128]{2,1,0:T(8,128)(2,1)} %get-tuple-element.36), channel_id=1, source_target_pairs={{0,2},{2,0},{4,6},{6,4},{8,10},{10,8},{12,14},{14,12},{16,18},{18,... | collective-permute-start | bytes 196616 | tf_op jit(solution)/shard_map/ppermute | solution.py:653
  9.6 2.5 %collective-permute-start.3 = (bf16[2,128,128]{2,1,0:T(8,128)(2,1)}, bf16[2,128,128]{2,1,0:T(8,128)(2,1)S(1)}, u32[]{:S(2)}, u32[]{:S(2)}) collective-permute-start(bf16[2,128,128]{2,1,0:T(8,128)(2,1)} %get-tuple-element.37), channel_id=1, source_target_pairs={{0,4},{2,6},{4,0},{6,2},{8,12},{10,14},{12,8},{14,10},{16,20},{18,... | collective-permute-start | bytes 196616 | tf_op jit(solution)/shard_map/ppermute | solution.py:653
  12.0 0.7 collective-permute-start.11
  12.7 0.7 collective-permute-start.12
  13.4 0.0 collective-permute-done.9
  13.4 0.7 collective-permute-start.13
  14.1 0.0 collective-permute-done.2.rest_1_
  14.2 1.8 %collective-permute-start.4 = (bf16[2,128,128]{2,1,0:T(8,128)(2,1)}, bf16[2,128,128]{2,1,0:T(8,128)(2,1)S(1)}, u32[]{:S(2)}, u32[]{:S(2)}) collective-permute-start(bf16[2,128,128]{2,1,0:T(8,128)(2,1)} %get-tuple-element.38), channel_id=1, source_target_pairs={{0,6},{2,4},{4,2},{6,0},{8,14},{10,12},{12,10},{14,8},{16,22},{18,... | collective-permute-start | bytes 196616 | tf_op jit(solution)/shard_map/ppermute | solution.py:653
  16.0 1.3 %collective-permute-start.10 = (bf16[1024,128]{1,0:T(8,128)(2,1)S(1)}, bf16[1024,128]{1,0:T(8,128)(2,1)S(1)}, u32[]{:S(2)}, u32[]{:S(2)}) collective-permute-start(bf16[1024,128]{1,0:T(8,128)(2,1)S(1)} %broadcast_select_fusion.2), channel_id=1, source_target_pairs={{8,0},{10,2},{12,4},{14,6},{24,16},{26,18},{28,20},{30,22},{9,1},{... | collective-permute-start | bytes 786440 | tf_op jit(solution)/shard_map/ppermute | solution.py:653
  17.2 0.0 copy-start
  17.3 0.0 copy-start.1
  17.3 8.0 %far_attention.1.far_hbm = bf16[4096,128]{1,0:T(8,128)(2,1)} custom-call(bf16[8192,128]{1,0:T(8,128)(2,1)} %bitcast.21, bf16[2048,128]{1,0:T(8,128)(2,1)} %bitcast.27, bf16[2048,128]{1,0:T(8,128)(2,1)} %bitcast.30, bf16[2048,128]{1,0:T(8,128)(2,1)} %bitcast.28, bf16[2048,128]{1,0:T(8,128)(2,1)} %bitcast.31), custom_call_target="tpu_custom_call" | custom-call | flops 2013265920 | bytes 6291456 | tf_op jit(solution)/shard_map/far_attention/pallas_call | solution.py:351
  25.3 0.7 plane_sums.1
  26.0 15.5 %collective-permute-start.7 = (bf16[2,128,128]{2,1,0:T(8,128)(2,1)S(1)}, bf16[2,128,128]{2,1,0:T(8,128)(2,1)S(1)}, u32[]{:S(2)}, u32[]{:S(2)}) collective-permute-start(bf16[2,128,128]{2,1,0:T(8,128)(2,1)S(1)} %get-tuple-element.44.rest_4_), channel_id=1, source_target_pairs={{0,24},{2,26},{4,28},{6,30},{8,16},{10,18},{12,20},{14,22},{16,8},... | collective-permute-start | bytes 196616 | tf_op jit(solution)/shard_map/ppermute | solution.py:653
  41.5 0.0 collective-permute-done.11
  41.5 0.0 collective-permute-start.6
  41.5 0.6 collective-permute-start.5
  42.2 0.0 collective-permute-done.13
  42.3 1.5 %collective-permute-done.7.rest_7_ = bf16[2,128,128]{2,1,0:T(8,128)(2,1)S(1)} collective-permute-done((bf16[2,128,128]{2,1,0:T(8,128)(2,1)S(1)}, bf16[2,128,128]{2,1,0:T(8,128)(2,1)S(1)}, u32[]{:S(2)}, u32[]{:S(2)}) %collective-permute-start.7) | collective-permute-done | bytes 65568 | tf_op jit(solution)/shard_map/ppermute | solution.py:653
  43.9 2.8 %collective-permute-done.6.rest_6_ = bf16[2,128,128]{2,1,0:T(8,128)(2,1)S(1)} collective-permute-done((bf16[2,128,128]{2,1,0:T(8,128)(2,1)S(1)}, bf16[2,128,128]{2,1,0:T(8,128)(2,1)S(1)}, u32[]{:S(2)}, u32[]{:S(2)}) %collective-permute-start.6) | collective-permute-done | bytes 65568 | tf_op jit(solution)/shard_map/ppermute | solution.py:653
  46.7 0.0 collective-permute-done.5.rest_5_
  46.7 0.1 add_convert_fusion.1
  46.7 0.7 collective-permute-start.20
  47.4 1.3 %collective-permute-start = (bf16[1024,128]{1,0:T(8,128)(2,1)S(1)}, bf16[1024,128]{1,0:T(8,128)(2,1)S(1)}, u32[]{:S(2)}, u32[]{:S(2)}) collective-permute-start(bf16[1024,128]{1,0:T(8,128)(2,1)S(1)} %bitcast.20), channel_id=1, source_target_pairs={{0,2},{2,4},{4,6},{6,8},{8,10},{10,12},{12,14},{14,16},{16,18},{18... | collective-permute-start | bytes 786440 | tf_op jit(solution)/shard_map/ppermute | solution.py:653
  48.8 1.8 %collective-permute-start.1 = (bf16[1024,128]{1,0:T(8,128)(2,1)S(1)}, bf16[1024,128]{1,0:T(8,128)(2,1)S(1)}, u32[]{:S(2)}, u32[]{:S(2)}) collective-permute-start(bf16[1024,128]{1,0:T(8,128)(2,1)S(1)} %bitcast.35), channel_id=1, source_target_pairs={{0,2},{2,4},{4,6},{6,8},{8,10},{10,12},{12,14},{14,16},{16,18},{18... | collective-permute-start | bytes 786440 | tf_op jit(solution)/shard_map/ppermute | solution.py:653
  50.5 0.1 broadcast_select_fusion
  50.6 1.3 %collective-permute-start.21 = (bf16[4,2,128,128]{3,2,1,0:T(8,128)(2,1)S(1)}, bf16[4,2,128,128]{3,2,1,0:T(8,128)(2,1)S(1)}, u32[]{:S(2)}, u32[]{:S(2)}) collective-permute-start(bf16[4,2,128,128]{3,2,1,0:T(8,128)(2,1)S(1)} %broadcast_select_fusion), channel_id=1, source_target_pairs={{8,0},{10,2},{12,4},{14,6},{24,16},{26,18},{28,20},{30,22},{9,1},{... | collective-permute-start | bytes 786440 | tf_op jit(solution)/shard_map/ppermute | solution.py:653
  51.9 0.8 cross_sums.1
  52.8 2.9 %collective-permute-start.14 = (bf16[2,128,128]{2,1,0:T(8,128)(2,1)S(1)}, bf16[2,128,128]{2,1,0:T(8,128)(2,1)S(1)}, u32[]{:S(2)}, u32[]{:S(2)}) collective-permute-start(bf16[2,128,128]{2,1,0:T(8,128)(2,1)S(1)} %get-tuple-element.49), channel_id=1, source_target_pairs={{0,2},{2,0},{4,6},{6,4},{8,10},{10,8},{12,14},{14,12},{16,18},{18,... | collective-permute-start | bytes 196616 | tf_op jit(solution)/shard_map/ppermute | solution.py:653
  55.6 3.4 %collective-permute-start.19 = (bf16[1024,128]{1,0:T(8,128)(2,1)S(1)}, bf16[1024,128]{1,0:T(8,128)(2,1)S(1)}, u32[]{:S(2)}, u32[]{:S(2)}) collective-permute-start(bf16[1024,128]{1,0:T(8,128)(2,1)S(1)} %broadcast_select_fusion.3.rest_0_), channel_id=1, source_target_pairs={{0,6},{2,4},{4,2},{6,0},{8,14},{10,12},{12,10},{14,8},{16,22},{18,... | collective-permute-start | bytes 786440 | tf_op jit(solution)/shard_map/ppermute | solution.py:653
  59.7 0.0 collective-permute-done.pk_ref
  59.7 0.0 copy-start.12
  59.7 0.1 collective-permute-start.18
  59.8 1.3 %collective-permute-done.1.pv_ref = bf16[1024,128]{1,0:T(8,128)(2,1)S(1)} collective-permute-done((bf16[1024,128]{1,0:T(8,128)(2,1)S(1)}, bf16[1024,128]{1,0:T(8,128)(2,1)S(1)}, u32[]{:S(2)}, u32[]{:S(2)}) %collective-permute-start.1) | collective-permute-done | bytes 262176 | tf_op jit(solution)/shard_map/ppermute | solution.py:653
  61.1 2.5 %collective-permute-start.17 = (bf16[1024,128]{1,0:T(8,128)(2,1)S(1)}, bf16[1024,128]{1,0:T(8,128)(2,1)S(1)}, u32[]{:S(2)}, u32[]{:S(2)}) collective-permute-start(bf16[1024,128]{1,0:T(8,128)(2,1)S(1)} %broadcast_select_fusion.3.rest_0_), channel_id=1, source_target_pairs={{0,2},{2,0},{4,6},{6,4},{8,10},{10,8},{12,14},{14,12},{16,18},{18,... | collective-permute-start | bytes 786440 | tf_op jit(solution)/shard_map/ppermute | solution.py:653
  63.6 0.0 collective-permute-done.14.rest_1_
  63.6 1.0 collective-permute-start.15
  64.6 0.0 collective-permute-done.21
  64.6 1.9 %collective-permute-start.16 = (bf16[2,128,128]{2,1,0:T(8,128)(2,1)S(1)}, bf16[2,128,128]{2,1,0:T(8,128)(2,1)S(1)}, u32[]{:S(2)}, u32[]{:S(2)}) collective-permute-start(bf16[2,128,128]{2,1,0:T(8,128)(2,1)S(1)} %get-tuple-element.51), channel_id=1, source_target_pairs={{0,6},{2,4},{4,2},{6,0},{8,14},{10,12},{12,10},{14,8},{16,22},{18,... | collective-permute-start | bytes 196616 | tf_op jit(solution)/shard_map/ppermute | solution.py:653
  66.5 0.1 add_convert_fusion.rest_0_
  66.6 4.4 %collective-permute-done.15.rest_2_ = bf16[2,128,128]{2,1,0:T(8,128)(2,1)S(1)} collective-permute-done((bf16[2,128,128]{2,1,0:T(8,128)(2,1)S(1)}, bf16[2,128,128]{2,1,0:T(8,128)(2,1)S(1)}, u32[]{:S(2)}, u32[]{:S(2)}) %collective-permute-start.15) | collective-permute-done | bytes 65568 | tf_op jit(solution)/shard_map/ppermute | solution.py:653
  71.0 1.2 %collective-permute-start.24 = (bf16[4,2,128,128]{3,2,1,0:T(8,128)(2,1)S(1)}, bf16[4,2,128,128]{3,2,1,0:T(8,128)(2,1)S(1)}, u32[]{:S(2)}, u32[]{:S(2)}) collective-permute-start(bf16[4,2,128,128]{3,2,1,0:T(8,128)(2,1)S(1)} %add_convert_fusion.rest_0_), channel_id=1, source_target_pairs={{0,6},{2,4},{4,2},{6,0},{8,14},{10,12},{12,10},{14,8},{16,22},{18,... | collective-permute-start | bytes 786440 | tf_op jit(solution)/shard_map/ppermute | solution.py:653
  72.2 1.5 %collective-permute-done.16.rest_3_ = bf16[2,128,128]{2,1,0:T(8,128)(2,1)S(1)} collective-permute-done((bf16[2,128,128]{2,1,0:T(8,128)(2,1)S(1)}, bf16[2,128,128]{2,1,0:T(8,128)(2,1)S(1)}, u32[]{:S(2)}, u32[]{:S(2)}) %collective-permute-start.16) | collective-permute-done | bytes 65568 | tf_op jit(solution)/shard_map/ppermute | solution.py:653
  73.7 0.6 collective-permute-start.23
  74.3 0.0 collective-permute-done.19.rest_3_
  74.3 3.5 %collective-permute-start.22 = (bf16[4,2,128,128]{3,2,1,0:T(8,128)(2,1)S(1)}, bf16[4,2,128,128]{3,2,1,0:T(8,128)(2,1)S(1)}, u32[]{:S(2)}, u32[]{:S(2)}) collective-permute-start(bf16[4,2,128,128]{3,2,1,0:T(8,128)(2,1)S(1)} %add_convert_fusion.rest_0_), channel_id=1, source_target_pairs={{0,2},{2,0},{4,6},{6,4},{8,10},{10,8},{12,14},{14,12},{16,18},{18,... | collective-permute-start | bytes 786440 | tf_op jit(solution)/shard_map/ppermute | solution.py:653
  77.8 12.9 %trunk_attention.1 = (f32[4096,128]{1,0:T(8,128)}, f32[4,8,128]{2,1,0:T(8,128)}) custom-call(s32[1]{0:T(128)} %bitcast.where_ref, f32[8,11]{1,0:T(8,128)} %gain_ref.7, bf16[4096,128]{1,0:T(8,128)(2,1)} %bitcast.24, bf16[4096,128]{1,0:T(8,128)(2,1)} %bitcast.15, bf16[4096,128]{1,0:T(8,128)(2,1)} %bitcast.17, bf16[4096,128]{1,0:T(8,128)(2,1)} %bitcast.25, ...), custom_call_target="tpu_custom_call" | custom-call | flops 2550136832 | bytes 6291456 | tf_op jit(solution)/shard_map/trunk_attention/pallas_call | solution.py:421
  90.7 0.0 collective-permute-done.18.rest_2_
  90.8 0.7 copy-done.15
  91.4 0.1 copy-done.16
  91.5 8.5 %near_attention.1.near_hbm = bf16[4096,128]{1,0:T(8,128)(2,1)} custom-call(s32[1]{0:T(128)} %bitcast.where_ref, s32[1]{0:T(128)S(6)} %copy.14.fork_ref, bf16[8192,128]{1,0:T(8,128)(2,1)} %bitcast.22, bf16[2048,128]{1,0:T(8,128)(2,1)} %bitcast.29, bf16[2048,128]{1,0:T(8,128)(2,1)} %bitcast.32, bf16[1024,128]{1,0:T(8,128)(2,1)} %copy-done.8, ...), custom_call_target="tpu_custom_call" | custom-call | flops 2013265920 | bytes 6291456 | tf_op jit(solution)/shard_map/near_attention/pallas_call | solution.py:470
  100.1 0.0 collective-permute-done.24.rest_3_
  100.1 0.0 collective-permute-done.23.rest_2_
  100.1 0.0 collective-permute-done.22.rest_1_
  100.1 0.7 copy-done.4
  100.8 0.1 copy-done.5
  100.9 0.1 copy-done.6
  101.0 9.9 %branch_linear.1 = (f32[8192,128]{1,0:T(8,128)}, f32[8,8,128]{2,1,0:T(8,128)}) custom-call(s32[1]{0:T(128)} %bitcast.where_ref, s32[1]{0:T(128)S(6)} %copy.14.fork_ref, bf16[8192,128]{1,0:T(8,128)(2,1)} %bitcast.13, bf16[4096,128]{1,0:T(8,128)(2,1)} %near_attention.1.near_hbm, bf16[4096,128]{1,0:T(8,128)(2,1)} %far_attention.1.far_hbm, ...), custom_call_target="tpu_custom_call" | custom-call | flops 536870912 | bytes 8388608 | tf_op jit(solution)/shard_map/branch_linear/pallas_call | solution.py:532
  110.9 4.7 %all-reduce.1 = (f32[4,8,128]{2,1,0:T(8,128)}, f32[8,8,128]{2,1,0:T(8,128)}) all-reduce(f32[4,8,128]{2,1,0:T(8,128)S(1)} %copy-done.10, f32[8,8,128]{2,1,0:T(8,128)} %get-tuple-element.65), channel_id=1, replica_groups=mesh['seq'=16,'head'=2] {'head'}, use_global_device_ids=true, to_apply=%region_0.1 | all-reduce | flops 12288 | bytes 98304 | tf_op jit(solution)/shard_map/psum | solution.py:706
  115.5 5.4 %normalize.1 = (bf16[4096,128]{1,0:T(8,128)(2,1)}, bf16[8192,128]{1,0:T(8,128)(2,1)}) custom-call(f32[4096,128]{1,0:T(8,128)} %get-tuple-element.54.trunk_hbm, f32[4,8,128]{2,1,0:T(8,128)} %get-tuple-element.68.trunk_square, f32[8192,128]{1,0:T(8,128)} %get-tuple-element.64.branch_hbm, f32[8,8,128]{2,1,0:T(8,128)} %get-tuple-element.69.branch_square), custom_call_target="tpu_custom_call" | custom-call | flops 3145728 | bytes 9437184 | tf_op jit(solution)/shard_map/normalize/pallas_call | solution.py:600
  (43 shorter events, 0.2 us)
Async XLA Ops:
  0.6 0.7 collective-permute-start.8
  1.4 12.0 %collective-permute-start.9 = (bf16[1024,128]{1,0:T(8,128)(2,1)S(1)}, bf16[1024,128]{1,0:T(8,128)(2,1)S(1)}, u32[]{:S(2)}, u32[]{:S(2)}) collective-permute-start(bf16[1024,128]{1,0:T(8,128)(2,1)S(1)} %broadcast_select_fusion.1), channel_id=1, source_target_pairs={{24,8},{26,10},{28,12},{30,14},{25,9},{27,11},{29,13},{31,15}} | collective-permute-start | bytes 786440 | tf_op jit(solution)/shard_map/ppermute | solution.py:653
  6.6 7.6 %collective-permute-start.2 = (bf16[2,128,128]{2,1,0:T(8,128)(2,1)}, bf16[2,128,128]{2,1,0:T(8,128)(2,1)S(1)}, u32[]{:S(2)}, u32[]{:S(2)}) collective-permute-start(bf16[2,128,128]{2,1,0:T(8,128)(2,1)} %get-tuple-element.36), channel_id=1, source_target_pairs={{0,2},{2,0},{4,6},{6,4},{8,10},{10,8},{12,14},{14,12},{16,18},{18,... | collective-permute-start | bytes 196616 | tf_op jit(solution)/shard_map/ppermute | solution.py:653
  9.6 6.4 %collective-permute-start.3 = (bf16[2,128,128]{2,1,0:T(8,128)(2,1)}, bf16[2,128,128]{2,1,0:T(8,128)(2,1)S(1)}, u32[]{:S(2)}, u32[]{:S(2)}) collective-permute-start(bf16[2,128,128]{2,1,0:T(8,128)(2,1)} %get-tuple-element.37), channel_id=1, source_target_pairs={{0,4},{2,6},{4,0},{6,2},{8,12},{10,14},{12,8},{14,10},{16,20},{18,... | collective-permute-start | bytes 196616 | tf_op jit(solution)/shard_map/ppermute | solution.py:653
  12.0 29.5 %collective-permute-start.11 = (bf16[3,2,128,128]{3,2,1,0:T(8,128)(2,1)}, bf16[3,2,128,128]{3,2,1,0:T(8,128)(2,1)S(1)}, u32[]{:S(2)}, u32[]{:S(2)}) collective-permute-start(bf16[3,2,128,128]{3,2,1,0:T(8,128)(2,1)} %get-tuple-element.40.rest_6_), channel_id=1, source_target_pairs={{30,28},{31,29}} | collective-permute-start | bytes 589832 | tf_op jit(solution)/shard_map/ppermute | solution.py:653
  12.7 28.8 %collective-permute-start.12 = (bf16[3,2,128,128]{3,2,1,0:T(8,128)(2,1)}, bf16[3,2,128,128]{3,2,1,0:T(8,128)(2,1)S(1)}, u32[]{:S(2)}, u32[]{:S(2)}) collective-permute-start(bf16[3,2,128,128]{3,2,1,0:T(8,128)(2,1)} %get-tuple-element.41.rest_5_), channel_id=1, source_target_pairs={{30,26},{31,27}} | collective-permute-start | bytes 589832 | tf_op jit(solution)/shard_map/ppermute | solution.py:653
  13.4 28.7 %collective-permute-start.13 = (bf16[3,2,128,128]{3,2,1,0:T(8,128)(2,1)}, bf16[3,2,128,128]{3,2,1,0:T(8,128)(2,1)S(1)}, u32[]{:S(2)}, u32[]{:S(2)}) collective-permute-start(bf16[3,2,128,128]{3,2,1,0:T(8,128)(2,1)} %get-tuple-element.42.rest_4_), channel_id=1, source_target_pairs={{30,24},{31,25}} | collective-permute-start | bytes 589832 | tf_op jit(solution)/shard_map/ppermute | solution.py:653
  14.2 11.1 %collective-permute-start.4 = (bf16[2,128,128]{2,1,0:T(8,128)(2,1)}, bf16[2,128,128]{2,1,0:T(8,128)(2,1)S(1)}, u32[]{:S(2)}, u32[]{:S(2)}) collective-permute-start(bf16[2,128,128]{2,1,0:T(8,128)(2,1)} %get-tuple-element.38), channel_id=1, source_target_pairs={{0,6},{2,4},{4,2},{6,0},{8,14},{10,12},{12,10},{14,8},{16,22},{18,... | collective-permute-start | bytes 196616 | tf_op jit(solution)/shard_map/ppermute | solution.py:653
  16.0 26.3 %collective-permute-start.10 = (bf16[1024,128]{1,0:T(8,128)(2,1)S(1)}, bf16[1024,128]{1,0:T(8,128)(2,1)S(1)}, u32[]{:S(2)}, u32[]{:S(2)}) collective-permute-start(bf16[1024,128]{1,0:T(8,128)(2,1)S(1)} %broadcast_select_fusion.2), channel_id=1, source_target_pairs={{8,0},{10,2},{12,4},{14,6},{24,16},{26,18},{28,20},{30,22},{9,1},{... | collective-permute-start | bytes 786440 | tf_op jit(solution)/shard_map/ppermute | solution.py:653
  17.2 8.0 %copy-start = (bf16[2,128,128]{2,1,0:T(8,128)(2,1)S(1)}, bf16[2,128,128]{2,1,0:T(8,128)(2,1)}, u32[]{:S(2)}) copy-start(bf16[2,128,128]{2,1,0:T(8,128)(2,1)} %get-tuple-element.35.rest_0_) | copy-start | bytes 196612
  17.3 8.0 %copy-start.1 = (f32[8,11]{1,0:T(8,128)S(1)}, f32[8,11]{1,0:T(8,128)}, u32[]{:S(2)}) copy-start(f32[8,11]{1,0:T(8,128)} %gain_ref.7) | copy-start | bytes 1060
  17.3 24.9 %copy-start.9 = (bf16[3,2,128,128]{3,2,1,0:T(8,128)(2,1)S(1)}, bf16[3,2,128,128]{3,2,1,0:T(8,128)(2,1)}, u32[]{:S(2)}) copy-start(bf16[3,2,128,128]{3,2,1,0:T(8,128)(2,1)} %get-tuple-element.43.rest_7_) | copy-start | bytes 589828
  25.3 22.2 %copy-start.7 = (bf16[512,2,128]{2,1,0:T(2,128)(2,1)S(1)}, bf16[512,2,128]{2,1,0:T(2,128)(2,1)}, u32[]{:S(2)}) copy-start(bf16[512,2,128]{2,1,0:T(2,128)(2,1)} %param.16) | copy-start | bytes 786436
  25.3 23.5 %copy-start.11 = (bf16[512,2,128]{2,1,0:T(2,128)(2,1)S(1)}, bf16[512,2,128]{2,1,0:T(2,128)(2,1)}, u32[]{:S(2)}) copy-start(bf16[512,2,128]{2,1,0:T(2,128)(2,1)} %param.17) | copy-start | bytes 786436
  26.0 17.9 %collective-permute-start.7 = (bf16[2,128,128]{2,1,0:T(8,128)(2,1)S(1)}, bf16[2,128,128]{2,1,0:T(8,128)(2,1)S(1)}, u32[]{:S(2)}, u32[]{:S(2)}) collective-permute-start(bf16[2,128,128]{2,1,0:T(8,128)(2,1)S(1)} %get-tuple-element.44.rest_4_), channel_id=1, source_target_pairs={{0,24},{2,26},{4,28},{6,30},{8,16},{10,18},{12,20},{14,22},{16,8},... | collective-permute-start | bytes 196616 | tf_op jit(solution)/shard_map/ppermute | solution.py:653
  41.5 5.2 %collective-permute-start.6 = (bf16[2,128,128]{2,1,0:T(8,128)(2,1)S(1)}, bf16[2,128,128]{2,1,0:T(8,128)(2,1)S(1)}, u32[]{:S(2)}, u32[]{:S(2)}) collective-permute-start(bf16[2,128,128]{2,1,0:T(8,128)(2,1)S(1)} %get-tuple-element.44.rest_4_), channel_id=1, source_target_pairs={{0,16},{2,18},{4,20},{6,22},{8,24},{10,26},{12,28},{14,30},{16,0},... | collective-permute-start | bytes 196616 | tf_op jit(solution)/shard_map/ppermute | solution.py:653
  41.5 5.2 %collective-permute-start.5 = (bf16[2,128,128]{2,1,0:T(8,128)(2,1)S(1)}, bf16[2,128,128]{2,1,0:T(8,128)(2,1)S(1)}, u32[]{:S(2)}, u32[]{:S(2)}) collective-permute-start(bf16[2,128,128]{2,1,0:T(8,128)(2,1)S(1)} %get-tuple-element.44.rest_4_), channel_id=1, source_target_pairs={{0,8},{2,10},{4,12},{6,14},{8,0},{10,2},{12,4},{14,6},{16,24},{18,... | collective-permute-start | bytes 196616 | tf_op jit(solution)/shard_map/ppermute | solution.py:653
  42.3 48.4 %copy-start.8 = (bf16[1024,128]{1,0:T(8,128)(2,1)}, bf16[1024,128]{1,0:T(8,128)(2,1)S(1)}, u32[]{:S(2)}) copy-start(bf16[1024,128]{1,0:T(8,128)(2,1)S(1)} %broadcast_select_fusion.3.rest_0_) | copy-start | bytes 786436
  46.7 3.8 %collective-permute-start.20 = (bf16[4,2,128,128]{3,2,1,0:T(8,128)(2,1)S(1)}, bf16[4,2,128,128]{3,2,1,0:T(8,128)(2,1)S(1)}, u32[]{:S(2)}, u32[]{:S(2)}) collective-permute-start(bf16[4,2,128,128]{3,2,1,0:T(8,128)(2,1)S(1)} %add_convert_fusion.1), channel_id=1, source_target_pairs={{24,8},{26,10},{28,12},{30,14},{25,9},{27,11},{29,13},{31,15}} | collective-permute-start | bytes 786440 | tf_op jit(solution)/shard_map/ppermute | solution.py:653
  47.4 12.3 %collective-permute-start = (bf16[1024,128]{1,0:T(8,128)(2,1)S(1)}, bf16[1024,128]{1,0:T(8,128)(2,1)S(1)}, u32[]{:S(2)}, u32[]{:S(2)}) collective-permute-start(bf16[1024,128]{1,0:T(8,128)(2,1)S(1)} %bitcast.20), channel_id=1, source_target_pairs={{0,2},{2,4},{4,6},{6,8},{8,10},{10,12},{12,14},{14,16},{16,18},{18... | collective-permute-start | bytes 786440 | tf_op jit(solution)/shard_map/ppermute | solution.py:653
  48.8 12.3 %collective-permute-start.1 = (bf16[1024,128]{1,0:T(8,128)(2,1)S(1)}, bf16[1024,128]{1,0:T(8,128)(2,1)S(1)}, u32[]{:S(2)}, u32[]{:S(2)}) collective-permute-start(bf16[1024,128]{1,0:T(8,128)(2,1)S(1)} %bitcast.35), channel_id=1, source_target_pairs={{0,2},{2,4},{4,6},{6,8},{8,10},{10,12},{12,14},{14,16},{16,18},{18... | collective-permute-start | bytes 786440 | tf_op jit(solution)/shard_map/ppermute | solution.py:653
  50.6 13.9 %collective-permute-start.21 = (bf16[4,2,128,128]{3,2,1,0:T(8,128)(2,1)S(1)}, bf16[4,2,128,128]{3,2,1,0:T(8,128)(2,1)S(1)}, u32[]{:S(2)}, u32[]{:S(2)}) collective-permute-start(bf16[4,2,128,128]{3,2,1,0:T(8,128)(2,1)S(1)} %broadcast_select_fusion), channel_id=1, source_target_pairs={{8,0},{10,2},{12,4},{14,6},{24,16},{26,18},{28,20},{30,22},{9,1},{... | collective-permute-start | bytes 786440 | tf_op jit(solution)/shard_map/ppermute | solution.py:653
  52.7 13.8 %copy-start.2 = (bf16[2,128,128]{2,1,0:T(8,128)(2,1)}, bf16[2,128,128]{2,1,0:T(8,128)(2,1)S(1)}, u32[]{:S(2)}) copy-start(bf16[2,128,128]{2,1,0:T(8,128)(2,1)S(1)} %get-tuple-element.48.rest_0_) | copy-start | bytes 196612
  52.8 10.8 %collective-permute-start.14 = (bf16[2,128,128]{2,1,0:T(8,128)(2,1)S(1)}, bf16[2,128,128]{2,1,0:T(8,128)(2,1)S(1)}, u32[]{:S(2)}, u32[]{:S(2)}) collective-permute-start(bf16[2,128,128]{2,1,0:T(8,128)(2,1)S(1)} %get-tuple-element.49), channel_id=1, source_target_pairs={{0,2},{2,0},{4,6},{6,4},{8,10},{10,8},{12,14},{14,12},{16,18},{18,... | collective-permute-start | bytes 196616 | tf_op jit(solution)/shard_map/ppermute | solution.py:653
  55.6 18.7 %collective-permute-start.19 = (bf16[1024,128]{1,0:T(8,128)(2,1)S(1)}, bf16[1024,128]{1,0:T(8,128)(2,1)S(1)}, u32[]{:S(2)}, u32[]{:S(2)}) collective-permute-start(bf16[1024,128]{1,0:T(8,128)(2,1)S(1)} %broadcast_select_fusion.3.rest_0_), channel_id=1, source_target_pairs={{0,6},{2,4},{4,2},{6,0},{8,14},{10,12},{12,10},{14,8},{16,22},{18,... | collective-permute-start | bytes 786440 | tf_op jit(solution)/shard_map/ppermute | solution.py:653
  59.7 18.0 %copy-start.12 = (bf16[1024,128]{1,0:T(8,128)(2,1)}, bf16[1024,128]{1,0:T(8,128)(2,1)S(1)}, u32[]{:S(2)}) copy-start(bf16[1024,128]{1,0:T(8,128)(2,1)S(1)} %collective-permute-done.pk_ref) | copy-start | bytes 786436
  59.7 31.0 %collective-permute-start.18 = (bf16[1024,128]{1,0:T(8,128)(2,1)S(1)}, bf16[1024,128]{1,0:T(8,128)(2,1)S(1)}, u32[]{:S(2)}, u32[]{:S(2)}) collective-permute-start(bf16[1024,128]{1,0:T(8,128)(2,1)S(1)} %broadcast_select_fusion.3.rest_0_), channel_id=1, source_target_pairs={{0,4},{2,6},{4,0},{6,2},{8,12},{10,14},{12,8},{14,10},{16,20},{18,... | collective-permute-start | bytes 786440 | tf_op jit(solution)/shard_map/ppermute | solution.py:653
  61.1 16.7 %copy-start.13 = (bf16[1024,128]{1,0:T(8,128)(2,1)}, bf16[1024,128]{1,0:T(8,128)(2,1)S(1)}, u32[]{:S(2)}) copy-start(bf16[1024,128]{1,0:T(8,128)(2,1)S(1)} %collective-permute-done.1.pv_ref) | copy-start | bytes 786436
  61.1 29.6 %collective-permute-start.17 = (bf16[1024,128]{1,0:T(8,128)(2,1)S(1)}, bf16[1024,128]{1,0:T(8,128)(2,1)S(1)}, u32[]{:S(2)}, u32[]{:S(2)}) collective-permute-start(bf16[1024,128]{1,0:T(8,128)(2,1)S(1)} %broadcast_select_fusion.3.rest_0_), channel_id=1, source_target_pairs={{0,2},{2,0},{4,6},{6,4},{8,10},{10,8},{12,14},{14,12},{16,18},{18,... | collective-permute-start | bytes 786440 | tf_op jit(solution)/shard_map/ppermute | solution.py:653
  63.6 14.2 %copy-start.17 = (bf16[2,128,128]{2,1,0:T(8,128)(2,1)}, bf16[2,128,128]{2,1,0:T(8,128)(2,1)S(1)}, u32[]{:S(2)}) copy-start(bf16[2,128,128]{2,1,0:T(8,128)(2,1)S(1)} %collective-permute-done.14.rest_1_) | copy-start | bytes 196612
  63.6 7.4 %collective-permute-start.15 = (bf16[2,128,128]{2,1,0:T(8,128)(2,1)S(1)}, bf16[2,128,128]{2,1,0:T(8,128)(2,1)S(1)}, u32[]{:S(2)}, u32[]{:S(2)}) collective-permute-start(bf16[2,128,128]{2,1,0:T(8,128)(2,1)S(1)} %get-tuple-element.50), channel_id=1, source_target_pairs={{0,4},{2,6},{4,0},{6,2},{8,12},{10,14},{12,8},{14,10},{16,20},{18,... | collective-permute-start | bytes 196616 | tf_op jit(solution)/shard_map/ppermute | solution.py:653
  64.6 9.2 %collective-permute-start.16 = (bf16[2,128,128]{2,1,0:T(8,128)(2,1)S(1)}, bf16[2,128,128]{2,1,0:T(8,128)(2,1)S(1)}, u32[]{:S(2)}, u32[]{:S(2)}) collective-permute-start(bf16[2,128,128]{2,1,0:T(8,128)(2,1)S(1)} %get-tuple-element.51), channel_id=1, source_target_pairs={{0,6},{2,4},{4,2},{6,0},{8,14},{10,12},{12,10},{14,8},{16,22},{18,... | collective-permute-start | bytes 196616 | tf_op jit(solution)/shard_map/ppermute | solution.py:653
  66.6 24.1 %copy-start.3 = (bf16[4,2,128,128]{3,2,1,0:T(8,128)(2,1)}, bf16[4,2,128,128]{3,2,1,0:T(8,128)(2,1)S(1)}, u32[]{:S(2)}) copy-start(bf16[4,2,128,128]{3,2,1,0:T(8,128)(2,1)S(1)} %add_convert_fusion.rest_0_) | copy-start | bytes 786436
  71.0 6.8 %copy-start.18 = (bf16[2,128,128]{2,1,0:T(8,128)(2,1)}, bf16[2,128,128]{2,1,0:T(8,128)(2,1)S(1)}, u32[]{:S(2)}) copy-start(bf16[2,128,128]{2,1,0:T(8,128)(2,1)S(1)} %collective-permute-done.15.rest_2_) | copy-start | bytes 196612
  71.0 29.1 %collective-permute-start.24 = (bf16[4,2,128,128]{3,2,1,0:T(8,128)(2,1)S(1)}, bf16[4,2,128,128]{3,2,1,0:T(8,128)(2,1)S(1)}, u32[]{:S(2)}, u32[]{:S(2)}) collective-permute-start(bf16[4,2,128,128]{3,2,1,0:T(8,128)(2,1)S(1)} %add_convert_fusion.rest_0_), channel_id=1, source_target_pairs={{0,6},{2,4},{4,2},{6,0},{8,14},{10,12},{12,10},{14,8},{16,22},{18,... | collective-permute-start | bytes 786440 | tf_op jit(solution)/shard_map/ppermute | solution.py:653
  73.7 4.1 %copy-start.19 = (bf16[2,128,128]{2,1,0:T(8,128)(2,1)}, bf16[2,128,128]{2,1,0:T(8,128)(2,1)S(1)}, u32[]{:S(2)}) copy-start(bf16[2,128,128]{2,1,0:T(8,128)(2,1)S(1)} %collective-permute-done.16.rest_3_) | copy-start | bytes 196612
  73.7 26.4 %collective-permute-start.23 = (bf16[4,2,128,128]{3,2,1,0:T(8,128)(2,1)S(1)}, bf16[4,2,128,128]{3,2,1,0:T(8,128)(2,1)S(1)}, u32[]{:S(2)}, u32[]{:S(2)}) collective-permute-start(bf16[4,2,128,128]{3,2,1,0:T(8,128)(2,1)S(1)} %add_convert_fusion.rest_0_), channel_id=1, source_target_pairs={{0,4},{2,6},{4,0},{6,2},{8,12},{10,14},{12,8},{14,10},{16,20},{18,... | collective-permute-start | bytes 786440 | tf_op jit(solution)/shard_map/ppermute | solution.py:653
  74.3 16.4 %copy-start.14 = (bf16[1024,128]{1,0:T(8,128)(2,1)}, bf16[1024,128]{1,0:T(8,128)(2,1)S(1)}, u32[]{:S(2)}) copy-start(bf16[1024,128]{1,0:T(8,128)(2,1)S(1)} %collective-permute-done.19.rest_3_) | copy-start | bytes 786436
  74.3 25.8 %collective-permute-start.22 = (bf16[4,2,128,128]{3,2,1,0:T(8,128)(2,1)S(1)}, bf16[4,2,128,128]{3,2,1,0:T(8,128)(2,1)S(1)}, u32[]{:S(2)}, u32[]{:S(2)}) collective-permute-start(bf16[4,2,128,128]{3,2,1,0:T(8,128)(2,1)S(1)} %add_convert_fusion.rest_0_), channel_id=1, source_target_pairs={{0,2},{2,0},{4,6},{6,4},{8,10},{10,8},{12,14},{14,12},{16,18},{18,... | collective-permute-start | bytes 786440 | tf_op jit(solution)/shard_map/ppermute | solution.py:653
  90.7 0.7 copy-start.15
  90.7 0.8 copy-start.16
  100.1 0.7 copy-start.4
  100.1 0.8 copy-start.5
  100.1 0.8 copy-start.6
  101.0 9.9 %copy-start.10 = (f32[4,8,128]{2,1,0:T(8,128)S(1)}, f32[4,8,128]{2,1,0:T(8,128)}, u32[]{:S(2)}) copy-start(f32[4,8,128]{2,1,0:T(8,128)} %get-tuple-element.55) | copy-start | bytes 49156

commit v4 on v3

v4 whole, which is shorter than its diff:
```python
import functools
import math

import jax
import jax.numpy as jnp
from jax import lax
from jax.experimental import pallas as pl
from jax.experimental.pallas import tpu as pltpu
from jax.sharding import PartitionSpec as P

BLK = 128
WIN = 512
COLS = 4
MASKED = -1e30
F32 = jnp.float32
BF16 = jnp.bfloat16
VMEM_BYTES = 60 * 1024 * 1024
SMALL_BYTES = 28 * 1024 * 1024


def params(limit=VMEM_BYTES):
    return pltpu.CompilerParams(vmem_limit_bytes=limit)


def hbm():
    return pl.BlockSpec(memory_space=pltpu.HBM)


def vmem():
    return pl.BlockSpec(memory_space=pltpu.VMEM)


def block_copy(src, dst, sems, block, rows, src_block=None):
    src_block = block if src_block is None else src_block
    return pltpu.make_async_copy(
        src.at[pl.ds(src_block * rows, rows)], dst.at[pl.ds(block * rows, rows)], sems.at[block]
    )


def smem():
    return pl.BlockSpec(memory_space=pltpu.SMEM)


def gain_factor(level, width):
    return 1.0 / math.sqrt(width * BLK * 2 ** max(level - 1, 0))


def every(rows_ref, wide, count, each):
    return wide[pl.ds(each, rows_ref.shape[0] // count, stride=count), :].astype(BF16)


def state_kernel(depth, heads, where_ref, gain_ref, k_hbm, v_hbm, *rest):
    out_refs = rest[:COLS]
    local_ref, keys, values, kf, vf, levels, outs, key_sems, value_sems = rest[COLS:]
    rows, width = kf.shape
    each = heads // COLS
    column = where_ref[0] & (COLS - 1)
    copies = [
        (block_copy(k_hbm, keys, key_sems, b, rows), block_copy(v_hbm, values, value_sems, b, rows))
        for b in range(1 << depth)
    ]
    for pair in copies:
        for copy in pair:
            copy.start()
    for b, pair in enumerate(copies):
        for copy in pair:
            copy.wait()
        kf[...] = keys[b * rows : (b + 1) * rows].astype(F32)
        vf[...] = values[b * rows : (b + 1) * rows].astype(F32)
        for h in range(heads):
            k = kf[pl.ds(h, BLK, stride=heads), :].astype(BF16)
            v = vf[pl.ds(h, BLK, stride=heads), :].astype(BF16)
            merged = lax.dot_general(k, v, (((0,), (0,)), ((), ())), preferred_element_type=F32)
            before = None
            for bit in range(depth):
                if b >> bit & 1:
                    part = levels[bit, h] * (gain_ref[h, bit + 1] * gain_factor(bit + 1, width))
                    before = part if before is None else before + part
            carry = 0
            while b >> carry & 1:
                merged = merged + levels[carry, h]
                carry += 1
            if before is not None:
                before = before.astype(BF16)
                local_ref[b - 1, h] = before
                outs[column ^ (h // each), b, h % each] = before
            if carry < depth:
                levels[carry, h] = merged
            else:
                outs[column ^ (h // each), 0, h % each] = merged.astype(BF16)
    for d in range(COLS):
        out_refs[d][...] = outs[d]


def block_sums(where, gain, keys, values, heads, depth):
    blocks = 1 << depth
    rows, width = keys.shape[0] // blocks, keys.shape[1]
    quarter = (blocks, heads // COLS, width, width)
    return pl.pallas_call(
        functools.partial(state_kernel, depth, heads),
        in_specs=[smem(), smem(), hbm(), hbm()],
        out_specs=[vmem()] * (COLS + 1),
        out_shape=[jax.ShapeDtypeStruct(quarter, BF16)] * COLS
        + [jax.ShapeDtypeStruct((blocks - 1, heads, width, width), BF16)],
        scratch_shapes=[
            pltpu.VMEM(keys.shape, BF16),
            pltpu.VMEM(values.shape, BF16),
            pltpu.VMEM((rows, width), F32),
            pltpu.VMEM((rows, width), F32),
            pltpu.VMEM((depth, heads, width, width), F32),
            pltpu.VMEM((COLS, *quarter), BF16),
            pltpu.SemaphoreType.DMA((blocks,)),
            pltpu.SemaphoreType.DMA((blocks,)),
        ],
        compiler_params=params(),
        cost_estimate=pl.CostEstimate(
            flops=2 * keys.size * width, bytes_accessed=4 * keys.size + 2 * heads * width * width * blocks, transcendentals=0
        ),
        name="block_sums",
    )(where, gain, keys, values)


def in_plane(sums, column, weight):
    total = None
    for bit in range(COLS.bit_length() - 1):
        if column >> bit & 1:
            first = ((column >> bit) ^ 1) << bit
            part = functools.reduce(jnp.add, sums[first : first + (1 << bit)]) * weight(bit)
            total = part if total is None else total + part
    return total


def level_weight(gain_ref, head, depth, width, bit):
    return gain_ref[head, depth + bit + 1] * gain_factor(depth + bit + 1, width)


def in_order(where_ref, refs, held):
    for d, ref in enumerate(refs):
        held[(where_ref[0] & (COLS - 1)) ^ d] = ref[...]


def plane_kernel(depth, where_ref, gain_ref, *rest):
    part_refs, (plane_ref, ends_ref, sums_ref, held) = rest[:COLS], rest[COLS:]
    blocks, each, width = held.shape[1:4]
    first = (where_ref[0] & (COLS - 1)) * each
    in_order(where_ref, part_refs, held)
    for j in range(each):
        sums = [held[c, 0, j].astype(F32) for c in range(COLS)]
        plane_ref[j] = functools.reduce(jnp.add, sums).astype(BF16)
        before = in_plane(sums, COLS - 1, lambda bit: level_weight(gain_ref, first + j, depth, width, bit))
        ends_ref[0, j] = before.astype(BF16)
        for b in range(1, blocks):
            ends_ref[b, j] = (before + held[COLS - 1, b, j].astype(F32)).astype(BF16)
        for c in range(COLS):
            sums_ref[c, j] = held[c, 0, j]


def plane_sums(where, gain, parts, depth):
    blocks, *quarter = parts[0].shape
    return pl.pallas_call(
        functools.partial(plane_kernel, depth),
        in_specs=[smem(), smem()] + [vmem()] * COLS,
        out_specs=[vmem()] * 3,
        out_shape=[
            jax.ShapeDtypeStruct(tuple(quarter), BF16),
            jax.ShapeDtypeStruct((blocks, *quarter), BF16),
            jax.ShapeDtypeStruct((COLS, *quarter), BF16),
        ],
        scratch_shapes=[pltpu.VMEM((COLS, blocks, *quarter), BF16)],
        compiler_params=params(SMALL_BYTES),
        cost_estimate=pl.CostEstimate(flops=16 * parts[0].size, bytes_accessed=16 * parts[0].size, transcendentals=0),
        name="plane_sums",
    )(where, gain, *parts)


def cross_kernel(depth, planes, where_ref, gain_ref, *rest):
    held, plane_refs = rest[0], rest[1 : 1 + planes]
    out_refs, (top_ref, states, outs) = rest[1 + planes : 1 + COLS + planes], rest[1 + COLS + planes :]
    each, width = top_ref.shape[:2]
    col_bits = COLS.bit_length() - 1
    plane = where_ref[0] >> col_bits
    column = where_ref[0] & (COLS - 1)
    for d, ref in enumerate(plane_refs):
        states[plane ^ d] = ref[...]
    for j in range(each):
        head = column * each + j
        sums = [held[c, j].astype(F32) for c in range(COLS)]
        above = jnp.zeros((width, width), F32)
        top = jnp.zeros((width, width), F32)
        for s in range(planes - 1):
            state = states[s, j].astype(F32)
            share = jnp.float32(0.0)
            for bit in range(planes.bit_length() - 1):
                weight = level_weight(gain_ref, head, depth, width, col_bits + bit)
                inside = jnp.logical_and((plane >> bit) & 1 == 1, (plane >> bit) ^ 1 == s >> bit)
                share = share + jnp.where(inside, weight, 0.0)
                if ((planes - 1) >> bit) ^ 1 == s >> bit:
                    top = top + state * weight
            above = above + state * share
        top_ref[j] = top
        for c in range(COLS):
            before = in_plane(sums, c, lambda bit: level_weight(gain_ref, head, depth, width, bit))
            outs[column ^ c, j] = (above if before is None else above + before).astype(BF16)
    for d in range(COLS):
        out_refs[d][...] = outs[d]


def cross_sums(where, gain, sums, planes, depth):
    quarter = sums.shape[1:]
    return pl.pallas_call(
        functools.partial(cross_kernel, depth, len(planes)),
        in_specs=[smem(), smem()] + [vmem()] * (1 + len(planes)),
        out_specs=[vmem()] * (COLS + 1),
        out_shape=[jax.ShapeDtypeStruct(quarter, BF16)] * COLS + [jax.ShapeDtypeStruct(quarter, F32)],
        scratch_shapes=[
            pltpu.VMEM((len(planes), *quarter), BF16),
            pltpu.VMEM((COLS, *quarter), BF16),
        ],
        compiler_params=params(SMALL_BYTES),
        cost_estimate=pl.CostEstimate(flops=15 * sums.size, bytes_accessed=8 * sums.size, transcendentals=0),
        name="cross_sums",
    )(where, gain, sums, *planes)


def place(src_ref, wide, dst, start, groups):
    tokens = src_ref.shape[0] // groups
    wide[...] = src_ref[...].astype(F32)
    for g in range(groups):
        part = wide[pl.ds(g, tokens, stride=groups), :].astype(BF16)
        dst[g, pl.ds(start, tokens), : src_ref.shape[1]] = part


def split_groups(wide):
    rows, width = wide.shape
    pairs = wide.reshape(rows // 16, 16, width)
    low, high = pairs[:, :8], pairs[:, 8:]
    upper = lax.broadcasted_iota(jnp.int32, low.shape, 1) < 4
    first = jnp.where(upper, low, pltpu.roll(high, 4, 1))
    second = jnp.where(upper, pltpu.roll(low, 4, 1), high)
    return [part.reshape(rows // 2, width) for part in (first, second)]


def join_groups(first, second):
    rows, width = first.shape
    first, second = (part.reshape(rows // 8, 8, width) for part in (first, second))
    upper = lax.broadcasted_iota(jnp.int32, first.shape, 1) < 4
    low = jnp.where(upper, first, pltpu.roll(second, 4, 1))
    high = jnp.where(upper, pltpu.roll(first, 4, 1), second)
    return jnp.concatenate([low, high], axis=1).reshape(2 * rows, width)


def window_logits(queries, keys, token, share, bias):
    rows = queries.shape[0]
    logits = lax.dot_general(queries, keys, (((1,), (1,)), ((), ())), preferred_element_type=F32)
    row = token + lax.broadcasted_iota(jnp.int32, (rows, BLK), 0) // share
    col = lax.broadcasted_iota(jnp.int32, (rows, BLK), 1)
    late = col > row
    first = jnp.where(late, logits[:, :BLK], MASKED)
    last = jnp.where(late, MASKED, logits[:, -BLK:])
    logits = jnp.concatenate([first, logits[:, BLK:-BLK], last], axis=1)
    return logits if bias is None else logits + bias


def window_outputs(logits, values, width):
    top = jnp.max(logits, axis=1, keepdims=True)
    weights = jnp.exp2((logits - top) * (math.log2(math.e) / math.sqrt(width))).astype(BF16)
    both = jnp.dot(weights, values, preferred_element_type=F32)
    return both[:, :width] / both[:, width:]


def window_block(q_ref, kh, vh, base, groups, bias=None):
    width = q_ref.shape[1]
    span = WIN + BLK
    share = q_ref.shape[0] // BLK // groups
    parts = [part.astype(BF16) for part in split_groups(q_ref[...].astype(F32))]
    chunks = [(g, c) for g in range(groups) for c in range(0, BLK * share, BLK)]

    def logits_of(chunk):
        g, c = chunk
        return window_logits(parts[g][c : c + BLK], kh[g, pl.ds(base, span), :], c // share, share, bias)

    outs = []
    ahead = logits_of(chunks[0])
    for i, (g, c) in enumerate(chunks):
        now = ahead
        if i + 1 < len(chunks):
            ahead = logits_of(chunks[i + 1])
        outs.append(window_outputs(now, vh[g, pl.ds(base, span), :], width))
    half = len(outs) // 2
    return join_groups(jnp.concatenate(outs[:half], axis=0), jnp.concatenate(outs[half:], axis=0))


def square_sums(full, heads):
    tokens = full.shape[0] // heads
    row = lax.broadcasted_iota(jnp.int32, (tokens, full.shape[0]), 1) // heads
    mine = row == lax.broadcasted_iota(jnp.int32, (tokens, full.shape[0]), 0)
    sums = jnp.dot(mine.astype(BF16), (full * full).astype(BF16), preferred_element_type=F32)
    ones = jnp.ones((8, full.shape[1]), F32)
    return lax.dot_general(
        ones, sums, (((1,), (1,)), ((), ())), precision=lax.Precision.HIGHEST, preferred_element_type=F32
    )


def far_kernel(heads, groups, q_ref, pk_ref, pv_ref, ck_ref, cv_ref, out_ref, kf, kh, vh):
    step = pl.program_id(0)
    width = q_ref.shape[1]

    @pl.when(step == 0)
    def _():
        vh[:, :, width:] = jnp.ones((groups, vh.shape[1], width), BF16)
        place(pk_ref, kf, kh, 0, groups)
        place(ck_ref, kf, kh, WIN, groups)
        place(pv_ref, kf, vh, 0, groups)
        place(cv_ref, kf, vh, WIN, groups)

    out_ref[...] = window_block(q_ref, kh, vh, pl.multiple_of(step * BLK, BLK), groups).astype(BF16)


def attention_cost(tokens, heads, width, extra=0):
    span = WIN + BLK
    return pl.CostEstimate(
        flops=6 * tokens * heads * span * width + extra,
        bytes_accessed=12 * tokens * heads * width,
        transcendentals=tokens * heads * span,
    )


def far_attention(queries, keys, values, heads, groups):
    width = queries.shape[1]
    steps = queries.shape[0] // (BLK * heads) - WIN // BLK
    skip = WIN // BLK
    at_first = pl.BlockSpec((WIN * groups, width), lambda i: (0, 0))
    at_next = pl.BlockSpec((WIN * groups, width), lambda i: (1, 0))
    return pl.pallas_call(
        functools.partial(far_kernel, heads, groups),
        grid=(steps,),
        in_specs=[
            pl.BlockSpec((BLK * heads, width), lambda i: (i + skip, 0)),
            at_first,
            at_first,
            at_next,
            at_next,
        ],
        out_specs=pl.BlockSpec((BLK * heads, width), lambda i: (i, 0)),
        out_shape=jax.ShapeDtypeStruct((steps * BLK * heads, width), BF16),
        scratch_shapes=[
            pltpu.VMEM((WIN * groups, width), F32),
            pltpu.VMEM((groups, 2 * WIN, width), BF16),
            pltpu.VMEM((groups, 2 * WIN, 2 * width), BF16),
        ],
        compiler_params=params(),
        cost_estimate=attention_cost(steps * BLK, heads, width),
        name="far_attention",
    )(queries, keys, values, keys, values)


def trunk_kernel(heads, groups, first, where_ref, gain_ref, q_ref, k_ref, v_ref, wq_ref, pk_ref, pv_ref, ck_ref, cv_ref, local_ref, out_ref, nf, tf, sf, kf, kh, vh, of):
    block = pl.program_id(0) + first
    width = q_ref.shape[1]

    @pl.when(pl.program_id(0) == 0)
    def _():
        vh[:, :, width:] = jnp.ones((groups, vh.shape[1], width), BF16)
        place(pk_ref, kf, kh, 0, groups)
        place(ck_ref, kf, kh, WIN, groups)
        place(pv_ref, kf, vh, 0, groups)
        place(cv_ref, kf, vh, WIN, groups)

    nf[...] = q_ref[...].astype(F32)
    tf[...] = k_ref[...].astype(F32)
    sf[...] = v_ref[...].astype(F32)
    base = pl.multiple_of(block * BLK, BLK)
    reach = jnp.where(where_ref[0] == 0, WIN - block * BLK, 0)
    bias = jnp.where(lax.broadcasted_iota(jnp.int32, (1, WIN + BLK), 1) < reach, MASKED, 0.0).astype(F32)
    row = lax.broadcasted_iota(jnp.int32, (BLK, BLK), 0)
    col = lax.broadcasted_iota(jnp.int32, (BLK, BLK), 1)
    inner = (block > 0).astype(F32).astype(BF16)
    q = [every(q_ref, nf, heads, h) for h in range(heads)]
    inside = [
        lax.dot_general(q[h], every(k_ref, tf, heads, h), (((1,), (1,)), ((), ())), preferred_element_type=F32)
        for h in range(heads)
    ]
    for h in range(heads):
        weight = jnp.where(col <= row, inside[h], 0.0) * (gain_ref[h, 0] * gain_factor(0, width))
        left = jnp.concatenate([weight.astype(BF16), q[h]], axis=1)
        right = jnp.concatenate([every(v_ref, sf, heads, h), local_ref[0, h] * inner], axis=0)
        of[pl.ds(h, BLK, stride=heads), :] = jnp.dot(left, right, preferred_element_type=F32)
    out_ref[...] = window_block(wq_ref, kh, vh, base, groups, bias) + of[...]


def trunk_attention(where, gain, q, k, v, wq, pk, pv, ck, cv, local, heads, groups, first, steps):
    width = q.shape[1]
    rows = BLK * heads
    at_block = pl.BlockSpec((rows, width), lambda i: (i + first, 0))
    whole = pl.BlockSpec((WIN * groups, width), lambda i: (0, 0))
    before = pl.BlockSpec((1, heads, width, width), lambda i: (jnp.maximum(i + first - 1, 0), 0, 0, 0))
    wide = pltpu.VMEM((rows, width), F32)
    return pl.pallas_call(
        functools.partial(trunk_kernel, heads, groups, first),
        grid=(steps,),
        in_specs=[smem(), smem()] + [at_block] * 4 + [whole] * 4 + [before],
        out_specs=pl.BlockSpec((rows, width), lambda i: (i, 0)),
        out_shape=jax.ShapeDtypeStruct((steps * rows, width), F32),
        scratch_shapes=[
            wide,
            wide,
            wide,
            pltpu.VMEM((WIN * groups, width), F32),
            pltpu.VMEM((groups, 2 * WIN, width), BF16),
            pltpu.VMEM((groups, 2 * WIN, 2 * width), BF16),
            wide,
        ],
        compiler_params=params(),
        cost_estimate=attention_cost(steps * BLK, heads, width, 2 * steps * BLK * BLK * heads * 3 * width),
        name=f"trunk_attention_{first}",
    )(where, gain, q, k, v, wq, pk, pv, ck, cv, local)


def near_kernel(groups, where_ref, fork_ref, q_ref, ck_ref, cv_ref, *rest):
    kv_refs, out_ref = rest[:COLS], rest[COLS]
    kf, kh, vh, kt = rest[COLS + 1 :]
    step = pl.program_id(0)
    width = q_ref.shape[1]
    column = where_ref[0] & (COLS - 1)
    start = pl.multiple_of(fork_ref[0] * BLK, BLK)

    @pl.when(step == 0)
    def _():
        for i in range(COLS):
            kt[column ^ i] = kv_refs[i][...]
        vh[:, :, width:] = jnp.ones((groups, vh.shape[1], width), BF16)
        place(kt.at[0], kf, vh, 0, groups)
        place(kt.at[1], kf, vh, WIN, groups)
        place(kt.at[2], kf, kh, 0, groups)
        place(kt.at[3], kf, kh, WIN, groups)
        place(ck_ref, kf, kh, pl.multiple_of(start + WIN, BLK), groups)
        place(cv_ref, kf, vh, pl.multiple_of(start + WIN, BLK), groups)

    base = pl.multiple_of(start + step * BLK, BLK)
    out_ref[...] = window_block(q_ref, kh, vh, base, groups).astype(BF16)


def near_attention(where, fork, wq, ck, cv, kvs, heads, groups):
    width = wq.shape[1]
    steps = WIN // BLK
    at_block = pl.BlockSpec((BLK * heads, width), lambda i: (i, 0))
    whole = pl.BlockSpec((WIN * groups, width), lambda i: (0, 0))
    return pl.pallas_call(
        functools.partial(near_kernel, groups),
        grid=(steps,),
        in_specs=[smem(), smem(), at_block, whole, whole] + [whole] * COLS,
        out_specs=at_block,
        out_shape=jax.ShapeDtypeStruct((steps * BLK * heads, width), BF16),
        scratch_shapes=[
            pltpu.VMEM((WIN * groups, width), F32),
            pltpu.VMEM((groups, 3 * WIN, width), BF16),
            pltpu.VMEM((groups, 3 * WIN, 2 * width), BF16),
            pltpu.VMEM((COLS, WIN * groups, width), BF16),
        ],
        compiler_params=params(),
        cost_estimate=attention_cost(steps * BLK, heads, width),
        name="near_attention",
    )(where, fork, wq, ck, cv, *kvs)


def final_kernel(heads, parts, where_ref, fork_ref, bq_hbm, tq_hbm, *rest):
    window_hbms, trunk_hbms = rest[:2], rest[2 : 2 + parts]
    end_hbms, cross_hbms = rest[2 + parts : 2 + parts + COLS], rest[2 + parts + COLS : 2 + parts + 2 * COLS]
    branch_full, trunk_full, square_ref, qs, ws, ts, nf, of, fs, es, cs = rest[2 + parts + 2 * COLS :][:11]
    q_sems, w_sems, f_sems, e_sems, c_sems = rest[2 + parts + 2 * COLS :][11:]
    rows = BLK * heads
    branch_blocks, trunk_blocks = ws.shape[0] // rows, ts.shape[0] // rows
    each = heads // COLS
    column = where_ref[0] & (COLS - 1)
    states = [
        pltpu.make_async_copy(end_hbms[i].at[fork_ref[0]], es.at[column ^ i], e_sems.at[i]) for i in range(COLS)
    ] + [pltpu.make_async_copy(cross_hbms[i], cs.at[column ^ i], c_sems.at[i]) for i in range(COLS)]

    def query_copy(src, b, slot):
        return pltpu.make_async_copy(src.at[pl.ds(b * rows, rows)], qs.at[pl.ds(slot * rows, rows)], q_sems.at[slot])

    def other_copy(src, b, dst, place_of, slot):
        return pltpu.make_async_copy(
            src.at[pl.ds(b * rows, rows)], dst.at[pl.ds(place_of * rows, rows)], w_sems.at[slot]
        )

    def result_copy(b, dst, slot):
        return pltpu.make_async_copy(fs.at[pl.ds(slot * rows, rows)], dst.at[pl.ds(b * rows, rows)], f_sems.at[slot])

    for copy in states:
        copy.start()
    per_window = branch_blocks // 2
    per_trunk = trunk_blocks // parts
    for b in range(branch_blocks):
        query_copy(bq_hbm, b, b).start()
        other_copy(window_hbms[b // per_window], b % per_window, ws, b, b).start()
    for b in range(trunk_blocks):
        query_copy(tq_hbm, b, branch_blocks + b).start()
        other_copy(trunk_hbms[b // per_trunk], b % per_trunk, ts, b, branch_blocks + b).start()
    for copy in states:
        copy.wait()

    def rest_of(slot, window, states_ref):
        at = pl.ds(pl.multiple_of(slot * rows, rows), rows)
        nf[...] = qs[at, :].astype(F32)
        for h in range(heads):
            q = nf[pl.ds(h, BLK, stride=heads), :].astype(BF16)
            of[pl.ds(h, BLK, stride=heads), :] = jnp.dot(
                q, states_ref[h // each, h % each], preferred_element_type=F32
            )
        full = window.astype(F32) + of[...]
        fs[at, :] = full
        square_ref[slot] = square_sums(full, heads)

    def branch_block(b, carry):
        query_copy(bq_hbm, b, b).wait()
        other_copy(window_hbms[0], 0, ws, b, b).wait()
        rest_of(b, ws[pl.ds(pl.multiple_of(b * rows, rows), rows), :], es)
        result_copy(b, branch_full, b).start()
        return carry

    def trunk_block(b, carry):
        slot = branch_blocks + b
        query_copy(tq_hbm, b, slot).wait()
        other_copy(trunk_hbms[0], 0, ts, b, slot).wait()
        rest_of(slot, ts[pl.ds(pl.multiple_of(b * rows, rows), rows), :], cs)
        result_copy(b, trunk_full, slot).start()
        return carry

    lax.fori_loop(0, branch_blocks, branch_block, 0)
    lax.fori_loop(0, trunk_blocks, trunk_block, 0)
    for b in range(branch_blocks):
        result_copy(b, branch_full, b).wait()
    for b in range(trunk_blocks):
        result_copy(b, trunk_full, branch_blocks + b).wait()


def final_linear(where, fork, bq, tq, windows, trunks, ends, cross, heads):
    width = bq.shape[1]
    rows = BLK * heads
    total = bq.shape[0] + tq.shape[0]
    blocks = total // rows
    wide = pltpu.VMEM((rows, width), F32)
    quarter = cross[0].shape
    return pl.pallas_call(
        functools.partial(final_kernel, heads, len(trunks)),
        in_specs=[smem(), smem()] + [hbm()] * (4 + len(trunks) + 2 * COLS),
        out_specs=[hbm(), hbm(), vmem()],
        out_shape=[
            jax.ShapeDtypeStruct(bq.shape, F32),
            jax.ShapeDtypeStruct(tq.shape, F32),
            jax.ShapeDtypeStruct((blocks, 8, BLK), F32),
        ],
        scratch_shapes=[
            pltpu.VMEM((total, width), BF16),
            pltpu.VMEM(bq.shape, BF16),
            pltpu.VMEM(tq.shape, F32),
            wide,
            wide,
            pltpu.VMEM((total, width), F32),
            pltpu.VMEM((COLS, *quarter), BF16),
            pltpu.VMEM((COLS, *quarter), BF16),
            pltpu.SemaphoreType.DMA((blocks,)),
            pltpu.SemaphoreType.DMA((blocks,)),
            pltpu.SemaphoreType.DMA((blocks,)),
            pltpu.SemaphoreType.DMA((COLS,)),
            pltpu.SemaphoreType.DMA((COLS,)),
        ],
        compiler_params=params(),
        cost_estimate=pl.CostEstimate(flops=4 * total * width * width, bytes_accessed=8 * total * width, transcendentals=0),
        name="final_linear",
    )(where, fork, bq, tq, *windows, *trunks, *ends, *cross)


def norm_kernel(heads, features, trunk_hbm, branch_hbm, square_ref, other_ref, trunk_out, branch_out, held, done, in_sems, out_sems):
    rows = BLK * heads
    width = held.shape[1]
    trunk_blocks = trunk_hbm.shape[0] // rows
    branch_blocks = branch_hbm.shape[0] // rows

    def arrive(src, block, slot):
        return pltpu.make_async_copy(
            src.at[pl.ds(block * rows, rows)], held.at[pl.ds(slot * rows, rows)], in_sems.at[slot]
        )

    def leave(dst, block, slot):
        return pltpu.make_async_copy(
            done.at[pl.ds(slot * rows, rows)], dst.at[pl.ds(block * rows, rows)], out_sems.at[slot]
        )

    parts = ((branch_hbm, branch_out, 0, branch_blocks), (trunk_hbm, trunk_out, branch_blocks, trunk_blocks))
    for src, _, first, blocks in parts:
        for b in range(blocks):
            arrive(src, b, first + b).start()
    for src, dst, first, blocks in parts:

        def one_block(b, carry):
            slot = first + b
            arrive(src, b, slot).wait()
            at = pl.ds(pl.multiple_of(slot * rows, rows), rows)
            square = square_ref[slot, 0:1, :] + other_ref[slot, 0:1, :]
            scale = lax.rsqrt(square / features + 1e-06)
            scale = jnp.broadcast_to(scale, (width, BLK)).T
            full = held[at, :].reshape(BLK, heads, width)
            done[at, :] = (full * scale[:, None, :]).astype(BF16).reshape(rows, width)
            leave(dst, b, slot).start()
            return carry

        lax.fori_loop(0, blocks, one_block, 0)
    for _, dst, first, blocks in parts:
        for b in range(blocks):
            leave(dst, b, first + b).wait()


def normalize(trunk, branch, square, other, heads, features):
    total = trunk.shape[0] + branch.shape[0]
    slots = total // (BLK * heads)
    return pl.pallas_call(
        functools.partial(norm_kernel, heads, features),
        in_specs=[hbm(), hbm(), vmem(), vmem()],
        out_specs=[hbm(), hbm()],
        out_shape=[jax.ShapeDtypeStruct(trunk.shape, BF16), jax.ShapeDtypeStruct(branch.shape, BF16)],
        scratch_shapes=[
            pltpu.VMEM((total, trunk.shape[1]), F32),
            pltpu.VMEM((total, trunk.shape[1]), BF16),
            pltpu.SemaphoreType.DMA((slots,)),
            pltpu.SemaphoreType.DMA((slots,)),
        ],
        compiler_params=params(),
        cost_estimate=pl.CostEstimate(
            flops=2 * (trunk.size + branch.size), bytes_accessed=6 * (trunk.size + branch.size), transcendentals=0
        ),
        name="normalize",
    )(trunk, branch, square, other)


def shards(
    trunk_query,
    trunk_key,
    trunk_value,
    trunk_wquery,
    trunk_wkey,
    trunk_wvalue,
    branch_query,
    branch_wquery,
    branch_wkey,
    branch_wvalue,
    level_gain,
    fork_block,
):
    tokens, heads, width = trunk_query.shape
    groups = trunk_wkey.shape[1]
    depth = (tokens // BLK).bit_length() - 1
    count = lax.axis_size("seq")
    planes = count // COLS
    features = heads * lax.axis_size("head") * width
    me = lax.axis_index("seq")
    column, plane = me % COLS, me // COLS
    where = me.astype(jnp.int32).reshape(1)
    root = count - 1
    top = planes - 1

    def flat(x):
        return x.reshape(x.shape[0] * x.shape[1], x.shape[2])

    tq, tk, tv, twq = flat(trunk_query), flat(trunk_key), flat(trunk_value), flat(trunk_wquery)
    twk, twv = flat(trunk_wkey), flat(trunk_wvalue)
    bq, bwq, bwk, bwv = flat(branch_query), flat(branch_wquery), flat(branch_wkey), flat(branch_wvalue)

    def send(x, pairs):
        return lax.ppermute(x, "seq", pairs)

    def down_step(x, step):
        starts = [p for p in range(planes) if (top - p) % (2 * step) == 0 and p >= step]
        pairs = [(p * COLS + c, (p - step) * COLS + c) for p in starts for c in range(COLS)]
        got = send(x, pairs)
        hit = functools.reduce(jnp.logical_or, [plane == p - step for p in starts])
        return jnp.where(hit, got, x)

    def down_first(x):
        return down_step(x, planes // 2)

    def down_rest(x):
        step = planes // 4
        while step:
            x = down_step(x, step)
            step //= 2
        return x

    def around(x):
        return [x] + [send(x, [(i, i ^ d) for i in range(count)]) for d in range(1, COLS)]

    def along(x):
        return [x] + [send(x, [(i, i ^ (d * COLS)) for i in range(count)]) for d in range(1, planes)]

    def swap(parts):
        return [parts[0]] + [send(parts[d], [(i, i ^ d) for i in range(count)]) for d in range(1, COLS)]

    tie = lax.optimization_barrier

    half = COLS // 2
    got = send(twv, [(root - i, root - i - half) for i in range(half)])
    shift = [(i, i + 1) for i in range(count - 1)]
    pk, pv = send(twk, shift), send(twv, shift)
    *parts, local = block_sums(where, level_gain, tk, tv, heads, depth)

    bwq, parts, got = tie((bwq, parts, got))
    kv = jnp.where(column >= half, twk, got)
    far = far_attention(bwq, bwk, bwv, heads, groups)
    parts = swap(parts)
    kv = down_first(kv)
    parts, kv, far, pk, pv = tie((parts, kv, far, pk, pv))
    plane_sum, ends, sums = plane_sums(where, level_gain, parts, depth)

    blocks = tokens // BLK
    first = blocks // 2

    def trunk_part(start, steps):
        return trunk_attention(
            where, level_gain, tq, tk, tv, twq, pk, pv, twk, twv, local, heads, groups, start, steps
        )

    twq, plane_sum, ends = tie((twq, plane_sum, ends))
    trunk_a = trunk_part(0, first)
    plane_list = along(plane_sum)
    kv = down_rest(kv)
    ends = down_first(ends)
    plane_list, kv, ends, trunk_a, twq = tie((plane_list, kv, ends, trunk_a, twq))
    *cross, above = cross_sums(where, level_gain, sums, plane_list, depth)

    twq, cross = tie((twq, cross))
    trunk_b = trunk_part(first, blocks - first)
    kvs = around(kv)
    ends = down_rest(ends)
    kvs, ends, trunk_b, bwq = tie((kvs, ends, trunk_b, bwq))
    ends = (ends.astype(F32) + above).astype(BF16)

    bwq, ends = tie((bwq, ends))
    near = near_attention(where, fork_block, bwq, bwk, bwv, kvs, heads, groups)
    ends = around(ends)
    cross = swap(cross)
    branch_full, trunk_full, square = final_linear(
        where, fork_block, bq, tq, (near, far), (trunk_a, trunk_b), ends, cross, heads
    )
    other = lax.ppermute(square, "head", [(0, 1), (1, 0)])
    trunk_out, branch_out = normalize(trunk_full, branch_full, square, other, heads, features)
    return trunk_out.reshape(trunk_query.shape), branch_out.reshape(branch_query.shape)


def solution(mesh):
    rows = P("seq", "head", None)
    return jax.shard_map(
        shards,
        mesh=mesh,
        in_specs=(rows,) * 10 + (P("head", None), P("seq")),
        out_specs=(rows, rows),
        check_vma=False,
    )
```

time: 122 us -> 123 us (level)
  the two profiles are of different devices: /device:TPU:0 before, /device:TPU:29 now
where the time goes in v4:
time: 123 us
  Pallas kernels  53.8 us (44%)
  starting transfers between devices  39.3 us (32%)
  waiting for transfers between devices  25.6 us (21%)
  local copies, waits for them, and re-layouts  2.13 us (2%)
  between operations  1.89 us (2%)
    ppermute x22, starting transfers between devices, send(): return lax.ppermute(x, 'seq', pairs)  37.3 us
    ppermute x22, waiting for transfers between devices, send(): return lax.ppermute(x, 'seq', pairs)  24.5 us
    pallas_call x1, Pallas kernels, final_linear(): pl.pallas_call(functools.partial(final_kernel, heads, len(trunks)), in_sp...  13.1 us
    pallas_call x2, Pallas kernels, trunk_attention(): pl.pallas_call(functools.partial(trunk_kernel, heads, groups, first), gri...  13 us
    pallas_call x1, Pallas kernels, near_attention(): pl.pallas_call(functools.partial(near_kernel, groups), grid=(steps,), in_...  8.25 us
    pallas_call x1, Pallas kernels, far_attention(): pl.pallas_call(functools.partial(far_kernel, heads, groups), grid=(steps,...  7.89 us
    pallas_call x1, Pallas kernels, normalize(): pl.pallas_call(functools.partial(norm_kernel, heads, features), in_specs=...  5.41 us
    pallas_call x1, Pallas kernels, block_sums(): pl.pallas_call(functools.partial(state_kernel, depth, heads), in_specs=[s...  4.6 us
  transfers between devices with their start and end apart: 23, of which 9 were waited for; matrix products, arithmetic and copies ran while one was open for 0% of the time, Pallas kernels for 28%

profile of v4, /device:TPU:29, one launch (start us, length us, event | category | flops | bytes accessed | tf_op | source)
XLA Modules:
  0.0 122.9 jit_solution(13789154279395825395)
XLA Ops:
  0.6 0.0 copy-start.5
  0.6 0.0 copy-start.4
  0.7 2.3 %collective-permute-start = (bf16[1024,128]{1,0:T(8,128)(2,1)}, bf16[1024,128]{1,0:T(8,128)(2,1)S(1)}, u32[]{:S(2)}, u32[]{:S(2)}) collective-permute-start(bf16[1024,128]{1,0:T(8,128)(2,1)} %bitcast.29), channel_id=1, source_target_pairs={{30,26},{28,24},{31,27},{29,25}} | collective-permute-start | bytes 786440 | tf_op jit(solution)/shard_map/ppermute | solution.py:671
  3.0 4.6 %block_sums.1 = (bf16[4,2,128,128]{3,2,1,0:T(8,128)(2,1)}, bf16[4,2,128,128]{3,2,1,0:T(8,128)(2,1)}, bf16[4,2,128,128]{3,2,1,0:T(8,128)(2,1)}, bf16[4,2,128,128]{3,2,1,0:T(8,128)(2,1)}, bf16[3,8,128,128]{3,2,1,0:T(8,128)(2,1)}) custom-call(s32[1]{0:T(128)} %bitcast.where_ref, f32[8,11]{1,0:T(8,128)} %gain_ref.9, bf16[4096,128]{1,0:T(8,128)(2,1)} %bitcast.13, ...), custom_call_target="tpu_custom_call" | custom-call | flops 134217728 | bytes 3145728 | tf_op jit(solution)/shard_map/block_sums/pallas_call | solution.py:99
  7.6 0.6 collective-permute-done
  8.2 1.3 %collective-permute-start.4 = (bf16[1024,128]{1,0:T(8,128)(2,1)S(1)}, bf16[1024,128]{1,0:T(8,128)(2,1)S(1)}, u32[]{:S(2)}, u32[]{:S(2)}) collective-permute-start(bf16[1024,128]{1,0:T(8,128)(2,1)S(1)} %broadcast_select_fusion.3), channel_id=1, source_target_pairs={{24,8},{26,10},{28,12},{30,14},{25,9},{27,11},{29,13},{31,15}} | collective-permute-start | bytes 786440 | tf_op jit(solution)/shard_map/ppermute | solution.py:671
  9.5 3.1 %collective-permute-start.5 = (bf16[1024,128]{1,0:T(8,128)(2,1)S(1)}, bf16[1024,128]{1,0:T(8,128)(2,1)S(1)}, u32[]{:S(2)}, u32[]{:S(2)}) collective-permute-start(bf16[1024,128]{1,0:T(8,128)(2,1)S(1)} %bitcast.27), channel_id=1, source_target_pairs={{0,2},{2,4},{4,6},{6,8},{8,10},{10,12},{12,14},{14,16},{16,18},{18... | collective-permute-start | bytes 786440 | tf_op jit(solution)/shard_map/ppermute | solution.py:671
  12.7 1.9 %collective-permute-start.6 = (bf16[1024,128]{1,0:T(8,128)(2,1)S(1)}, bf16[1024,128]{1,0:T(8,128)(2,1)S(1)}, u32[]{:S(2)}, u32[]{:S(2)}) collective-permute-start(bf16[1024,128]{1,0:T(8,128)(2,1)S(1)} %bitcast.32), channel_id=1, source_target_pairs={{0,2},{2,4},{4,6},{6,8},{8,10},{10,12},{12,14},{14,16},{16,18},{18... | collective-permute-start | bytes 786440 | tf_op jit(solution)/shard_map/ppermute | solution.py:671
  14.6 0.1 collective-permute-start.1
  14.7 2.6 %collective-permute-start.2 = (bf16[4,2,128,128]{3,2,1,0:T(8,128)(2,1)}, bf16[4,2,128,128]{3,2,1,0:T(8,128)(2,1)S(1)}, u32[]{:S(2)}, u32[]{:S(2)}) collective-permute-start(bf16[4,2,128,128]{3,2,1,0:T(8,128)(2,1)} %get-tuple-element.65), channel_id=1, source_target_pairs={{0,4},{2,6},{4,0},{6,2},{8,12},{10,14},{12,8},{14,10},{16,20},{18,... | collective-permute-start | bytes 786440 | tf_op jit(solution)/shard_map/ppermute | solution.py:671
  17.3 0.0 collective-permute-done.4
  17.3 0.6 collective-permute-start.3
  18.0 7.9 %far_attention.1.rest_1_ = bf16[4096,128]{1,0:T(8,128)(2,1)} custom-call(bf16[8192,128]{1,0:T(8,128)(2,1)} %bitcast.33, bf16[2048,128]{1,0:T(8,128)(2,1)} %bitcast.37, bf16[2048,128]{1,0:T(8,128)(2,1)} %bitcast.40, bf16[2048,128]{1,0:T(8,128)(2,1)} %bitcast.38, bf16[2048,128]{1,0:T(8,128)(2,1)} %bitcast.41), custom_call_target="tpu_custom_call" | custom-call | flops 2013265920 | bytes 6291456 | tf_op jit(solution)/shard_map/far_attention/pallas_call | solution.py:334
  25.9 0.0 collective-permute-done.5.pk_ref
  25.9 0.0 collective-permute-done.6.pv_ref
  25.9 7.7 %collective-permute-done.1.rest_1_ = bf16[4,2,128,128]{3,2,1,0:T(8,128)(2,1)S(1)} collective-permute-done((bf16[4,2,128,128]{3,2,1,0:T(8,128)(2,1)}, bf16[4,2,128,128]{3,2,1,0:T(8,128)(2,1)S(1)}, u32[]{:S(2)}, u32[]{:S(2)}) %collective-permute-start.1) | collective-permute-done | bytes 262176 | tf_op jit(solution)/shard_map/ppermute | solution.py:671
  33.6 0.5 collective-permute-done.2.rest_2_
  34.1 2.3 %collective-permute-done.3.rest_3_ = bf16[4,2,128,128]{3,2,1,0:T(8,128)(2,1)S(1)} collective-permute-done((bf16[4,2,128,128]{3,2,1,0:T(8,128)(2,1)}, bf16[4,2,128,128]{3,2,1,0:T(8,128)(2,1)S(1)}, u32[]{:S(2)}, u32[]{:S(2)}) %collective-permute-start.3) | collective-permute-done | bytes 262176 | tf_op jit(solution)/shard_map/ppermute | solution.py:671
  36.4 0.8 plane_sums.1
  37.2 1.3 %collective-permute-start.11 = (bf16[4,2,128,128]{3,2,1,0:T(8,128)(2,1)S(1)}, bf16[4,2,128,128]{3,2,1,0:T(8,128)(2,1)S(1)}, u32[]{:S(2)}, u32[]{:S(2)}) collective-permute-start(bf16[4,2,128,128]{3,2,1,0:T(8,128)(2,1)S(1)} %get-tuple-element.77), channel_id=1, source_target_pairs={{24,8},{26,10},{28,12},{30,14},{25,9},{27,11},{29,13},{31,15}} | collective-permute-start | bytes 786440 | tf_op jit(solution)/shard_map/ppermute | solution.py:671
  38.5 0.1 collective-permute-start.9
  38.6 0.1 collective-permute-start.8
  38.7 3.5 %collective-permute-start.7 = (bf16[2,128,128]{2,1,0:T(8,128)(2,1)S(1)}, bf16[2,128,128]{2,1,0:T(8,128)(2,1)S(1)}, u32[]{:S(2)}, u32[]{:S(2)}) collective-permute-start(bf16[2,128,128]{2,1,0:T(8,128)(2,1)S(1)} %get-tuple-element.86.rest_1_), channel_id=1, source_target_pairs={{0,8},{2,10},{4,12},{6,14},{8,0},{10,2},{12,4},{14,6},{16,24},{18,... | collective-permute-start | bytes 196616 | tf_op jit(solution)/shard_map/ppermute | solution.py:671
  42.1 1.9 %collective-permute-start.10 = (bf16[1024,128]{1,0:T(8,128)(2,1)S(1)}, bf16[1024,128]{1,0:T(8,128)(2,1)S(1)}, u32[]{:S(2)}, u32[]{:S(2)}) collective-permute-start(bf16[1024,128]{1,0:T(8,128)(2,1)S(1)} %broadcast_select_fusion.4), channel_id=1, source_target_pairs={{8,0},{10,2},{12,4},{14,6},{24,16},{26,18},{28,20},{30,22},{9,1},{... | collective-permute-start | bytes 786440 | tf_op jit(solution)/shard_map/ppermute | solution.py:671
  44.1 0.0 copy-start.2
  44.1 6.5 %trunk_attention_0.1.rest_2_ = f32[2048,128]{1,0:T(8,128)} custom-call(s32[1]{0:T(128)} %bitcast.where_ref, f32[8,11]{1,0:T(8,128)} %gain_ref.9, bf16[4096,128]{1,0:T(8,128)(2,1)} %bitcast.19, bf16[4096,128]{1,0:T(8,128)(2,1)} %bitcast.14, bf16[4096,128]{1,0:T(8,128)(2,1)} %bitcast.17, bf16[4096,128]{1,0:T(8,128)(2,1)} %bitcast.22, ...), custom_call_target="tpu_custom_call" | custom-call | flops 1207959552 | bytes 3145728 | tf_op jit(solution)/shard_map/trunk_attention_0/pallas_call | solution.py:398
  50.6 0.0 collective-permute-done.11
  50.6 1.4 %collective-permute-done.10 = bf16[1024,128]{1,0:T(8,128)(2,1)S(1)} collective-permute-done((bf16[1024,128]{1,0:T(8,128)(2,1)S(1)}, bf16[1024,128]{1,0:T(8,128)(2,1)S(1)}, u32[]{:S(2)}, u32[]{:S(2)}) %collective-permute-start.10) | collective-permute-done | bytes 262176 | tf_op jit(solution)/shard_map/ppermute | solution.py:671
  52.1 0.0 collective-permute-done.9.rest_4_
  52.1 0.0 collective-permute-done.8.rest_3_
  52.1 0.0 collective-permute-done.7.rest_2_
  52.1 4.3 %collective-permute-start.15 = (bf16[4,2,128,128]{3,2,1,0:T(8,128)(2,1)S(1)}, bf16[4,2,128,128]{3,2,1,0:T(8,128)(2,1)S(1)}, u32[]{:S(2)}, u32[]{:S(2)}) collective-permute-start(bf16[4,2,128,128]{3,2,1,0:T(8,128)(2,1)S(1)} %broadcast_select_fusion.1), channel_id=1, source_target_pairs={{8,0},{10,2},{12,4},{14,6},{24,16},{26,18},{28,20},{30,22},{9,1},{... | collective-permute-start | bytes 786440 | tf_op jit(solution)/shard_map/ppermute | solution.py:671
  56.4 0.1 collective-permute-start.14
  56.5 5.8 %collective-permute-start.13 = (bf16[1024,128]{1,0:T(8,128)(2,1)S(1)}, bf16[1024,128]{1,0:T(8,128)(2,1)S(1)}, u32[]{:S(2)}, u32[]{:S(2)}) collective-permute-start(bf16[1024,128]{1,0:T(8,128)(2,1)S(1)} %broadcast_select_fusion.2.rest_0_), channel_id=1, source_target_pairs={{0,4},{2,6},{4,0},{6,2},{8,12},{10,14},{12,8},{14,10},{16,20},{18,... | collective-permute-start | bytes 786440 | tf_op jit(solution)/shard_map/ppermute | solution.py:671
  62.3 1.1 collective-permute-start.12
  63.5 0.8 cross_sums.1
  64.2 0.6 copy-done.3
  64.8 6.5 %trunk_attention_2.1.rest_3_ = f32[2048,128]{1,0:T(8,128)} custom-call(s32[1]{0:T(128)} %bitcast.where_ref, f32[8,11]{1,0:T(8,128)} %gain_ref.9, bf16[4096,128]{1,0:T(8,128)(2,1)} %bitcast.20, bf16[4096,128]{1,0:T(8,128)(2,1)} %bitcast.15, bf16[4096,128]{1,0:T(8,128)(2,1)} %bitcast.18, bf16[4096,128]{1,0:T(8,128)(2,1)} %bitcast.23, ...), custom_call_target="tpu_custom_call" | custom-call | flops 1207959552 | bytes 3145728 | tf_op jit(solution)/shard_map/trunk_attention_2/pallas_call | solution.py:398
  71.4 0.0 collective-permute-done.15
  71.4 0.0 collective-permute-done.14.rest_3_
  71.4 1.7 %collective-permute-done.13.rest_2_ = bf16[1024,128]{1,0:T(8,128)(2,1)S(1)} collective-permute-done((bf16[1024,128]{1,0:T(8,128)(2,1)S(1)}, bf16[1024,128]{1,0:T(8,128)(2,1)S(1)}, u32[]{:S(2)}, u32[]{:S(2)}) %collective-permute-start.13) | collective-permute-done | bytes 262176 | tf_op jit(solution)/shard_map/ppermute | solution.py:671
  73.1 1.0 collective-permute-done.12.rest_1_
  74.1 0.1 add_convert_fusion.rest_4_
  74.2 0.8 collective-permute-start.18
  75.0 2.2 %collective-permute-start.17 = (bf16[4,2,128,128]{3,2,1,0:T(8,128)(2,1)S(1)}, bf16[4,2,128,128]{3,2,1,0:T(8,128)(2,1)S(1)}, u32[]{:S(2)}, u32[]{:S(2)}) collective-permute-start(bf16[4,2,128,128]{3,2,1,0:T(8,128)(2,1)S(1)} %add_convert_fusion.rest_4_), channel_id=1, source_target_pairs={{0,4},{2,6},{4,0},{6,2},{8,12},{10,14},{12,8},{14,10},{16,20},{18,... | collective-permute-start | bytes 786440 | tf_op jit(solution)/shard_map/ppermute | solution.py:671
  77.2 0.0 collective-permute-start.16
  77.2 1.5 %collective-permute-start.19 = (bf16[2,128,128]{2,1,0:T(8,128)(2,1)S(1)}, bf16[2,128,128]{2,1,0:T(8,128)(2,1)S(1)}, u32[]{:S(2)}, u32[]{:S(2)}) collective-permute-start(bf16[2,128,128]{2,1,0:T(8,128)(2,1)S(1)} %get-tuple-element.108), channel_id=1, source_target_pairs={{0,2},{2,0},{4,6},{6,4},{8,10},{10,8},{12,14},{14,12},{16,18},{18,... | collective-permute-start | bytes 196616 | tf_op jit(solution)/shard_map/ppermute | solution.py:671
  79.3 0.1 collective-permute-start.20
  79.4 9.3 %collective-permute-done.19.rest_9_ = bf16[2,128,128]{2,1,0:T(8,128)(2,1)S(1)} collective-permute-done((bf16[2,128,128]{2,1,0:T(8,128)(2,1)S(1)}, bf16[2,128,128]{2,1,0:T(8,128)(2,1)S(1)}, u32[]{:S(2)}, u32[]{:S(2)}) %collective-permute-start.19) | collective-permute-done | bytes 65568 | tf_op jit(solution)/shard_map/ppermute | solution.py:671
  88.6 2.7 %collective-permute-start.21 = (bf16[2,128,128]{2,1,0:T(8,128)(2,1)S(1)}, bf16[2,128,128]{2,1,0:T(8,128)(2,1)S(1)}, u32[]{:S(2)}, u32[]{:S(2)}) collective-permute-start(bf16[2,128,128]{2,1,0:T(8,128)(2,1)S(1)} %get-tuple-element.110), channel_id=1, source_target_pairs={{0,6},{2,4},{4,2},{6,0},{8,14},{10,12},{12,10},{14,8},{16,22},{18,... | collective-permute-start | bytes 196616 | tf_op jit(solution)/shard_map/ppermute | solution.py:671
  91.3 8.3 %near_attention.1.rest_0_ = bf16[4096,128]{1,0:T(8,128)(2,1)} custom-call(s32[1]{0:T(128)} %bitcast.where_ref, s32[1]{0:T(128)S(6)} %copy.14.fork_ref, bf16[8192,128]{1,0:T(8,128)(2,1)} %bitcast.34, bf16[2048,128]{1,0:T(8,128)(2,1)} %bitcast.39, bf16[2048,128]{1,0:T(8,128)(2,1)} %bitcast.42, bf16[1024,128]{1,0:T(8,128)(2,1)} %copy-done.12, ...), custom_call_target="tpu_custom_call" | custom-call | flops 2013265920 | bytes 6291456 | tf_op jit(solution)/shard_map/near_attention/pallas_call | solution.py:448
  99.6 0.0 collective-permute-done.21.rest_11_
  99.6 0.0 collective-permute-done.18.rest_7_
  99.7 0.0 collective-permute-done.16.rest_5_
  99.7 0.5 copy-done.14
  100.2 0.0 copy-done.15
  100.3 0.1 copy-done.9
  100.4 0.1 copy-done.10
  100.5 0.1 copy-done.11
  100.5 13.1 %final_linear.1 = (f32[8192,128]{1,0:T(8,128)}, f32[4096,128]{1,0:T(8,128)}, f32[12,8,128]{2,1,0:T(8,128)}) custom-call(s32[1]{0:T(128)} %bitcast.where_ref, s32[1]{0:T(128)S(6)} %copy.14.fork_ref, bf16[8192,128]{1,0:T(8,128)(2,1)} %bitcast.28, bf16[4096,128]{1,0:T(8,128)(2,1)} %bitcast.21, bf16[4096,128]{1,0:T(8,128)(2,1)} %near_attention.1.rest_0_, ...), custom_call_target="tpu_custom_call" | custom-call | flops 805306368 | bytes 12582912 | tf_op jit(solution)/shard_map/final_linear/pallas_call | solution.py:545
  113.6 2.0 %collective-permute-start.22 = (f32[12,8,128]{2,1,0:T(8,128)}, f32[12,8,128]{2,1,0:T(8,128)S(1)}, u32[]{:S(2)}, u32[]{:S(2)}) collective-permute-start(f32[12,8,128]{2,1,0:T(8,128)} %get-tuple-element.113.square_ref), channel_id=1, source_target_pairs={{0,1},{1,0},{2,3},{3,2},{4,5},{5,4},{6,7},{7,6},{8,9},{9,8},{10,11... | collective-permute-start | bytes 147464 | tf_op jit(solution)/shard_map/ppermute | solution.py:745
  115.7 1.1 collective-permute-done.22.other_ref
  116.7 0.6 copy-done.16
  117.4 5.4 %normalize.1 = (bf16[4096,128]{1,0:T(8,128)(2,1)}, bf16[8192,128]{1,0:T(8,128)(2,1)}) custom-call(f32[4096,128]{1,0:T(8,128)} %get-tuple-element.111.trunk_hbm, f32[8192,128]{1,0:T(8,128)} %get-tuple-element.112.branch_hbm, f32[12,8,128]{2,1,0:T(8,128)} %get-tuple-element.113.square_ref, f32[12,8,128]{2,1,0:T(8,128)} %copy-done.16), custom_call_target="tpu_custom_call" | custom-call | flops 3145728 | bytes 9437184 | tf_op jit(solution)/shard_map/normalize/pallas_call | solution.py:618
  (37 shorter events, 0.2 us)
Async XLA Ops:
  0.6 12.0 %copy-start.5 = (bf16[512,2,128]{2,1,0:T(2,128)(2,1)S(1)}, bf16[512,2,128]{2,1,0:T(2,128)(2,1)}, u32[]{:S(2)}) copy-start(bf16[512,2,128]{2,1,0:T(2,128)(2,1)} %param.17) | copy-start | bytes 786436
  0.6 7.6 %copy-start.4 = (bf16[512,2,128]{2,1,0:T(2,128)(2,1)S(1)}, bf16[512,2,128]{2,1,0:T(2,128)(2,1)}, u32[]{:S(2)}) copy-start(bf16[512,2,128]{2,1,0:T(2,128)(2,1)} %param.16) | copy-start | bytes 786436
  0.7 7.5 %collective-permute-start = (bf16[1024,128]{1,0:T(8,128)(2,1)}, bf16[1024,128]{1,0:T(8,128)(2,1)S(1)}, u32[]{:S(2)}, u32[]{:S(2)}) collective-permute-start(bf16[1024,128]{1,0:T(8,128)(2,1)} %bitcast.29), channel_id=1, source_target_pairs={{30,26},{28,24},{31,27},{29,25}} | collective-permute-start | bytes 786440 | tf_op jit(solution)/shard_map/ppermute | solution.py:671
  8.2 9.1 %collective-permute-start.4 = (bf16[1024,128]{1,0:T(8,128)(2,1)S(1)}, bf16[1024,128]{1,0:T(8,128)(2,1)S(1)}, u32[]{:S(2)}, u32[]{:S(2)}) collective-permute-start(bf16[1024,128]{1,0:T(8,128)(2,1)S(1)} %broadcast_select_fusion.3), channel_id=1, source_target_pairs={{24,8},{26,10},{28,12},{30,14},{25,9},{27,11},{29,13},{31,15}} | collective-permute-start | bytes 786440 | tf_op jit(solution)/shard_map/ppermute | solution.py:671
  9.5 16.4 %collective-permute-start.5 = (bf16[1024,128]{1,0:T(8,128)(2,1)S(1)}, bf16[1024,128]{1,0:T(8,128)(2,1)S(1)}, u32[]{:S(2)}, u32[]{:S(2)}) collective-permute-start(bf16[1024,128]{1,0:T(8,128)(2,1)S(1)} %bitcast.27), channel_id=1, source_target_pairs={{0,2},{2,4},{4,6},{6,8},{8,10},{10,12},{12,14},{14,16},{16,18},{18... | collective-permute-start | bytes 786440 | tf_op jit(solution)/shard_map/ppermute | solution.py:671
  12.7 13.2 %collective-permute-start.6 = (bf16[1024,128]{1,0:T(8,128)(2,1)S(1)}, bf16[1024,128]{1,0:T(8,128)(2,1)S(1)}, u32[]{:S(2)}, u32[]{:S(2)}) collective-permute-start(bf16[1024,128]{1,0:T(8,128)(2,1)S(1)} %bitcast.32), channel_id=1, source_target_pairs={{0,2},{2,4},{4,6},{6,8},{8,10},{10,12},{12,14},{14,16},{16,18},{18... | collective-permute-start | bytes 786440 | tf_op jit(solution)/shard_map/ppermute | solution.py:671
  14.6 19.0 %collective-permute-start.1 = (bf16[4,2,128,128]{3,2,1,0:T(8,128)(2,1)}, bf16[4,2,128,128]{3,2,1,0:T(8,128)(2,1)S(1)}, u32[]{:S(2)}, u32[]{:S(2)}) collective-permute-start(bf16[4,2,128,128]{3,2,1,0:T(8,128)(2,1)} %get-tuple-element.64), channel_id=1, source_target_pairs={{0,2},{2,0},{4,6},{6,4},{8,10},{10,8},{12,14},{14,12},{16,18},{18,... | collective-permute-start | bytes 786440 | tf_op jit(solution)/shard_map/ppermute | solution.py:671
  14.7 19.4 %collective-permute-start.2 = (bf16[4,2,128,128]{3,2,1,0:T(8,128)(2,1)}, bf16[4,2,128,128]{3,2,1,0:T(8,128)(2,1)S(1)}, u32[]{:S(2)}, u32[]{:S(2)}) collective-permute-start(bf16[4,2,128,128]{3,2,1,0:T(8,128)(2,1)} %get-tuple-element.65), channel_id=1, source_target_pairs={{0,4},{2,6},{4,0},{6,2},{8,12},{10,14},{12,8},{14,10},{16,20},{18,... | collective-permute-start | bytes 786440 | tf_op jit(solution)/shard_map/ppermute | solution.py:671
  17.3 19.1 %collective-permute-start.3 = (bf16[4,2,128,128]{3,2,1,0:T(8,128)(2,1)}, bf16[4,2,128,128]{3,2,1,0:T(8,128)(2,1)S(1)}, u32[]{:S(2)}, u32[]{:S(2)}) collective-permute-start(bf16[4,2,128,128]{3,2,1,0:T(8,128)(2,1)} %get-tuple-element.66), channel_id=1, source_target_pairs={{0,6},{2,4},{4,2},{6,0},{8,14},{10,12},{12,10},{14,8},{16,22},{18,... | collective-permute-start | bytes 786440 | tf_op jit(solution)/shard_map/ppermute | solution.py:671
  18.0 18.5 %copy-start = (bf16[4,2,128,128]{3,2,1,0:T(8,128)(2,1)S(1)}, bf16[4,2,128,128]{3,2,1,0:T(8,128)(2,1)}, u32[]{:S(2)}) copy-start(bf16[4,2,128,128]{3,2,1,0:T(8,128)(2,1)} %get-tuple-element.69.rest_0_) | copy-start | bytes 786436
  18.0 18.5 %copy-start.1 = (f32[8,11]{1,0:T(8,128)S(1)}, f32[8,11]{1,0:T(8,128)}, u32[]{:S(2)}) copy-start(f32[8,11]{1,0:T(8,128)} %gain_ref.9) | copy-start | bytes 1060
  25.9 18.2 %copy-start.6 = (bf16[1024,128]{1,0:T(8,128)(2,1)}, bf16[1024,128]{1,0:T(8,128)(2,1)S(1)}, u32[]{:S(2)}) copy-start(bf16[1024,128]{1,0:T(8,128)(2,1)S(1)} %collective-permute-done.5.pk_ref) | copy-start | bytes 786436
  25.9 18.1 %copy-start.7 = (bf16[1024,128]{1,0:T(8,128)(2,1)}, bf16[1024,128]{1,0:T(8,128)(2,1)S(1)}, u32[]{:S(2)}) copy-start(bf16[1024,128]{1,0:T(8,128)(2,1)S(1)} %collective-permute-done.6.pv_ref) | copy-start | bytes 786436
  37.2 13.4 %collective-permute-start.11 = (bf16[4,2,128,128]{3,2,1,0:T(8,128)(2,1)S(1)}, bf16[4,2,128,128]{3,2,1,0:T(8,128)(2,1)S(1)}, u32[]{:S(2)}, u32[]{:S(2)}) collective-permute-start(bf16[4,2,128,128]{3,2,1,0:T(8,128)(2,1)S(1)} %get-tuple-element.77), channel_id=1, source_target_pairs={{24,8},{26,10},{28,12},{30,14},{25,9},{27,11},{29,13},{31,15}} | collective-permute-start | bytes 786440 | tf_op jit(solution)/shard_map/ppermute | solution.py:671
  38.5 13.6 %collective-permute-start.9 = (bf16[2,128,128]{2,1,0:T(8,128)(2,1)S(1)}, bf16[2,128,128]{2,1,0:T(8,128)(2,1)S(1)}, u32[]{:S(2)}, u32[]{:S(2)}) collective-permute-start(bf16[2,128,128]{2,1,0:T(8,128)(2,1)S(1)} %get-tuple-element.86.rest_1_), channel_id=1, source_target_pairs={{0,24},{2,26},{4,28},{6,30},{8,16},{10,18},{12,20},{14,22},{16,8},... | collective-permute-start | bytes 196616 | tf_op jit(solution)/shard_map/ppermute | solution.py:671
  38.6 13.5 %collective-permute-start.8 = (bf16[2,128,128]{2,1,0:T(8,128)(2,1)S(1)}, bf16[2,128,128]{2,1,0:T(8,128)(2,1)S(1)}, u32[]{:S(2)}, u32[]{:S(2)}) collective-permute-start(bf16[2,128,128]{2,1,0:T(8,128)(2,1)S(1)} %get-tuple-element.86.rest_1_), channel_id=1, source_target_pairs={{0,16},{2,18},{4,20},{6,22},{8,24},{10,26},{12,28},{14,30},{16,0},... | collective-permute-start | bytes 196616 | tf_op jit(solution)/shard_map/ppermute | solution.py:671
  38.7 13.4 %collective-permute-start.7 = (bf16[2,128,128]{2,1,0:T(8,128)(2,1)S(1)}, bf16[2,128,128]{2,1,0:T(8,128)(2,1)S(1)}, u32[]{:S(2)}, u32[]{:S(2)}) collective-permute-start(bf16[2,128,128]{2,1,0:T(8,128)(2,1)S(1)} %get-tuple-element.86.rest_1_), channel_id=1, source_target_pairs={{0,8},{2,10},{4,12},{6,14},{8,0},{10,2},{12,4},{14,6},{16,24},{18,... | collective-permute-start | bytes 196616 | tf_op jit(solution)/shard_map/ppermute | solution.py:671
  42.1 9.9 %collective-permute-start.10 = (bf16[1024,128]{1,0:T(8,128)(2,1)S(1)}, bf16[1024,128]{1,0:T(8,128)(2,1)S(1)}, u32[]{:S(2)}, u32[]{:S(2)}) collective-permute-start(bf16[1024,128]{1,0:T(8,128)(2,1)S(1)} %broadcast_select_fusion.4), channel_id=1, source_target_pairs={{8,0},{10,2},{12,4},{14,6},{24,16},{26,18},{28,20},{30,22},{9,1},{... | collective-permute-start | bytes 786440 | tf_op jit(solution)/shard_map/ppermute | solution.py:671
  44.1 19.4 %copy-start.2 = (f32[8,11]{1,0:T(8,128)S(1)}, f32[8,11]{1,0:T(8,128)}, u32[]{:S(2)}) copy-start(f32[8,11]{1,0:T(8,128)} %gain_ref.9) | copy-start | bytes 1060
  52.1 19.3 %copy-start.12 = (bf16[1024,128]{1,0:T(8,128)(2,1)}, bf16[1024,128]{1,0:T(8,128)(2,1)S(1)}, u32[]{:S(2)}) copy-start(bf16[1024,128]{1,0:T(8,128)(2,1)S(1)} %broadcast_select_fusion.2.rest_0_) | copy-start | bytes 786436
  52.1 19.3 %collective-permute-start.15 = (bf16[4,2,128,128]{3,2,1,0:T(8,128)(2,1)S(1)}, bf16[4,2,128,128]{3,2,1,0:T(8,128)(2,1)S(1)}, u32[]{:S(2)}, u32[]{:S(2)}) collective-permute-start(bf16[4,2,128,128]{3,2,1,0:T(8,128)(2,1)S(1)} %broadcast_select_fusion.1), channel_id=1, source_target_pairs={{8,0},{10,2},{12,4},{14,6},{24,16},{26,18},{28,20},{30,22},{9,1},{... | collective-permute-start | bytes 786440 | tf_op jit(solution)/shard_map/ppermute | solution.py:671
  56.4 15.0 %collective-permute-start.14 = (bf16[1024,128]{1,0:T(8,128)(2,1)S(1)}, bf16[1024,128]{1,0:T(8,128)(2,1)S(1)}, u32[]{:S(2)}, u32[]{:S(2)}) collective-permute-start(bf16[1024,128]{1,0:T(8,128)(2,1)S(1)} %broadcast_select_fusion.2.rest_0_), channel_id=1, source_target_pairs={{0,6},{2,4},{4,2},{6,0},{8,14},{10,12},{12,10},{14,8},{16,22},{18,... | collective-permute-start | bytes 786440 | tf_op jit(solution)/shard_map/ppermute | solution.py:671
  56.5 16.6 %collective-permute-start.13 = (bf16[1024,128]{1,0:T(8,128)(2,1)S(1)}, bf16[1024,128]{1,0:T(8,128)(2,1)S(1)}, u32[]{:S(2)}, u32[]{:S(2)}) collective-permute-start(bf16[1024,128]{1,0:T(8,128)(2,1)S(1)} %broadcast_select_fusion.2.rest_0_), channel_id=1, source_target_pairs={{0,4},{2,6},{4,0},{6,2},{8,12},{10,14},{12,8},{14,10},{16,20},{18,... | collective-permute-start | bytes 786440 | tf_op jit(solution)/shard_map/ppermute | solution.py:671
  62.3 11.8 %collective-permute-start.12 = (bf16[1024,128]{1,0:T(8,128)(2,1)S(1)}, bf16[1024,128]{1,0:T(8,128)(2,1)S(1)}, u32[]{:S(2)}, u32[]{:S(2)}) collective-permute-start(bf16[1024,128]{1,0:T(8,128)(2,1)S(1)} %broadcast_select_fusion.2.rest_0_), channel_id=1, source_target_pairs={{0,2},{2,0},{4,6},{6,4},{8,10},{10,8},{12,14},{14,12},{16,18},{18,... | collective-permute-start | bytes 786440 | tf_op jit(solution)/shard_map/ppermute | solution.py:671
  64.2 0.6 copy-start.3
  71.4 19.9 %copy-start.17 = (bf16[1024,128]{1,0:T(8,128)(2,1)}, bf16[1024,128]{1,0:T(8,128)(2,1)S(1)}, u32[]{:S(2)}) copy-start(bf16[1024,128]{1,0:T(8,128)(2,1)S(1)} %collective-permute-done.14.rest_3_) | copy-start | bytes 786436
  73.1 18.2 %copy-start.18 = (bf16[1024,128]{1,0:T(8,128)(2,1)}, bf16[1024,128]{1,0:T(8,128)(2,1)S(1)}, u32[]{:S(2)}) copy-start(bf16[1024,128]{1,0:T(8,128)(2,1)S(1)} %collective-permute-done.13.rest_2_) | copy-start | bytes 786436
  74.1 17.2 %copy-start.19 = (bf16[1024,128]{1,0:T(8,128)(2,1)}, bf16[1024,128]{1,0:T(8,128)(2,1)S(1)}, u32[]{:S(2)}) copy-start(bf16[1024,128]{1,0:T(8,128)(2,1)S(1)} %collective-permute-done.12.rest_1_) | copy-start | bytes 786436
  74.2 25.4 %copy-start.8 = (bf16[4,2,128,128]{3,2,1,0:T(8,128)(2,1)}, bf16[4,2,128,128]{3,2,1,0:T(8,128)(2,1)S(1)}, u32[]{:S(2)}) copy-start(bf16[4,2,128,128]{3,2,1,0:T(8,128)(2,1)S(1)} %add_convert_fusion.rest_4_) | copy-start | bytes 786436
  74.2 25.4 %collective-permute-start.18 = (bf16[4,2,128,128]{3,2,1,0:T(8,128)(2,1)S(1)}, bf16[4,2,128,128]{3,2,1,0:T(8,128)(2,1)S(1)}, u32[]{:S(2)}, u32[]{:S(2)}) collective-permute-start(bf16[4,2,128,128]{3,2,1,0:T(8,128)(2,1)S(1)} %add_convert_fusion.rest_4_), channel_id=1, source_target_pairs={{0,6},{2,4},{4,2},{6,0},{8,14},{10,12},{12,10},{14,8},{16,22},{18,... | collective-permute-start | bytes 786440 | tf_op jit(solution)/shard_map/ppermute | solution.py:671
  75.0 24.7 %collective-permute-start.17 = (bf16[4,2,128,128]{3,2,1,0:T(8,128)(2,1)S(1)}, bf16[4,2,128,128]{3,2,1,0:T(8,128)(2,1)S(1)}, u32[]{:S(2)}, u32[]{:S(2)}) collective-permute-start(bf16[4,2,128,128]{3,2,1,0:T(8,128)(2,1)S(1)} %add_convert_fusion.rest_4_), channel_id=1, source_target_pairs={{0,4},{2,6},{4,0},{6,2},{8,12},{10,14},{12,8},{14,10},{16,20},{18,... | collective-permute-start | bytes 786440 | tf_op jit(solution)/shard_map/ppermute | solution.py:671
  77.2 22.5 %collective-permute-start.16 = (bf16[4,2,128,128]{3,2,1,0:T(8,128)(2,1)S(1)}, bf16[4,2,128,128]{3,2,1,0:T(8,128)(2,1)S(1)}, u32[]{:S(2)}, u32[]{:S(2)}) collective-permute-start(bf16[4,2,128,128]{3,2,1,0:T(8,128)(2,1)S(1)} %add_convert_fusion.rest_4_), channel_id=1, source_target_pairs={{0,2},{2,0},{4,6},{6,4},{8,10},{10,8},{12,14},{14,12},{16,18},{18,... | collective-permute-start | bytes 786440 | tf_op jit(solution)/shard_map/ppermute | solution.py:671
  77.2 11.5 %collective-permute-start.19 = (bf16[2,128,128]{2,1,0:T(8,128)(2,1)S(1)}, bf16[2,128,128]{2,1,0:T(8,128)(2,1)S(1)}, u32[]{:S(2)}, u32[]{:S(2)}) collective-permute-start(bf16[2,128,128]{2,1,0:T(8,128)(2,1)S(1)} %get-tuple-element.108), channel_id=1, source_target_pairs={{0,2},{2,0},{4,6},{6,4},{8,10},{10,8},{12,14},{14,12},{16,18},{18,... | collective-permute-start | bytes 196616 | tf_op jit(solution)/shard_map/ppermute | solution.py:671
  79.3 20.3 %collective-permute-start.20 = (bf16[2,128,128]{2,1,0:T(8,128)(2,1)S(1)}, bf16[2,128,128]{2,1,0:T(8,128)(2,1)S(1)}, u32[]{:S(2)}, u32[]{:S(2)}) collective-permute-start(bf16[2,128,128]{2,1,0:T(8,128)(2,1)S(1)} %get-tuple-element.109), channel_id=1, source_target_pairs={{0,4},{2,6},{4,0},{6,2},{8,12},{10,14},{12,8},{14,10},{16,20},{18,... | collective-permute-start | bytes 196616 | tf_op jit(solution)/shard_map/ppermute | solution.py:671
  88.6 11.0 %copy-start.13 = (bf16[2,128,128]{2,1,0:T(8,128)(2,1)}, bf16[2,128,128]{2,1,0:T(8,128)(2,1)S(1)}, u32[]{:S(2)}) copy-start(bf16[2,128,128]{2,1,0:T(8,128)(2,1)S(1)} %collective-permute-done.19.rest_9_) | copy-start | bytes 196612
  88.6 11.0 %collective-permute-start.21 = (bf16[2,128,128]{2,1,0:T(8,128)(2,1)S(1)}, bf16[2,128,128]{2,1,0:T(8,128)(2,1)S(1)}, u32[]{:S(2)}, u32[]{:S(2)}) collective-permute-start(bf16[2,128,128]{2,1,0:T(8,128)(2,1)S(1)} %get-tuple-element.110), channel_id=1, source_target_pairs={{0,6},{2,4},{4,2},{6,0},{8,14},{10,12},{12,10},{14,8},{16,22},{18,... | collective-permute-start | bytes 196616 | tf_op jit(solution)/shard_map/ppermute | solution.py:671
  99.6 0.6 copy-start.14
  99.6 0.6 copy-start.15
  99.7 0.7 copy-start.9
  99.7 0.8 copy-start.10
  99.7 0.9 copy-start.11
  113.6 3.1 %collective-permute-start.22 = (f32[12,8,128]{2,1,0:T(8,128)}, f32[12,8,128]{2,1,0:T(8,128)S(1)}, u32[]{:S(2)}, u32[]{:S(2)}) collective-permute-start(f32[12,8,128]{2,1,0:T(8,128)} %get-tuple-element.113.square_ref), channel_id=1, source_target_pairs={{0,1},{1,0},{2,3},{3,2},{4,5},{5,4},{6,7},{7,6},{8,9},{9,8},{10,11... | collective-permute-start | bytes 147464 | tf_op jit(solution)/shard_map/ppermute | solution.py:745
  116.7 0.6 copy-start.16

commit v5 on v4

--- a/solution.py
+++ b/solution.py
@@ -49,12 +49,20 @@
     return wide[pl.ds(each, rows_ref.shape[0] // count, stride=count), :].astype(BF16)
 
 
-def state_kernel(depth, heads, where_ref, gain_ref, k_hbm, v_hbm, *rest):
-    out_refs = rest[:COLS]
-    local_ref, keys, values, kf, vf, levels, outs, key_sems, value_sems = rest[COLS:]
-    rows, width = kf.shape
+def masked_copies(x, count):
+    rows, width = x.shape
+    tiles = x.reshape(rows // 16, 16, width)
+    row = lax.broadcasted_iota(jnp.int32, (16, width), 0) & (count - 1)
+    kept = [tiles * jnp.where(row == m, 1.0, 0.0).astype(BF16)[None] for m in range(count)]
+    return jnp.concatenate([part.reshape(rows, width) for part in kept], axis=1)
+
+
+def state_kernel(depth, heads, gain_ref, k_hbm, v_hbm, *rest):
+    piece_refs = rest[:COLS]
+    local_ref, sum_ref, keys, values, levels, key_sems, value_sems = rest[COLS:]
+    width = keys.shape[1]
+    rows = keys.shape[0] >> depth
     each = heads // COLS
-    column = where_ref[0] & (COLS - 1)
     copies = [
         (block_copy(k_hbm, keys, key_sems, b, rows), block_copy(v_hbm, values, value_sems, b, rows))
         for b in range(1 << depth)
@@ -65,12 +73,14 @@
     for b, pair in enumerate(copies):
         for copy in pair:
             copy.wait()
-        kf[...] = keys[b * rows : (b + 1) * rows].astype(F32)
-        vf[...] = values[b * rows : (b + 1) * rows].astype(F32)
+        states = lax.dot_general(
+            keys[b * rows : (b + 1) * rows],
+            masked_copies(values[b * rows : (b + 1) * rows], heads),
+            (((0,), (0,)), ((), ())),
+            preferred_element_type=F32,
+        )
         for h in range(heads):
-            k = kf[pl.ds(h, BLK, stride=heads), :].astype(BF16)
-            v = vf[pl.ds(h, BLK, stride=heads), :].astype(BF16)
-            merged = lax.dot_general(k, v, (((0,), (0,)), ((), ())), preferred_element_type=F32)
+            merged = states[:, h * width : (h + 1) * width]
             before = None
             for bit in range(depth):
                 if b >> bit & 1:
@@ -83,32 +93,30 @@
             if before is not None:
                 before = before.astype(BF16)
                 local_ref[b - 1, h] = before
-                outs[column ^ (h // each), b, h % each] = before
+                piece_refs[h // each][b - 1, h % each] = before
             if carry < depth:
                 levels[carry, h] = merged
             else:
-                outs[column ^ (h // each), 0, h % each] = merged.astype(BF16)
-    for d in range(COLS):
-        out_refs[d][...] = outs[d]
-
-
-def block_sums(where, gain, keys, values, heads, depth):
+                sum_ref[h // each, h % each] = merged.astype(BF16)
+
+
+def block_sums(gain, keys, values, heads, depth):
     blocks = 1 << depth
-    rows, width = keys.shape[0] // blocks, keys.shape[1]
-    quarter = (blocks, heads // COLS, width, width)
+    width = keys.shape[1]
+    each = heads // COLS
     return pl.pallas_call(
         functools.partial(state_kernel, depth, heads),
-        in_specs=[smem(), smem(), hbm(), hbm()],
-        out_specs=[vmem()] * (COLS + 1),
-        out_shape=[jax.ShapeDtypeStruct(quarter, BF16)] * COLS
-        + [jax.ShapeDtypeStruct((blocks - 1, heads, width, width), BF16)],
+        in_specs=[smem(), hbm(), hbm()],
+        out_specs=[vmem()] * (COLS + 2),
+        out_shape=[jax.ShapeDtypeStruct((blocks - 1, each, width, width), BF16)] * COLS
+        + [
+            jax.ShapeDtypeStruct((blocks - 1, heads, width, width), BF16),
+            jax.ShapeDtypeStruct((COLS, each, width, width), BF16),
+        ],
         scratch_shapes=[
             pltpu.VMEM(keys.shape, BF16),
             pltpu.VMEM(values.shape, BF16),
-            pltpu.VMEM((rows, width), F32),
-            pltpu.VMEM((rows, width), F32),
             pltpu.VMEM((depth, heads, width, width), F32),
-            pltpu.VMEM((COLS, *quarter), BF16),
             pltpu.SemaphoreType.DMA((blocks,)),
             pltpu.SemaphoreType.DMA((blocks,)),
         ],
@@ -117,7 +125,7 @@
             flops=2 * keys.size * width, bytes_accessed=4 * keys.size + 2 * heads * width * width * blocks, transcendentals=0
         ),
         name="block_sums",
-    )(where, gain, keys, values)
+    )(gain, keys, values)
 
 
 def in_plane(sums, column, weight):
@@ -134,92 +142,72 @@
     return gain_ref[head, depth + bit + 1] * gain_factor(depth + bit + 1, width)
 
 
-def in_order(where_ref, refs, held):
-    for d, ref in enumerate(refs):
-        held[(where_ref[0] & (COLS - 1)) ^ d] = ref[...]
-
-
-def plane_kernel(depth, where_ref, gain_ref, *rest):
-    part_refs, (plane_ref, ends_ref, sums_ref, held) = rest[:COLS], rest[COLS:]
-    blocks, each, width = held.shape[1:4]
+def plane_kernel(depth, where_ref, gain_ref, sums_ref, local_ref, plane_ref, ends_ref):
+    each, width = sums_ref.shape[1], sums_ref.shape[2]
     first = (where_ref[0] & (COLS - 1)) * each
-    in_order(where_ref, part_refs, held)
     for j in range(each):
-        sums = [held[c, 0, j].astype(F32) for c in range(COLS)]
-        plane_ref[j] = functools.reduce(jnp.add, sums).astype(BF16)
+        sums = [sums_ref[c, j].astype(F32) for c in range(COLS)]
+        whole = functools.reduce(jnp.add, sums).astype(BF16)
+        for p in range(plane_ref.shape[0]):
+            plane_ref[p, j] = whole
         before = in_plane(sums, COLS - 1, lambda bit: level_weight(gain_ref, first + j, depth, width, bit))
         ends_ref[0, j] = before.astype(BF16)
-        for b in range(1, blocks):
-            ends_ref[b, j] = (before + held[COLS - 1, b, j].astype(F32)).astype(BF16)
-        for c in range(COLS):
-            sums_ref[c, j] = held[c, 0, j]
-
-
-def plane_sums(where, gain, parts, depth):
-    blocks, *quarter = parts[0].shape
+        for f in range(local_ref.shape[0]):
+            ends_ref[f + 1, j] = (before + local_ref[f, j].astype(F32)).astype(BF16)
+
+
+def plane_sums(where, gain, sums, local, planes, depth):
+    quarter = sums.shape[1:]
     return pl.pallas_call(
         functools.partial(plane_kernel, depth),
-        in_specs=[smem(), smem()] + [vmem()] * COLS,
-        out_specs=[vmem()] * 3,
+        in_specs=[smem(), smem(), vmem(), vmem()],
+        out_specs=[vmem(), vmem()],
         out_shape=[
-            jax.ShapeDtypeStruct(tuple(quarter), BF16),
-            jax.ShapeDtypeStruct((blocks, *quarter), BF16),
-            jax.ShapeDtypeStruct((COLS, *quarter), BF16),
-        ],
-        scratch_shapes=[pltpu.VMEM((COLS, blocks, *quarter), BF16)],
+            jax.ShapeDtypeStruct((planes, *quarter), BF16),
+            jax.ShapeDtypeStruct((local.shape[0] + 1, *quarter), BF16),
+        ],
         compiler_params=params(SMALL_BYTES),
-        cost_estimate=pl.CostEstimate(flops=16 * parts[0].size, bytes_accessed=16 * parts[0].size, transcendentals=0),
+        cost_estimate=pl.CostEstimate(flops=4 * sums.size, bytes_accessed=8 * sums.size, transcendentals=0),
         name="plane_sums",
-    )(where, gain, *parts)
-
-
-def cross_kernel(depth, planes, where_ref, gain_ref, *rest):
-    held, plane_refs = rest[0], rest[1 : 1 + planes]
-    out_refs, (top_ref, states, outs) = rest[1 + planes : 1 + COLS + planes], rest[1 + COLS + planes :]
-    each, width = top_ref.shape[:2]
+    )(where, gain, sums, local)
+
+
+def cross_kernel(depth, where_ref, gain_ref, sums_ref, planes_ref, out_ref, top_ref):
+    each, width = sums_ref.shape[1], sums_ref.shape[2]
+    planes = planes_ref.shape[0]
     col_bits = COLS.bit_length() - 1
     plane = where_ref[0] >> col_bits
-    column = where_ref[0] & (COLS - 1)
-    for d, ref in enumerate(plane_refs):
-        states[plane ^ d] = ref[...]
+    first = (where_ref[0] & (COLS - 1)) * each
     for j in range(each):
-        head = column * each + j
-        sums = [held[c, j].astype(F32) for c in range(COLS)]
+        sums = [sums_ref[c, j].astype(F32) for c in range(COLS)]
         above = jnp.zeros((width, width), F32)
         top = jnp.zeros((width, width), F32)
         for s in range(planes - 1):
-            state = states[s, j].astype(F32)
+            state = planes_ref[s, j].astype(F32)
             share = jnp.float32(0.0)
             for bit in range(planes.bit_length() - 1):
-                weight = level_weight(gain_ref, head, depth, width, col_bits + bit)
-                inside = jnp.logical_and((plane >> bit) & 1 == 1, (plane >> bit) ^ 1 == s >> bit)
-                share = share + jnp.where(inside, weight, 0.0)
+                weight = level_weight(gain_ref, first + j, depth, width, col_bits + bit)
+                held = jnp.logical_and((plane >> bit) & 1 == 1, (plane >> bit) ^ 1 == s >> bit)
+                share = share + jnp.where(held, weight, 0.0)
                 if ((planes - 1) >> bit) ^ 1 == s >> bit:
                     top = top + state * weight
             above = above + state * share
         top_ref[j] = top
         for c in range(COLS):
-            before = in_plane(sums, c, lambda bit: level_weight(gain_ref, head, depth, width, bit))
-            outs[column ^ c, j] = (above if before is None else above + before).astype(BF16)
-    for d in range(COLS):
-        out_refs[d][...] = outs[d]
+            before = in_plane(sums, c, lambda bit: level_weight(gain_ref, first + j, depth, width, bit))
+            out_ref[c, j] = (above if before is None else above + before).astype(BF16)
 
 
 def cross_sums(where, gain, sums, planes, depth):
-    quarter = sums.shape[1:]
     return pl.pallas_call(
-        functools.partial(cross_kernel, depth, len(planes)),
-        in_specs=[smem(), smem()] + [vmem()] * (1 + len(planes)),
-        out_specs=[vmem()] * (COLS + 1),
-        out_shape=[jax.ShapeDtypeStruct(quarter, BF16)] * COLS + [jax.ShapeDtypeStruct(quarter, F32)],
-        scratch_shapes=[
-            pltpu.VMEM((len(planes), *quarter), BF16),
-            pltpu.VMEM((COLS, *quarter), BF16),
-        ],
+        functools.partial(cross_kernel, depth),
+        in_specs=[smem(), smem(), vmem(), vmem()],
+        out_specs=[vmem(), vmem()],
+        out_shape=[jax.ShapeDtypeStruct(sums.shape, BF16), jax.ShapeDtypeStruct(sums.shape[1:], F32)],
         compiler_params=params(SMALL_BYTES),
-        cost_estimate=pl.CostEstimate(flops=15 * sums.size, bytes_accessed=8 * sums.size, transcendentals=0),
+        cost_estimate=pl.CostEstimate(flops=20 * sums.size, bytes_accessed=8 * sums.size, transcendentals=0),
         name="cross_sums",
-    )(where, gain, sums, *planes)
+    )(where, gain, sums, planes)
 
 
 def place(src_ref, wide, dst, start, groups):
@@ -290,11 +278,13 @@
     return join_groups(jnp.concatenate(outs[:half], axis=0), jnp.concatenate(outs[half:], axis=0))
 
 
-def square_sums(full, heads):
-    tokens = full.shape[0] // heads
-    row = lax.broadcasted_iota(jnp.int32, (tokens, full.shape[0]), 1) // heads
-    mine = row == lax.broadcasted_iota(jnp.int32, (tokens, full.shape[0]), 0)
-    sums = jnp.dot(mine.astype(BF16), (full * full).astype(BF16), preferred_element_type=F32)
+def token_rows(tokens, heads):
+    row = lax.broadcasted_iota(jnp.int32, (tokens, tokens * heads), 1) // heads
+    return (row == lax.broadcasted_iota(jnp.int32, (tokens, tokens * heads), 0)).astype(F32).astype(BF16)
+
+
+def square_sums(full, mine):
+    sums = jnp.dot(mine, (full * full).astype(BF16), preferred_element_type=F32)
     ones = jnp.ones((8, full.shape[1]), F32)
     return lax.dot_general(
         ones, sums, (((1,), (1,)), ((), ())), precision=lax.Precision.HIGHEST, preferred_element_type=F32
@@ -463,18 +453,17 @@
     )(where, fork, wq, ck, cv, *kvs)
 
 
-def final_kernel(heads, parts, where_ref, fork_ref, bq_hbm, tq_hbm, *rest):
-    window_hbms, trunk_hbms = rest[:2], rest[2 : 2 + parts]
-    end_hbms, cross_hbms = rest[2 + parts : 2 + parts + COLS], rest[2 + parts + COLS : 2 + parts + 2 * COLS]
-    branch_full, trunk_full, square_ref, qs, ws, ts, nf, of, fs, es, cs = rest[2 + parts + 2 * COLS :][:11]
-    q_sems, w_sems, f_sems, e_sems, c_sems = rest[2 + parts + 2 * COLS :][11:]
+def final_kernel(heads, where_ref, fork_ref, bq_hbm, tq_hbm, near_hbm, far_hbm, trunk_hbm, cross_hbm, *rest):
+    end_hbms, (branch_full, trunk_full, square_ref, qs, ws, ts, fs, es, cs, stacked, mine) = rest[:COLS], rest[COLS : COLS + 11]
+    q_sems, w_sems, f_sems, e_sems = rest[COLS + 11 :]
+    window_hbms = (near_hbm, far_hbm)
     rows = BLK * heads
     branch_blocks, trunk_blocks = ws.shape[0] // rows, ts.shape[0] // rows
     each = heads // COLS
     column = where_ref[0] & (COLS - 1)
     states = [
         pltpu.make_async_copy(end_hbms[i].at[fork_ref[0]], es.at[column ^ i], e_sems.at[i]) for i in range(COLS)
-    ] + [pltpu.make_async_copy(cross_hbms[i], cs.at[column ^ i], c_sems.at[i]) for i in range(COLS)]
+    ] + [pltpu.make_async_copy(cross_hbm, cs, e_sems.at[COLS])]
 
     def query_copy(src, b, slot):
         return pltpu.make_async_copy(src.at[pl.ds(b * rows, rows)], qs.at[pl.ds(slot * rows, rows)], q_sems.at[slot])
@@ -490,40 +479,41 @@
     for copy in states:
         copy.start()
     per_window = branch_blocks // 2
-    per_trunk = trunk_blocks // parts
     for b in range(branch_blocks):
         query_copy(bq_hbm, b, b).start()
         other_copy(window_hbms[b // per_window], b % per_window, ws, b, b).start()
     for b in range(trunk_blocks):
         query_copy(tq_hbm, b, branch_blocks + b).start()
-        other_copy(trunk_hbms[b // per_trunk], b % per_trunk, ts, b, branch_blocks + b).start()
+        other_copy(trunk_hbm, b, ts, b, branch_blocks + b).start()
+    mine[...] = token_rows(BLK, heads)
     for copy in states:
         copy.wait()
-
-    def rest_of(slot, window, states_ref):
+    width = qs.shape[1]
+    for i, held in enumerate((es, cs)):
+        for h in range(heads):
+            m, n = h % COLS, h // COLS
+            stacked[i, m * width : (m + 1) * width, n * width : (n + 1) * width] = held[h // each, h % each]
+
+    def rest_of(slot, window, which):
         at = pl.ds(pl.multiple_of(slot * rows, rows), rows)
-        nf[...] = qs[at, :].astype(F32)
-        for h in range(heads):
-            q = nf[pl.ds(h, BLK, stride=heads), :].astype(BF16)
-            of[pl.ds(h, BLK, stride=heads), :] = jnp.dot(
-                q, states_ref[h // each, h % each], preferred_element_type=F32
-            )
-        full = window.astype(F32) + of[...]
+        both = jnp.dot(masked_copies(qs[at, :], COLS), stacked[which], preferred_element_type=F32)
+        upper = (lax.broadcasted_iota(jnp.int32, (rows, width), 0) & (heads - 1)) < COLS
+        full = window.astype(F32) + jnp.where(upper, both[:, :width], both[:, width:])
         fs[at, :] = full
-        square_ref[slot] = square_sums(full, heads)
+        square_ref[slot] = square_sums(full, mine[...])
 
     def branch_block(b, carry):
         query_copy(bq_hbm, b, b).wait()
         other_copy(window_hbms[0], 0, ws, b, b).wait()
-        rest_of(b, ws[pl.ds(pl.multiple_of(b * rows, rows), rows), :], es)
+        rest_of(b, ws[pl.ds(pl.multiple_of(b * rows, rows), rows), :], 0)
         result_copy(b, branch_full, b).start()
         return carry
 
     def trunk_block(b, carry):
         slot = branch_blocks + b
         query_copy(tq_hbm, b, slot).wait()
-        other_copy(trunk_hbms[0], 0, ts, b, slot).wait()
-        rest_of(slot, ts[pl.ds(pl.multiple_of(b * rows, rows), rows), :], cs)
+        other_copy(trunk_hbm, 0, ts, b, slot).wait()
+        rest_of(slot, ts[pl.ds(pl.multiple_of(b * rows, rows), rows), :], 1)
         result_copy(b, trunk_full, slot).start()
         return carry
 
@@ -535,16 +525,14 @@
         result_copy(b, trunk_full, branch_blocks + b).wait()
 
 
-def final_linear(where, fork, bq, tq, windows, trunks, ends, cross, heads):
+def final_linear(where, fork, bq, tq, near, far, trunk, cross, ends, heads):
     width = bq.shape[1]
     rows = BLK * heads
     total = bq.shape[0] + tq.shape[0]
     blocks = total // rows
-    wide = pltpu.VMEM((rows, width), F32)
-    quarter = cross[0].shape
     return pl.pallas_call(
-        functools.partial(final_kernel, heads, len(trunks)),
-        in_specs=[smem(), smem()] + [hbm()] * (4 + len(trunks) + 2 * COLS),
+        functools.partial(final_kernel, heads),
+        in_specs=[smem(), smem()] + [hbm()] * (6 + COLS),
         out_specs=[hbm(), hbm(), vmem()],
         out_shape=[
             jax.ShapeDtypeStruct(bq.shape, F32),
@@ -555,21 +543,20 @@
             pltpu.VMEM((total, width), BF16),
             pltpu.VMEM(bq.shape, BF16),
             pltpu.VMEM(tq.shape, F32),
-            wide,
-            wide,
             pltpu.VMEM((total, width), F32),
-            pltpu.VMEM((COLS, *quarter), BF16),
-            pltpu.VMEM((COLS, *quarter), BF16),
+            pltpu.VMEM(cross.shape, BF16),
+            pltpu.VMEM(cross.shape, BF16),
+            pltpu.VMEM((2, COLS * width, heads // COLS * width), BF16),
+            pltpu.VMEM((BLK, rows), BF16),
             pltpu.SemaphoreType.DMA((blocks,)),
             pltpu.SemaphoreType.DMA((blocks,)),
             pltpu.SemaphoreType.DMA((blocks,)),
-            pltpu.SemaphoreType.DMA((COLS,)),
-            pltpu.SemaphoreType.DMA((COLS,)),
+            pltpu.SemaphoreType.DMA((COLS + 1,)),
         ],
         compiler_params=params(),
         cost_estimate=pl.CostEstimate(flops=4 * total * width * width, bytes_accessed=8 * total * width, transcendentals=0),
         name="final_linear",
-    )(where, fork, bq, tq, *windows, *trunks, *ends, *cross)
+    )(where, fork, bq, tq, near, far, trunk, cross, *ends)
 
 
 def norm_kernel(heads, features, trunk_hbm, branch_hbm, square_ref, other_ref, trunk_out, branch_out, held, done, in_sems, out_sems):
@@ -690,57 +677,47 @@
     def around(x):
         return [x] + [send(x, [(i, i ^ d) for i in range(count)]) for d in range(1, COLS)]
 
-    def along(x):
-        return [x] + [send(x, [(i, i ^ (d * COLS)) for i in range(count)]) for d in range(1, planes)]
-
-    def swap(parts):
-        return [parts[0]] + [send(parts[d], [(i, i ^ d) for i in range(count)]) for d in range(1, COLS)]
-
+    def in_groups(x, groups_of):
+        return lax.all_to_all(x, "seq", 0, 0, tiled=True, axis_index_groups=groups_of)
+
+    in_one_plane = [[p * COLS + c for c in range(COLS)] for p in range(planes)]
+    in_one_column = [[p * COLS + c for p in range(planes)] for c in range(COLS)]
     tie = lax.optimization_barrier
 
     half = COLS // 2
     got = send(twv, [(root - i, root - i - half) for i in range(half)])
+    *pieces, local, shard_sum = block_sums(level_gain, tk, tv, heads, depth)
+    mine = pieces[COLS - 1]
+    for c in range(COLS - 1):
+        mine = jnp.where(column == c, send(pieces[c], [(root, root - (COLS - 1) + c)]), mine)
+    sums = in_groups(shard_sum, in_one_plane)
+    got, sums = tie((got, sums))
+    kv = down_first(jnp.where(column >= half, twk, got))
+    plane_sum, ends = plane_sums(where, level_gain, sums, mine, planes, depth)
+    plane_sum = in_groups(plane_sum, in_one_column)
+
+    plane_sum, kv, ends, bwq, twk, twv = tie((plane_sum, kv, ends, bwq, twk, twv))
     shift = [(i, i + 1) for i in range(count - 1)]
     pk, pv = send(twk, shift), send(twv, shift)
-    *parts, local = block_sums(where, level_gain, tk, tv, heads, depth)
-
-    bwq, parts, got = tie((bwq, parts, got))
-    kv = jnp.where(column >= half, twk, got)
+    kv, ends = down_rest(kv), down_first(ends)
     far = far_attention(bwq, bwk, bwv, heads, groups)
-    parts = swap(parts)
-    kv = down_first(kv)
-    parts, kv, far, pk, pv = tie((parts, kv, far, pk, pv))
-    plane_sum, ends, sums = plane_sums(where, level_gain, parts, depth)
-
-    blocks = tokens // BLK
-    first = blocks // 2
-
-    def trunk_part(start, steps):
-        return trunk_attention(
-            where, level_gain, tq, tk, tv, twq, pk, pv, twk, twv, local, heads, groups, start, steps
-        )
-
-    twq, plane_sum, ends = tie((twq, plane_sum, ends))
-    trunk_a = trunk_part(0, first)
-    plane_list = along(plane_sum)
-    kv = down_rest(kv)
-    ends = down_first(ends)
-    plane_list, kv, ends, trunk_a, twq = tie((plane_list, kv, ends, trunk_a, twq))
-    *cross, above = cross_sums(where, level_gain, sums, plane_list, depth)
-
-    twq, cross = tie((twq, cross))
-    trunk_b = trunk_part(first, blocks - first)
+    kv, ends, far, pk, pv, plane_sum = tie((kv, ends, far, pk, pv, plane_sum))
+
+    cross, above = cross_sums(where, level_gain, sums, plane_sum, depth)
+    cross = in_groups(cross, in_one_plane)
+    cross, twq, kv = tie((cross, twq, kv))
     kvs = around(kv)
     ends = down_rest(ends)
-    kvs, ends, trunk_b, bwq = tie((kvs, ends, trunk_b, bwq))
+    trunk = trunk_attention(
+        where, level_gain, tq, tk, tv, twq, pk, pv, twk, twv, local, heads, groups, 0, tokens // BLK
+    )
+    kvs, ends, trunk, bwq = tie((kvs, ends, trunk, bwq))
     ends = (ends.astype(F32) + above).astype(BF16)
-
     bwq, ends = tie((bwq, ends))
     near = near_attention(where, fork_block, bwq, bwk, bwv, kvs, heads, groups)
     ends = around(ends)
-    cross = swap(cross)
     branch_full, trunk_full, square = final_linear(
-        where, fork_block, bq, tq, (near, far), (trunk_a, trunk_b), ends, cross, heads
+        where, fork_block, bq, tq, near, far, trunk, cross, ends, heads
     )
     other = lax.ppermute(square, "head", [(0, 1), (1, 0)])
     trunk_out, branch_out = normalize(trunk_full, branch_full, square, other, heads, features)

time: 123 us -> 127 us (1.033)
  the two profiles are of different devices: /device:TPU:29 before, /device:TPU:0 now
where the time goes in v5:
time: 127 us; the launch traced here: 126 us
  Pallas kernels  57 us (45%)
  starting transfers between devices  44.8 us (35%)
  waiting for transfers between devices  20.7 us (16%)
  between operations  1.68 us (1%)
  local copies, waits for them, and re-layouts  1.54 us (1%)
    all_to_all x3, starting transfers between devices, in_groups(): lax.all_to_all(x, 'seq', 0, 0, tiled=True, axis_index_groups=groups_of)  28.3 us
    all_to_all x3, waiting for transfers between devices, in_groups(): lax.all_to_all(x, 'seq', 0, 0, tiled=True, axis_index_groups=groups_of)  18.5 us
    pallas_call x1, Pallas kernels, final_linear(): pl.pallas_call(functools.partial(final_kernel, heads), in_specs=[smem(),...  16.9 us
    ppermute x16, starting transfers between devices, send(): return lax.ppermute(x, 'seq', pairs)  16.4 us
    pallas_call x1, Pallas kernels, trunk_attention(): pl.pallas_call(functools.partial(trunk_kernel, heads, groups, first), gri...  10.4 us
    pallas_call x1, Pallas kernels, near_attention(): pl.pallas_call(functools.partial(near_kernel, groups), grid=(steps,), in_...  8.48 us
    pallas_call x1, Pallas kernels, far_attention(): pl.pallas_call(functools.partial(far_kernel, heads, groups), grid=(steps,...  8.09 us
    pallas_call x1, Pallas kernels, normalize(): pl.pallas_call(functools.partial(norm_kernel, heads, features), in_specs=...  5.41 us
  transfers between devices with their start and end apart: 20, of which 5 were waited for; matrix products, arithmetic and copies ran while one was open for 0% of the time, Pallas kernels for 26%

profile of v5, /device:TPU:0, one launch (start us, length us, event | category | flops | bytes accessed | tf_op | source)
XLA Modules:
  0.0 126.0 jit_solution(14605794762011536117)
XLA Ops:
  0.6 0.0 copy-start.6
  0.6 0.8 collective-permute-start
  1.5 0.0 copy-start
  1.5 5.0 %block_sums.1 = (bf16[3,2,128,128]{3,2,1,0:T(8,128)(2,1)}, bf16[3,2,128,128]{3,2,1,0:T(8,128)(2,1)}, bf16[3,2,128,128]{3,2,1,0:T(8,128)(2,1)}, bf16[3,2,128,128]...) custom-call(f32[8,11]{1,0:T(8,128)} %gain_ref.7, bf16[4096,128]{1,0:T(8,128)(2,1)} %bitcast.16, ...), custom_call_target="tpu_custom_call" | custom-call | flops 134217728 | bytes 3145728 | tf_op jit(solution)/shard_map/block_sums/pallas_call | solution.py:107
  6.5 0.0 copy-start.9
  6.5 5.3 %all-to-all-start = ((bf16[4,2,128,128]{3,2,1,0:T(8,128)(2,1)}), bf16[4,2,128,128]{3,2,1,0:T(8,128)(2,1)S(1)}, u32[]{:S(2)}, u32[]{:S(2)}) async-start(bf16[4,2,128,128]{3,2,1,0:T(8,128)(2,1)} %get-tuple-element.43), calls=%async_computation | async-start | bytes 524288 | tf_op jit(solution)/shard_map/all_to_all | solution.py:681
  11.8 0.7 collective-permute-start.1
  12.5 0.7 collective-permute-start.2
  13.2 0.7 collective-permute-start.3
  13.9 3.3 %all-to-all-done.sums_ref = bf16[4,2,128,128]{3,2,1,0:T(8,128)(2,1)S(1)} async-done(((bf16[4,2,128,128]{3,2,1,0:T(8,128)(2,1)}), bf16[4,2,128,128]{3,2,1,0:T(8,128)(2,1)S(1)}, u32[]{:S(2)}, u32[]{:S(2)}) %all-to-all-start) | async-done | bytes 262176 | tf_op jit(solution)/shard_map/all_to_all | solution.py:681
  17.2 0.0 collective-permute-done
  17.2 0.0 copy-done.6
  17.2 0.7 collective-permute-start.4
  17.9 0.0 collective-permute-done.1
  17.9 0.0 collective-permute-done.2
  17.9 0.0 collective-permute-done.3
  18.0 0.1 select_select_fusion.local_ref
  18.0 0.0 copy-done
  18.0 1.3 %plane_sums.1 = (bf16[4,2,128,128]{3,2,1,0:T(8,128)(2,1)}, bf16[4,2,128,128]{3,2,1,0:T(8,128)(2,1)S(1)}) custom-call(s32[1]{0:T(128)} %bitcast.where_ref, f32[8,11]{1,0:T(8,128)S(1)} %copy-done, bf16[4,2,128,128]{3,2,1,0:T(8,128)(2,1)S(1)} %all-to-all-done.sums_ref, bf16[3,2,128,128]{3,2,1,0:T(8,128)(2,1)S(1)} %select_select_fusion.local_ref), custom_call_target="tpu_custom_call" | custom-call | flops 524288 | bytes 1048576 | tf_op jit(solution)/shard_map/plane_sums/pallas_call | solution.py:161
  19.4 15.0 %all-to-all-start.1 = ((bf16[4,2,128,128]{3,2,1,0:T(8,128)(2,1)}), bf16[4,2,128,128]{3,2,1,0:T(8,128)(2,1)S(1)}, u32[]{:S(2)}, u32[]{:S(2)}) async-start(bf16[4,2,128,128]{3,2,1,0:T(8,128)(2,1)} %get-tuple-element.49), calls=%async_computation.1 | async-start | bytes 524288 | tf_op jit(solution)/shard_map/all_to_all | solution.py:681
  34.4 0.0 collective-permute-done.4
  34.4 8.1 %all-to-all-done.1.planes_ref = bf16[4,2,128,128]{3,2,1,0:T(8,128)(2,1)S(1)} async-done(((bf16[4,2,128,128]{3,2,1,0:T(8,128)(2,1)}), bf16[4,2,128,128]{3,2,1,0:T(8,128)(2,1)S(1)}, u32[]{:S(2)}, u32[]{:S(2)}) %all-to-all-start.1) | async-done | bytes 262176 | tf_op jit(solution)/shard_map/all_to_all | solution.py:681
  42.5 0.7 collective-permute-start.6
  43.2 1.3 %collective-permute-start.5 = (bf16[1024,128]{1,0:T(8,128)(2,1)S(1)}, bf16[1024,128]{1,0:T(8,128)(2,1)S(1)}, u32[]{:S(2)}, u32[]{:S(2)}) collective-permute-start(bf16[1024,128]{1,0:T(8,128)(2,1)S(1)} %broadcast_select_fusion.3), channel_id=1, source_target_pairs={{8,0},{10,2},{12,4},{14,6},{24,16},{26,18},{28,20},{30,22},{9,1},{... | collective-permute-start | bytes 786440 | tf_op jit(solution)/shard_map/ppermute | solution.py:658
  44.5 1.3 %collective-permute-start.7 = (bf16[1024,128]{1,0:T(8,128)(2,1)S(1)}, bf16[1024,128]{1,0:T(8,128)(2,1)S(1)}, u32[]{:S(2)}, u32[]{:S(2)}) collective-permute-start(bf16[1024,128]{1,0:T(8,128)(2,1)S(1)} %bitcast.22), channel_id=1, source_target_pairs={{0,2},{2,4},{4,6},{6,8},{8,10},{10,12},{12,14},{14,16},{16,18},{18... | collective-permute-start | bytes 786440 | tf_op jit(solution)/shard_map/ppermute | solution.py:658
  45.8 0.0 copy-done.9
  45.9 1.3 %collective-permute-start.8 = (bf16[1024,128]{1,0:T(8,128)(2,1)S(1)}, bf16[1024,128]{1,0:T(8,128)(2,1)S(1)}, u32[]{:S(2)}, u32[]{:S(2)}) collective-permute-start(bf16[1024,128]{1,0:T(8,128)(2,1)S(1)} %bitcast.36), channel_id=1, source_target_pairs={{0,2},{2,4},{4,6},{6,8},{8,10},{10,12},{12,14},{14,16},{16,18},{18... | collective-permute-start | bytes 786440 | tf_op jit(solution)/shard_map/ppermute | solution.py:658
  47.2 8.1 %far_attention.1.far_hbm = bf16[4096,128]{1,0:T(8,128)(2,1)} custom-call(bf16[8192,128]{1,0:T(8,128)(2,1)} %bitcast.23, bf16[2048,128]{1,0:T(8,128)(2,1)} %bitcast.28, bf16[2048,128]{1,0:T(8,128)(2,1)} %bitcast.31, bf16[2048,128]{1,0:T(8,128)(2,1)} %bitcast.29, bf16[2048,128]{1,0:T(8,128)(2,1)} %bitcast.32), custom_call_target="tpu_custom_call" | custom-call | flops 2013265920 | bytes 6291456 | tf_op jit(solution)/shard_map/far_attention/pallas_call | solution.py:324
  55.3 0.0 collective-permute-done.6
  55.3 0.0 collective-permute-done.5
  55.4 0.0 collective-permute-done.7.pk_ref
  55.4 0.0 copy-start.10
  55.4 0.0 collective-permute-done.8.pv_ref
  55.4 1.4 %cross_sums.1 = (bf16[4,2,128,128]{3,2,1,0:T(8,128)(2,1)}, f32[2,128,128]{2,1,0:T(8,128)S(1)}) custom-call(s32[1]{0:T(128)} %bitcast.where_ref, f32[8,11]{1,0:T(8,128)S(1)} %copy-done, bf16[4,2,128,128]{3,2,1,0:T(8,128)(2,1)S(1)} %all-to-all-done.sums_ref, bf16[4,2,128,128]{3,2,1,0:T(8,128)(2,1)S(1)} %all-to-all-done.1.planes_ref), custom_call_target="tpu_custom_call" | custom-call | flops 2621440 | bytes 1048576 | tf_op jit(solution)/shard_map/cross_sums/pallas_call | solution.py:202
  56.8 8.1 %all-to-all-start.2 = ((bf16[4,2,128,128]{3,2,1,0:T(8,128)(2,1)}), bf16[4,2,128,128]{3,2,1,0:T(8,128)(2,1)S(1)}, u32[]{:S(2)}, u32[]{:S(2)}) async-start(bf16[4,2,128,128]{3,2,1,0:T(8,128)(2,1)} %get-tuple-element.59), calls=%async_computation.2 | async-start | bytes 524288 | tf_op jit(solution)/shard_map/all_to_all | solution.py:681
  64.9 1.3 %collective-permute-start.12 = (bf16[4,2,128,128]{3,2,1,0:T(8,128)(2,1)S(1)}, bf16[4,2,128,128]{3,2,1,0:T(8,128)(2,1)S(1)}, u32[]{:S(2)}, u32[]{:S(2)}) collective-permute-start(bf16[4,2,128,128]{3,2,1,0:T(8,128)(2,1)S(1)} %broadcast_select_fusion.1), channel_id=1, source_target_pairs={{8,0},{10,2},{12,4},{14,6},{24,16},{26,18},{28,20},{30,22},{9,1},{... | collective-permute-start | bytes 786440 | tf_op jit(solution)/shard_map/ppermute | solution.py:658
  66.1 7.0 %all-to-all-done.2.cross_hbm = bf16[4,2,128,128]{3,2,1,0:T(8,128)(2,1)S(1)} async-done(((bf16[4,2,128,128]{3,2,1,0:T(8,128)(2,1)}), bf16[4,2,128,128]{3,2,1,0:T(8,128)(2,1)S(1)}, u32[]{:S(2)}, u32[]{:S(2)}) %all-to-all-start.2) | async-done | bytes 262176 | tf_op jit(solution)/shard_map/all_to_all | solution.py:681
  73.2 1.0 collective-permute-start.11
  74.2 1.9 %collective-permute-start.10 = (bf16[1024,128]{1,0:T(8,128)(2,1)S(1)}, bf16[1024,128]{1,0:T(8,128)(2,1)S(1)}, u32[]{:S(2)}, u32[]{:S(2)}) collective-permute-start(bf16[1024,128]{1,0:T(8,128)(2,1)S(1)} %broadcast_select_fusion.4.rest_0_), channel_id=1, source_target_pairs={{0,4},{2,6},{4,0},{6,2},{8,12},{10,14},{12,8},{14,10},{16,20},{18,... | collective-permute-start | bytes 786440 | tf_op jit(solution)/shard_map/ppermute | solution.py:658
  76.1 0.6 collective-permute-start.9
  76.7 0.0 copy-done.10
  76.7 10.4 %trunk_attention_0.1.trunk_hbm = f32[4096,128]{1,0:T(8,128)} custom-call(s32[1]{0:T(128)} %bitcast.where_ref, f32[8,11]{1,0:T(8,128)} %gain_ref.7, bf16[4096,128]{1,0:T(8,128)(2,1)} %bitcast.14, bf16[4096,128]{1,0:T(8,128)(2,1)} %bitcast.17, bf16[4096,128]{1,0:T(8,128)(2,1)} %bitcast.19, bf16[4096,128]{1,0:T(8,128)(2,1)} %bitcast.26, ...), custom_call_target="tpu_custom_call" | custom-call | flops 2415919104 | bytes 6291456 | tf_op jit(solution)/shard_map/trunk_attention_0/pallas_call | solution.py:388
  87.1 0.0 copy-done.1
  87.1 0.0 collective-permute-done.12
  87.1 0.0 collective-permute-done.11.rest_3_
  87.1 0.7 collective-permute-done.10.rest_2_
  87.8 0.0 collective-permute-done.9.rest_1_
  87.8 0.1 add_convert_fusion.rest_0_
  87.9 0.6 collective-permute-start.15
  88.5 1.7 %collective-permute-start.14 = (bf16[4,2,128,128]{3,2,1,0:T(8,128)(2,1)S(1)}, bf16[4,2,128,128]{3,2,1,0:T(8,128)(2,1)S(1)}, u32[]{:S(2)}, u32[]{:S(2)}) collective-permute-start(bf16[4,2,128,128]{3,2,1,0:T(8,128)(2,1)S(1)} %add_convert_fusion.rest_0_), channel_id=1, source_target_pairs={{0,4},{2,6},{4,0},{6,2},{8,12},{10,14},{12,8},{14,10},{16,20},{18,... | collective-permute-start | bytes 786440 | tf_op jit(solution)/shard_map/ppermute | solution.py:658
  90.2 1.3 collective-permute-start.13
  92.1 8.5 %near_attention.1.near_hbm = bf16[4096,128]{1,0:T(8,128)(2,1)} custom-call(s32[1]{0:T(128)} %bitcast.where_ref, s32[1]{0:T(128)S(6)} %copy.14.fork_ref, bf16[8192,128]{1,0:T(8,128)(2,1)} %bitcast.24, bf16[2048,128]{1,0:T(8,128)(2,1)} %bitcast.30, bf16[2048,128]{1,0:T(8,128)(2,1)} %bitcast.33, bf16[1024,128]{1,0:T(8,128)(2,1)} %copy-done.7, ...), custom_call_target="tpu_custom_call" | custom-call | flops 2013265920 | bytes 6291456 | tf_op jit(solution)/shard_map/near_attention/pallas_call | solution.py:438
  100.6 0.0 collective-permute-done.15.rest_3_
  100.6 0.0 collective-permute-done.14.rest_2_
  100.7 0.0 collective-permute-done.13.rest_1_
  100.7 0.0 copy-start.5
  100.7 0.7 copy-done.3
  101.4 0.1 copy-done.4
  101.5 0.1 copy-done.5
  101.6 16.9 %final_linear.1 = (f32[8192,128]{1,0:T(8,128)}, f32[4096,128]{1,0:T(8,128)}, f32[12,8,128]{2,1,0:T(8,128)}) custom-call(s32[1]{0:T(128)} %bitcast.where_ref, s32[1]{0:T(128)S(6)} %copy.14.fork_ref, bf16[8192,128]{1,0:T(8,128)(2,1)} %bitcast.13, bf16[4096,128]{1,0:T(8,128)(2,1)} %bitcast.15, bf16[4096,128]{1,0:T(8,128)(2,1)} %near_attention.1.near_hbm, ...), custom_call_target="tpu_custom_call" | custom-call | flops 805306368 | bytes 12582912 | tf_op jit(solution)/shard_map/final_linear/pallas_call | solution.py:533
  118.4 0.1 collective-permute-start.16
  118.5 1.4 %collective-permute-done.16.other_ref = f32[12,8,128]{2,1,0:T(8,128)S(1)} collective-permute-done((f32[12,8,128]{2,1,0:T(8,128)}, f32[12,8,128]{2,1,0:T(8,128)S(1)}, u32[]{:S(2)}, u32[]{:S(2)}) %collective-permute-start.16) | collective-permute-done | bytes 49184 | tf_op jit(solution)/shard_map/ppermute | solution.py:722
  119.9 0.6 copy-done.8
  120.5 5.4 %normalize.1 = (bf16[4096,128]{1,0:T(8,128)(2,1)}, bf16[8192,128]{1,0:T(8,128)(2,1)}) custom-call(f32[4096,128]{1,0:T(8,128)} %get-tuple-element.79.trunk_hbm, f32[8192,128]{1,0:T(8,128)} %get-tuple-element.80.branch_hbm, f32[12,8,128]{2,1,0:T(8,128)} %get-tuple-element.81.square_ref, f32[12,8,128]{2,1,0:T(8,128)} %copy-done.8), custom_call_target="tpu_custom_call" | custom-call | flops 3145728 | bytes 9437184 | tf_op jit(solution)/shard_map/normalize/pallas_call | solution.py:605
  (21 shorter events, 0.2 us)
Async XLA Ops:
  0.6 16.6 %copy-start.6 = (bf16[512,2,128]{2,1,0:T(2,128)(2,1)S(1)}, bf16[512,2,128]{2,1,0:T(2,128)(2,1)}, u32[]{:S(2)}) copy-start(bf16[512,2,128]{2,1,0:T(2,128)(2,1)} %param.16) | copy-start | bytes 786436
  0.6 16.6 %collective-permute-start = (bf16[1024,128]{1,0:T(8,128)(2,1)}, bf16[1024,128]{1,0:T(8,128)(2,1)S(1)}, u32[]{:S(2)}, u32[]{:S(2)}) collective-permute-start(bf16[1024,128]{1,0:T(8,128)(2,1)} %bitcast.34), channel_id=1, source_target_pairs={{30,26},{28,24},{31,27},{29,25}} | collective-permute-start | bytes 786440 | tf_op jit(solution)/shard_map/ppermute | solution.py:658
  1.5 16.6 %copy-start = (f32[8,11]{1,0:T(8,128)S(1)}, f32[8,11]{1,0:T(8,128)}, u32[]{:S(2)}) copy-start(f32[8,11]{1,0:T(8,128)} %gain_ref.7) | copy-start | bytes 1060
  6.5 39.3 %copy-start.9 = (bf16[512,2,128]{2,1,0:T(2,128)(2,1)S(1)}, bf16[512,2,128]{2,1,0:T(2,128)(2,1)}, u32[]{:S(2)}) copy-start(bf16[512,2,128]{2,1,0:T(2,128)(2,1)} %param.17) | copy-start | bytes 786436
  6.5 10.7 %all-to-all-start = ((bf16[4,2,128,128]{3,2,1,0:T(8,128)(2,1)}), bf16[4,2,128,128]{3,2,1,0:T(8,128)(2,1)S(1)}, u32[]{:S(2)}, u32[]{:S(2)}) async-start(bf16[4,2,128,128]{3,2,1,0:T(8,128)(2,1)} %get-tuple-element.43), calls=%async_computation | async-start | bytes 524288 | tf_op jit(solution)/shard_map/all_to_all | solution.py:681
  11.8 6.1 %collective-permute-start.1 = (bf16[3,2,128,128]{3,2,1,0:T(8,128)(2,1)}, bf16[3,2,128,128]{3,2,1,0:T(8,128)(2,1)S(1)}, u32[]{:S(2)}, u32[]{:S(2)}) collective-permute-start(bf16[3,2,128,128]{3,2,1,0:T(8,128)(2,1)} %get-tuple-element.45), channel_id=1, source_target_pairs={{30,28},{31,29}} | collective-permute-start | bytes 589832 | tf_op jit(solution)/shard_map/ppermute | solution.py:658
  12.5 5.4 %collective-permute-start.2 = (bf16[3,2,128,128]{3,2,1,0:T(8,128)(2,1)}, bf16[3,2,128,128]{3,2,1,0:T(8,128)(2,1)S(1)}, u32[]{:S(2)}, u32[]{:S(2)}) collective-permute-start(bf16[3,2,128,128]{3,2,1,0:T(8,128)(2,1)} %get-tuple-element.46), channel_id=1, source_target_pairs={{30,26},{31,27}} | collective-permute-start | bytes 589832 | tf_op jit(solution)/shard_map/ppermute | solution.py:658
  13.2 4.8 %collective-permute-start.3 = (bf16[3,2,128,128]{3,2,1,0:T(8,128)(2,1)}, bf16[3,2,128,128]{3,2,1,0:T(8,128)(2,1)S(1)}, u32[]{:S(2)}, u32[]{:S(2)}) collective-permute-start(bf16[3,2,128,128]{3,2,1,0:T(8,128)(2,1)} %get-tuple-element.47), channel_id=1, source_target_pairs={{30,24},{31,25}} | collective-permute-start | bytes 589832 | tf_op jit(solution)/shard_map/ppermute | solution.py:658
  17.2 17.1 %collective-permute-start.4 = (bf16[1024,128]{1,0:T(8,128)(2,1)S(1)}, bf16[1024,128]{1,0:T(8,128)(2,1)S(1)}, u32[]{:S(2)}, u32[]{:S(2)}) collective-permute-start(bf16[1024,128]{1,0:T(8,128)(2,1)S(1)} %broadcast_select_fusion.2), channel_id=1, source_target_pairs={{24,8},{26,10},{28,12},{30,14},{25,9},{27,11},{29,13},{31,15}} | collective-permute-start | bytes 786440 | tf_op jit(solution)/shard_map/ppermute | solution.py:658
  19.4 23.2 %all-to-all-start.1 = ((bf16[4,2,128,128]{3,2,1,0:T(8,128)(2,1)}), bf16[4,2,128,128]{3,2,1,0:T(8,128)(2,1)S(1)}, u32[]{:S(2)}, u32[]{:S(2)}) async-start(bf16[4,2,128,128]{3,2,1,0:T(8,128)(2,1)} %get-tuple-element.49), calls=%async_computation.1 | async-start | bytes 524288 | tf_op jit(solution)/shard_map/all_to_all | solution.py:681
  42.5 12.7 %collective-permute-start.6 = (bf16[4,2,128,128]{3,2,1,0:T(8,128)(2,1)S(1)}, bf16[4,2,128,128]{3,2,1,0:T(8,128)(2,1)S(1)}, u32[]{:S(2)}, u32[]{:S(2)}) collective-permute-start(bf16[4,2,128,128]{3,2,1,0:T(8,128)(2,1)S(1)} %get-tuple-element.53), channel_id=1, source_target_pairs={{24,8},{26,10},{28,12},{30,14},{25,9},{27,11},{29,13},{31,15}} | collective-permute-start | bytes 786440 | tf_op jit(solution)/shard_map/ppermute | solution.py:658
  43.2 12.1 %collective-permute-start.5 = (bf16[1024,128]{1,0:T(8,128)(2,1)S(1)}, bf16[1024,128]{1,0:T(8,128)(2,1)S(1)}, u32[]{:S(2)}, u32[]{:S(2)}) collective-permute-start(bf16[1024,128]{1,0:T(8,128)(2,1)S(1)} %broadcast_select_fusion.3), channel_id=1, source_target_pairs={{8,0},{10,2},{12,4},{14,6},{24,16},{26,18},{28,20},{30,22},{9,1},{... | collective-permute-start | bytes 786440 | tf_op jit(solution)/shard_map/ppermute | solution.py:658
  44.5 10.8 %collective-permute-start.7 = (bf16[1024,128]{1,0:T(8,128)(2,1)S(1)}, bf16[1024,128]{1,0:T(8,128)(2,1)S(1)}, u32[]{:S(2)}, u32[]{:S(2)}) collective-permute-start(bf16[1024,128]{1,0:T(8,128)(2,1)S(1)} %bitcast.22), channel_id=1, source_target_pairs={{0,2},{2,4},{4,6},{6,8},{8,10},{10,12},{12,14},{14,16},{16,18},{18... | collective-permute-start | bytes 786440 | tf_op jit(solution)/shard_map/ppermute | solution.py:658
  45.9 9.5 %collective-permute-start.8 = (bf16[1024,128]{1,0:T(8,128)(2,1)S(1)}, bf16[1024,128]{1,0:T(8,128)(2,1)S(1)}, u32[]{:S(2)}, u32[]{:S(2)}) collective-permute-start(bf16[1024,128]{1,0:T(8,128)(2,1)S(1)} %bitcast.36), channel_id=1, source_target_pairs={{0,2},{2,4},{4,6},{6,8},{8,10},{10,12},{12,14},{14,16},{16,18},{18... | collective-permute-start | bytes 786440 | tf_op jit(solution)/shard_map/ppermute | solution.py:658
  55.3 31.7 %copy-start.7 = (bf16[1024,128]{1,0:T(8,128)(2,1)}, bf16[1024,128]{1,0:T(8,128)(2,1)S(1)}, u32[]{:S(2)}) copy-start(bf16[1024,128]{1,0:T(8,128)(2,1)S(1)} %broadcast_select_fusion.4.rest_0_) | copy-start | bytes 786436
  55.4 21.3 %copy-start.10 = (bf16[1024,128]{1,0:T(8,128)(2,1)}, bf16[1024,128]{1,0:T(8,128)(2,1)S(1)}, u32[]{:S(2)}) copy-start(bf16[1024,128]{1,0:T(8,128)(2,1)S(1)} %collective-permute-done.7.pk_ref) | copy-start | bytes 786436
  55.4 21.3 %copy-start.11 = (bf16[1024,128]{1,0:T(8,128)(2,1)}, bf16[1024,128]{1,0:T(8,128)(2,1)S(1)}, u32[]{:S(2)}) copy-start(bf16[1024,128]{1,0:T(8,128)(2,1)S(1)} %collective-permute-done.8.pv_ref) | copy-start | bytes 786436
  56.8 16.4 %all-to-all-start.2 = ((bf16[4,2,128,128]{3,2,1,0:T(8,128)(2,1)}), bf16[4,2,128,128]{3,2,1,0:T(8,128)(2,1)S(1)}, u32[]{:S(2)}, u32[]{:S(2)}) async-start(bf16[4,2,128,128]{3,2,1,0:T(8,128)(2,1)} %get-tuple-element.59), calls=%async_computation.2 | async-start | bytes 524288 | tf_op jit(solution)/shard_map/all_to_all | solution.py:681
  64.9 22.2 %collective-permute-start.12 = (bf16[4,2,128,128]{3,2,1,0:T(8,128)(2,1)S(1)}, bf16[4,2,128,128]{3,2,1,0:T(8,128)(2,1)S(1)}, u32[]{:S(2)}, u32[]{:S(2)}) collective-permute-start(bf16[4,2,128,128]{3,2,1,0:T(8,128)(2,1)S(1)} %broadcast_select_fusion.1), channel_id=1, source_target_pairs={{8,0},{10,2},{12,4},{14,6},{24,16},{26,18},{28,20},{30,22},{9,1},{... | collective-permute-start | bytes 786440 | tf_op jit(solution)/shard_map/ppermute | solution.py:658
  73.2 13.9 %copy-start.1 = (bf16[4,2,128,128]{3,2,1,0:T(8,128)(2,1)}, bf16[4,2,128,128]{3,2,1,0:T(8,128)(2,1)S(1)}, u32[]{:S(2)}) copy-start(bf16[4,2,128,128]{3,2,1,0:T(8,128)(2,1)S(1)} %all-to-all-done.2.cross_hbm) | copy-start | bytes 786436
  73.2 13.9 %collective-permute-start.11 = (bf16[1024,128]{1,0:T(8,128)(2,1)S(1)}, bf16[1024,128]{1,0:T(8,128)(2,1)S(1)}, u32[]{:S(2)}, u32[]{:S(2)}) collective-permute-start(bf16[1024,128]{1,0:T(8,128)(2,1)S(1)} %broadcast_select_fusion.4.rest_0_), channel_id=1, source_target_pairs={{0,6},{2,4},{4,2},{6,0},{8,14},{10,12},{12,10},{14,8},{16,22},{18,... | collective-permute-start | bytes 786440 | tf_op jit(solution)/shard_map/ppermute | solution.py:658
  74.2 13.6 %collective-permute-start.10 = (bf16[1024,128]{1,0:T(8,128)(2,1)S(1)}, bf16[1024,128]{1,0:T(8,128)(2,1)S(1)}, u32[]{:S(2)}, u32[]{:S(2)}) collective-permute-start(bf16[1024,128]{1,0:T(8,128)(2,1)S(1)} %broadcast_select_fusion.4.rest_0_), channel_id=1, source_target_pairs={{0,4},{2,6},{4,0},{6,2},{8,12},{10,14},{12,8},{14,10},{16,20},{18,... | collective-permute-start | bytes 786440 | tf_op jit(solution)/shard_map/ppermute | solution.py:658
  76.1 11.8 %collective-permute-start.9 = (bf16[1024,128]{1,0:T(8,128)(2,1)S(1)}, bf16[1024,128]{1,0:T(8,128)(2,1)S(1)}, u32[]{:S(2)}, u32[]{:S(2)}) collective-permute-start(bf16[1024,128]{1,0:T(8,128)(2,1)S(1)} %broadcast_select_fusion.4.rest_0_), channel_id=1, source_target_pairs={{0,2},{2,0},{4,6},{6,4},{8,10},{10,8},{12,14},{14,12},{16,18},{18,... | collective-permute-start | bytes 786440 | tf_op jit(solution)/shard_map/ppermute | solution.py:658
  87.1 5.0 %copy-start.12 = (bf16[1024,128]{1,0:T(8,128)(2,1)}, bf16[1024,128]{1,0:T(8,128)(2,1)S(1)}, u32[]{:S(2)}) copy-start(bf16[1024,128]{1,0:T(8,128)(2,1)S(1)} %collective-permute-done.11.rest_3_) | copy-start | bytes 786436
  87.8 4.3 %copy-start.13 = (bf16[1024,128]{1,0:T(8,128)(2,1)}, bf16[1024,128]{1,0:T(8,128)(2,1)S(1)}, u32[]{:S(2)}) copy-start(bf16[1024,128]{1,0:T(8,128)(2,1)S(1)} %collective-permute-done.10.rest_2_) | copy-start | bytes 786436
  87.8 4.3 %copy-start.14 = (bf16[1024,128]{1,0:T(8,128)(2,1)}, bf16[1024,128]{1,0:T(8,128)(2,1)S(1)}, u32[]{:S(2)}) copy-start(bf16[1024,128]{1,0:T(8,128)(2,1)S(1)} %collective-permute-done.9.rest_1_) | copy-start | bytes 786436
  87.9 12.7 %copy-start.2 = (bf16[4,2,128,128]{3,2,1,0:T(8,128)(2,1)}, bf16[4,2,128,128]{3,2,1,0:T(8,128)(2,1)S(1)}, u32[]{:S(2)}) copy-start(bf16[4,2,128,128]{3,2,1,0:T(8,128)(2,1)S(1)} %add_convert_fusion.rest_0_) | copy-start | bytes 786436
  87.9 12.7 %collective-permute-start.15 = (bf16[4,2,128,128]{3,2,1,0:T(8,128)(2,1)S(1)}, bf16[4,2,128,128]{3,2,1,0:T(8,128)(2,1)S(1)}, u32[]{:S(2)}, u32[]{:S(2)}) collective-permute-start(bf16[4,2,128,128]{3,2,1,0:T(8,128)(2,1)S(1)} %add_convert_fusion.rest_0_), channel_id=1, source_target_pairs={{0,6},{2,4},{4,2},{6,0},{8,14},{10,12},{12,10},{14,8},{16,22},{18,... | collective-permute-start | bytes 786440 | tf_op jit(solution)/shard_map/ppermute | solution.py:658
  88.5 12.1 %collective-permute-start.14 = (bf16[4,2,128,128]{3,2,1,0:T(8,128)(2,1)S(1)}, bf16[4,2,128,128]{3,2,1,0:T(8,128)(2,1)S(1)}, u32[]{:S(2)}, u32[]{:S(2)}) collective-permute-start(bf16[4,2,128,128]{3,2,1,0:T(8,128)(2,1)S(1)} %add_convert_fusion.rest_0_), channel_id=1, source_target_pairs={{0,4},{2,6},{4,0},{6,2},{8,12},{10,14},{12,8},{14,10},{16,20},{18,... | collective-permute-start | bytes 786440 | tf_op jit(solution)/shard_map/ppermute | solution.py:658
  90.2 10.5 %collective-permute-start.13 = (bf16[4,2,128,128]{3,2,1,0:T(8,128)(2,1)S(1)}, bf16[4,2,128,128]{3,2,1,0:T(8,128)(2,1)S(1)}, u32[]{:S(2)}, u32[]{:S(2)}) collective-permute-start(bf16[4,2,128,128]{3,2,1,0:T(8,128)(2,1)S(1)} %add_convert_fusion.rest_0_), channel_id=1, source_target_pairs={{0,2},{2,0},{4,6},{6,4},{8,10},{10,8},{12,14},{14,12},{16,18},{18,... | collective-permute-start | bytes 786440 | tf_op jit(solution)/shard_map/ppermute | solution.py:658
  100.6 0.7 copy-start.3
  100.7 0.8 copy-start.4
  100.7 0.9 copy-start.5
  118.4 1.5 %collective-permute-start.16 = (f32[12,8,128]{2,1,0:T(8,128)}, f32[12,8,128]{2,1,0:T(8,128)S(1)}, u32[]{:S(2)}, u32[]{:S(2)}) collective-permute-start(f32[12,8,128]{2,1,0:T(8,128)} %get-tuple-element.81.square_ref), channel_id=1, source_target_pairs={{0,1},{1,0},{2,3},{3,2},{4,5},{5,4},{6,7},{7,6},{8,9},{9,8},{10,11... | collective-permute-start | bytes 147464 | tf_op jit(solution)/shard_map/ppermute | solution.py:722
  119.9 0.6 copy-start.8

commit v6 on v5

--- a/solution.py
+++ b/solution.py
@@ -49,19 +49,10 @@
     return wide[pl.ds(each, rows_ref.shape[0] // count, stride=count), :].astype(BF16)
 
 
-def masked_copies(x, count):
-    rows, width = x.shape
-    tiles = x.reshape(rows // 16, 16, width)
-    row = lax.broadcasted_iota(jnp.int32, (16, width), 0) & (count - 1)
-    kept = [tiles * jnp.where(row == m, 1.0, 0.0).astype(BF16)[None] for m in range(count)]
-    return jnp.concatenate([part.reshape(rows, width) for part in kept], axis=1)
-
-
 def state_kernel(depth, heads, gain_ref, k_hbm, v_hbm, *rest):
     piece_refs = rest[:COLS]
-    local_ref, sum_ref, keys, values, levels, key_sems, value_sems = rest[COLS:]
-    width = keys.shape[1]
-    rows = keys.shape[0] >> depth
+    local_ref, sum_ref, keys, values, kf, vf, levels, key_sems, value_sems = rest[COLS:]
+    rows, width = kf.shape
     each = heads // COLS
     copies = [
         (block_copy(k_hbm, keys, key_sems, b, rows), block_copy(v_hbm, values, value_sems, b, rows))
@@ -73,14 +64,12 @@
     for b, pair in enumerate(copies):
         for copy in pair:
             copy.wait()
-        states = lax.dot_general(
-            keys[b * rows : (b + 1) * rows],
-            masked_copies(values[b * rows : (b + 1) * rows], heads),
-            (((0,), (0,)), ((), ())),
-            preferred_element_type=F32,
-        )
+        kf[...] = keys[b * rows : (b + 1) * rows].astype(F32)
+        vf[...] = values[b * rows : (b + 1) * rows].astype(F32)
         for h in range(heads):
-            merged = states[:, h * width : (h + 1) * width]
+            k = kf[pl.ds(h, BLK, stride=heads), :].astype(BF16)
+            v = vf[pl.ds(h, BLK, stride=heads), :].astype(BF16)
+            merged = lax.dot_general(k, v, (((0,), (0,)), ((), ())), preferred_element_type=F32)
             before = None
             for bit in range(depth):
                 if b >> bit & 1:
@@ -116,6 +105,8 @@
         scratch_shapes=[
             pltpu.VMEM(keys.shape, BF16),
             pltpu.VMEM(values.shape, BF16),
+            pltpu.VMEM((keys.shape[0] // blocks, width), F32),
+            pltpu.VMEM((keys.shape[0] // blocks, width), F32),
             pltpu.VMEM((depth, heads, width, width), F32),
             pltpu.SemaphoreType.DMA((blocks,)),
             pltpu.SemaphoreType.DMA((blocks,)),
@@ -378,17 +369,18 @@
     out_ref[...] = window_block(wq_ref, kh, vh, base, groups, bias) + of[...]
 
 
-def trunk_attention(where, gain, q, k, v, wq, pk, pv, ck, cv, local, heads, groups, first, steps):
+def trunk_attention(where, gain, q, k, v, wq, before_kv, ck, cv, local, heads, groups, first, steps):
     width = q.shape[1]
     rows = BLK * heads
     at_block = pl.BlockSpec((rows, width), lambda i: (i + first, 0))
     whole = pl.BlockSpec((WIN * groups, width), lambda i: (0, 0))
+    second = pl.BlockSpec((WIN * groups, width), lambda i: (1, 0))
     before = pl.BlockSpec((1, heads, width, width), lambda i: (jnp.maximum(i + first - 1, 0), 0, 0, 0))
     wide = pltpu.VMEM((rows, width), F32)
     return pl.pallas_call(
         functools.partial(trunk_kernel, heads, groups, first),
         grid=(steps,),
-        in_specs=[smem(), smem()] + [at_block] * 4 + [whole] * 4 + [before],
+        in_specs=[smem(), smem()] + [at_block] * 4 + [whole, second, whole, whole, before],
         out_specs=pl.BlockSpec((rows, width), lambda i: (i, 0)),
         out_shape=jax.ShapeDtypeStruct((steps * rows, width), F32),
         scratch_shapes=[
@@ -402,8 +394,8 @@
         ],
         compiler_params=params(),
         cost_estimate=attention_cost(steps * BLK, heads, width, 2 * steps * BLK * BLK * heads * 3 * width),
-        name=f"trunk_attention_{first}",
-    )(where, gain, q, k, v, wq, pk, pv, ck, cv, local)
+        name="trunk_attention",
+    )(where, gain, q, k, v, wq, before_kv, before_kv, ck, cv, local)
 
 
 def near_kernel(groups, where_ref, fork_ref, q_ref, ck_ref, cv_ref, *rest):
@@ -454,8 +446,8 @@
 
 
 def final_kernel(heads, where_ref, fork_ref, bq_hbm, tq_hbm, near_hbm, far_hbm, trunk_hbm, cross_hbm, *rest):
-    end_hbms, (branch_full, trunk_full, square_ref, qs, ws, ts, fs, es, cs, stacked, mine) = rest[:COLS], rest[COLS : COLS + 11]
-    q_sems, w_sems, f_sems, e_sems = rest[COLS + 11 :]
+    end_hbms, (branch_full, trunk_full, square_ref, qs, ws, ts, nf, of, fs, es, cs, mine) = rest[:COLS], rest[COLS : COLS + 12]
+    q_sems, w_sems, f_sems, e_sems = rest[COLS + 12 :]
     window_hbms = (near_hbm, far_hbm)
     rows = BLK * heads
     branch_blocks, trunk_blocks = ws.shape[0] // rows, ts.shape[0] // rows
@@ -488,24 +480,23 @@
     mine[...] = token_rows(BLK, heads)
     for copy in states:
         copy.wait()
-    width = qs.shape[1]
-    for i, held in enumerate((es, cs)):
+
+    def rest_of(slot, window, states_ref):
+        at = pl.ds(pl.multiple_of(slot * rows, rows), rows)
+        nf[...] = qs[at, :].astype(F32)
         for h in range(heads):
-            m, n = h % COLS, h // COLS
-            stacked[i, m * width : (m + 1) * width, n * width : (n + 1) * width] = held[h // each, h % each]
-
-    def rest_of(slot, window, which):
-        at = pl.ds(pl.multiple_of(slot * rows, rows), rows)
-        both = jnp.dot(masked_copies(qs[at, :], COLS), stacked[which], preferred_element_type=F32)
-        upper = (lax.broadcasted_iota(jnp.int32, (rows, width), 0) & (heads - 1)) < COLS
-        full = window.astype(F32) + jnp.where(upper, both[:, :width], both[:, width:])
+            q = nf[pl.ds(h, BLK, stride=heads), :].astype(BF16)
+            of[pl.ds(h, BLK, stride=heads), :] = jnp.dot(
+                q, states_ref[h // each, h % each], preferred_element_type=F32
+            )
+        full = window.astype(F32) + of[...]
         fs[at, :] = full
         square_ref[slot] = square_sums(full, mine[...])
 
     def branch_block(b, carry):
         query_copy(bq_hbm, b, b).wait()
         other_copy(window_hbms[0], 0, ws, b, b).wait()
-        rest_of(b, ws[pl.ds(pl.multiple_of(b * rows, rows), rows), :], 0)
+        rest_of(b, ws[pl.ds(pl.multiple_of(b * rows, rows), rows), :], es)
         result_copy(b, branch_full, b).start()
         return carry
 
@@ -513,7 +504,7 @@
         slot = branch_blocks + b
         query_copy(tq_hbm, b, slot).wait()
         other_copy(trunk_hbm, 0, ts, b, slot).wait()
-        rest_of(slot, ts[pl.ds(pl.multiple_of(b * rows, rows), rows), :], 1)
+        rest_of(slot, ts[pl.ds(pl.multiple_of(b * rows, rows), rows), :], cs)
         result_copy(b, trunk_full, slot).start()
         return carry
 
@@ -543,10 +534,11 @@
             pltpu.VMEM((total, width), BF16),
             pltpu.VMEM(bq.shape, BF16),
             pltpu.VMEM(tq.shape, F32),
+            pltpu.VMEM((rows, width), F32),
+            pltpu.VMEM((rows, width), F32),
             pltpu.VMEM((total, width), F32),
             pltpu.VMEM(cross.shape, BF16),
             pltpu.VMEM(cross.shape, BF16),
-            pltpu.VMEM((2, COLS * width, heads // COLS * width), BF16),
             pltpu.VMEM((BLK, rows), BF16),
             pltpu.SemaphoreType.DMA((blocks,)),
             pltpu.SemaphoreType.DMA((blocks,)),
@@ -684,38 +676,34 @@
     in_one_column = [[p * COLS + c for p in range(planes)] for c in range(COLS)]
     tie = lax.optimization_barrier
 
+    def down(x):
+        return down_rest(down_first(x))
+
     half = COLS // 2
     got = send(twv, [(root - i, root - i - half) for i in range(half)])
+    kv = down(jnp.where(column >= half, twk, got))
+    before_kv = send(jnp.concatenate([twk, twv], axis=0), [(i, i + 1) for i in range(count - 1)])
+
     *pieces, local, shard_sum = block_sums(level_gain, tk, tv, heads, depth)
     mine = pieces[COLS - 1]
     for c in range(COLS - 1):
         mine = jnp.where(column == c, send(pieces[c], [(root, root - (COLS - 1) + c)]), mine)
     sums = in_groups(shard_sum, in_one_plane)
-    got, sums = tie((got, sums))
-    kv = down_first(jnp.where(column >= half, twk, got))
     plane_sum, ends = plane_sums(where, level_gain, sums, mine, planes, depth)
     plane_sum = in_groups(plane_sum, in_one_column)
-
-    plane_sum, kv, ends, bwq, twk, twv = tie((plane_sum, kv, ends, bwq, twk, twv))
-    shift = [(i, i + 1) for i in range(count - 1)]
-    pk, pv = send(twk, shift), send(twv, shift)
-    kv, ends = down_rest(kv), down_first(ends)
-    far = far_attention(bwq, bwk, bwv, heads, groups)
-    kv, ends, far, pk, pv, plane_sum = tie((kv, ends, far, pk, pv, plane_sum))
-
+    ends = down(ends)
     cross, above = cross_sums(where, level_gain, sums, plane_sum, depth)
     cross = in_groups(cross, in_one_plane)
-    cross, twq, kv = tie((cross, twq, kv))
+
+    far = far_attention(bwq, bwk, bwv, heads, groups)
+    kv, far = tie((kv, far))
     kvs = around(kv)
-    ends = down_rest(ends)
+    ends = around((ends.astype(F32) + above).astype(BF16))
     trunk = trunk_attention(
-        where, level_gain, tq, tk, tv, twq, pk, pv, twk, twv, local, heads, groups, 0, tokens // BLK
+        where, level_gain, tq, tk, tv, twq, before_kv, twk, twv, local, heads, groups, 0, tokens // BLK
     )
-    kvs, ends, trunk, bwq = tie((kvs, ends, trunk, bwq))
-    ends = (ends.astype(F32) + above).astype(BF16)
-    bwq, ends = tie((bwq, ends))
+    trunk, bwq = tie((trunk, bwq))
     near = near_attention(where, fork_block, bwq, bwk, bwv, kvs, heads, groups)
-    ends = around(ends)
     branch_full, trunk_full, square = final_linear(
         where, fork_block, bq, tq, near, far, trunk, cross, ends, heads
     )

time: 127 us -> 108 us (0.85)
  waiting for transfers between devices: 20.7 us -> 6.18 us
  Pallas kernels: 57 us -> 52.9 us
  local copies, waits for them, and re-layouts: 1.54 us -> 3.04 us
  starting transfers between devices: 44.8 us -> 43.5 us
    all_to_all x3, waiting for transfers between devices: 18.5 us -> 2.47 us  [in_groups(): lax.all_to_all(x, 'seq', 0, 0, tiled=True, axis_index_groups=groups_of)]
    all_to_all x3, starting transfers between devices: 28.3 us -> 23.8 us  [in_groups(): lax.all_to_all(x, 'seq', 0, 0, tiled=True, axis_index_groups=groups_of)]
    pallas_call x1, Pallas kernels: 16.9 us -> 13.2 us  [final_linear(): pl.pallas_call(functools.partial(final_kernel, heads), in_specs=[smem(),...]
    ppermute x16 -> x15, starting transfers between devices: 16.4 us -> 19.7 us  [send(): return lax.ppermute(x, 'seq', pairs)]
    ppermute x16 -> x15, waiting for transfers between devices: 0.72 us -> 2.28 us  [send(): return lax.ppermute(x, 'seq', pairs)]
    unnamed x30 -> x28, local copies, waits for them, and re-layouts: 1.54 us -> 3.04 us
  transfers between devices with their start and end apart: 20 -> 19, of which waited for: 5 -> 3; matrix products, arithmetic and copies ran while one was open for 0% -> 0% of each run, Pallas kernels for 26% -> 32%
where the time goes in v6:
time: 108 us
  Pallas kernels  52.9 us (49%)
  starting transfers between devices  43.5 us (40%)
  waiting for transfers between devices  6.18 us (6%)
  local copies, waits for them, and re-layouts  3.04 us (3%)
  between operations  1.67 us (2%)
    all_to_all x3, starting transfers between devices, in_groups(): lax.all_to_all(x, 'seq', 0, 0, tiled=True, axis_index_groups=groups_of)  23.8 us
    ppermute x15, starting transfers between devices, send(): return lax.ppermute(x, 'seq', pairs)  19.7 us
    pallas_call x1, Pallas kernels, final_linear(): pl.pallas_call(functools.partial(final_kernel, heads), in_specs=[smem(),...  13.2 us
    pallas_call x1, Pallas kernels, trunk_attention(): pl.pallas_call(functools.partial(trunk_kernel, heads, groups, first), gri...  10.4 us
    pallas_call x1, Pallas kernels, near_attention(): pl.pallas_call(functools.partial(near_kernel, groups), grid=(steps,), in_...  8.45 us
    pallas_call x1, Pallas kernels, far_attention(): pl.pallas_call(functools.partial(far_kernel, heads, groups), grid=(steps,...  8.08 us
    pallas_call x1, Pallas kernels, normalize(): pl.pallas_call(functools.partial(norm_kernel, heads, features), in_specs=...  5.41 us
    pallas_call x1, Pallas kernels, block_sums(): pl.pallas_call(functools.partial(state_kernel, depth, heads), in_specs=[s...  4.64 us
  transfers between devices with their start and end apart: 19, of which 3 were waited for; matrix products, arithmetic and copies ran while one was open for 0% of the time, Pallas kernels for 32%

profile of v6, /device:TPU:0, one launch (start us, length us, event | category | flops | bytes accessed | tf_op | source)
XLA Modules:
  0.0 107.6 jit_solution(8083179550799877694)
XLA Ops:
  0.6 0.0 copy-start.3
  0.6 0.8 collective-permute-start.1
  1.5 0.0 copy-start
  1.5 0.0 copy-start.7
  1.5 4.6 %block_sums.1 = (bf16[3,2,128,128]{3,2,1,0:T(8,128)(2,1)}, bf16[3,2,128,128]{3,2,1,0:T(8,128)(2,1)}, bf16[3,2,128,128]{3,2,1,0:T(8,128)(2,1)}, bf16[3,2,128,128]...) custom-call(f32[8,11]{1,0:T(8,128)} %gain_ref.7, bf16[4096,128]{1,0:T(8,128)(2,1)} %bitcast.16, ...), custom_call_target="tpu_custom_call" | custom-call | flops 134217728 | bytes 3145728 | tf_op jit(solution)/shard_map/block_sums/pallas_call | solution.py:96
  6.1 5.2 %all-to-all-start = ((bf16[4,2,128,128]{3,2,1,0:T(8,128)(2,1)}), bf16[4,2,128,128]{3,2,1,0:T(8,128)(2,1)S(1)}, u32[]{:S(2)}, u32[]{:S(2)}) async-start(bf16[4,2,128,128]{3,2,1,0:T(8,128)(2,1)} %get-tuple-element.26), calls=%async_computation | async-start | bytes 524288 | tf_op jit(solution)/shard_map/all_to_all | solution.py:673
  11.3 0.7 collective-permute-start.7
  12.0 0.7 collective-permute-start.8
  12.7 0.7 collective-permute-start.9
  13.4 0.0 collective-permute-done.1
  13.4 0.0 copy-done.3
  13.4 0.7 collective-permute-start.2
  14.1 0.0 collective-permute-done.7
  14.1 0.0 collective-permute-done.8
  14.1 0.0 collective-permute-done.9
  14.1 0.1 select_select_fusion.local_ref
  14.2 2.5 %all-to-all-done.sums_ref = bf16[4,2,128,128]{3,2,1,0:T(8,128)(2,1)S(1)} async-done(((bf16[4,2,128,128]{3,2,1,0:T(8,128)(2,1)}), bf16[4,2,128,128]{3,2,1,0:T(8,128)(2,1)S(1)}, u32[]{:S(2)}, u32[]{:S(2)}) %all-to-all-start) | async-done | bytes 262176 | tf_op jit(solution)/shard_map/all_to_all | solution.py:673
  16.7 0.0 copy-done
  16.7 1.3 %plane_sums.1 = (bf16[4,2,128,128]{3,2,1,0:T(8,128)(2,1)}, bf16[4,2,128,128]{3,2,1,0:T(8,128)(2,1)S(1)}) custom-call(s32[1]{0:T(128)} %bitcast.where_ref, f32[8,11]{1,0:T(8,128)S(1)} %copy-done, bf16[4,2,128,128]{3,2,1,0:T(8,128)(2,1)S(1)} %all-to-all-done.sums_ref, bf16[3,2,128,128]{3,2,1,0:T(8,128)(2,1)S(1)} %select_select_fusion.local_ref), custom_call_target="tpu_custom_call" | custom-call | flops 524288 | bytes 1048576 | tf_op jit(solution)/shard_map/plane_sums/pallas_call | solution.py:152
  18.0 0.7 collective-permute-start.10
  18.7 0.0 copy-done.7
  18.8 3.2 %collective-permute-start = (bf16[2048,128]{1,0:T(8,128)(2,1)S(1)}, bf16[2048,128]{1,0:T(8,128)(2,1)S(1)}, u32[]{:S(2)}, u32[]{:S(2)}) collective-permute-start(bf16[2048,128]{1,0:T(8,128)(2,1)S(1)} %pad_maximum_fusion), channel_id=1, source_target_pairs={{0,2},{2,4},{4,6},{6,8},{8,10},{10,12},{12,14},{14,16},{16,18},{18... | collective-permute-start | bytes 1572872 | tf_op jit(solution)/shard_map/ppermute | solution.py:650
  22.0 15.2 %all-to-all-start.1 = ((bf16[4,2,128,128]{3,2,1,0:T(8,128)(2,1)}), bf16[4,2,128,128]{3,2,1,0:T(8,128)(2,1)S(1)}, u32[]{:S(2)}, u32[]{:S(2)}) async-start(bf16[4,2,128,128]{3,2,1,0:T(8,128)(2,1)} %get-tuple-element.31), calls=%async_computation.1 | async-start | bytes 524288 | tf_op jit(solution)/shard_map/all_to_all | solution.py:673
  37.2 0.0 collective-permute-done.2
  37.2 1.3 %collective-permute-start.3 = (bf16[1024,128]{1,0:T(8,128)(2,1)S(1)}, bf16[1024,128]{1,0:T(8,128)(2,1)S(1)}, u32[]{:S(2)}, u32[]{:S(2)}) collective-permute-start(bf16[1024,128]{1,0:T(8,128)(2,1)S(1)} %broadcast_select_fusion.2), channel_id=1, source_target_pairs={{8,0},{10,2},{12,4},{14,6},{24,16},{26,18},{28,20},{30,22},{9,1},{... | collective-permute-start | bytes 786440 | tf_op jit(solution)/shard_map/ppermute | solution.py:650
  38.5 0.0 collective-permute-done.10
  38.6 1.3 %collective-permute-start.11 = (bf16[4,2,128,128]{3,2,1,0:T(8,128)(2,1)S(1)}, bf16[4,2,128,128]{3,2,1,0:T(8,128)(2,1)S(1)}, u32[]{:S(2)}, u32[]{:S(2)}) collective-permute-start(bf16[4,2,128,128]{3,2,1,0:T(8,128)(2,1)S(1)} %broadcast_select_fusion), channel_id=1, source_target_pairs={{8,0},{10,2},{12,4},{14,6},{24,16},{26,18},{28,20},{30,22},{9,1},{... | collective-permute-start | bytes 786440 | tf_op jit(solution)/shard_map/ppermute | solution.py:650
  39.9 8.1 %far_attention.1.far_hbm = bf16[4096,128]{1,0:T(8,128)(2,1)} custom-call(bf16[8192,128]{1,0:T(8,128)(2,1)} %bitcast.26, bf16[2048,128]{1,0:T(8,128)(2,1)} %bitcast.31, bf16[2048,128]{1,0:T(8,128)(2,1)} %bitcast.34, bf16[2048,128]{1,0:T(8,128)(2,1)} %bitcast.32, bf16[2048,128]{1,0:T(8,128)(2,1)} %bitcast.35), custom_call_target="tpu_custom_call" | custom-call | flops 2013265920 | bytes 6291456 | tf_op jit(solution)/shard_map/far_attention/pallas_call | solution.py:315
  47.9 2.2 %collective-permute-done.3 = bf16[1024,128]{1,0:T(8,128)(2,1)S(1)} collective-permute-done((bf16[1024,128]{1,0:T(8,128)(2,1)S(1)}, bf16[1024,128]{1,0:T(8,128)(2,1)S(1)}, u32[]{:S(2)}, u32[]{:S(2)}) %collective-permute-start.3) | collective-permute-done | bytes 262176 | tf_op jit(solution)/shard_map/ppermute | solution.py:650
  50.2 0.0 copy-start.8
  50.2 2.7 %collective-permute-start.6 = (bf16[1024,128]{1,0:T(8,128)(2,1)S(1)}, bf16[1024,128]{1,0:T(8,128)(2,1)S(1)}, u32[]{:S(2)}, u32[]{:S(2)}) collective-permute-start(bf16[1024,128]{1,0:T(8,128)(2,1)S(1)} %broadcast_select_fusion.3.rest_0_), channel_id=1, source_target_pairs={{0,6},{2,4},{4,2},{6,0},{8,14},{10,12},{12,10},{14,8},{16,22},{18,... | collective-permute-start | bytes 786440 | tf_op jit(solution)/shard_map/ppermute | solution.py:650
  53.6 0.0 all-to-all-done.1.planes_ref
  53.6 1.4 %cross_sums.1 = (bf16[4,2,128,128]{3,2,1,0:T(8,128)(2,1)}, f32[2,128,128]{2,1,0:T(8,128)S(1)}) custom-call(s32[1]{0:T(128)} %bitcast.where_ref, f32[8,11]{1,0:T(8,128)S(1)} %copy-done, bf16[4,2,128,128]{3,2,1,0:T(8,128)(2,1)S(1)} %all-to-all-done.sums_ref, bf16[4,2,128,128]{3,2,1,0:T(8,128)(2,1)S(1)} %all-to-all-done.1.planes_ref), custom_call_target="tpu_custom_call" | custom-call | flops 2621440 | bytes 1048576 | tf_op jit(solution)/shard_map/cross_sums/pallas_call | solution.py:193
  55.0 3.4 %all-to-all-start.2 = ((bf16[4,2,128,128]{3,2,1,0:T(8,128)(2,1)}), bf16[4,2,128,128]{3,2,1,0:T(8,128)(2,1)S(1)}, u32[]{:S(2)}, u32[]{:S(2)}) async-start(bf16[4,2,128,128]{3,2,1,0:T(8,128)(2,1)} %get-tuple-element.32), calls=%async_computation.2 | async-start | bytes 524288 | tf_op jit(solution)/shard_map/all_to_all | solution.py:673
  58.4 2.0 %collective-permute-start.5 = (bf16[1024,128]{1,0:T(8,128)(2,1)S(1)}, bf16[1024,128]{1,0:T(8,128)(2,1)S(1)}, u32[]{:S(2)}, u32[]{:S(2)}) collective-permute-start(bf16[1024,128]{1,0:T(8,128)(2,1)S(1)} %broadcast_select_fusion.3.rest_0_), channel_id=1, source_target_pairs={{0,4},{2,6},{4,0},{6,2},{8,12},{10,14},{12,8},{14,10},{16,20},{18,... | collective-permute-start | bytes 786440 | tf_op jit(solution)/shard_map/ppermute | solution.py:650
  60.4 1.5 %collective-permute-start.4 = (bf16[1024,128]{1,0:T(8,128)(2,1)S(1)}, bf16[1024,128]{1,0:T(8,128)(2,1)S(1)}, u32[]{:S(2)}, u32[]{:S(2)}) collective-permute-start(bf16[1024,128]{1,0:T(8,128)(2,1)S(1)} %broadcast_select_fusion.3.rest_0_), channel_id=1, source_target_pairs={{0,2},{2,0},{4,6},{6,4},{8,10},{10,8},{12,14},{14,12},{16,18},{18,... | collective-permute-start | bytes 786440 | tf_op jit(solution)/shard_map/ppermute | solution.py:650
  61.9 0.0 collective-permute-done.11
  61.9 0.1 add_convert_fusion.rest_0_
  62.0 0.0 copy-start.1
  62.0 0.2 collective-permute-start.14
  62.2 0.0 collective-permute-done.pk_ref.pv_ref
  62.2 1.9 %collective-permute-start.13 = (bf16[4,2,128,128]{3,2,1,0:T(8,128)(2,1)S(1)}, bf16[4,2,128,128]{3,2,1,0:T(8,128)(2,1)S(1)}, u32[]{:S(2)}, u32[]{:S(2)}) collective-permute-start(bf16[4,2,128,128]{3,2,1,0:T(8,128)(2,1)S(1)} %add_convert_fusion.rest_0_), channel_id=1, source_target_pairs={{0,4},{2,6},{4,0},{6,2},{8,12},{10,14},{12,8},{14,10},{16,20},{18,... | collective-permute-start | bytes 786440 | tf_op jit(solution)/shard_map/ppermute | solution.py:650
  64.1 0.0 collective-permute-done.6.rest_3_
  64.1 1.5 %collective-permute-start.12 = (bf16[4,2,128,128]{3,2,1,0:T(8,128)(2,1)S(1)}, bf16[4,2,128,128]{3,2,1,0:T(8,128)(2,1)S(1)}, u32[]{:S(2)}, u32[]{:S(2)}) collective-permute-start(bf16[4,2,128,128]{3,2,1,0:T(8,128)(2,1)S(1)} %add_convert_fusion.rest_0_), channel_id=1, source_target_pairs={{0,2},{2,0},{4,6},{6,4},{8,10},{10,8},{12,14},{14,12},{16,18},{18,... | collective-permute-start | bytes 786440 | tf_op jit(solution)/shard_map/ppermute | solution.py:650
  65.6 10.4 %trunk_attention.1.trunk_hbm = f32[4096,128]{1,0:T(8,128)} custom-call(s32[1]{0:T(128)} %bitcast.where_ref, f32[8,11]{1,0:T(8,128)} %gain_ref.7, bf16[4096,128]{1,0:T(8,128)(2,1)} %bitcast.14, bf16[4096,128]{1,0:T(8,128)(2,1)} %bitcast.17, bf16[4096,128]{1,0:T(8,128)(2,1)} %bitcast.19, bf16[4096,128]{1,0:T(8,128)(2,1)} %bitcast.29, ...), custom_call_target="tpu_custom_call" | custom-call | flops 2415919104 | bytes 6291456 | tf_op jit(solution)/shard_map/trunk_attention/pallas_call | solution.py:380
  76.0 0.0 collective-permute-done.5.rest_2_
  76.0 0.0 copy-start.12
  76.0 0.0 collective-permute-done.4.rest_1_
  76.0 0.7 copy-done.12
  76.7 0.7 copy-done.13
  77.4 8.4 %near_attention.1.near_hbm = bf16[4096,128]{1,0:T(8,128)(2,1)} custom-call(s32[1]{0:T(128)} %bitcast.where_ref, s32[1]{0:T(128)S(6)} %copy.14.fork_ref, bf16[8192,128]{1,0:T(8,128)(2,1)} %bitcast.27, bf16[2048,128]{1,0:T(8,128)(2,1)} %bitcast.33, bf16[2048,128]{1,0:T(8,128)(2,1)} %bitcast.36, bf16[1024,128]{1,0:T(8,128)(2,1)} %copy-done.8, ...), custom_call_target="tpu_custom_call" | custom-call | flops 2013265920 | bytes 6291456 | tf_op jit(solution)/shard_map/near_attention/pallas_call | solution.py:430
  85.8 0.0 all-to-all-done.2.cross_hbm
  85.8 0.0 collective-permute-done.14.rest_3_
  85.9 0.0 collective-permute-done.13.rest_2_
  85.9 0.0 collective-permute-done.12.rest_1_
  85.9 0.7 copy-done.2
  86.6 0.1 copy-done.4
  86.7 0.1 copy-done.5
  86.8 0.1 copy-done.6
  86.9 13.2 %final_linear.1 = (f32[8192,128]{1,0:T(8,128)}, f32[4096,128]{1,0:T(8,128)}, f32[12,8,128]{2,1,0:T(8,128)}) custom-call(s32[1]{0:T(128)} %bitcast.where_ref, s32[1]{0:T(128)S(6)} %copy.14.fork_ref, bf16[8192,128]{1,0:T(8,128)(2,1)} %bitcast.13, bf16[4096,128]{1,0:T(8,128)(2,1)} %bitcast.15, bf16[4096,128]{1,0:T(8,128)(2,1)} %near_attention.1.near_hbm, ...), custom_call_target="tpu_custom_call" | custom-call | flops 805306368 | bytes 12582912 | tf_op jit(solution)/shard_map/final_linear/pallas_call | solution.py:524
  100.1 0.1 collective-permute-start.15
  100.2 1.4 %collective-permute-done.15.other_ref = f32[12,8,128]{2,1,0:T(8,128)S(1)} collective-permute-done((f32[12,8,128]{2,1,0:T(8,128)}, f32[12,8,128]{2,1,0:T(8,128)S(1)}, u32[]{:S(2)}, u32[]{:S(2)}) %collective-permute-start.15) | collective-permute-done | bytes 49184 | tf_op jit(solution)/shard_map/ppermute | solution.py:710
  101.6 0.6 copy-done.9
  102.2 5.4 %normalize.1 = (bf16[4096,128]{1,0:T(8,128)(2,1)}, bf16[8192,128]{1,0:T(8,128)(2,1)}) custom-call(f32[4096,128]{1,0:T(8,128)} %get-tuple-element.35.trunk_hbm, f32[8192,128]{1,0:T(8,128)} %get-tuple-element.36.branch_hbm, f32[12,8,128]{2,1,0:T(8,128)} %get-tuple-element.37.square_ref, f32[12,8,128]{2,1,0:T(8,128)} %copy-done.9), custom_call_target="tpu_custom_call" | custom-call | flops 3145728 | bytes 9437184 | tf_op jit(solution)/shard_map/normalize/pallas_call | solution.py:597
  (17 shorter events, 0.2 us)
Async XLA Ops:
  0.6 12.7 %copy-start.3 = (bf16[512,2,128]{2,1,0:T(2,128)(2,1)S(1)}, bf16[512,2,128]{2,1,0:T(2,128)(2,1)}, u32[]{:S(2)}) copy-start(bf16[512,2,128]{2,1,0:T(2,128)(2,1)} %param.16) | copy-start | bytes 786436
  0.6 12.7 %collective-permute-start.1 = (bf16[1024,128]{1,0:T(8,128)(2,1)}, bf16[1024,128]{1,0:T(8,128)(2,1)S(1)}, u32[]{:S(2)}, u32[]{:S(2)}) collective-permute-start(bf16[1024,128]{1,0:T(8,128)(2,1)} %bitcast.23), channel_id=1, source_target_pairs={{30,26},{28,24},{31,27},{29,25}} | collective-permute-start | bytes 786440 | tf_op jit(solution)/shard_map/ppermute | solution.py:650
  1.5 15.2 %copy-start = (f32[8,11]{1,0:T(8,128)S(1)}, f32[8,11]{1,0:T(8,128)}, u32[]{:S(2)}) copy-start(f32[8,11]{1,0:T(8,128)} %gain_ref.7) | copy-start | bytes 1060
  1.5 17.2 %copy-start.7 = (bf16[512,2,128]{2,1,0:T(2,128)(2,1)S(1)}, bf16[512,2,128]{2,1,0:T(2,128)(2,1)}, u32[]{:S(2)}) copy-start(bf16[512,2,128]{2,1,0:T(2,128)(2,1)} %param.17) | copy-start | bytes 786436
  6.1 10.5 %all-to-all-start = ((bf16[4,2,128,128]{3,2,1,0:T(8,128)(2,1)}), bf16[4,2,128,128]{3,2,1,0:T(8,128)(2,1)S(1)}, u32[]{:S(2)}, u32[]{:S(2)}) async-start(bf16[4,2,128,128]{3,2,1,0:T(8,128)(2,1)} %get-tuple-element.26), calls=%async_computation | async-start | bytes 524288 | tf_op jit(solution)/shard_map/all_to_all | solution.py:673
  11.3 2.8 %collective-permute-start.7 = (bf16[3,2,128,128]{3,2,1,0:T(8,128)(2,1)}, bf16[3,2,128,128]{3,2,1,0:T(8,128)(2,1)S(1)}, u32[]{:S(2)}, u32[]{:S(2)}) collective-permute-start(bf16[3,2,128,128]{3,2,1,0:T(8,128)(2,1)} %get-tuple-element.27), channel_id=1, source_target_pairs={{30,28},{31,29}} | collective-permute-start | bytes 589832 | tf_op jit(solution)/shard_map/ppermute | solution.py:650
  12.0 2.1 %collective-permute-start.8 = (bf16[3,2,128,128]{3,2,1,0:T(8,128)(2,1)}, bf16[3,2,128,128]{3,2,1,0:T(8,128)(2,1)S(1)}, u32[]{:S(2)}, u32[]{:S(2)}) collective-permute-start(bf16[3,2,128,128]{3,2,1,0:T(8,128)(2,1)} %get-tuple-element.28), channel_id=1, source_target_pairs={{30,26},{31,27}} | collective-permute-start | bytes 589832 | tf_op jit(solution)/shard_map/ppermute | solution.py:650
  12.7 1.5 %collective-permute-start.9 = (bf16[3,2,128,128]{3,2,1,0:T(8,128)(2,1)}, bf16[3,2,128,128]{3,2,1,0:T(8,128)(2,1)S(1)}, u32[]{:S(2)}, u32[]{:S(2)}) collective-permute-start(bf16[3,2,128,128]{3,2,1,0:T(8,128)(2,1)} %get-tuple-element.29), channel_id=1, source_target_pairs={{30,24},{31,25}} | collective-permute-start | bytes 589832 | tf_op jit(solution)/shard_map/ppermute | solution.py:650
  13.4 23.8 %collective-permute-start.2 = (bf16[1024,128]{1,0:T(8,128)(2,1)S(1)}, bf16[1024,128]{1,0:T(8,128)(2,1)S(1)}, u32[]{:S(2)}, u32[]{:S(2)}) collective-permute-start(bf16[1024,128]{1,0:T(8,128)(2,1)S(1)} %broadcast_select_fusion.1), channel_id=1, source_target_pairs={{24,8},{26,10},{28,12},{30,14},{25,9},{27,11},{29,13},{31,15}} | collective-permute-start | bytes 786440 | tf_op jit(solution)/shard_map/ppermute | solution.py:650
  18.0 20.5 %collective-permute-start.10 = (bf16[4,2,128,128]{3,2,1,0:T(8,128)(2,1)S(1)}, bf16[4,2,128,128]{3,2,1,0:T(8,128)(2,1)S(1)}, u32[]{:S(2)}, u32[]{:S(2)}) collective-permute-start(bf16[4,2,128,128]{3,2,1,0:T(8,128)(2,1)S(1)} %get-tuple-element.33), channel_id=1, source_target_pairs={{24,8},{26,10},{28,12},{30,14},{25,9},{27,11},{29,13},{31,15}} | collective-permute-start | bytes 786440 | tf_op jit(solution)/shard_map/ppermute | solution.py:650
  18.8 43.4 %collective-permute-start = (bf16[2048,128]{1,0:T(8,128)(2,1)S(1)}, bf16[2048,128]{1,0:T(8,128)(2,1)S(1)}, u32[]{:S(2)}, u32[]{:S(2)}) collective-permute-start(bf16[2048,128]{1,0:T(8,128)(2,1)S(1)} %pad_maximum_fusion), channel_id=1, source_target_pairs={{0,2},{2,4},{4,6},{6,8},{8,10},{10,12},{12,14},{14,16},{16,18},{18... | collective-permute-start | bytes 1572872 | tf_op jit(solution)/shard_map/ppermute | solution.py:650
  22.0 31.6 %all-to-all-start.1 = ((bf16[4,2,128,128]{3,2,1,0:T(8,128)(2,1)}), bf16[4,2,128,128]{3,2,1,0:T(8,128)(2,1)S(1)}, u32[]{:S(2)}, u32[]{:S(2)}) async-start(bf16[4,2,128,128]{3,2,1,0:T(8,128)(2,1)} %get-tuple-element.31), calls=%async_computation.1 | async-start | bytes 524288 | tf_op jit(solution)/shard_map/all_to_all | solution.py:673
  37.2 13.0 %collective-permute-start.3 = (bf16[1024,128]{1,0:T(8,128)(2,1)S(1)}, bf16[1024,128]{1,0:T(8,128)(2,1)S(1)}, u32[]{:S(2)}, u32[]{:S(2)}) collective-permute-start(bf16[1024,128]{1,0:T(8,128)(2,1)S(1)} %broadcast_select_fusion.2), channel_id=1, source_target_pairs={{8,0},{10,2},{12,4},{14,6},{24,16},{26,18},{28,20},{30,22},{9,1},{... | collective-permute-start | bytes 786440 | tf_op jit(solution)/shard_map/ppermute | solution.py:650
  38.6 23.3 %collective-permute-start.11 = (bf16[4,2,128,128]{3,2,1,0:T(8,128)(2,1)S(1)}, bf16[4,2,128,128]{3,2,1,0:T(8,128)(2,1)S(1)}, u32[]{:S(2)}, u32[]{:S(2)}) collective-permute-start(bf16[4,2,128,128]{3,2,1,0:T(8,128)(2,1)S(1)} %broadcast_select_fusion), channel_id=1, source_target_pairs={{8,0},{10,2},{12,4},{14,6},{24,16},{26,18},{28,20},{30,22},{9,1},{... | collective-permute-start | bytes 786440 | tf_op jit(solution)/shard_map/ppermute | solution.py:650
  50.2 25.7 %copy-start.8 = (bf16[1024,128]{1,0:T(8,128)(2,1)}, bf16[1024,128]{1,0:T(8,128)(2,1)S(1)}, u32[]{:S(2)}) copy-start(bf16[1024,128]{1,0:T(8,128)(2,1)S(1)} %broadcast_select_fusion.3.rest_0_) | copy-start | bytes 786436
  50.2 13.9 %collective-permute-start.6 = (bf16[1024,128]{1,0:T(8,128)(2,1)S(1)}, bf16[1024,128]{1,0:T(8,128)(2,1)S(1)}, u32[]{:S(2)}, u32[]{:S(2)}) collective-permute-start(bf16[1024,128]{1,0:T(8,128)(2,1)S(1)} %broadcast_select_fusion.3.rest_0_), channel_id=1, source_target_pairs={{0,6},{2,4},{4,2},{6,0},{8,14},{10,12},{12,10},{14,8},{16,22},{18,... | collective-permute-start | bytes 786440 | tf_op jit(solution)/shard_map/ppermute | solution.py:650
  55.0 30.8 %all-to-all-start.2 = ((bf16[4,2,128,128]{3,2,1,0:T(8,128)(2,1)}), bf16[4,2,128,128]{3,2,1,0:T(8,128)(2,1)S(1)}, u32[]{:S(2)}, u32[]{:S(2)}) async-start(bf16[4,2,128,128]{3,2,1,0:T(8,128)(2,1)} %get-tuple-element.32), calls=%async_computation.2 | async-start | bytes 524288 | tf_op jit(solution)/shard_map/all_to_all | solution.py:673
  58.4 17.5 %collective-permute-start.5 = (bf16[1024,128]{1,0:T(8,128)(2,1)S(1)}, bf16[1024,128]{1,0:T(8,128)(2,1)S(1)}, u32[]{:S(2)}, u32[]{:S(2)}) collective-permute-start(bf16[1024,128]{1,0:T(8,128)(2,1)S(1)} %broadcast_select_fusion.3.rest_0_), channel_id=1, source_target_pairs={{0,4},{2,6},{4,0},{6,2},{8,12},{10,14},{12,8},{14,10},{16,20},{18,... | collective-permute-start | bytes 786440 | tf_op jit(solution)/shard_map/ppermute | solution.py:650
  60.4 15.5 %collective-permute-start.4 = (bf16[1024,128]{1,0:T(8,128)(2,1)S(1)}, bf16[1024,128]{1,0:T(8,128)(2,1)S(1)}, u32[]{:S(2)}, u32[]{:S(2)}) collective-permute-start(bf16[1024,128]{1,0:T(8,128)(2,1)S(1)} %broadcast_select_fusion.3.rest_0_), channel_id=1, source_target_pairs={{0,2},{2,0},{4,6},{6,4},{8,10},{10,8},{12,14},{14,12},{16,18},{18,... | collective-permute-start | bytes 786440 | tf_op jit(solution)/shard_map/ppermute | solution.py:650
  62.0 13.9 %copy-start.1 = (bf16[4,2,128,128]{3,2,1,0:T(8,128)(2,1)}, bf16[4,2,128,128]{3,2,1,0:T(8,128)(2,1)S(1)}, u32[]{:S(2)}) copy-start(bf16[4,2,128,128]{3,2,1,0:T(8,128)(2,1)S(1)} %add_convert_fusion.rest_0_) | copy-start | bytes 786436
  62.0 23.8 %collective-permute-start.14 = (bf16[4,2,128,128]{3,2,1,0:T(8,128)(2,1)S(1)}, bf16[4,2,128,128]{3,2,1,0:T(8,128)(2,1)S(1)}, u32[]{:S(2)}, u32[]{:S(2)}) collective-permute-start(bf16[4,2,128,128]{3,2,1,0:T(8,128)(2,1)S(1)} %add_convert_fusion.rest_0_), channel_id=1, source_target_pairs={{0,6},{2,4},{4,2},{6,0},{8,14},{10,12},{12,10},{14,8},{16,22},{18,... | collective-permute-start | bytes 786440 | tf_op jit(solution)/shard_map/ppermute | solution.py:650
  62.2 3.4 %copy-start.10 = (bf16[2048,128]{1,0:T(8,128)(2,1)}, bf16[2048,128]{1,0:T(8,128)(2,1)S(1)}, u32[]{:S(2)}) copy-start(bf16[2048,128]{1,0:T(8,128)(2,1)S(1)} %collective-permute-done.pk_ref.pv_ref) | copy-start | bytes 1572868
  62.2 23.7 %collective-permute-start.13 = (bf16[4,2,128,128]{3,2,1,0:T(8,128)(2,1)S(1)}, bf16[4,2,128,128]{3,2,1,0:T(8,128)(2,1)S(1)}, u32[]{:S(2)}, u32[]{:S(2)}) collective-permute-start(bf16[4,2,128,128]{3,2,1,0:T(8,128)(2,1)S(1)} %add_convert_fusion.rest_0_), channel_id=1, source_target_pairs={{0,4},{2,6},{4,0},{6,2},{8,12},{10,14},{12,8},{14,10},{16,20},{18,... | collective-permute-start | bytes 786440 | tf_op jit(solution)/shard_map/ppermute | solution.py:650
  64.1 11.8 %copy-start.11 = (bf16[1024,128]{1,0:T(8,128)(2,1)}, bf16[1024,128]{1,0:T(8,128)(2,1)S(1)}, u32[]{:S(2)}) copy-start(bf16[1024,128]{1,0:T(8,128)(2,1)S(1)} %collective-permute-done.6.rest_3_) | copy-start | bytes 786436
  64.1 21.8 %collective-permute-start.12 = (bf16[4,2,128,128]{3,2,1,0:T(8,128)(2,1)S(1)}, bf16[4,2,128,128]{3,2,1,0:T(8,128)(2,1)S(1)}, u32[]{:S(2)}, u32[]{:S(2)}) collective-permute-start(bf16[4,2,128,128]{3,2,1,0:T(8,128)(2,1)S(1)} %add_convert_fusion.rest_0_), channel_id=1, source_target_pairs={{0,2},{2,0},{4,6},{6,4},{8,10},{10,8},{12,14},{14,12},{16,18},{18,... | collective-permute-start | bytes 786440 | tf_op jit(solution)/shard_map/ppermute | solution.py:650
  76.0 0.7 copy-start.12
  76.7 0.7 copy-start.13
  85.8 0.8 copy-start.2
  85.8 0.9 copy-start.4
  85.9 1.0 copy-start.5
  85.9 1.0 copy-start.6
  100.1 1.5 %collective-permute-start.15 = (f32[12,8,128]{2,1,0:T(8,128)}, f32[12,8,128]{2,1,0:T(8,128)S(1)}, u32[]{:S(2)}, u32[]{:S(2)}) collective-permute-start(f32[12,8,128]{2,1,0:T(8,128)} %get-tuple-element.37.square_ref), channel_id=1, source_target_pairs={{0,1},{1,0},{2,3},{3,2},{4,5},{5,4},{6,7},{7,6},{8,9},{9,8},{10,11... | collective-permute-start | bytes 147464 | tf_op jit(solution)/shard_map/ppermute | solution.py:710
  101.6 0.6 copy-start.9

commit v7 on v6

--- a/solution.py
+++ b/solution.py
@@ -12,6 +12,7 @@
 WIN = 512
 COLS = 4
 MASKED = -1e30
+CHUNK = 32
 F32 = jnp.float32
 BF16 = jnp.bfloat16
 VMEM_BYTES = 60 * 1024 * 1024
@@ -228,45 +229,37 @@
     return jnp.concatenate([low, high], axis=1).reshape(2 * rows, width)
 
 
-def window_logits(queries, keys, token, share, bias):
-    rows = queries.shape[0]
-    logits = lax.dot_general(queries, keys, (((1,), (1,)), ((), ())), preferred_element_type=F32)
-    row = token + lax.broadcasted_iota(jnp.int32, (rows, BLK), 0) // share
-    col = lax.broadcasted_iota(jnp.int32, (rows, BLK), 1)
-    late = col > row
-    first = jnp.where(late, logits[:, :BLK], MASKED)
-    last = jnp.where(late, MASKED, logits[:, -BLK:])
-    logits = jnp.concatenate([first, logits[:, BLK:-BLK], last], axis=1)
-    return logits if bias is None else logits + bias
-
-
-def window_outputs(logits, values, width):
-    top = jnp.max(logits, axis=1, keepdims=True)
-    weights = jnp.exp2((logits - top) * (math.log2(math.e) / math.sqrt(width))).astype(BF16)
-    both = jnp.dot(weights, values, preferred_element_type=F32)
-    return both[:, :width] / both[:, width:]
-
-
-def window_block(q_ref, kh, vh, base, groups, bias=None):
+def window_block(q_ref, kh, vh, logits, weights, base, groups, bias=None):
     width = q_ref.shape[1]
     span = WIN + BLK
     share = q_ref.shape[0] // BLK // groups
     parts = [part.astype(BF16) for part in split_groups(q_ref[...].astype(F32))]
-    chunks = [(g, c) for g in range(groups) for c in range(0, BLK * share, BLK)]
-
-    def logits_of(chunk):
-        g, c = chunk
-        return window_logits(parts[g][c : c + BLK], kh[g, pl.ds(base, span), :], c // share, share, bias)
-
+    scale = math.log2(math.e) / math.sqrt(width)
+    for g in range(groups):
+        logits[g] = lax.dot_general(
+            parts[g], kh[g, pl.ds(base, span), :], (((1,), (1,)), ((), ())), preferred_element_type=F32
+        )
+    row = lax.broadcasted_iota(jnp.int32, (CHUNK, BLK), 0) // share
+    ahead = lax.broadcasted_iota(jnp.int32, (CHUNK, BLK), 1) - row
     outs = []
-    ahead = logits_of(chunks[0])
-    for i, (g, c) in enumerate(chunks):
-        now = ahead
-        if i + 1 < len(chunks):
-            ahead = logits_of(chunks[i + 1])
-        outs.append(window_outputs(now, vh[g, pl.ds(base, span), :], width))
-    half = len(outs) // 2
-    return join_groups(jnp.concatenate(outs[:half], axis=0), jnp.concatenate(outs[half:], axis=0))
+    for g in range(groups):
+        for r in range(0, BLK * share, CHUNK):
+            late = ahead > r // share
+            first = jnp.where(late, logits[g, r : r + CHUNK, :BLK], MASKED)
+            last = jnp.where(late, MASKED, logits[g, r : r + CHUNK, WIN:])
+            now = jnp.concatenate([first, logits[g, r : r + CHUNK, BLK:WIN], last], axis=1)
+            if bias is not None:
+                now = now + bias
+            top = jnp.max(now, axis=1, keepdims=True)
+            weights[g, r : r + CHUNK, :] = jnp.exp2((now - top) * scale).astype(BF16)
+        both = jnp.dot(weights[g], vh[g, pl.ds(base, span), :], preferred_element_type=F32)
+        outs.append(both[:, :width] / both[:, width:])
+    return join_groups(*outs)
+
+
+def window_scratch(heads, groups):
+    rows = BLK * heads // groups
+    return [pltpu.VMEM((groups, rows, WIN + BLK), F32), pltpu.VMEM((groups, rows, WIN + BLK), BF16)]
 
 
 def token_rows(tokens, heads):
@@ -282,7 +275,7 @@
     )
 
 
-def far_kernel(heads, groups, q_ref, pk_ref, pv_ref, ck_ref, cv_ref, out_ref, kf, kh, vh):
+def far_kernel(heads, groups, q_ref, pk_ref, pv_ref, ck_ref, cv_ref, out_ref, kf, kh, vh, logits, weights):
     step = pl.program_id(0)
     width = q_ref.shape[1]
 
@@ -294,7 +287,7 @@
         place(pv_ref, kf, vh, 0, groups)
         place(cv_ref, kf, vh, WIN, groups)
 
-    out_ref[...] = window_block(q_ref, kh, vh, pl.multiple_of(step * BLK, BLK), groups).astype(BF16)
+    out_ref[...] = window_block(q_ref, kh, vh, logits, weights, pl.multiple_of(step * BLK, BLK), groups).astype(BF16)
 
 
 def attention_cost(tokens, heads, width, extra=0):
@@ -328,6 +321,7 @@
             pltpu.VMEM((WIN * groups, width), F32),
             pltpu.VMEM((groups, 2 * WIN, width), BF16),
             pltpu.VMEM((groups, 2 * WIN, 2 * width), BF16),
+            *window_scratch(heads, groups),
         ],
         compiler_params=params(),
         cost_estimate=attention_cost(steps * BLK, heads, width),
@@ -335,7 +329,7 @@
     )(queries, keys, values, keys, values)
 
 
-def trunk_kernel(heads, groups, first, where_ref, gain_ref, q_ref, k_ref, v_ref, wq_ref, pk_ref, pv_ref, ck_ref, cv_ref, local_ref, out_ref, nf, tf, sf, kf, kh, vh, of):
+def trunk_kernel(heads, groups, first, where_ref, gain_ref, q_ref, k_ref, v_ref, wq_ref, pk_ref, pv_ref, ck_ref, cv_ref, local_ref, cross_ref, out_ref, square_ref, nf, tf, sf, kf, kh, vh, of, mine, logits, weights):
     block = pl.program_id(0) + first
     width = q_ref.shape[1]
 
@@ -346,6 +340,7 @@
         place(ck_ref, kf, kh, WIN, groups)
         place(pv_ref, kf, vh, 0, groups)
         place(cv_ref, kf, vh, WIN, groups)
+        mine[...] = token_rows(BLK, heads)
 
     nf[...] = q_ref[...].astype(F32)
     tf[...] = k_ref[...].astype(F32)
@@ -356,6 +351,7 @@
     row = lax.broadcasted_iota(jnp.int32, (BLK, BLK), 0)
     col = lax.broadcasted_iota(jnp.int32, (BLK, BLK), 1)
     inner = (block > 0).astype(F32).astype(BF16)
+    each = heads // COLS
     q = [every(q_ref, nf, heads, h) for h in range(heads)]
     inside = [
         lax.dot_general(q[h], every(k_ref, tf, heads, h), (((1,), (1,)), ((), ())), preferred_element_type=F32)
@@ -363,13 +359,16 @@
     ]
     for h in range(heads):
         weight = jnp.where(col <= row, inside[h], 0.0) * (gain_ref[h, 0] * gain_factor(0, width))
-        left = jnp.concatenate([weight.astype(BF16), q[h]], axis=1)
-        right = jnp.concatenate([every(v_ref, sf, heads, h), local_ref[0, h] * inner], axis=0)
+        left = jnp.concatenate([weight.astype(BF16), q[h], q[h]], axis=1)
+        cross = cross_ref[h // each, h % each]
+        right = jnp.concatenate([every(v_ref, sf, heads, h), cross, local_ref[0, h] * inner], axis=0)
         of[pl.ds(h, BLK, stride=heads), :] = jnp.dot(left, right, preferred_element_type=F32)
-    out_ref[...] = window_block(wq_ref, kh, vh, base, groups, bias) + of[...]
-
-
-def trunk_attention(where, gain, q, k, v, wq, before_kv, ck, cv, local, heads, groups, first, steps):
+    full = window_block(wq_ref, kh, vh, logits, weights, base, groups, bias) + of[...]
+    out_ref[...] = full
+    square_ref[0] = square_sums(full, mine[...])
+
+
+def trunk_attention(where, gain, q, k, v, wq, before_kv, ck, cv, local, cross, heads, groups, first, steps):
     width = q.shape[1]
     rows = BLK * heads
     at_block = pl.BlockSpec((rows, width), lambda i: (i + first, 0))
@@ -380,9 +379,12 @@
     return pl.pallas_call(
         functools.partial(trunk_kernel, heads, groups, first),
         grid=(steps,),
-        in_specs=[smem(), smem()] + [at_block] * 4 + [whole, second, whole, whole, before],
-        out_specs=pl.BlockSpec((rows, width), lambda i: (i, 0)),
-        out_shape=jax.ShapeDtypeStruct((steps * rows, width), F32),
+        in_specs=[smem(), smem()] + [at_block] * 4 + [whole, second, whole, whole, before, pl.BlockSpec(cross.shape, lambda i: (0, 0, 0, 0))],
+        out_specs=[pl.BlockSpec((rows, width), lambda i: (i, 0)), pl.BlockSpec((1, 8, BLK), lambda i: (i, 0, 0))],
+        out_shape=[
+            jax.ShapeDtypeStruct((steps * rows, width), F32),
+            jax.ShapeDtypeStruct((steps, 8, BLK), F32),
+        ],
         scratch_shapes=[
             wide,
             wide,
@@ -391,16 +393,18 @@
             pltpu.VMEM((groups, 2 * WIN, width), BF16),
             pltpu.VMEM((groups, 2 * WIN, 2 * width), BF16),
             wide,
+            pltpu.VMEM((BLK, rows), BF16),
+            *window_scratch(heads, groups),
         ],
         compiler_params=params(),
         cost_estimate=attention_cost(steps * BLK, heads, width, 2 * steps * BLK * BLK * heads * 3 * width),
         name="trunk_attention",
-    )(where, gain, q, k, v, wq, before_kv, before_kv, ck, cv, local)
+    )(where, gain, q, k, v, wq, before_kv, before_kv, ck, cv, local, cross)
 
 
 def near_kernel(groups, where_ref, fork_ref, q_ref, ck_ref, cv_ref, *rest):
     kv_refs, out_ref = rest[:COLS], rest[COLS]
-    kf, kh, vh, kt = rest[COLS + 1 :]
+    kf, kh, vh, kt, logits, weights = rest[COLS + 1 :]
     step = pl.program_id(0)
     width = q_ref.shape[1]
     column = where_ref[0] & (COLS - 1)
@@ -419,7 +423,7 @@
         place(cv_ref, kf, vh, pl.multiple_of(start + WIN, BLK), groups)
 
     base = pl.multiple_of(start + step * BLK, BLK)
-    out_ref[...] = window_block(q_ref, kh, vh, base, groups).astype(BF16)
+    out_ref[...] = window_block(q_ref, kh, vh, logits, weights, base, groups).astype(BF16)
 
 
 def near_attention(where, fork, wq, ck, cv, kvs, heads, groups):
@@ -438,6 +442,7 @@
             pltpu.VMEM((groups, 3 * WIN, width), BF16),
             pltpu.VMEM((groups, 3 * WIN, 2 * width), BF16),
             pltpu.VMEM((COLS, WIN * groups, width), BF16),
+            *window_scratch(heads, groups),
         ],
         compiler_params=params(),
         cost_estimate=attention_cost(steps * BLK, heads, width),
@@ -445,110 +450,75 @@
     )(where, fork, wq, ck, cv, *kvs)
 
 
-def final_kernel(heads, where_ref, fork_ref, bq_hbm, tq_hbm, near_hbm, far_hbm, trunk_hbm, cross_hbm, *rest):
-    end_hbms, (branch_full, trunk_full, square_ref, qs, ws, ts, nf, of, fs, es, cs, mine) = rest[:COLS], rest[COLS : COLS + 12]
-    q_sems, w_sems, f_sems, e_sems = rest[COLS + 12 :]
-    window_hbms = (near_hbm, far_hbm)
+def branch_kernel(heads, where_ref, fork_ref, trunk_square, q_hbm, near_hbm, far_hbm, *rest):
+    end_hbms, (full_hbm, square_ref, qs, ws, nf, of, fs, es, mine) = rest[:COLS], rest[COLS : COLS + 9]
+    q_sems, w_sems, f_sems, e_sems = rest[COLS + 9 :]
     rows = BLK * heads
-    branch_blocks, trunk_blocks = ws.shape[0] // rows, ts.shape[0] // rows
+    blocks = ws.shape[0] // rows
+    near = near_hbm.shape[0] // rows
     each = heads // COLS
     column = where_ref[0] & (COLS - 1)
     states = [
         pltpu.make_async_copy(end_hbms[i].at[fork_ref[0]], es.at[column ^ i], e_sems.at[i]) for i in range(COLS)
-    ] + [pltpu.make_async_copy(cross_hbm, cs, e_sems.at[COLS])]
-
-    def query_copy(src, b, slot):
-        return pltpu.make_async_copy(src.at[pl.ds(b * rows, rows)], qs.at[pl.ds(slot * rows, rows)], q_sems.at[slot])
-
-    def other_copy(src, b, dst, place_of, slot):
-        return pltpu.make_async_copy(
-            src.at[pl.ds(b * rows, rows)], dst.at[pl.ds(place_of * rows, rows)], w_sems.at[slot]
-        )
-
-    def result_copy(b, dst, slot):
-        return pltpu.make_async_copy(fs.at[pl.ds(slot * rows, rows)], dst.at[pl.ds(b * rows, rows)], f_sems.at[slot])
-
+    ]
     for copy in states:
         copy.start()
-    per_window = branch_blocks // 2
-    for b in range(branch_blocks):
-        query_copy(bq_hbm, b, b).start()
-        other_copy(window_hbms[b // per_window], b % per_window, ws, b, b).start()
-    for b in range(trunk_blocks):
-        query_copy(tq_hbm, b, branch_blocks + b).start()
-        other_copy(trunk_hbm, b, ts, b, branch_blocks + b).start()
+    for b in range(blocks):
+        block_copy(q_hbm, qs, q_sems, b, rows).start()
+        if b < near:
+            block_copy(near_hbm, ws, w_sems, b, rows).start()
+        else:
+            block_copy(far_hbm, ws, w_sems, b, rows, b - near).start()
     mine[...] = token_rows(BLK, heads)
+    square_ref[blocks:] = trunk_square[...]
     for copy in states:
         copy.wait()
 
-    def rest_of(slot, window, states_ref):
-        at = pl.ds(pl.multiple_of(slot * rows, rows), rows)
+    def one_block(b, carry):
+        block_copy(q_hbm, qs, q_sems, b, rows).wait()
+        block_copy(near_hbm, ws, w_sems, b, rows, 0).wait()
+        at = pl.ds(pl.multiple_of(b * rows, rows), rows)
         nf[...] = qs[at, :].astype(F32)
         for h in range(heads):
             q = nf[pl.ds(h, BLK, stride=heads), :].astype(BF16)
-            of[pl.ds(h, BLK, stride=heads), :] = jnp.dot(
-                q, states_ref[h // each, h % each], preferred_element_type=F32
-            )
-        full = window.astype(F32) + of[...]
+            of[pl.ds(h, BLK, stride=heads), :] = jnp.dot(q, es[h // each, h % each], preferred_element_type=F32)
+        full = ws[at, :].astype(F32) + of[...]
         fs[at, :] = full
-        square_ref[slot] = square_sums(full, mine[...])
-
-    def branch_block(b, carry):
-        query_copy(bq_hbm, b, b).wait()
-        other_copy(window_hbms[0], 0, ws, b, b).wait()
-        rest_of(b, ws[pl.ds(pl.multiple_of(b * rows, rows), rows), :], es)
-        result_copy(b, branch_full, b).start()
+        block_copy(fs, full_hbm, f_sems, b, rows).start()
+        square_ref[b] = square_sums(full, mine[...])
         return carry
 
-    def trunk_block(b, carry):
-        slot = branch_blocks + b
-        query_copy(tq_hbm, b, slot).wait()
-        other_copy(trunk_hbm, 0, ts, b, slot).wait()
-        rest_of(slot, ts[pl.ds(pl.multiple_of(b * rows, rows), rows), :], cs)
-        result_copy(b, trunk_full, slot).start()
-        return carry
-
-    lax.fori_loop(0, branch_blocks, branch_block, 0)
-    lax.fori_loop(0, trunk_blocks, trunk_block, 0)
-    for b in range(branch_blocks):
-        result_copy(b, branch_full, b).wait()
-    for b in range(trunk_blocks):
-        result_copy(b, trunk_full, branch_blocks + b).wait()
-
-
-def final_linear(where, fork, bq, tq, near, far, trunk, cross, ends, heads):
-    width = bq.shape[1]
+    lax.fori_loop(0, blocks, one_block, 0)
+    for b in range(blocks):
+        block_copy(fs, full_hbm, f_sems, b, rows).wait()
+
+
+def branch_linear(where, fork, trunk_square, q, near, far, ends, heads):
+    width = q.shape[1]
     rows = BLK * heads
-    total = bq.shape[0] + tq.shape[0]
-    blocks = total // rows
-    return pl.pallas_call(
-        functools.partial(final_kernel, heads),
-        in_specs=[smem(), smem()] + [hbm()] * (6 + COLS),
-        out_specs=[hbm(), hbm(), vmem()],
-        out_shape=[
-            jax.ShapeDtypeStruct(bq.shape, F32),
-            jax.ShapeDtypeStruct(tq.shape, F32),
-            jax.ShapeDtypeStruct((blocks, 8, BLK), F32),
-        ],
+    blocks = q.shape[0] // rows
+    return pl.pallas_call(
+        functools.partial(branch_kernel, heads),
+        in_specs=[smem(), smem(), vmem()] + [hbm()] * (3 + COLS),
+        out_specs=[hbm(), vmem()],
+        out_shape=[jax.ShapeDtypeStruct(q.shape, F32), jax.ShapeDtypeStruct((blocks + trunk_square.shape[0], 8, BLK), F32)],
         scratch_shapes=[
-            pltpu.VMEM((total, width), BF16),
-            pltpu.VMEM(bq.shape, BF16),
-            pltpu.VMEM(tq.shape, F32),
+            pltpu.VMEM(q.shape, BF16),
+            pltpu.VMEM(q.shape, BF16),
             pltpu.VMEM((rows, width), F32),
             pltpu.VMEM((rows, width), F32),
-            pltpu.VMEM((total, width), F32),
-            pltpu.VMEM(cross.shape, BF16),
-            pltpu.VMEM(cross.shape, BF16),
+            pltpu.VMEM(q.shape, F32),
+            pltpu.VMEM((COLS, heads // COLS, width, width), BF16),
             pltpu.VMEM((BLK, rows), BF16),
             pltpu.SemaphoreType.DMA((blocks,)),
             pltpu.SemaphoreType.DMA((blocks,)),
             pltpu.SemaphoreType.DMA((blocks,)),
-            pltpu.SemaphoreType.DMA((COLS + 1,)),
+            pltpu.SemaphoreType.DMA((COLS,)),
         ],
         compiler_params=params(),
-        cost_estimate=pl.CostEstimate(flops=4 * total * width * width, bytes_accessed=8 * total * width, transcendentals=0),
-        name="final_linear",
-    )(where, fork, bq, tq, near, far, trunk, cross, *ends)
+        cost_estimate=pl.CostEstimate(flops=4 * q.size * width, bytes_accessed=8 * q.size, transcendentals=0),
+        name="branch_linear",
+    )(where, fork, trunk_square, q, near, far, *ends)
 
 
 def norm_kernel(heads, features, trunk_hbm, branch_hbm, square_ref, other_ref, trunk_out, branch_out, held, done, in_sems, out_sems):
@@ -699,14 +669,12 @@
     kv, far = tie((kv, far))
     kvs = around(kv)
     ends = around((ends.astype(F32) + above).astype(BF16))
-    trunk = trunk_attention(
-        where, level_gain, tq, tk, tv, twq, before_kv, twk, twv, local, heads, groups, 0, tokens // BLK
+    trunk_full, trunk_square = trunk_attention(
+        where, level_gain, tq, tk, tv, twq, before_kv, twk, twv, local, cross, heads, groups, 0, tokens // BLK
     )
-    trunk, bwq = tie((trunk, bwq))
+    trunk_full, bwq = tie((trunk_full, bwq))
     near = near_attention(where, fork_block, bwq, bwk, bwv, kvs, heads, groups)
-    branch_full, trunk_full, square = final_linear(
-        where, fork_block, bq, tq, near, far, trunk, cross, ends, heads
-    )
+    branch_full, square = branch_linear(where, fork_block, trunk_square, bq, near, far, ends, heads)
     other = lax.ppermute(square, "head", [(0, 1), (1, 0)])
     trunk_out, branch_out = normalize(trunk_full, branch_full, square, other, heads, features)
     return trunk_out.reshape(trunk_query.shape), branch_out.reshape(branch_query.shape)

time: 108 us -> 108 us (level); the launches traced: 108 us -> 106 us
  Pallas kernels: 52.9 us -> 50.7 us
    pallas_call x1, Pallas kernels: 13.2 us -> 9.95 us  [branch_linear(): pl.pallas_call(functools.partial(branch_kernel, heads), in_specs=[smem(),...]
    pallas_call x1, Pallas kernels: 10.4 us -> 12.3 us  [trunk_attention(): pl.pallas_call(functools.partial(trunk_kernel, heads, groups, first), gri...]
  transfers between devices with their start and end apart: 19 -> 19, of which waited for: 3 -> 3; matrix products, arithmetic and copies ran while one was open for 0% -> 0% of each run, Pallas kernels for 32% -> 33%
where the time goes in v7:
time: 108 us; the launch traced here: 106 us
  Pallas kernels  50.7 us (47%)
  starting transfers between devices  43.5 us (40%)
  waiting for transfers between devices  6.63 us (6%)
  local copies, waits for them, and re-layouts  3.57 us (3%)
  between operations  1.66 us (2%)
    all_to_all x3, starting transfers between devices, in_groups(): lax.all_to_all(x, 'seq', 0, 0, tiled=True, axis_index_groups=groups_of)  23.8 us
    ppermute x15, starting transfers between devices, send(): return lax.ppermute(x, 'seq', pairs)  19.7 us
    pallas_call x1, Pallas kernels, trunk_attention(): pl.pallas_call(functools.partial(trunk_kernel, heads, groups, first), gri...  12.3 us
    pallas_call x1, Pallas kernels, branch_linear(): pl.pallas_call(functools.partial(branch_kernel, heads), in_specs=[smem(),...  9.95 us
    pallas_call x1, Pallas kernels, near_attention(): pl.pallas_call(functools.partial(near_kernel, groups), grid=(steps,), in_...  7.99 us
    pallas_call x1, Pallas kernels, far_attention(): pl.pallas_call(functools.partial(far_kernel, heads, groups), grid=(steps,...  7.62 us
    pallas_call x1, Pallas kernels, normalize(): pl.pallas_call(functools.partial(norm_kernel, heads, features), in_specs=...  5.41 us
    pallas_call x1, Pallas kernels, block_sums(): pl.pallas_call(functools.partial(state_kernel, depth, heads), in_specs=[s...  4.64 us
  transfers between devices with their start and end apart: 19, of which 3 were waited for; matrix products, arithmetic and copies ran while one was open for 0% of the time, Pallas kernels for 33%

profile of v7, /device:TPU:0, one launch (start us, length us, event | category | flops | bytes accessed | tf_op | source)
XLA Modules:
  0.0 106.4 jit_solution(12322083516311690480)
XLA Ops:
  0.6 0.0 copy-start.2
  0.6 0.8 collective-permute-start.4
  1.5 0.0 copy-start
  1.5 0.0 copy-start.7
  1.5 4.6 %block_sums.1 = (bf16[3,2,128,128]{3,2,1,0:T(8,128)(2,1)}, bf16[3,2,128,128]{3,2,1,0:T(8,128)(2,1)}, bf16[3,2,128,128]{3,2,1,0:T(8,128)(2,1)}, bf16[3,2,128,128]...) custom-call(f32[8,11]{1,0:T(8,128)} %gain_ref.7, bf16[4096,128]{1,0:T(8,128)(2,1)} %bitcast.14, ...), custom_call_target="tpu_custom_call" | custom-call | flops 134217728 | bytes 3145728 | tf_op jit(solution)/shard_map/block_sums/pallas_call | solution.py:97
  6.1 5.2 %all-to-all-start = ((bf16[4,2,128,128]{3,2,1,0:T(8,128)(2,1)}), bf16[4,2,128,128]{3,2,1,0:T(8,128)(2,1)S(1)}, u32[]{:S(2)}, u32[]{:S(2)}) async-start(bf16[4,2,128,128]{3,2,1,0:T(8,128)(2,1)} %get-tuple-element.23), calls=%async_computation | async-start | bytes 524288 | tf_op jit(solution)/shard_map/all_to_all | solution.py:643
  11.3 0.7 collective-permute-start.1
  12.0 0.7 collective-permute-start.2
  12.7 0.7 collective-permute-start.3
  13.4 0.0 collective-permute-done.4
  13.4 0.0 copy-done.2
  13.4 0.7 collective-permute-start.5
  14.1 0.0 collective-permute-done.1
  14.1 0.0 collective-permute-done.2
  14.1 0.0 collective-permute-done.3
  14.1 0.1 select_select_fusion.local_ref
  14.2 2.5 %all-to-all-done.sums_ref = bf16[4,2,128,128]{3,2,1,0:T(8,128)(2,1)S(1)} async-done(((bf16[4,2,128,128]{3,2,1,0:T(8,128)(2,1)}), bf16[4,2,128,128]{3,2,1,0:T(8,128)(2,1)S(1)}, u32[]{:S(2)}, u32[]{:S(2)}) %all-to-all-start) | async-done | bytes 262176 | tf_op jit(solution)/shard_map/all_to_all | solution.py:643
  16.7 0.0 copy-done
  16.7 1.3 %plane_sums.1 = (bf16[4,2,128,128]{3,2,1,0:T(8,128)(2,1)}, bf16[4,2,128,128]{3,2,1,0:T(8,128)(2,1)S(1)}) custom-call(s32[1]{0:T(128)} %bitcast.where_ref, f32[8,11]{1,0:T(8,128)S(1)} %copy-done, bf16[4,2,128,128]{3,2,1,0:T(8,128)(2,1)S(1)} %all-to-all-done.sums_ref, bf16[3,2,128,128]{3,2,1,0:T(8,128)(2,1)S(1)} %select_select_fusion.local_ref), custom_call_target="tpu_custom_call" | custom-call | flops 524288 | bytes 1048576 | tf_op jit(solution)/shard_map/plane_sums/pallas_call | solution.py:153
  18.0 0.7 collective-permute-start.10
  18.7 0.0 copy-done.7
  18.8 3.2 %collective-permute-start = (bf16[2048,128]{1,0:T(8,128)(2,1)S(1)}, bf16[2048,128]{1,0:T(8,128)(2,1)S(1)}, u32[]{:S(2)}, u32[]{:S(2)}) collective-permute-start(bf16[2048,128]{1,0:T(8,128)(2,1)S(1)} %pad_maximum_fusion), channel_id=1, source_target_pairs={{0,2},{2,4},{4,6},{6,8},{8,10},{10,12},{12,14},{14,16},{16,18},{18... | collective-permute-start | bytes 1572872 | tf_op jit(solution)/shard_map/ppermute | solution.py:620
  22.0 15.2 %all-to-all-start.1 = ((bf16[4,2,128,128]{3,2,1,0:T(8,128)(2,1)}), bf16[4,2,128,128]{3,2,1,0:T(8,128)(2,1)S(1)}, u32[]{:S(2)}, u32[]{:S(2)}) async-start(bf16[4,2,128,128]{3,2,1,0:T(8,128)(2,1)} %get-tuple-element.28), calls=%async_computation.1 | async-start | bytes 524288 | tf_op jit(solution)/shard_map/all_to_all | solution.py:643
  37.2 0.0 collective-permute-done.5
  37.2 1.3 %collective-permute-start.6 = (bf16[1024,128]{1,0:T(8,128)(2,1)S(1)}, bf16[1024,128]{1,0:T(8,128)(2,1)S(1)}, u32[]{:S(2)}, u32[]{:S(2)}) collective-permute-start(bf16[1024,128]{1,0:T(8,128)(2,1)S(1)} %broadcast_select_fusion.2), channel_id=1, source_target_pairs={{8,0},{10,2},{12,4},{14,6},{24,16},{26,18},{28,20},{30,22},{9,1},{... | collective-permute-start | bytes 786440 | tf_op jit(solution)/shard_map/ppermute | solution.py:620
  38.5 0.0 collective-permute-done.10
  38.6 1.3 %collective-permute-start.11 = (bf16[4,2,128,128]{3,2,1,0:T(8,128)(2,1)S(1)}, bf16[4,2,128,128]{3,2,1,0:T(8,128)(2,1)S(1)}, u32[]{:S(2)}, u32[]{:S(2)}) collective-permute-start(bf16[4,2,128,128]{3,2,1,0:T(8,128)(2,1)S(1)} %broadcast_select_fusion), channel_id=1, source_target_pairs={{8,0},{10,2},{12,4},{14,6},{24,16},{26,18},{28,20},{30,22},{9,1},{... | collective-permute-start | bytes 786440 | tf_op jit(solution)/shard_map/ppermute | solution.py:620
  39.9 7.6 %far_attention.1.far_hbm = bf16[4096,128]{1,0:T(8,128)(2,1)} custom-call(bf16[8192,128]{1,0:T(8,128)(2,1)} %bitcast.24, bf16[2048,128]{1,0:T(8,128)(2,1)} %bitcast.30, bf16[2048,128]{1,0:T(8,128)(2,1)} %bitcast.33, bf16[2048,128]{1,0:T(8,128)(2,1)} %bitcast.31, bf16[2048,128]{1,0:T(8,128)(2,1)} %bitcast.34), custom_call_target="tpu_custom_call" | custom-call | flops 2013265920 | bytes 6291456 | tf_op jit(solution)/shard_map/far_attention/pallas_call | solution.py:308
  47.5 2.7 %collective-permute-done.6 = bf16[1024,128]{1,0:T(8,128)(2,1)S(1)} collective-permute-done((bf16[1024,128]{1,0:T(8,128)(2,1)S(1)}, bf16[1024,128]{1,0:T(8,128)(2,1)S(1)}, u32[]{:S(2)}, u32[]{:S(2)}) %collective-permute-start.6) | collective-permute-done | bytes 262176 | tf_op jit(solution)/shard_map/ppermute | solution.py:620
  50.2 0.0 copy-start.8
  50.2 2.7 %collective-permute-start.9 = (bf16[1024,128]{1,0:T(8,128)(2,1)S(1)}, bf16[1024,128]{1,0:T(8,128)(2,1)S(1)}, u32[]{:S(2)}, u32[]{:S(2)}) collective-permute-start(bf16[1024,128]{1,0:T(8,128)(2,1)S(1)} %broadcast_select_fusion.3.rest_0_), channel_id=1, source_target_pairs={{0,6},{2,4},{4,2},{6,0},{8,14},{10,12},{12,10},{14,8},{16,22},{18,... | collective-permute-start | bytes 786440 | tf_op jit(solution)/shard_map/ppermute | solution.py:620
  53.6 0.0 all-to-all-done.1.planes_ref
  53.6 1.4 %cross_sums.1 = (bf16[4,2,128,128]{3,2,1,0:T(8,128)(2,1)}, f32[2,128,128]{2,1,0:T(8,128)S(1)}) custom-call(s32[1]{0:T(128)} %bitcast.where_ref, f32[8,11]{1,0:T(8,128)S(1)} %copy-done, bf16[4,2,128,128]{3,2,1,0:T(8,128)(2,1)S(1)} %all-to-all-done.sums_ref, bf16[4,2,128,128]{3,2,1,0:T(8,128)(2,1)S(1)} %all-to-all-done.1.planes_ref), custom_call_target="tpu_custom_call" | custom-call | flops 2621440 | bytes 1048576 | tf_op jit(solution)/shard_map/cross_sums/pallas_call | solution.py:194
  55.0 3.4 %all-to-all-start.2 = ((bf16[4,2,128,128]{3,2,1,0:T(8,128)(2,1)}), bf16[4,2,128,128]{3,2,1,0:T(8,128)(2,1)S(1)}, u32[]{:S(2)}, u32[]{:S(2)}) async-start(bf16[4,2,128,128]{3,2,1,0:T(8,128)(2,1)} %get-tuple-element.29), calls=%async_computation.2 | async-start | bytes 524288 | tf_op jit(solution)/shard_map/all_to_all | solution.py:643
  58.4 2.0 %collective-permute-start.8 = (bf16[1024,128]{1,0:T(8,128)(2,1)S(1)}, bf16[1024,128]{1,0:T(8,128)(2,1)S(1)}, u32[]{:S(2)}, u32[]{:S(2)}) collective-permute-start(bf16[1024,128]{1,0:T(8,128)(2,1)S(1)} %broadcast_select_fusion.3.rest_0_), channel_id=1, source_target_pairs={{0,4},{2,6},{4,0},{6,2},{8,12},{10,14},{12,8},{14,10},{16,20},{18,... | collective-permute-start | bytes 786440 | tf_op jit(solution)/shard_map/ppermute | solution.py:620
  60.4 1.5 %collective-permute-start.7 = (bf16[1024,128]{1,0:T(8,128)(2,1)S(1)}, bf16[1024,128]{1,0:T(8,128)(2,1)S(1)}, u32[]{:S(2)}, u32[]{:S(2)}) collective-permute-start(bf16[1024,128]{1,0:T(8,128)(2,1)S(1)} %broadcast_select_fusion.3.rest_0_), channel_id=1, source_target_pairs={{0,2},{2,0},{4,6},{6,4},{8,10},{10,8},{12,14},{14,12},{16,18},{18,... | collective-permute-start | bytes 786440 | tf_op jit(solution)/shard_map/ppermute | solution.py:620
  61.9 0.0 collective-permute-done.11
  61.9 0.1 add_convert_fusion.rest_0_
  62.0 0.0 copy-start.1
  62.0 0.2 collective-permute-start.14
  62.2 0.0 collective-permute-done.pk_ref.pv_ref
  62.2 1.9 %collective-permute-start.13 = (bf16[4,2,128,128]{3,2,1,0:T(8,128)(2,1)S(1)}, bf16[4,2,128,128]{3,2,1,0:T(8,128)(2,1)S(1)}, u32[]{:S(2)}, u32[]{:S(2)}) collective-permute-start(bf16[4,2,128,128]{3,2,1,0:T(8,128)(2,1)S(1)} %add_convert_fusion.rest_0_), channel_id=1, source_target_pairs={{0,4},{2,6},{4,0},{6,2},{8,12},{10,14},{12,8},{14,10},{16,20},{18,... | collective-permute-start | bytes 786440 | tf_op jit(solution)/shard_map/ppermute | solution.py:620
  64.1 0.0 collective-permute-done.9.rest_3_
  64.1 1.5 %collective-permute-start.12 = (bf16[4,2,128,128]{3,2,1,0:T(8,128)(2,1)S(1)}, bf16[4,2,128,128]{3,2,1,0:T(8,128)(2,1)S(1)}, u32[]{:S(2)}, u32[]{:S(2)}) collective-permute-start(bf16[4,2,128,128]{3,2,1,0:T(8,128)(2,1)S(1)} %add_convert_fusion.rest_0_), channel_id=1, source_target_pairs={{0,2},{2,0},{4,6},{6,4},{8,10},{10,8},{12,14},{14,12},{16,18},{18,... | collective-permute-start | bytes 786440 | tf_op jit(solution)/shard_map/ppermute | solution.py:620
  65.6 0.0 all-to-all-done.2.cross_ref
  65.6 0.7 copy-done.6
  66.2 12.3 %trunk_attention.1 = (f32[4096,128]{1,0:T(8,128)}, f32[4,8,128]{2,1,0:T(8,128)}) custom-call(s32[1]{0:T(128)} %bitcast.where_ref, f32[8,11]{1,0:T(8,128)} %gain_ref.7, bf16[4096,128]{1,0:T(8,128)(2,1)} %bitcast.27, bf16[4096,128]{1,0:T(8,128)(2,1)} %bitcast.15, bf16[4096,128]{1,0:T(8,128)(2,1)} %bitcast.17, bf16[4096,128]{1,0:T(8,128)(2,1)} %bitcast.28, ...), custom_call_target="tpu_custom_call" | custom-call | flops 2415919104 | bytes 6291456 | tf_op jit(solution)/shard_map/trunk_attention/pallas_call | solution.py:379
  78.6 0.0 collective-permute-done.8.rest_2_
  78.6 0.0 collective-permute-done.7.rest_1_
  78.6 0.0 copy-done.11
  78.6 0.7 copy-done.12
  79.3 0.7 copy-done.13
  80.0 8.0 %near_attention.1.near_hbm = bf16[4096,128]{1,0:T(8,128)(2,1)} custom-call(s32[1]{0:T(128)} %bitcast.where_ref, s32[1]{0:T(128)S(6)} %copy.14.fork_ref, bf16[8192,128]{1,0:T(8,128)(2,1)} %bitcast.25, bf16[2048,128]{1,0:T(8,128)(2,1)} %bitcast.32, bf16[2048,128]{1,0:T(8,128)(2,1)} %bitcast.35, bf16[1024,128]{1,0:T(8,128)(2,1)} %copy-done.8, ...), custom_call_target="tpu_custom_call" | custom-call | flops 2013265920 | bytes 6291456 | tf_op jit(solution)/shard_map/near_attention/pallas_call | solution.py:434
  88.0 0.0 collective-permute-done.14.rest_3_
  88.0 0.0 collective-permute-done.13.rest_2_
  88.0 0.0 collective-permute-done.12.rest_1_
  88.0 0.6 copy-done.3
  88.7 0.1 copy-done.4
  88.8 0.1 copy-done.5
  88.9 10.0 %branch_linear.1 = (f32[8192,128]{1,0:T(8,128)}, f32[12,8,128]{2,1,0:T(8,128)}) custom-call(s32[1]{0:T(128)} %bitcast.where_ref, s32[1]{0:T(128)S(6)} %copy.14.fork_ref, f32[4,8,128]{2,1,0:T(8,128)} %get-tuple-element.32.trunk_square, bf16[8192,128]{1,0:T(8,128)(2,1)} %bitcast.13, bf16[4096,128]{1,0:T(8,128)(2,1)} %near_attention.1.near_hbm, ...), custom_call_target="tpu_custom_call" | custom-call | flops 536870912 | bytes 8388608 | tf_op jit(solution)/shard_map/branch_linear/pallas_call | solution.py:500
  98.9 0.1 collective-permute-start.15
  98.9 1.4 %collective-permute-done.15.other_ref = f32[12,8,128]{2,1,0:T(8,128)S(1)} collective-permute-done((f32[12,8,128]{2,1,0:T(8,128)}, f32[12,8,128]{2,1,0:T(8,128)S(1)}, u32[]{:S(2)}, u32[]{:S(2)}) %collective-permute-start.15) | collective-permute-done | bytes 49184 | tf_op jit(solution)/shard_map/ppermute | solution.py:678
  100.4 0.6 copy-done.9
  101.0 5.4 %normalize.1 = (bf16[4096,128]{1,0:T(8,128)(2,1)}, bf16[8192,128]{1,0:T(8,128)(2,1)}) custom-call(f32[4096,128]{1,0:T(8,128)} %get-tuple-element.31.trunk_hbm, f32[8192,128]{1,0:T(8,128)} %get-tuple-element.38.branch_hbm, f32[12,8,128]{2,1,0:T(8,128)} %get-tuple-element.39.square_ref, f32[12,8,128]{2,1,0:T(8,128)} %copy-done.9), custom_call_target="tpu_custom_call" | custom-call | flops 3145728 | bytes 9437184 | tf_op jit(solution)/shard_map/normalize/pallas_call | solution.py:567
  (17 shorter events, 0.2 us)
Async XLA Ops:
  0.6 12.7 %copy-start.2 = (bf16[512,2,128]{2,1,0:T(2,128)(2,1)S(1)}, bf16[512,2,128]{2,1,0:T(2,128)(2,1)}, u32[]{:S(2)}) copy-start(bf16[512,2,128]{2,1,0:T(2,128)(2,1)} %param.16) | copy-start | bytes 786436
  0.6 12.7 %collective-permute-start.4 = (bf16[1024,128]{1,0:T(8,128)(2,1)}, bf16[1024,128]{1,0:T(8,128)(2,1)S(1)}, u32[]{:S(2)}, u32[]{:S(2)}) collective-permute-start(bf16[1024,128]{1,0:T(8,128)(2,1)} %bitcast.21), channel_id=1, source_target_pairs={{30,26},{28,24},{31,27},{29,25}} | collective-permute-start | bytes 786440 | tf_op jit(solution)/shard_map/ppermute | solution.py:620
  1.5 15.2 %copy-start = (f32[8,11]{1,0:T(8,128)S(1)}, f32[8,11]{1,0:T(8,128)}, u32[]{:S(2)}) copy-start(f32[8,11]{1,0:T(8,128)} %gain_ref.7) | copy-start | bytes 1060
  1.5 17.2 %copy-start.7 = (bf16[512,2,128]{2,1,0:T(2,128)(2,1)S(1)}, bf16[512,2,128]{2,1,0:T(2,128)(2,1)}, u32[]{:S(2)}) copy-start(bf16[512,2,128]{2,1,0:T(2,128)(2,1)} %param.17) | copy-start | bytes 786436
  6.1 10.5 %all-to-all-start = ((bf16[4,2,128,128]{3,2,1,0:T(8,128)(2,1)}), bf16[4,2,128,128]{3,2,1,0:T(8,128)(2,1)S(1)}, u32[]{:S(2)}, u32[]{:S(2)}) async-start(bf16[4,2,128,128]{3,2,1,0:T(8,128)(2,1)} %get-tuple-element.23), calls=%async_computation | async-start | bytes 524288 | tf_op jit(solution)/shard_map/all_to_all | solution.py:643
  11.3 2.8 %collective-permute-start.1 = (bf16[3,2,128,128]{3,2,1,0:T(8,128)(2,1)}, bf16[3,2,128,128]{3,2,1,0:T(8,128)(2,1)S(1)}, u32[]{:S(2)}, u32[]{:S(2)}) collective-permute-start(bf16[3,2,128,128]{3,2,1,0:T(8,128)(2,1)} %get-tuple-element.24), channel_id=1, source_target_pairs={{30,28},{31,29}} | collective-permute-start | bytes 589832 | tf_op jit(solution)/shard_map/ppermute | solution.py:620
  12.0 2.1 %collective-permute-start.2 = (bf16[3,2,128,128]{3,2,1,0:T(8,128)(2,1)}, bf16[3,2,128,128]{3,2,1,0:T(8,128)(2,1)S(1)}, u32[]{:S(2)}, u32[]{:S(2)}) collective-permute-start(bf16[3,2,128,128]{3,2,1,0:T(8,128)(2,1)} %get-tuple-element.25), channel_id=1, source_target_pairs={{30,26},{31,27}} | collective-permute-start | bytes 589832 | tf_op jit(solution)/shard_map/ppermute | solution.py:620
  12.7 1.5 %collective-permute-start.3 = (bf16[3,2,128,128]{3,2,1,0:T(8,128)(2,1)}, bf16[3,2,128,128]{3,2,1,0:T(8,128)(2,1)S(1)}, u32[]{:S(2)}, u32[]{:S(2)}) collective-permute-start(bf16[3,2,128,128]{3,2,1,0:T(8,128)(2,1)} %get-tuple-element.26), channel_id=1, source_target_pairs={{30,24},{31,25}} | collective-permute-start | bytes 589832 | tf_op jit(solution)/shard_map/ppermute | solution.py:620
  13.4 23.8 %collective-permute-start.5 = (bf16[1024,128]{1,0:T(8,128)(2,1)S(1)}, bf16[1024,128]{1,0:T(8,128)(2,1)S(1)}, u32[]{:S(2)}, u32[]{:S(2)}) collective-permute-start(bf16[1024,128]{1,0:T(8,128)(2,1)S(1)} %broadcast_select_fusion.1), channel_id=1, source_target_pairs={{24,8},{26,10},{28,12},{30,14},{25,9},{27,11},{29,13},{31,15}} | collective-permute-start | bytes 786440 | tf_op jit(solution)/shard_map/ppermute | solution.py:620
  18.0 20.5 %collective-permute-start.10 = (bf16[4,2,128,128]{3,2,1,0:T(8,128)(2,1)S(1)}, bf16[4,2,128,128]{3,2,1,0:T(8,128)(2,1)S(1)}, u32[]{:S(2)}, u32[]{:S(2)}) collective-permute-start(bf16[4,2,128,128]{3,2,1,0:T(8,128)(2,1)S(1)} %get-tuple-element.36), channel_id=1, source_target_pairs={{24,8},{26,10},{28,12},{30,14},{25,9},{27,11},{29,13},{31,15}} | collective-permute-start | bytes 786440 | tf_op jit(solution)/shard_map/ppermute | solution.py:620
  18.8 43.4 %collective-permute-start = (bf16[2048,128]{1,0:T(8,128)(2,1)S(1)}, bf16[2048,128]{1,0:T(8,128)(2,1)S(1)}, u32[]{:S(2)}, u32[]{:S(2)}) collective-permute-start(bf16[2048,128]{1,0:T(8,128)(2,1)S(1)} %pad_maximum_fusion), channel_id=1, source_target_pairs={{0,2},{2,4},{4,6},{6,8},{8,10},{10,12},{12,14},{14,16},{16,18},{18... | collective-permute-start | bytes 1572872 | tf_op jit(solution)/shard_map/ppermute | solution.py:620
  22.0 31.6 %all-to-all-start.1 = ((bf16[4,2,128,128]{3,2,1,0:T(8,128)(2,1)}), bf16[4,2,128,128]{3,2,1,0:T(8,128)(2,1)S(1)}, u32[]{:S(2)}, u32[]{:S(2)}) async-start(bf16[4,2,128,128]{3,2,1,0:T(8,128)(2,1)} %get-tuple-element.28), calls=%async_computation.1 | async-start | bytes 524288 | tf_op jit(solution)/shard_map/all_to_all | solution.py:643
  37.2 13.0 %collective-permute-start.6 = (bf16[1024,128]{1,0:T(8,128)(2,1)S(1)}, bf16[1024,128]{1,0:T(8,128)(2,1)S(1)}, u32[]{:S(2)}, u32[]{:S(2)}) collective-permute-start(bf16[1024,128]{1,0:T(8,128)(2,1)S(1)} %broadcast_select_fusion.2), channel_id=1, source_target_pairs={{8,0},{10,2},{12,4},{14,6},{24,16},{26,18},{28,20},{30,22},{9,1},{... | collective-permute-start | bytes 786440 | tf_op jit(solution)/shard_map/ppermute | solution.py:620
  38.6 23.3 %collective-permute-start.11 = (bf16[4,2,128,128]{3,2,1,0:T(8,128)(2,1)S(1)}, bf16[4,2,128,128]{3,2,1,0:T(8,128)(2,1)S(1)}, u32[]{:S(2)}, u32[]{:S(2)}) collective-permute-start(bf16[4,2,128,128]{3,2,1,0:T(8,128)(2,1)S(1)} %broadcast_select_fusion), channel_id=1, source_target_pairs={{8,0},{10,2},{12,4},{14,6},{24,16},{26,18},{28,20},{30,22},{9,1},{... | collective-permute-start | bytes 786440 | tf_op jit(solution)/shard_map/ppermute | solution.py:620
  50.2 28.4 %copy-start.8 = (bf16[1024,128]{1,0:T(8,128)(2,1)}, bf16[1024,128]{1,0:T(8,128)(2,1)S(1)}, u32[]{:S(2)}) copy-start(bf16[1024,128]{1,0:T(8,128)(2,1)S(1)} %broadcast_select_fusion.3.rest_0_) | copy-start | bytes 786436
  50.2 13.9 %collective-permute-start.9 = (bf16[1024,128]{1,0:T(8,128)(2,1)S(1)}, bf16[1024,128]{1,0:T(8,128)(2,1)S(1)}, u32[]{:S(2)}, u32[]{:S(2)}) collective-permute-start(bf16[1024,128]{1,0:T(8,128)(2,1)S(1)} %broadcast_select_fusion.3.rest_0_), channel_id=1, source_target_pairs={{0,6},{2,4},{4,2},{6,0},{8,14},{10,12},{12,10},{14,8},{16,22},{18,... | collective-permute-start | bytes 786440 | tf_op jit(solution)/shard_map/ppermute | solution.py:620
  55.0 10.5 %all-to-all-start.2 = ((bf16[4,2,128,128]{3,2,1,0:T(8,128)(2,1)}), bf16[4,2,128,128]{3,2,1,0:T(8,128)(2,1)S(1)}, u32[]{:S(2)}, u32[]{:S(2)}) async-start(bf16[4,2,128,128]{3,2,1,0:T(8,128)(2,1)} %get-tuple-element.29), calls=%async_computation.2 | async-start | bytes 524288 | tf_op jit(solution)/shard_map/all_to_all | solution.py:643
  58.4 20.2 %collective-permute-start.8 = (bf16[1024,128]{1,0:T(8,128)(2,1)S(1)}, bf16[1024,128]{1,0:T(8,128)(2,1)S(1)}, u32[]{:S(2)}, u32[]{:S(2)}) collective-permute-start(bf16[1024,128]{1,0:T(8,128)(2,1)S(1)} %broadcast_select_fusion.3.rest_0_), channel_id=1, source_target_pairs={{0,4},{2,6},{4,0},{6,2},{8,12},{10,14},{12,8},{14,10},{16,20},{18,... | collective-permute-start | bytes 786440 | tf_op jit(solution)/shard_map/ppermute | solution.py:620
  60.4 18.2 %collective-permute-start.7 = (bf16[1024,128]{1,0:T(8,128)(2,1)S(1)}, bf16[1024,128]{1,0:T(8,128)(2,1)S(1)}, u32[]{:S(2)}, u32[]{:S(2)}) collective-permute-start(bf16[1024,128]{1,0:T(8,128)(2,1)S(1)} %broadcast_select_fusion.3.rest_0_), channel_id=1, source_target_pairs={{0,2},{2,0},{4,6},{6,4},{8,10},{10,8},{12,14},{14,12},{16,18},{18,... | collective-permute-start | bytes 786440 | tf_op jit(solution)/shard_map/ppermute | solution.py:620
  62.0 16.6 %copy-start.1 = (bf16[4,2,128,128]{3,2,1,0:T(8,128)(2,1)}, bf16[4,2,128,128]{3,2,1,0:T(8,128)(2,1)S(1)}, u32[]{:S(2)}) copy-start(bf16[4,2,128,128]{3,2,1,0:T(8,128)(2,1)S(1)} %add_convert_fusion.rest_0_) | copy-start | bytes 786436
  62.0 26.0 %collective-permute-start.14 = (bf16[4,2,128,128]{3,2,1,0:T(8,128)(2,1)S(1)}, bf16[4,2,128,128]{3,2,1,0:T(8,128)(2,1)S(1)}, u32[]{:S(2)}, u32[]{:S(2)}) collective-permute-start(bf16[4,2,128,128]{3,2,1,0:T(8,128)(2,1)S(1)} %add_convert_fusion.rest_0_), channel_id=1, source_target_pairs={{0,6},{2,4},{4,2},{6,0},{8,14},{10,12},{12,10},{14,8},{16,22},{18,... | collective-permute-start | bytes 786440 | tf_op jit(solution)/shard_map/ppermute | solution.py:620
  62.2 3.4 %copy-start.10 = (bf16[2048,128]{1,0:T(8,128)(2,1)}, bf16[2048,128]{1,0:T(8,128)(2,1)S(1)}, u32[]{:S(2)}) copy-start(bf16[2048,128]{1,0:T(8,128)(2,1)S(1)} %collective-permute-done.pk_ref.pv_ref) | copy-start | bytes 1572868
  62.2 25.9 %collective-permute-start.13 = (bf16[4,2,128,128]{3,2,1,0:T(8,128)(2,1)S(1)}, bf16[4,2,128,128]{3,2,1,0:T(8,128)(2,1)S(1)}, u32[]{:S(2)}, u32[]{:S(2)}) collective-permute-start(bf16[4,2,128,128]{3,2,1,0:T(8,128)(2,1)S(1)} %add_convert_fusion.rest_0_), channel_id=1, source_target_pairs={{0,4},{2,6},{4,0},{6,2},{8,12},{10,14},{12,8},{14,10},{16,20},{18,... | collective-permute-start | bytes 786440 | tf_op jit(solution)/shard_map/ppermute | solution.py:620
  64.1 14.5 %copy-start.11 = (bf16[1024,128]{1,0:T(8,128)(2,1)}, bf16[1024,128]{1,0:T(8,128)(2,1)S(1)}, u32[]{:S(2)}) copy-start(bf16[1024,128]{1,0:T(8,128)(2,1)S(1)} %collective-permute-done.9.rest_3_) | copy-start | bytes 786436
  64.1 23.9 %collective-permute-start.12 = (bf16[4,2,128,128]{3,2,1,0:T(8,128)(2,1)S(1)}, bf16[4,2,128,128]{3,2,1,0:T(8,128)(2,1)S(1)}, u32[]{:S(2)}, u32[]{:S(2)}) collective-permute-start(bf16[4,2,128,128]{3,2,1,0:T(8,128)(2,1)S(1)} %add_convert_fusion.rest_0_), channel_id=1, source_target_pairs={{0,2},{2,0},{4,6},{6,4},{8,10},{10,8},{12,14},{14,12},{16,18},{18,... | collective-permute-start | bytes 786440 | tf_op jit(solution)/shard_map/ppermute | solution.py:620
  65.6 0.7 copy-start.6
  78.6 0.7 copy-start.12
  79.3 0.7 copy-start.13
  88.0 0.7 copy-start.3
  88.0 0.8 copy-start.4
  88.0 0.9 copy-start.5
  98.9 1.5 %collective-permute-start.15 = (f32[12,8,128]{2,1,0:T(8,128)}, f32[12,8,128]{2,1,0:T(8,128)S(1)}, u32[]{:S(2)}, u32[]{:S(2)}) collective-permute-start(f32[12,8,128]{2,1,0:T(8,128)} %get-tuple-element.39.square_ref), channel_id=1, source_target_pairs={{0,1},{1,0},{2,3},{3,2},{4,5},{5,4},{6,7},{7,6},{8,9},{9,8},{10,11... | collective-permute-start | bytes 147464 | tf_op jit(solution)/shard_map/ppermute | solution.py:678
  100.4 0.6 copy-start.9

commit v8 on v7

--- a/solution.py
+++ b/solution.py
@@ -134,7 +134,7 @@
     return gain_ref[head, depth + bit + 1] * gain_factor(depth + bit + 1, width)
 
 
-def plane_kernel(depth, where_ref, gain_ref, sums_ref, local_ref, plane_ref, ends_ref):
+def plane_kernel(depth, where_ref, gain_ref, sums_ref, plane_ref, before_ref):
     each, width = sums_ref.shape[1], sums_ref.shape[2]
     first = (where_ref[0] & (COLS - 1)) * each
     for j in range(each):
@@ -142,26 +142,20 @@
         whole = functools.reduce(jnp.add, sums).astype(BF16)
         for p in range(plane_ref.shape[0]):
             plane_ref[p, j] = whole
-        before = in_plane(sums, COLS - 1, lambda bit: level_weight(gain_ref, first + j, depth, width, bit))
-        ends_ref[0, j] = before.astype(BF16)
-        for f in range(local_ref.shape[0]):
-            ends_ref[f + 1, j] = (before + local_ref[f, j].astype(F32)).astype(BF16)
-
-
-def plane_sums(where, gain, sums, local, planes, depth):
+        before_ref[j] = in_plane(sums, COLS - 1, lambda bit: level_weight(gain_ref, first + j, depth, width, bit))
+
+
+def plane_sums(where, gain, sums, planes, depth):
     quarter = sums.shape[1:]
     return pl.pallas_call(
         functools.partial(plane_kernel, depth),
-        in_specs=[smem(), smem(), vmem(), vmem()],
+        in_specs=[smem(), smem(), vmem()],
         out_specs=[vmem(), vmem()],
-        out_shape=[
-            jax.ShapeDtypeStruct((planes, *quarter), BF16),
-            jax.ShapeDtypeStruct((local.shape[0] + 1, *quarter), BF16),
-        ],
+        out_shape=[jax.ShapeDtypeStruct((planes, *quarter), BF16), jax.ShapeDtypeStruct(quarter, F32)],
         compiler_params=params(SMALL_BYTES),
         cost_estimate=pl.CostEstimate(flops=4 * sums.size, bytes_accessed=8 * sums.size, transcendentals=0),
         name="plane_sums",
-    )(where, gain, sums, local)
+    )(where, gain, sums)
 
 
 def cross_kernel(depth, where_ref, gain_ref, sums_ref, planes_ref, out_ref, top_ref):
@@ -651,17 +645,23 @@
 
     half = COLS // 2
     got = send(twv, [(root - i, root - i - half) for i in range(half)])
-    kv = down(jnp.where(column >= half, twk, got))
     before_kv = send(jnp.concatenate([twk, twv], axis=0), [(i, i + 1) for i in range(count - 1)])
 
     *pieces, local, shard_sum = block_sums(level_gain, tk, tv, heads, depth)
+    gots = [send(pieces[c], [(root, root - (COLS - 1) + c)]) for c in range(COLS - 1)]
+    sums = in_groups(shard_sum, in_one_plane)
+    kv = jnp.where(column >= half, twk, got)
+    sums, kv = tie((sums, kv))
+    kv = down_first(kv)
+    plane_sum, before = plane_sums(where, level_gain, sums, planes, depth)
+    plane_sum = in_groups(plane_sum, in_one_column)
+    gots, plane_sum, kv = tie((gots, plane_sum, kv))
+    kv = down_rest(kv)
     mine = pieces[COLS - 1]
     for c in range(COLS - 1):
-        mine = jnp.where(column == c, send(pieces[c], [(root, root - (COLS - 1) + c)]), mine)
-    sums = in_groups(shard_sum, in_one_plane)
-    plane_sum, ends = plane_sums(where, level_gain, sums, mine, planes, depth)
-    plane_sum = in_groups(plane_sum, in_one_column)
-    ends = down(ends)
+        mine = jnp.where(column == c, gots[c], mine)
+    ends = jnp.concatenate([jnp.zeros_like(mine[:1]), mine], axis=0)
+    ends = down((before[None] + ends.astype(F32)).astype(BF16))
     cross, above = cross_sums(where, level_gain, sums, plane_sum, depth)
     cross = in_groups(cross, in_one_plane)
 

time: 108 us -> 112 us (1.037)
  the two profiles are of different devices: /device:TPU:0 before, /device:TPU:9 now
where the time goes in v8:
time: 112 us; the launch traced here: 111 us
  Pallas kernels  50.5 us (45%)
  starting transfers between devices  44.9 us (40%)
  waiting for transfers between devices  11 us (10%)
  local copies, waits for them, and re-layouts  2.91 us (3%)
  between operations  1.69 us (2%)
    ppermute x15, starting transfers between devices, send(): return lax.ppermute(x, 'seq', pairs)  20.9 us
    all_to_all x3, starting transfers between devices, in_groups(): lax.all_to_all(x, 'seq', 0, 0, tiled=True, axis_index_groups=groups_of)  13.3 us
    pallas_call x1, Pallas kernels, trunk_attention(): pl.pallas_call(functools.partial(trunk_kernel, heads, groups, first), gri...  12.3 us
    ppermute x1, starting transfers between devices, shards(): other = lax.ppermute(square, 'head', [(0, 1), (1, 0)])  10.7 us
    pallas_call x1, Pallas kernels, branch_linear(): pl.pallas_call(functools.partial(branch_kernel, heads), in_specs=[smem(),...  9.86 us
    pallas_call x1, Pallas kernels, near_attention(): pl.pallas_call(functools.partial(near_kernel, groups), grid=(steps,), in_...  8 us
    pallas_call x1, Pallas kernels, far_attention(): pl.pallas_call(functools.partial(far_kernel, heads, groups), grid=(steps,...  7.63 us
    all_to_all x3, waiting for transfers between devices, in_groups(): lax.all_to_all(x, 'seq', 0, 0, tiled=True, axis_index_groups=groups_of)  7.46 us
  transfers between devices with their start and end apart: 19, of which 4 were waited for; matrix products, arithmetic and copies ran while one was open for 0% of the time, Pallas kernels for 32%

profile of v8, /device:TPU:9, one launch (start us, length us, event | category | flops | bytes accessed | tf_op | source)
XLA Modules:
  0.0 111.4 jit_solution(6614874272291843521)
XLA Ops:
  0.6 0.0 copy-start
  0.6 0.0 copy-start.2
  0.7 0.8 collective-permute-start.1
  1.5 4.5 %block_sums.1 = (bf16[3,2,128,128]{3,2,1,0:T(8,128)(2,1)}, bf16[3,2,128,128]{3,2,1,0:T(8,128)(2,1)}, bf16[3,2,128,128]{3,2,1,0:T(8,128)(2,1)}, bf16[3,2,128,128]...) custom-call(f32[8,11]{1,0:T(8,128)} %gain_ref.7, bf16[4096,128]{1,0:T(8,128)(2,1)} %bitcast.14, ...), custom_call_target="tpu_custom_call" | custom-call | flops 134217728 | bytes 3145728 | tf_op jit(solution)/shard_map/block_sums/pallas_call | solution.py:97
  6.0 0.0 copy-start.16
  6.0 0.0 copy-start.15
  6.0 0.0 copy-start.14
  6.0 0.0 copy-start.9
  6.0 3.6 %all-to-all-start = ((bf16[4,2,128,128]{3,2,1,0:T(8,128)(2,1)}), bf16[4,2,128,128]{3,2,1,0:T(8,128)(2,1)S(1)}, u32[]{:S(2)}, u32[]{:S(2)}) async-start(bf16[4,2,128,128]{3,2,1,0:T(8,128)(2,1)} %get-tuple-element.30), calls=%async_computation | async-start | bytes 524288 | tf_op jit(solution)/shard_map/all_to_all | solution.py:637
  9.6 0.0 collective-permute-done.1
  9.6 0.0 copy-done.2
  9.7 4.2 %all-to-all-done.sums_ref = bf16[4,2,128,128]{3,2,1,0:T(8,128)(2,1)S(1)} async-done(((bf16[4,2,128,128]{3,2,1,0:T(8,128)(2,1)}), bf16[4,2,128,128]{3,2,1,0:T(8,128)(2,1)S(1)}, u32[]{:S(2)}, u32[]{:S(2)}) %all-to-all-start) | async-done | bytes 262176 | tf_op jit(solution)/shard_map/all_to_all | solution.py:637
  13.8 1.3 %collective-permute-start.5 = (bf16[1024,128]{1,0:T(8,128)(2,1)S(1)}, bf16[1024,128]{1,0:T(8,128)(2,1)S(1)}, u32[]{:S(2)}, u32[]{:S(2)}) collective-permute-start(bf16[1024,128]{1,0:T(8,128)(2,1)S(1)} %broadcast_select_fusion.3), channel_id=1, source_target_pairs={{24,8},{26,10},{28,12},{30,14},{25,9},{27,11},{29,13},{31,15}} | collective-permute-start | bytes 786440 | tf_op jit(solution)/shard_map/ppermute | solution.py:614
  15.1 0.0 copy-done
  15.1 1.3 %plane_sums.1 = (bf16[4,2,128,128]{3,2,1,0:T(8,128)(2,1)}, f32[2,128,128]{2,1,0:T(8,128)S(1)}) custom-call(s32[1]{0:T(128)} %bitcast.where_ref, f32[8,11]{1,0:T(8,128)S(1)} %copy-done, bf16[4,2,128,128]{3,2,1,0:T(8,128)(2,1)S(1)} %all-to-all-done.sums_ref), custom_call_target="tpu_custom_call" | custom-call | flops 524288 | bytes 1048576 | tf_op jit(solution)/shard_map/plane_sums/pallas_call | solution.py:150
  16.5 6.2 %all-to-all-start.1 = ((bf16[4,2,128,128]{3,2,1,0:T(8,128)(2,1)}), bf16[4,2,128,128]{3,2,1,0:T(8,128)(2,1)S(1)}, u32[]{:S(2)}, u32[]{:S(2)}) async-start(bf16[4,2,128,128]{3,2,1,0:T(8,128)(2,1)} %get-tuple-element.35), calls=%async_computation.1 | async-start | bytes 524288 | tf_op jit(solution)/shard_map/all_to_all | solution.py:637
  22.7 0.7 collective-permute-start.2
  23.4 0.0 copy-done.15
  23.4 0.7 collective-permute-start.3
  24.1 0.7 collective-permute-start.4
  24.8 0.0 collective-permute-done.5
  24.8 0.0 collective-permute-done.2
  24.9 0.0 collective-permute-done.3
  24.9 0.0 collective-permute-done.4
  24.9 3.3 %all-to-all-done.1.planes_ref = bf16[4,2,128,128]{3,2,1,0:T(8,128)(2,1)S(1)} async-done(((bf16[4,2,128,128]{3,2,1,0:T(8,128)(2,1)}), bf16[4,2,128,128]{3,2,1,0:T(8,128)(2,1)S(1)}, u32[]{:S(2)}, u32[]{:S(2)}) %all-to-all-start.1) | async-done | bytes 262176 | tf_op jit(solution)/shard_map/all_to_all | solution.py:637
  28.3 1.3 %collective-permute-start.10 = (bf16[4,2,128,128]{3,2,1,0:T(8,128)(2,1)S(1)}, bf16[4,2,128,128]{3,2,1,0:T(8,128)(2,1)S(1)}, u32[]{:S(2)}, u32[]{:S(2)}) collective-permute-start(bf16[4,2,128,128]{3,2,1,0:T(8,128)(2,1)S(1)} %add_convert_fusion.1), channel_id=1, source_target_pairs={{24,8},{26,10},{28,12},{30,14},{25,9},{27,11},{29,13},{31,15}} | collective-permute-start | bytes 786440 | tf_op jit(solution)/shard_map/ppermute | solution.py:614
  29.6 2.9 %collective-permute-start = (bf16[2048,128]{1,0:T(8,128)(2,1)S(1)}, bf16[2048,128]{1,0:T(8,128)(2,1)S(1)}, u32[]{:S(2)}, u32[]{:S(2)}) collective-permute-start(bf16[2048,128]{1,0:T(8,128)(2,1)S(1)} %pad_maximum_fusion), channel_id=1, source_target_pairs={{0,2},{2,4},{4,6},{6,8},{8,10},{10,12},{12,14},{14,16},{16,18},{18... | collective-permute-start | bytes 1572872 | tf_op jit(solution)/shard_map/ppermute | solution.py:614
  32.5 2.6 %collective-permute-start.6 = (bf16[1024,128]{1,0:T(8,128)(2,1)S(1)}, bf16[1024,128]{1,0:T(8,128)(2,1)S(1)}, u32[]{:S(2)}, u32[]{:S(2)}) collective-permute-start(bf16[1024,128]{1,0:T(8,128)(2,1)S(1)} %broadcast_select_fusion.2), channel_id=1, source_target_pairs={{8,0},{10,2},{12,4},{14,6},{24,16},{26,18},{28,20},{30,22},{9,1},{... | collective-permute-start | bytes 786440 | tf_op jit(solution)/shard_map/ppermute | solution.py:614
  35.1 2.4 %collective-permute-done.10 = bf16[4,2,128,128]{3,2,1,0:T(8,128)(2,1)S(1)} collective-permute-done((bf16[4,2,128,128]{3,2,1,0:T(8,128)(2,1)S(1)}, bf16[4,2,128,128]{3,2,1,0:T(8,128)(2,1)S(1)}, u32[]{:S(2)}, u32[]{:S(2)}) %collective-permute-start.10) | collective-permute-done | bytes 262176 | tf_op jit(solution)/shard_map/ppermute | solution.py:614
  37.6 0.1 broadcast_select_fusion
  37.6 1.3 %collective-permute-start.11 = (bf16[4,2,128,128]{3,2,1,0:T(8,128)(2,1)S(1)}, bf16[4,2,128,128]{3,2,1,0:T(8,128)(2,1)S(1)}, u32[]{:S(2)}, u32[]{:S(2)}) collective-permute-start(bf16[4,2,128,128]{3,2,1,0:T(8,128)(2,1)S(1)} %broadcast_select_fusion), channel_id=1, source_target_pairs={{8,0},{10,2},{12,4},{14,6},{24,16},{26,18},{28,20},{30,22},{9,1},{... | collective-permute-start | bytes 786440 | tf_op jit(solution)/shard_map/ppermute | solution.py:614
  39.0 7.6 %far_attention.1.far_hbm = bf16[4096,128]{1,0:T(8,128)(2,1)} custom-call(bf16[8192,128]{1,0:T(8,128)(2,1)} %bitcast.24, bf16[2048,128]{1,0:T(8,128)(2,1)} %bitcast.30, bf16[2048,128]{1,0:T(8,128)(2,1)} %bitcast.33, bf16[2048,128]{1,0:T(8,128)(2,1)} %bitcast.31, bf16[2048,128]{1,0:T(8,128)(2,1)} %bitcast.34), custom_call_target="tpu_custom_call" | custom-call | flops 2013265920 | bytes 6291456 | tf_op jit(solution)/shard_map/far_attention/pallas_call | solution.py:302
  46.6 0.0 collective-permute-done.6
  46.6 3.3 %collective-permute-start.9 = (bf16[1024,128]{1,0:T(8,128)(2,1)S(1)}, bf16[1024,128]{1,0:T(8,128)(2,1)S(1)}, u32[]{:S(2)}, u32[]{:S(2)}) collective-permute-start(bf16[1024,128]{1,0:T(8,128)(2,1)S(1)} %broadcast_select_fusion.1.rest_0_), channel_id=1, source_target_pairs={{0,6},{2,4},{4,2},{6,0},{8,14},{10,12},{12,10},{14,8},{16,22},{18,... | collective-permute-start | bytes 786440 | tf_op jit(solution)/shard_map/ppermute | solution.py:614
  50.6 1.4 %cross_sums.1 = (bf16[4,2,128,128]{3,2,1,0:T(8,128)(2,1)}, f32[2,128,128]{2,1,0:T(8,128)S(1)}) custom-call(s32[1]{0:T(128)} %bitcast.where_ref, f32[8,11]{1,0:T(8,128)S(1)} %copy-done, bf16[4,2,128,128]{3,2,1,0:T(8,128)(2,1)S(1)} %all-to-all-done.sums_ref, bf16[4,2,128,128]{3,2,1,0:T(8,128)(2,1)S(1)} %all-to-all-done.1.planes_ref), custom_call_target="tpu_custom_call" | custom-call | flops 2621440 | bytes 1048576 | tf_op jit(solution)/shard_map/cross_sums/pallas_call | solution.py:188
  52.0 3.5 %all-to-all-start.2 = ((bf16[4,2,128,128]{3,2,1,0:T(8,128)(2,1)}), bf16[4,2,128,128]{3,2,1,0:T(8,128)(2,1)S(1)}, u32[]{:S(2)}, u32[]{:S(2)}) async-start(bf16[4,2,128,128]{3,2,1,0:T(8,128)(2,1)} %get-tuple-element.38), calls=%async_computation.2 | async-start | bytes 524288 | tf_op jit(solution)/shard_map/all_to_all | solution.py:637
  55.5 1.5 %collective-permute-start.8 = (bf16[1024,128]{1,0:T(8,128)(2,1)S(1)}, bf16[1024,128]{1,0:T(8,128)(2,1)S(1)}, u32[]{:S(2)}, u32[]{:S(2)}) collective-permute-start(bf16[1024,128]{1,0:T(8,128)(2,1)S(1)} %broadcast_select_fusion.1.rest_0_), channel_id=1, source_target_pairs={{0,4},{2,6},{4,0},{6,2},{8,12},{10,14},{12,8},{14,10},{16,20},{18,... | collective-permute-start | bytes 786440 | tf_op jit(solution)/shard_map/ppermute | solution.py:614
  57.0 1.2 %collective-permute-start.7 = (bf16[1024,128]{1,0:T(8,128)(2,1)S(1)}, bf16[1024,128]{1,0:T(8,128)(2,1)}, u32[]{:S(2)}, u32[]{:S(2)}) collective-permute-start(bf16[1024,128]{1,0:T(8,128)(2,1)S(1)} %broadcast_select_fusion.1.rest_0_), channel_id=1, source_target_pairs={{0,2},{2,0},{4,6},{6,4},{8,10},{10,8},{12,14},{14,12},{16,18},{18,... | collective-permute-start | bytes 786440 | tf_op jit(solution)/shard_map/ppermute | solution.py:614
  58.2 0.0 collective-permute-done.11
  58.2 0.1 add_convert_fusion.rest_0_
  58.3 0.8 collective-permute-start.14
  59.1 0.0 collective-permute-done.pk_ref.pv_ref
  59.1 0.7 collective-permute-start.13
  59.8 0.0 collective-permute-done.9.rest_3_
  59.8 1.2 %collective-permute-start.12 = (bf16[4,2,128,128]{3,2,1,0:T(8,128)(2,1)S(1)}, bf16[4,2,128,128]{3,2,1,0:T(8,128)(2,1)S(1)}, u32[]{:S(2)}, u32[]{:S(2)}) collective-permute-start(bf16[4,2,128,128]{3,2,1,0:T(8,128)(2,1)S(1)} %add_convert_fusion.rest_0_), channel_id=1, source_target_pairs={{0,2},{2,0},{4,6},{6,4},{8,10},{10,8},{12,14},{14,12},{16,18},{18,... | collective-permute-start | bytes 786440 | tf_op jit(solution)/shard_map/ppermute | solution.py:614
  61.0 0.0 all-to-all-done.2.cross_ref
  61.0 0.7 copy-done.6
  61.7 12.3 %trunk_attention.1 = (f32[4096,128]{1,0:T(8,128)}, f32[4,8,128]{2,1,0:T(8,128)}) custom-call(s32[1]{0:T(128)} %bitcast.where_ref, f32[8,11]{1,0:T(8,128)} %gain_ref.7, bf16[4096,128]{1,0:T(8,128)(2,1)} %bitcast.27, bf16[4096,128]{1,0:T(8,128)(2,1)} %bitcast.15, bf16[4096,128]{1,0:T(8,128)(2,1)} %bitcast.17, bf16[4096,128]{1,0:T(8,128)(2,1)} %bitcast.28, ...), custom_call_target="tpu_custom_call" | custom-call | flops 2415919104 | bytes 6291456 | tf_op jit(solution)/shard_map/trunk_attention/pallas_call | solution.py:373
  74.1 0.0 copy-done.1
  74.1 0.0 collective-permute-done.8.rest_2_
  74.1 0.0 collective-permute-done.7.rest_1_
  74.1 0.7 copy-done.13
  74.8 8.0 %near_attention.1.near_hbm = bf16[4096,128]{1,0:T(8,128)(2,1)} custom-call(s32[1]{0:T(128)} %bitcast.where_ref, s32[1]{0:T(128)S(6)} %copy.14.fork_ref, bf16[8192,128]{1,0:T(8,128)(2,1)} %bitcast.25, bf16[2048,128]{1,0:T(8,128)(2,1)} %bitcast.32, bf16[2048,128]{1,0:T(8,128)(2,1)} %bitcast.35, bf16[1024,128]{1,0:T(8,128)(2,1)} %copy-done.8, ...), custom_call_target="tpu_custom_call" | custom-call | flops 2013265920 | bytes 6291456 | tf_op jit(solution)/shard_map/near_attention/pallas_call | solution.py:428
  82.8 0.0 collective-permute-done.14.rest_3_
  82.8 0.0 collective-permute-done.13.rest_2_
  82.8 0.0 collective-permute-done.12.rest_1_
  82.8 0.7 copy-done.3
  83.5 0.1 copy-done.4
  83.6 0.1 copy-done.5
  83.7 9.9 %branch_linear.1 = (f32[8192,128]{1,0:T(8,128)}, f32[12,8,128]{2,1,0:T(8,128)}) custom-call(s32[1]{0:T(128)} %bitcast.where_ref, s32[1]{0:T(128)S(6)} %copy.14.fork_ref, f32[4,8,128]{2,1,0:T(8,128)} %get-tuple-element.41.trunk_square, bf16[8192,128]{1,0:T(8,128)(2,1)} %bitcast.13, bf16[4096,128]{1,0:T(8,128)(2,1)} %near_attention.1.near_hbm, ...), custom_call_target="tpu_custom_call" | custom-call | flops 536870912 | bytes 8388608 | tf_op jit(solution)/shard_map/branch_linear/pallas_call | solution.py:494
  93.6 10.7 %collective-permute-start.15 = (f32[12,8,128]{2,1,0:T(8,128)}, f32[12,8,128]{2,1,0:T(8,128)S(1)}, u32[]{:S(2)}, u32[]{:S(2)}) collective-permute-start(f32[12,8,128]{2,1,0:T(8,128)} %get-tuple-element.53.square_ref), channel_id=1, source_target_pairs={{0,1},{1,0},{2,3},{3,2},{4,5},{5,4},{6,7},{7,6},{8,9},{9,8},{10,11... | collective-permute-start | bytes 147464 | tf_op jit(solution)/shard_map/ppermute | solution.py:678
  104.3 1.1 collective-permute-done.15.other_ref
  105.4 0.6 copy-done.10
  106.0 5.4 %normalize.1 = (bf16[4096,128]{1,0:T(8,128)(2,1)}, bf16[8192,128]{1,0:T(8,128)(2,1)}) custom-call(f32[4096,128]{1,0:T(8,128)} %get-tuple-element.40.trunk_hbm, f32[8192,128]{1,0:T(8,128)} %get-tuple-element.52.branch_hbm, f32[12,8,128]{2,1,0:T(8,128)} %get-tuple-element.53.square_ref, f32[12,8,128]{2,1,0:T(8,128)} %copy-done.10), custom_call_target="tpu_custom_call" | custom-call | flops 3145728 | bytes 9437184 | tf_op jit(solution)/shard_map/normalize/pallas_call | solution.py:561
  (24 shorter events, 0.2 us)
Async XLA Ops:
  0.6 14.5 %copy-start = (f32[8,11]{1,0:T(8,128)S(1)}, f32[8,11]{1,0:T(8,128)}, u32[]{:S(2)}) copy-start(f32[8,11]{1,0:T(8,128)} %gain_ref.7) | copy-start | bytes 1060
  0.6 9.0 %copy-start.2 = (bf16[512,2,128]{2,1,0:T(2,128)(2,1)S(1)}, bf16[512,2,128]{2,1,0:T(2,128)(2,1)}, u32[]{:S(2)}) copy-start(bf16[512,2,128]{2,1,0:T(2,128)(2,1)} %param.16) | copy-start | bytes 786436
  0.7 9.0 %collective-permute-start.1 = (bf16[1024,128]{1,0:T(8,128)(2,1)}, bf16[1024,128]{1,0:T(8,128)(2,1)S(1)}, u32[]{:S(2)}, u32[]{:S(2)}) collective-permute-start(bf16[1024,128]{1,0:T(8,128)(2,1)} %bitcast.21), channel_id=1, source_target_pairs={{30,26},{28,24},{31,27},{29,25}} | collective-permute-start | bytes 786440 | tf_op jit(solution)/shard_map/ppermute | solution.py:614
  6.0 16.7 %copy-start.16 = (bf16[3,2,128,128]{3,2,1,0:T(8,128)(2,1)S(1)}, bf16[3,2,128,128]{3,2,1,0:T(8,128)(2,1)}, u32[]{:S(2)}) copy-start(bf16[3,2,128,128]{3,2,1,0:T(8,128)(2,1)} %get-tuple-element.32) | copy-start | bytes 589828
  6.0 17.4 %copy-start.15 = (bf16[3,2,128,128]{3,2,1,0:T(8,128)(2,1)S(1)}, bf16[3,2,128,128]{3,2,1,0:T(8,128)(2,1)}, u32[]{:S(2)}) copy-start(bf16[3,2,128,128]{3,2,1,0:T(8,128)(2,1)} %get-tuple-element.33) | copy-start | bytes 589828
  6.0 18.1 %copy-start.14 = (bf16[3,2,128,128]{3,2,1,0:T(8,128)(2,1)S(1)}, bf16[3,2,128,128]{3,2,1,0:T(8,128)(2,1)}, u32[]{:S(2)}) copy-start(bf16[3,2,128,128]{3,2,1,0:T(8,128)(2,1)} %get-tuple-element.34) | copy-start | bytes 589828
  6.0 22.1 %copy-start.9 = (bf16[3,2,128,128]{3,2,1,0:T(8,128)(2,1)S(1)}, bf16[3,2,128,128]{3,2,1,0:T(8,128)(2,1)}, u32[]{:S(2)}) copy-start(bf16[3,2,128,128]{3,2,1,0:T(8,128)(2,1)} %get-tuple-element.50) | copy-start | bytes 589828
  6.0 7.8 %all-to-all-start = ((bf16[4,2,128,128]{3,2,1,0:T(8,128)(2,1)}), bf16[4,2,128,128]{3,2,1,0:T(8,128)(2,1)S(1)}, u32[]{:S(2)}, u32[]{:S(2)}) async-start(bf16[4,2,128,128]{3,2,1,0:T(8,128)(2,1)} %get-tuple-element.30), calls=%async_computation | async-start | bytes 524288 | tf_op jit(solution)/shard_map/all_to_all | solution.py:637
  9.6 20.0 %copy-start.7 = (bf16[512,2,128]{2,1,0:T(2,128)(2,1)S(1)}, bf16[512,2,128]{2,1,0:T(2,128)(2,1)}, u32[]{:S(2)}) copy-start(bf16[512,2,128]{2,1,0:T(2,128)(2,1)} %param.17) | copy-start | bytes 786436
  13.8 10.9 %collective-permute-start.5 = (bf16[1024,128]{1,0:T(8,128)(2,1)S(1)}, bf16[1024,128]{1,0:T(8,128)(2,1)S(1)}, u32[]{:S(2)}, u32[]{:S(2)}) collective-permute-start(bf16[1024,128]{1,0:T(8,128)(2,1)S(1)} %broadcast_select_fusion.3), channel_id=1, source_target_pairs={{24,8},{26,10},{28,12},{30,14},{25,9},{27,11},{29,13},{31,15}} | collective-permute-start | bytes 786440 | tf_op jit(solution)/shard_map/ppermute | solution.py:614
  16.5 11.7 %all-to-all-start.1 = ((bf16[4,2,128,128]{3,2,1,0:T(8,128)(2,1)}), bf16[4,2,128,128]{3,2,1,0:T(8,128)(2,1)S(1)}, u32[]{:S(2)}, u32[]{:S(2)}) async-start(bf16[4,2,128,128]{3,2,1,0:T(8,128)(2,1)} %get-tuple-element.35), calls=%async_computation.1 | async-start | bytes 524288 | tf_op jit(solution)/shard_map/all_to_all | solution.py:637
  22.7 2.1 %collective-permute-start.2 = (bf16[3,2,128,128]{3,2,1,0:T(8,128)(2,1)S(1)}, bf16[3,2,128,128]{3,2,1,0:T(8,128)(2,1)S(1)}, u32[]{:S(2)}, u32[]{:S(2)}) collective-permute-start(bf16[3,2,128,128]{3,2,1,0:T(8,128)(2,1)S(1)} %copy-done.16), channel_id=1, source_target_pairs={{30,24},{31,25}} | collective-permute-start | bytes 589832 | tf_op jit(solution)/shard_map/ppermute | solution.py:614
  23.4 1.5 %collective-permute-start.3 = (bf16[3,2,128,128]{3,2,1,0:T(8,128)(2,1)S(1)}, bf16[3,2,128,128]{3,2,1,0:T(8,128)(2,1)S(1)}, u32[]{:S(2)}, u32[]{:S(2)}) collective-permute-start(bf16[3,2,128,128]{3,2,1,0:T(8,128)(2,1)S(1)} %copy-done.15), channel_id=1, source_target_pairs={{30,26},{31,27}} | collective-permute-start | bytes 589832 | tf_op jit(solution)/shard_map/ppermute | solution.py:614
  24.1 0.8 collective-permute-start.4
  28.3 9.3 %collective-permute-start.10 = (bf16[4,2,128,128]{3,2,1,0:T(8,128)(2,1)S(1)}, bf16[4,2,128,128]{3,2,1,0:T(8,128)(2,1)S(1)}, u32[]{:S(2)}, u32[]{:S(2)}) collective-permute-start(bf16[4,2,128,128]{3,2,1,0:T(8,128)(2,1)S(1)} %add_convert_fusion.1), channel_id=1, source_target_pairs={{24,8},{26,10},{28,12},{30,14},{25,9},{27,11},{29,13},{31,15}} | collective-permute-start | bytes 786440 | tf_op jit(solution)/shard_map/ppermute | solution.py:614
  29.6 29.5 %collective-permute-start = (bf16[2048,128]{1,0:T(8,128)(2,1)S(1)}, bf16[2048,128]{1,0:T(8,128)(2,1)S(1)}, u32[]{:S(2)}, u32[]{:S(2)}) collective-permute-start(bf16[2048,128]{1,0:T(8,128)(2,1)S(1)} %pad_maximum_fusion), channel_id=1, source_target_pairs={{0,2},{2,4},{4,6},{6,8},{8,10},{10,12},{12,14},{14,16},{16,18},{18... | collective-permute-start | bytes 1572872 | tf_op jit(solution)/shard_map/ppermute | solution.py:614
  32.5 14.1 %collective-permute-start.6 = (bf16[1024,128]{1,0:T(8,128)(2,1)S(1)}, bf16[1024,128]{1,0:T(8,128)(2,1)S(1)}, u32[]{:S(2)}, u32[]{:S(2)}) collective-permute-start(bf16[1024,128]{1,0:T(8,128)(2,1)S(1)} %broadcast_select_fusion.2), channel_id=1, source_target_pairs={{8,0},{10,2},{12,4},{14,6},{24,16},{26,18},{28,20},{30,22},{9,1},{... | collective-permute-start | bytes 786440 | tf_op jit(solution)/shard_map/ppermute | solution.py:614
  37.6 20.5 %collective-permute-start.11 = (bf16[4,2,128,128]{3,2,1,0:T(8,128)(2,1)S(1)}, bf16[4,2,128,128]{3,2,1,0:T(8,128)(2,1)S(1)}, u32[]{:S(2)}, u32[]{:S(2)}) collective-permute-start(bf16[4,2,128,128]{3,2,1,0:T(8,128)(2,1)S(1)} %broadcast_select_fusion), channel_id=1, source_target_pairs={{8,0},{10,2},{12,4},{14,6},{24,16},{26,18},{28,20},{30,22},{9,1},{... | collective-permute-start | bytes 786440 | tf_op jit(solution)/shard_map/ppermute | solution.py:614
  46.6 27.5 %copy-start.8 = (bf16[1024,128]{1,0:T(8,128)(2,1)}, bf16[1024,128]{1,0:T(8,128)(2,1)S(1)}, u32[]{:S(2)}) copy-start(bf16[1024,128]{1,0:T(8,128)(2,1)S(1)} %broadcast_select_fusion.1.rest_0_) | copy-start | bytes 786436
  46.6 13.2 %collective-permute-start.9 = (bf16[1024,128]{1,0:T(8,128)(2,1)S(1)}, bf16[1024,128]{1,0:T(8,128)(2,1)S(1)}, u32[]{:S(2)}, u32[]{:S(2)}) collective-permute-start(bf16[1024,128]{1,0:T(8,128)(2,1)S(1)} %broadcast_select_fusion.1.rest_0_), channel_id=1, source_target_pairs={{0,6},{2,4},{4,2},{6,0},{8,14},{10,12},{12,10},{14,8},{16,22},{18,... | collective-permute-start | bytes 786440 | tf_op jit(solution)/shard_map/ppermute | solution.py:614
  52.0 9.0 %all-to-all-start.2 = ((bf16[4,2,128,128]{3,2,1,0:T(8,128)(2,1)}), bf16[4,2,128,128]{3,2,1,0:T(8,128)(2,1)S(1)}, u32[]{:S(2)}, u32[]{:S(2)}) async-start(bf16[4,2,128,128]{3,2,1,0:T(8,128)(2,1)} %get-tuple-element.38), calls=%async_computation.2 | async-start | bytes 524288 | tf_op jit(solution)/shard_map/all_to_all | solution.py:637
  55.5 18.6 %collective-permute-start.8 = (bf16[1024,128]{1,0:T(8,128)(2,1)S(1)}, bf16[1024,128]{1,0:T(8,128)(2,1)S(1)}, u32[]{:S(2)}, u32[]{:S(2)}) collective-permute-start(bf16[1024,128]{1,0:T(8,128)(2,1)S(1)} %broadcast_select_fusion.1.rest_0_), channel_id=1, source_target_pairs={{0,4},{2,6},{4,0},{6,2},{8,12},{10,14},{12,8},{14,10},{16,20},{18,... | collective-permute-start | bytes 786440 | tf_op jit(solution)/shard_map/ppermute | solution.py:614
  57.0 17.1 %collective-permute-start.7 = (bf16[1024,128]{1,0:T(8,128)(2,1)S(1)}, bf16[1024,128]{1,0:T(8,128)(2,1)}, u32[]{:S(2)}, u32[]{:S(2)}) collective-permute-start(bf16[1024,128]{1,0:T(8,128)(2,1)S(1)} %broadcast_select_fusion.1.rest_0_), channel_id=1, source_target_pairs={{0,2},{2,0},{4,6},{6,4},{8,10},{10,8},{12,14},{14,12},{16,18},{18,... | collective-permute-start | bytes 786440 | tf_op jit(solution)/shard_map/ppermute | solution.py:614
  58.3 15.8 %copy-start.1 = (bf16[4,2,128,128]{3,2,1,0:T(8,128)(2,1)}, bf16[4,2,128,128]{3,2,1,0:T(8,128)(2,1)S(1)}, u32[]{:S(2)}) copy-start(bf16[4,2,128,128]{3,2,1,0:T(8,128)(2,1)S(1)} %add_convert_fusion.rest_0_) | copy-start | bytes 786436
  58.3 24.5 %collective-permute-start.14 = (bf16[4,2,128,128]{3,2,1,0:T(8,128)(2,1)S(1)}, bf16[4,2,128,128]{3,2,1,0:T(8,128)(2,1)S(1)}, u32[]{:S(2)}, u32[]{:S(2)}) collective-permute-start(bf16[4,2,128,128]{3,2,1,0:T(8,128)(2,1)S(1)} %add_convert_fusion.rest_0_), channel_id=1, source_target_pairs={{0,6},{2,4},{4,2},{6,0},{8,14},{10,12},{12,10},{14,8},{16,22},{18,... | collective-permute-start | bytes 786440 | tf_op jit(solution)/shard_map/ppermute | solution.py:614
  59.1 1.9 %copy-start.11 = (bf16[2048,128]{1,0:T(8,128)(2,1)}, bf16[2048,128]{1,0:T(8,128)(2,1)S(1)}, u32[]{:S(2)}) copy-start(bf16[2048,128]{1,0:T(8,128)(2,1)S(1)} %collective-permute-done.pk_ref.pv_ref) | copy-start | bytes 1572868
  59.1 23.7 %collective-permute-start.13 = (bf16[4,2,128,128]{3,2,1,0:T(8,128)(2,1)S(1)}, bf16[4,2,128,128]{3,2,1,0:T(8,128)(2,1)S(1)}, u32[]{:S(2)}, u32[]{:S(2)}) collective-permute-start(bf16[4,2,128,128]{3,2,1,0:T(8,128)(2,1)S(1)} %add_convert_fusion.rest_0_), channel_id=1, source_target_pairs={{0,4},{2,6},{4,0},{6,2},{8,12},{10,14},{12,8},{14,10},{16,20},{18,... | collective-permute-start | bytes 786440 | tf_op jit(solution)/shard_map/ppermute | solution.py:614
  59.8 14.3 %copy-start.12 = (bf16[1024,128]{1,0:T(8,128)(2,1)}, bf16[1024,128]{1,0:T(8,128)(2,1)S(1)}, u32[]{:S(2)}) copy-start(bf16[1024,128]{1,0:T(8,128)(2,1)S(1)} %collective-permute-done.9.rest_3_) | copy-start | bytes 786436
  59.8 23.0 %collective-permute-start.12 = (bf16[4,2,128,128]{3,2,1,0:T(8,128)(2,1)S(1)}, bf16[4,2,128,128]{3,2,1,0:T(8,128)(2,1)S(1)}, u32[]{:S(2)}, u32[]{:S(2)}) collective-permute-start(bf16[4,2,128,128]{3,2,1,0:T(8,128)(2,1)S(1)} %add_convert_fusion.rest_0_), channel_id=1, source_target_pairs={{0,2},{2,0},{4,6},{6,4},{8,10},{10,8},{12,14},{14,12},{16,18},{18,... | collective-permute-start | bytes 786440 | tf_op jit(solution)/shard_map/ppermute | solution.py:614
  61.0 0.7 copy-start.6
  74.1 0.7 copy-start.13
  82.8 0.7 copy-start.3
  82.8 0.8 copy-start.4
  82.8 0.9 copy-start.5
  93.6 11.8 %collective-permute-start.15 = (f32[12,8,128]{2,1,0:T(8,128)}, f32[12,8,128]{2,1,0:T(8,128)S(1)}, u32[]{:S(2)}, u32[]{:S(2)}) collective-permute-start(f32[12,8,128]{2,1,0:T(8,128)} %get-tuple-element.53.square_ref), channel_id=1, source_target_pairs={{0,1},{1,0},{2,3},{3,2},{4,5},{5,4},{6,7},{7,6},{8,9},{9,8},{10,11... | collective-permute-start | bytes 147464 | tf_op jit(solution)/shard_map/ppermute | solution.py:678
  105.4 0.6 copy-start.10
